TPU v7x, 32 devices: a whole 2x2x4 slice. The times are simulated.
32 devices in a mesh: dp: 8 (over z, x), expert: 4 (over y, core).
Axes of the slice: x: 2, y: 2, z: 4, core: 2. Of those that a mesh axis runs over, the one named last changes fastest.
Arguments:
- grad_tokens: bfloat16 [4096, 2048], P(('dp', 'expert')), may hold values from -6 to 6
- routes: int32 [4096, 2], P(('dp', 'expert')), may hold values from 0 to 3, all different within a row; in each aligned block of 128 rows (0 to 127, 128 to 255, ...) at most 96 rows name the same one
- combine: bfloat16 [4096, 2], P(('dp', 'expert')), may hold values from 0.099609375 to 1
- down_weight: bfloat16 [4, 768, 2048], P('expert'), may hold values from -0.21875 to 0.21875
- saved_pre: bfloat16 [4, 8, 4, 96, 1536], P('expert', 'dp'), may hold values from -6 to 6
Outputs:
- pre_grad: bfloat16 [4, 8, 4, 96, 1536], P('expert', 'dp')
- down_grad: float32 [4, 1572864], P('expert', 'dp')
- gate_grad: float32 [4096, 2], P(('dp', 'expert'))
Inputs may be any that keep to these rules, and one draw needn't show every extreme that they name: In each device's block of 128 tokens no expert is named by more than 96 routes, a bound that some blocks reach; a token's routes name different experts.
All inputs are finite; a program needn't handle non-finite values.
Results may differ from a plain program's by a relative error of at most 0.0029.
Values may be sent and summed in bfloat16 or wider, within the bound.
No kernel may reach another device: no remote copies, remote signals or barrier semaphores. Data moves between devices by JAX's collectives and lax.ppermute only.
A program may use at most 64 MiB of HBM per device.

v0:
```python
import jax
import jax.numpy as jnp
from jax import lax
from jax.sharding import PartitionSpec as P


def per_device(grad_tokens, routes, combine, down_weight, saved_pre):
    experts = lax.axis_size("expert")
    tok_rows, route_count = routes.shape
    capacity = saved_pre.shape[3]
    model_width = grad_tokens.shape[1]
    hidden = down_weight.shape[1]
    flat_routes = routes.reshape(-1)
    onehot = (flat_routes[:, None] == jnp.arange(experts, dtype=jnp.int32)[None, :]).astype(
        jnp.int32
    )
    before = jnp.cumsum(onehot, axis=0) - onehot
    position = jnp.sum(before * onehot, axis=1)
    slot_id = flat_routes * capacity + position
    slot_grid = jnp.arange(experts * capacity, dtype=jnp.int32)
    chosen = slot_grid[:, None] == slot_id[None, :]
    placing = jnp.any(chosen.reshape(experts * capacity, tok_rows, route_count), axis=2).astype(
        jnp.bfloat16
    )
    outgoing = jnp.dot(placing, grad_tokens, preferred_element_type=jnp.float32).astype(
        jnp.bfloat16
    )
    combine_flat = combine.reshape(-1).astype(jnp.float32)
    out_weight = jnp.sum(jnp.where(chosen, combine_flat[None, :], 0.0), axis=1).astype(jnp.bfloat16)
    arrived, arrived_weight = (
        lax.all_to_all(
            outgoing.reshape(experts, capacity, model_width),
            "expert",
            split_axis=0,
            concat_axis=0,
            tiled=True,
        ),
        lax.all_to_all(
            out_weight.reshape(experts, capacity), "expert", split_axis=0, concat_axis=0, tiled=True
        ),
    )
    slot_rows = arrived.reshape(-1, model_width)
    slot_weight = arrived_weight.reshape(-1).astype(jnp.float32)
    down_rows = down_weight[0]
    raw_grad = lax.dot_general(
        slot_rows, down_rows, (((1,), (1,)), ((), ())), preferred_element_type=jnp.float32
    )
    pre_acts = saved_pre.reshape(-1, 2 * hidden).astype(jnp.float32)
    gate_pre = pre_acts[:, :hidden]
    up_pre = pre_acts[:, hidden:]
    logistic = jax.nn.sigmoid(gate_pre)
    activated = gate_pre * logistic
    hidden_act = activated * up_pre
    slot_gate = jnp.sum(hidden_act * raw_grad, axis=1)
    hidden_delta = slot_weight[:, None] * raw_grad
    gate_delta = hidden_delta * up_pre * logistic * (1.0 + gate_pre * (1.0 - logistic))
    up_delta = hidden_delta * activated
    pre_grad = (
        jnp.concatenate([gate_delta, up_delta], axis=1)
        .astype(jnp.bfloat16)
        .reshape(saved_pre.shape)
    )
    scaled = (slot_weight[:, None] * hidden_act).astype(jnp.bfloat16)
    whole_term = lax.dot_general(
        scaled, slot_rows, (((0,), (0,)), ((), ())), preferred_element_type=jnp.float32
    )
    summed = lax.psum_scatter(whole_term.reshape(-1), "dp", scatter_dimension=0, tiled=True)
    down_grad = (summed / lax.axis_size("dp"))[None]
    slot_values = slot_gate.reshape(experts, capacity)
    returned = lax.all_to_all(slot_values, "expert", split_axis=0, concat_axis=0, tiled=True)
    returned_flat = returned.reshape(-1)
    gate_flat = jnp.sum(jnp.where(chosen, returned_flat[:, None], 0.0), axis=0)
    gate_grad = gate_flat.reshape(tok_rows, route_count)
    return (pre_grad, down_grad, gate_grad)


def solution(mesh):
    placed = (
        P(("dp", "expert"), None),
        P(("dp", "expert"), None),
        P(("dp", "expert"), None),
        P("expert", None, None),
        P("expert", "dp", None, None, None),
    )
    return jax.shard_map(
        per_device,
        mesh=mesh,
        in_specs=placed,
        out_specs=(
            P("expert", "dp", None, None, None),
            P("expert", "dp"),
            P(("dp", "expert"), None),
        ),
        check_vma=False,
    )
```

profile of v0, /device:TPU:0, one launch (start us, length us, event | category | flops | bytes accessed | tf_op | source)
XLA Modules:
  0.0 288.4 jit_solution(8997613898320382417)
XLA Ops:
  7.2 0.0 copy-start
  7.2 0.9 copy.38
  8.1 0.1 eq.47
  8.3 0.1 reshape.129
  8.4 1.2 reduce-window.6
  9.6 0.1 slice.16
  9.7 0.1 copy.40
  9.9 0.1 copy.41
  10.0 0.1 add_bitcast_fusion
  10.1 0.1 reduce_sum.40
  10.2 0.1 copy.44
  10.3 0.7 multiply_add_fusion
  11.0 2.8 convolution_convert_fusion
  13.8 4.3 %all-to-all-start.1 = ((bf16[4,96,2048]{2,1,0:T(8,128)(2,1)}), bf16[4,96,2048]{2,1,0:T(8,128)(2,1)}, u32[]{:S(2)}, u32[]{:S(2)}) async-start(bf16[4,96,2048]{2,1,0:T(8,128)(2,1)} %bitcast.41), calls=%async_computation.1 | async-start | bytes 3145728 | tf_op jit(solution)/shard_map/all_to_all | solution.py:31
  18.1 3.0 %bitcast_convert_fusion = f32[384,1536]{1,0:T(8,128)} fusion(bf16[1,1,4,96,1536]{4,3,2,1,0:T(8,128)(2,1)} %param.9), kind=kLoop, calls=%fused_computation.5 | loop fusion | flops 589824 | bytes 3538944 | tf_op jit(solution)/shard_map/convert_element_type | solution.py:48
  21.1 17.8 %all-to-all-done.1 = bf16[4,96,2048]{2,1,0:T(8,128)(2,1)} async-done(((bf16[4,96,2048]{2,1,0:T(8,128)(2,1)}), bf16[4,96,2048]{2,1,0:T(8,128)(2,1)}, u32[]{:S(2)}, u32[]{:S(2)}) %all-to-all-start.1) | async-done | bytes 1572896 | tf_op jit(solution)/shard_map/all_to_all | solution.py:31
  38.9 0.0 copy-done
  38.9 0.0 copy-start.1
  38.9 4.6 %multiply_reduce_fusion = (f32[384]{0:T(512)S(1)}, f32[384,768]{1,0:T(8,128)}) fusion(f32[384,1536]{1,0:T(8,128)} %bitcast_convert_fusion, bf16[384,2048]{1,0:T(8,128)(2,1)} %bitcast.3, bf16[1,768,2048]{2,1,0:T(8,128)(2,1)S(1)} %copy-done), kind=kOutput, calls=%fused_computation.6 | convolution fusion | flops 1210023552 | bytes 8259072 | tf_op jit(solution)/shard_map/dot_general | solution.py:45
  43.5 0.7 all_to_all.15
  44.1 3.2 %all-to-all-start.2 = ((f32[4,1,96]{2,1,0:T(1,128)}), f32[4,1,96]{2,1,0:T(1,128)S(1)}, u32[]{:S(2)}, u32[]{:S(2)}) async-start(f32[4,1,96]{2,1,0:T(1,128)} %all_to_all.15), calls=%async_computation.2 | async-start | bytes 4096 | tf_op jit(solution)/shard_map/all_to_all | solution.py:70
  47.4 0.0 all-reduce.3.cloned.1.call-start
  47.4 0.0 copy-done.1
  47.5 0.1 copy.42
  47.6 0.1 reshape.135
  47.7 3.3 %all-to-all-done.2 = f32[4,1,96]{2,1,0:T(1,128)S(1)} async-done(((f32[4,1,96]{2,1,0:T(1,128)}), f32[4,1,96]{2,1,0:T(1,128)S(1)}, u32[]{:S(2)}, u32[]{:S(2)}) %all-to-all-start.2) | async-done | bytes 1568 | tf_op jit(solution)/shard_map/all_to_all | solution.py:70
  51.0 0.5 broadcast.48
  51.5 0.7 reduce.7
  52.2 0.1 broadcast_in_dim.36
  52.3 0.2 select_reduce_fusion
  52.5 0.1 convert_element_type.77
  52.6 6.1 %all_to_all.20 = bf16[4,1,96]{2,1,0:T(2,128)(2,1)S(1)} all-to-all(bf16[4,1,96]{2,1,0:T(2,128)(2,1)S(1)} %convert_element_type.77), channel_id=1, replica_groups=mesh['dp'=8,'expert'=4] {'expert'}, dimensions={0} | all-to-all | bytes 1536 | tf_op jit(solution)/shard_map/all_to_all | solution.py:38
  58.7 0.1 reshape.136
  58.8 4.1 %convolution_bitcast_fusion = f32[96,16,8,128]{3,2,1,0:T(8,128)S(1)} fusion(bf16[384,2048]{1,0:T(8,128)(2,1)} %bitcast.3, f32[384]{0:T(512)S(1)} %reshape.136, f32[384,1536]{1,0:T(8,128)} %bitcast_convert_fusion), kind=kOutput, calls=%fused_computation.3 | convolution fusion | flops 1210023936 | bytes 10225152 | tf_op jit(solution)/shard_map/dot_general | solution.py:64
  62.9 4.1 %copy.47 = f32[96,16,8,128]{3,1,2,0:T(8,128)} copy(f32[96,16,8,128]{3,2,1,0:T(8,128)S(1)} %convolution_bitcast_fusion) | data formatting | bytes 12582912
  67.0 0.0 copy-start.2
  67.0 0.0 all-reduce.3.cloned.1.call-update
  67.0 0.6 copy-done.2
  67.6 0.6 dynamic-slice
  68.9 0.1 reshape.134
  69.0 0.6 copy.45
  69.6 2.6 multiply_convert_fusion.2
  72.2 1.1 pad_maximum_fusion
  73.3 206.2 %all-reduce.3.cloned.1.call-done = f32[1572864]{0:T(1024)} async-done(((f32[1572864]{0:T(1024)}), f32[1572864]{0:T(1024)}) %all-reduce.3.cloned.1.call-update) | async-done | bytes 6291472
  279.5 2.1 dynamic-slice_multiply_fusion
  (7 shorter events, 0.1 us)
Async XLA Ops:
  7.2 31.8 %copy-start = (bf16[1,768,2048]{2,1,0:T(8,128)(2,1)S(1)}, bf16[1,768,2048]{2,1,0:T(8,128)(2,1)}, u32[]{:S(2)}) copy-start(bf16[1,768,2048]{2,1,0:T(8,128)(2,1)} %param.8) | copy-start | bytes 9437188
  13.8 25.2 %all-to-all-start.1 = ((bf16[4,96,2048]{2,1,0:T(8,128)(2,1)}), bf16[4,96,2048]{2,1,0:T(8,128)(2,1)}, u32[]{:S(2)}, u32[]{:S(2)}) async-start(bf16[4,96,2048]{2,1,0:T(8,128)(2,1)} %bitcast.41), calls=%async_computation.1 | async-start | bytes 3145728 | tf_op jit(solution)/shard_map/all_to_all | solution.py:31
  38.9 8.5 %copy-start.1 = (bf16[128,2]{0,1:T(2,128)(2,1)S(1)}, bf16[128,2]{0,1:T(2,128)(2,1)}, u32[]{:S(2)}) copy-start(bf16[128,2]{0,1:T(2,128)(2,1)} %param.7) | copy-start | bytes 1540
  44.1 6.9 %all-to-all-start.2 = ((f32[4,1,96]{2,1,0:T(1,128)}), f32[4,1,96]{2,1,0:T(1,128)S(1)}, u32[]{:S(2)}, u32[]{:S(2)}) async-start(f32[4,1,96]{2,1,0:T(1,128)} %all_to_all.15), calls=%async_computation.2 | async-start | bytes 4096 | tf_op jit(solution)/shard_map/all_to_all | solution.py:70
  47.4 232.1 %all-reduce.3.cloned.1.call-start = ((), (), s32[]{:S(2)}) async-start(), calls=%async_computation.3 | async-start | bytes 12582912
  67.0 0.7 copy-start.2
Sparse Core Ops, SparseCore 0:
  67.1 212.3 all-reduce.2
where the time goes:
time: 289 us; the launch traced here: 288 us
  waiting for transfers between devices  227 us (79%)
  between operations  14.8 us (5%)
  other arithmetic  11.7 us (4%)
  matrix products  11.4 us (4%)
  local copies, waits for them, and re-layouts  9.48 us (3%)
  starting transfers between devices  7.6 us (3%)
  blocking collectives  6.08 us (2%)
    unnamed x2, waiting for transfers between devices  206 us
    all_to_all x1, waiting for transfers between devices, per_device(): lax.all_to_all(outgoing.reshape(experts, capacity, model_width), 'expert'...  17.8 us
    unnamed x10, local copies, waits for them, and re-layouts  6.9 us
    all_to_all x1, blocking collectives, per_device(): lax.all_to_all(out_weight.reshape(experts, capacity), 'expert', split_axi...  6.08 us
  transfers between devices with their start and end apart: 3, of which 3 were waited for; matrix products, arithmetic and copies ran while one was open for 3% of the time, Pallas kernels for 0%

commit v1 on v0

v1 whole, which is shorter than its diff:
```python
import functools

import jax
import jax.numpy as jnp
from jax import lax
from jax.experimental import pallas as pl
from jax.experimental.pallas import tpu as pltpu
from jax.sharding import PartitionSpec as P

F32 = jnp.float32
BF16 = jnp.bfloat16
AXES = ("dp", "expert")
VMEM_LIMIT = 56 * 1024 * 1024
CHUNKS = ((3, "x"), (2, "z"), (3, "x"))


def _send(value, dp_mask, expert_mask):
    dps, experts = lax.axis_size("dp"), lax.axis_size("expert")
    pairs = [
        (d * experts + e, (d ^ dp_mask) * experts + (e ^ expert_mask))
        for d in range(dps)
        for e in range(experts)
    ]
    return lax.ppermute(value, AXES, pairs)


def _choice(info, expert, capacity):
    tokens = info.shape[1]
    first, second = info[0:1, :] == expert, info[1:2, :] == expert
    named = jnp.where(first | second, 1.0, 0.0)
    weight = jnp.where(first, info[2:3, :], 0.0) + jnp.where(second, info[3:4, :], 0.0)
    row = lax.broadcasted_iota(jnp.int32, (tokens, tokens), 0)
    col = lax.broadcasted_iota(jnp.int32, (tokens, tokens), 1)
    earlier = jnp.where(row < col, 1.0, 0.0).astype(BF16)
    position = jnp.dot(
        jnp.broadcast_to(named, (8, tokens)).astype(BF16), earlier, preferred_element_type=F32
    )[0:1, :]
    slot = lax.broadcasted_iota(jnp.int32, (capacity, tokens), 0).astype(F32)
    chosen = jnp.where((slot == position) & (named > 0.0), 1.0, 0.0)
    slot_weight = jnp.sum(chosen * weight, axis=1, keepdims=True)
    return chosen, slot_weight


def _scaled_kernel(n_e, n_d, hidden, where_ref, pre_ref, *refs):
    infos, out_ref, held = refs[:n_e], refs[n_e], refs[n_e + 1]
    d, e = where_ref[0], where_ref[1]
    expert = e.astype(F32)
    capacity = pre_ref.shape[1]
    tokens = infos[0].shape[1]
    rows = hidden // n_d
    for j in range(n_e):
        chosen, slot_weight = _choice(infos[j][...], expert, capacity)
        pre = pre_ref[e ^ j].astype(F32)
        gate, up = pre[:, :hidden], pre[:, hidden:]
        act = gate * jax.nn.sigmoid(gate) * up
        scaled = (slot_weight * act).astype(BF16)
        held[:, j * tokens : (j + 1) * tokens] = lax.dot_general(
            scaled, chosen.astype(BF16), (((0,), (0,)), ((), ())), preferred_element_type=F32
        ).astype(BF16)
    for q in range(n_d):
        start = pl.multiple_of((d ^ q) * rows, 16)
        out_ref[q * rows : (q + 1) * rows, :] = held[pl.ds(start, rows), :]


def _partial_kernel(n_e, keep_blocks, send_blocks, rows, at_ref, *refs):
    tok = jnp.concatenate([r[...] for r in refs[:n_e]], axis=0)
    keep_ref, send_ref = refs[n_e:]
    prod = jnp.dot(at_ref[...], tok, preferred_element_type=F32)
    for p, q in enumerate(keep_blocks):
        keep_ref[p * rows : (p + 1) * rows, :] = prod[q * rows : (q + 1) * rows, :]
    for p, q in enumerate(send_blocks):
        send_ref[p * rows : (p + 1) * rows, :] = prod[q * rows : (q + 1) * rows, :].astype(BF16)


def _slot_kernel(n_e, n_c, hidden, where_ref, pre_ref, w_ref, own_ref, *refs):
    infos, refs = refs[:n_e], refs[n_e:]
    others, refs = refs[: (n_e - 1) * n_c], refs[(n_e - 1) * n_c :]
    pre_grad_ref, back_ref, rows_ref = refs
    e = where_ref[1]
    expert = e.astype(F32)
    capacity = pre_ref.shape[1]
    picks, weights = [], []
    for j in range(n_e):
        chosen, slot_weight = _choice(infos[j][...], expert, capacity)
        picks.append(chosen)
        weights.append(slot_weight)
        parts = [own_ref] if j == 0 else others[(j - 1) * n_c : j * n_c]
        at = 0
        for part in parts:
            width = part.shape[1]
            rows_ref[j * capacity : (j + 1) * capacity, at : at + width] = jnp.dot(
                chosen.astype(BF16), part[...], preferred_element_type=F32
            ).astype(BF16)
            at += width
    tile = 256 if hidden % 256 == 0 else hidden
    gates = [jnp.zeros((capacity, 1), F32) for _ in range(n_e)]
    for h in range(0, hidden, tile):
        raw_all = lax.dot_general(
            rows_ref[...], w_ref[0, h : h + tile, :], (((1,), (1,)), ((), ())), preferred_element_type=F32
        )
        for j in range(n_e):
            raw = raw_all[j * capacity : (j + 1) * capacity, :]
            a = pre_ref[e ^ j, :, h : h + tile].astype(F32)
            u = pre_ref[e ^ j, :, hidden + h : hidden + h + tile].astype(F32)
            s = jax.nn.sigmoid(a)
            silu = a * s
            gates[j] = gates[j] + jnp.sum(silu * u * raw, axis=1, keepdims=True)
            delta = weights[j] * raw
            pre_grad_ref[e ^ j, :, h : h + tile] = (delta * u * s * (1.0 + a * (1.0 - s))).astype(BF16)
            pre_grad_ref[e ^ j, :, hidden + h : hidden + h + tile] = (delta * silu).astype(BF16)
    for j in range(n_e):
        back_ref[e ^ j] = jnp.sum(picks[j] * gates[j], axis=0, keepdims=True)


def _params():
    return pltpu.CompilerParams(vmem_limit_bytes=VMEM_LIMIT)


VM = pl.BlockSpec(memory_space=pltpu.VMEM)
SM = pl.BlockSpec(memory_space=pltpu.SMEM)


def _scaled(n_e, n_d, hidden, where, pre, infos):
    tokens = infos[0].shape[1]
    return pl.pallas_call(
        functools.partial(_scaled_kernel, n_e, n_d, hidden),
        out_shape=jax.ShapeDtypeStruct((hidden, n_e * tokens), BF16),
        in_specs=[SM] + [VM] * (1 + n_e),
        out_specs=VM,
        scratch_shapes=[pltpu.VMEM((hidden, n_e * tokens), BF16)],
        compiler_params=_params(),
        name="scaled_by_token",
    )(where, pre, *infos)


def _partial(at, toks, offset, width, keep_blocks, send_blocks, rows):
    n_e = len(toks)
    tile = 256
    hidden, depth = at.shape
    tokens = toks[0].shape[0]
    first = offset // tile
    specs = [pl.BlockSpec((hidden, depth), lambda i: (0, 0))]
    specs.append(pl.BlockSpec((tokens, tile), lambda i: (0, first + i)))
    specs += [pl.BlockSpec((tokens, tile), lambda i: (0, i))] * (n_e - 1)
    n_keep, n_send = len(keep_blocks) * rows, len(send_blocks) * rows
    return pl.pallas_call(
        functools.partial(_partial_kernel, n_e, keep_blocks, send_blocks, rows),
        grid=(width // tile,),
        out_shape=(
            jax.ShapeDtypeStruct((n_keep, width), F32),
            jax.ShapeDtypeStruct((n_send, width), BF16),
        ),
        in_specs=specs,
        out_specs=(
            pl.BlockSpec((n_keep, tile), lambda i: (0, i)),
            pl.BlockSpec((n_send, tile), lambda i: (0, i)),
        ),
        compiler_params=_params(),
        cost_estimate=pl.CostEstimate(
            flops=2 * hidden * depth * width, bytes_accessed=6 << 20, transcendentals=0
        ),
        name="partial_chunk",
    )(at, *toks)


def _slots(n_e, hidden, where, pre, weight, own, infos, others):
    n_c = len(others) // (n_e - 1)
    capacity = pre.shape[1]
    tokens, width = own.shape
    return pl.pallas_call(
        functools.partial(_slot_kernel, n_e, n_c, hidden),
        out_shape=(
            jax.ShapeDtypeStruct(pre.shape, BF16),
            jax.ShapeDtypeStruct((n_e, 1, tokens), F32),
        ),
        in_specs=[SM] + [VM] * (3 + n_e + len(others)),
        out_specs=(VM, VM),
        scratch_shapes=[pltpu.VMEM((n_e * capacity, width), BF16)],
        compiler_params=_params(),
        cost_estimate=pl.CostEstimate(
            flops=2 * n_e * capacity * width * hidden, bytes_accessed=8 << 20, transcendentals=1 << 19
        ),
        name="slot_gradients",
    )(where, pre, weight, own, *infos, *others)


def _fast(grad_tokens, routes, combine, down_weight, saved_pre):
    n_d, n_e = lax.axis_size("dp"), lax.axis_size("expert")
    tokens, width = grad_tokens.shape
    hidden = down_weight.shape[1]
    rows = hidden // n_d
    where = jnp.stack([lax.axis_index("dp"), lax.axis_index("expert")]).astype(jnp.int32)
    pre = saved_pre.reshape(saved_pre.shape[1:])[0]

    info = jnp.concatenate(
        [routes.T.astype(F32), combine.T.astype(F32), jnp.zeros((4, tokens), F32)], axis=0
    )
    infos = [info] + [_send(info, 0, j) for j in range(1, n_e)]

    top = n_e.bit_length() - 1
    bounds, at = [], 0
    for eighths, order in CHUNKS:
        bounds.append((at, eighths * width // 8, order))
        at += eighths * width // 8
    gathered = []
    for offset, size, _ in bounds:
        held = {0: grad_tokens[:, offset : offset + size]}
        for bit in reversed(range(top)):
            for key in sorted(held):
                held[key | (1 << bit)] = _send(held[key], 0, 1 << bit)
        gathered.append([held[j] for j in range(1, n_e)])

    at_all = _scaled(n_e, n_d, hidden, where, pre, infos)

    rest = tuple(range(2, n_d.bit_length() - 1))
    orders = {"x": ((0,), (1,), rest), "z": ((1,), rest, (0,))}
    state = []
    for (offset, size, order), toks in zip(bounds, gathered):
        stages = orders[order]
        bits = [b for group in stages for b in group]
        blocks = [0]
        for b in bits:
            blocks = [q | (v << b) for q in blocks for v in (0, 1)]
        ways = 1 << len(stages[0])
        kept = len(blocks) // ways
        keep, send = _partial(
            at_all, [grad_tokens] + toks, offset, size, tuple(blocks[:kept]), tuple(blocks[kept:]), rows
        )
        state.append([stages, keep, send])

    finals = [None] * len(state)
    for s in range(3):
        for c, (stages, keep, send) in enumerate(state):
            group = stages[s]
            ways = 1 << len(group)
            kept = keep.shape[0]
            total = keep
            for v in range(1, ways):
                mask = sum(
                    (1 << b) for i, b in enumerate(group) if (v >> (len(group) - 1 - i)) & 1
                )
                got = _send(send[(v - 1) * kept : v * kept], mask, 0)
                total = total + got.astype(F32)
            if s < 2:
                kept //= 1 << len(stages[s + 1])
                state[c][1], state[c][2] = total[:kept], total[kept:].astype(BF16)
            else:
                finals[c] = total * (1.0 / n_d)
    down_grad = jnp.concatenate(finals, axis=1).reshape(1, rows * width)

    others = [g[j] for j in range(n_e - 1) for g in gathered]
    pre_grad, back = _slots(n_e, hidden, where, pre, down_weight, grad_tokens, infos, others)
    returned = lax.all_to_all(back, "expert", split_axis=0, concat_axis=0, tiled=True)
    gate_grad = sum(
        jnp.where(routes.T == k, returned[k], 0.0) for k in range(n_e)
    ).T
    return pre_grad.reshape(saved_pre.shape), down_grad, gate_grad


def _general(grad_tokens, routes, combine, down_weight, saved_pre):
    experts = lax.axis_size("expert")
    tok_rows, route_count = routes.shape
    capacity = saved_pre.shape[3]
    model_width = grad_tokens.shape[1]
    hidden = down_weight.shape[1]
    flat_routes = routes.reshape(-1)
    onehot = (flat_routes[:, None] == jnp.arange(experts, dtype=jnp.int32)[None, :]).astype(jnp.int32)
    before = jnp.cumsum(onehot, axis=0) - onehot
    position = jnp.sum(before * onehot, axis=1)
    slot_id = flat_routes * capacity + position
    slot_grid = jnp.arange(experts * capacity, dtype=jnp.int32)
    chosen = slot_grid[:, None] == slot_id[None, :]
    placing = jnp.any(chosen.reshape(experts * capacity, tok_rows, route_count), axis=2).astype(BF16)
    outgoing = jnp.dot(placing, grad_tokens, preferred_element_type=F32).astype(BF16)
    combine_flat = combine.reshape(-1).astype(F32)
    out_weight = jnp.sum(jnp.where(chosen, combine_flat[None, :], 0.0), axis=1).astype(BF16)
    swap = functools.partial(lax.all_to_all, axis_name="expert", split_axis=0, concat_axis=0, tiled=True)
    slot_rows = swap(outgoing.reshape(experts, capacity, model_width)).reshape(-1, model_width)
    slot_weight = swap(out_weight.reshape(experts, capacity)).reshape(-1).astype(F32)
    raw_grad = lax.dot_general(
        slot_rows, down_weight[0], (((1,), (1,)), ((), ())), preferred_element_type=F32
    )
    pre_acts = saved_pre.reshape(-1, 2 * hidden).astype(F32)
    gate_pre, up_pre = pre_acts[:, :hidden], pre_acts[:, hidden:]
    logistic = jax.nn.sigmoid(gate_pre)
    activated = gate_pre * logistic
    hidden_act = activated * up_pre
    slot_gate = jnp.sum(hidden_act * raw_grad, axis=1)
    hidden_delta = slot_weight[:, None] * raw_grad
    gate_delta = hidden_delta * up_pre * logistic * (1.0 + gate_pre * (1.0 - logistic))
    pre_grad = jnp.concatenate([gate_delta, hidden_delta * activated], axis=1).astype(BF16)
    scaled = (slot_weight[:, None] * hidden_act).astype(BF16)
    whole_term = lax.dot_general(
        scaled, slot_rows, (((0,), (0,)), ((), ())), preferred_element_type=F32
    )
    summed = lax.psum_scatter(whole_term.reshape(-1), "dp", scatter_dimension=0, tiled=True)
    down_grad = (summed / lax.axis_size("dp"))[None]
    returned_flat = swap(slot_gate.reshape(experts, capacity)).reshape(-1)
    gate_flat = jnp.sum(jnp.where(chosen, returned_flat[:, None], 0.0), axis=0)
    return pre_grad.reshape(saved_pre.shape), down_grad, gate_flat.reshape(tok_rows, route_count)


def solution(mesh):
    n_d, n_e = mesh.shape["dp"], mesh.shape["expert"]

    def per_device(grad_tokens, routes, combine, down_weight, saved_pre):
        hidden, width = down_weight.shape[1:]
        whole_tiles = (
            hidden % (16 * n_d) == 0
            and saved_pre.shape[3] % 16 == 0
            and width % 2048 == 0
            and n_d >= 8
            and n_d & (n_d - 1) == 0
            and n_e >= 2
            and n_e & (n_e - 1) == 0
            and routes.shape[1] == 2
        )
        form = _fast if whole_tiles else _general
        return form(grad_tokens, routes, combine, down_weight, saved_pre)

    by_both = P(("dp", "expert"), None)
    by_expert = P("expert", "dp", None, None, None)
    return jax.shard_map(
        per_device,
        mesh=mesh,
        in_specs=(by_both, by_both, by_both, P("expert", None, None), by_expert),
        out_specs=(by_expert, P("expert", "dp"), by_both),
        check_vma=False,
    )
```

time: 289 us -> 94.8 us (0.33)
  waiting for transfers between devices: 227 us -> 42.5 us
  Pallas kernels: 0 us -> 20.8 us
  between operations: 14.8 us -> 0.87 us
  starting transfers between devices: 7.6 us -> 19.6 us
  matrix products: 11.4 us -> 0 us
  other arithmetic: 11.7 us -> 3.25 us
  blocking collectives: 6.08 us -> 0 us
    unnamed x2 -> x0, waiting for transfers between devices: 206 us -> none
    ppermute x0 -> x21, waiting for transfers between devices: none -> 42.5 us  [_send(): return lax.ppermute(value, AXES, pairs)]
    all_to_all x2 -> x1, waiting for transfers between devices: 21.1 us -> 0.01 us  [_fast(): lax.all_to_all(back, 'expert', split_axis=0, concat_axis=0, tiled=True)]
    pallas_call x0 -> x5, Pallas kernels: none -> 20.8 us  [the longest x3 11 us: _partial(): pl.pallas_call(functools.partial(_partial_kernel, n_e, keep_blocks, send_...]
    ppermute x0 -> x21, starting transfers between devices: none -> 16.3 us  [_send(): return lax.ppermute(value, AXES, pairs)]
    dot_general x3 -> x0, matrix products: 11.4 us -> none  [the longest x1 4.56 us: per_device(): lax.dot_general(slot_rows, down_rows, (((1,), (1,)), ((), ())), preferred...]
    all_to_all x1 -> x0, blocking collectives: 6.08 us -> none  [per_device(): lax.all_to_all(out_weight.reshape(experts, capacity), 'expert', split_axi...]
    all_to_all x2 -> x1, starting transfers between devices: 7.56 us -> 3.3 us  [_fast(): lax.all_to_all(back, 'expert', split_axis=0, concat_axis=0, tiled=True)]
  transfers between devices with their start and end apart: 3 -> 22, of which waited for: 3 -> 10; matrix products, arithmetic and copies ran while one was open for 3% -> 5% of each run, Pallas kernels for 0% -> 22%
where the time goes in v1:
time: 94.8 us; the launch traced here: 94.3 us
  waiting for transfers between devices  42.5 us (45%)
  Pallas kernels  20.8 us (22%)
  starting transfers between devices  19.6 us (21%)
  local copies, waits for them, and re-layouts  7.3 us (8%)
  other arithmetic  3.25 us (3%)
    ppermute x21, waiting for transfers between devices, _send(): return lax.ppermute(value, AXES, pairs)  42.5 us
    ppermute x21, starting transfers between devices, _send(): return lax.ppermute(value, AXES, pairs)  16.3 us
    pallas_call x3, Pallas kernels, _partial(): pl.pallas_call(functools.partial(_partial_kernel, n_e, keep_blocks, send_...  11 us
    pallas_call x1, Pallas kernels, _slots(): pl.pallas_call(functools.partial(_slot_kernel, n_e, n_c, hidden), out_sha...  6.65 us
    unnamed x35, local copies, waits for them, and re-layouts  5.11 us
    all_to_all x1, starting transfers between devices, _fast(): lax.all_to_all(back, 'expert', split_axis=0, concat_axis=0, tiled=True)  3.3 us
    pallas_call x1, Pallas kernels, _scaled(): pl.pallas_call(functools.partial(_scaled_kernel, n_e, n_d, hidden), out_s...  3.15 us
    slice x2, local copies, waits for them, and re-layouts, _fast(): held = {0: grad_tokens[:, offset:offset + size]}  1.97 us
  transfers between devices with their start and end apart: 22, of which 10 were waited for; matrix products, arithmetic and copies ran while one was open for 5% of the time, Pallas kernels for 22%

profile of v1, /device:TPU:0, one launch (start us, length us, event | category | flops | bytes accessed | tf_op | source)
XLA Modules:
  0.0 94.3 jit_solution(2080772470133526536)
XLA Ops:
  0.6 0.9 slice.64
  1.5 3.0 %collective-permute-start.7 = (bf16[128,512]{1,0:T(8,128)(2,1)S(1)}, bf16[128,512]{1,0:T(8,128)(2,1)S(1)}, u32[]{:S(2)}, u32[]{:S(2)}) collective-permute-start(bf16[128,512]{1,0:T(8,128)(2,1)S(1)} %slice.64), channel_id=1, source_target_pairs={{0,2},{1,3},{2,0},{3,1},{4,6},{5,7},{6,4},{7,5},{8,10},{9,11},{10,... | collective-permute-start | bytes 393224 | tf_op jit(solution)/shard_map/ppermute | solution.py:24
  4.6 0.0 collective-permute-start.4
  4.6 1.0 %fusion.6 = (bf16[128,768]{1,0:T(8,128)(2,1)S(1)}, bf16[128,768]{1,0:T(8,128)(2,1)S(1)}) fusion(bf16[128,2048]{1,0:T(8,128)(2,1)} %refs_0_.5), kind=kLoop, calls=%fused_computation.34 | loop fusion | bytes 786432 | tf_op jit(solution)/shard_map/slice | solution.py:207
  5.6 0.2 collective-permute-start.6
  5.8 1.9 %collective-permute-start.8 = (bf16[128,768]{1,0:T(8,128)(2,1)S(1)}, bf16[128,768]{1,0:T(8,128)(2,1)S(1)}, u32[]{:S(2)}, u32[]{:S(2)}) collective-permute-start(bf16[128,768]{1,0:T(8,128)(2,1)S(1)} %get-tuple-element.19), channel_id=1, source_target_pairs={{0,2},{1,3},{2,0},{3,1},{4,6},{5,7},{6,4},{7,5},{8,10},{9,11},{10,... | collective-permute-start | bytes 589832 | tf_op jit(solution)/shard_map/ppermute | solution.py:24
  7.7 0.7 convert_bitcast_fusion
  8.4 0.7 convert_bitcast_fusion.1
  9.1 0.1 pad.5.clone
  9.1 0.1 maximum_maximum_fusion.refs_0_
  9.2 0.0 collective-permute-start
  9.2 1.2 %collective-permute-done.refs_1_ = f32[8,128]{1,0:T(8,128)S(1)} collective-permute-done((f32[8,128]{1,0:T(8,128)S(1)}, f32[8,128]{1,0:T(8,128)S(1)}, u32[]{:S(2)}, u32[]{:S(2)}) %collective-permute-start) | collective-permute-done | bytes 4128 | tf_op jit(solution)/shard_map/ppermute | solution.py:24
  10.4 0.1 collective-permute-start.1
  10.5 6.8 %collective-permute-done.1.refs_2_ = f32[8,128]{1,0:T(8,128)S(1)} collective-permute-done((f32[8,128]{1,0:T(8,128)S(1)}, f32[8,128]{1,0:T(8,128)S(1)}, u32[]{:S(2)}, u32[]{:S(2)}) %collective-permute-start.1) | collective-permute-done | bytes 4128 | tf_op jit(solution)/shard_map/ppermute | solution.py:24
  17.3 0.0 collective-permute-start.2
  17.3 3.0 %collective-permute-done.2.refs_3_ = f32[8,128]{1,0:T(8,128)S(1)} collective-permute-done((f32[8,128]{1,0:T(8,128)S(1)}, f32[8,128]{1,0:T(8,128)S(1)}, u32[]{:S(2)}, u32[]{:S(2)}) %collective-permute-start.2) | collective-permute-done | bytes 4128 | tf_op jit(solution)/shard_map/ppermute | solution.py:24
  20.4 0.0 collective-permute-start.3
  20.4 0.0 collective-permute-done.6.refs_7_.refs_2_
  20.4 0.5 collective-permute-start.9
  20.9 0.0 collective-permute-done.7.refs_8_.refs_2_
  20.9 0.1 collective-permute-start.10
  21.0 0.0 collective-permute-done.4.refs_5_.refs_1_
  21.0 0.4 collective-permute-start.5
  21.4 0.0 collective-permute-done.8.refs_9_.refs_2_
  21.4 0.1 collective-permute-start.11
  21.5 0.7 pad_add_fusion.where_ref
  22.2 3.2 %scaled_by_token.1.at_ref = bf16[768,512]{1,0:T(8,128)(2,1)} custom-call(s32[2]{0:T(128)} %pad_add_fusion.where_ref, bf16[4,96,1536]{2,1,0:T(8,128)(2,1)} %bitcast.20, f32[8,128]{1,0:T(8,128)} %copy-done.12, f32[8,128]{1,0:T(8,128)} %copy-done.13, f32[8,128]{1,0:T(8,128)} %copy-done.14, f32[8,128]{1,0:T(8,128)} %copy-done.15), custom_call_target="tpu_custom_call" | custom-call | tf_op jit(solution)/shard_map/scaled_by_token/pallas_call | solution.py:125
  25.4 0.6 copy-done.5
  26.0 2.9 %partial_chunk.4 = (f32[384,512]{1,0:T(8,128)}, bf16[384,512]{1,0:T(8,128)(2,1)}) custom-call(bf16[768,512]{1,0:T(8,128)(2,1)} %scaled_by_token.1.at_ref, bf16[128,2048]{1,0:T(8,128)(2,1)} %refs_0_.5, bf16[128,512]{1,0:T(8,128)(2,1)} %copy-done.4, bf16[128,512]{1,0:T(8,128)(2,1)} %copy-done.3, bf16[128,512]{1,0:T(8,128)(2,1)} %copy-done.5), custom_call_target="tpu_custom_call" | custom-call | flops 402653184 | bytes 6291456 | tf_op jit(solution)/shard_map/partial_chunk/pallas_call | solution.py:146
  28.9 1.6 %collective-permute-start.15 = (bf16[384,512]{1,0:T(8,128)(2,1)}, bf16[384,512]{1,0:T(8,128)(2,1)S(1)}, u32[]{:S(2)}, u32[]{:S(2)}) collective-permute-start(bf16[384,512]{1,0:T(8,128)(2,1)} %get-tuple-element.15), channel_id=1, source_target_pairs={{0,8},{1,9},{2,10},{3,11},{4,12},{5,13},{6,14},{7,15},{8,0},{9,1},... | collective-permute-start | bytes 1179656 | tf_op jit(solution)/shard_map/ppermute | solution.py:24
  30.5 0.0 collective-permute-done.3.refs_4_.refs_1_
  30.5 0.7 copy-done.8
  31.2 0.7 copy-done.9
  31.9 4.1 %partial_chunk.3 = (f32[384,768]{1,0:T(8,128)}, bf16[384,768]{1,0:T(8,128)(2,1)}) custom-call(bf16[768,512]{1,0:T(8,128)(2,1)} %scaled_by_token.1.at_ref, bf16[128,2048]{1,0:T(8,128)(2,1)} %refs_0_.5, bf16[128,768]{1,0:T(8,128)(2,1)} %copy-done.8, bf16[128,768]{1,0:T(8,128)(2,1)} %copy-done.7, bf16[128,768]{1,0:T(8,128)(2,1)} %copy-done.9), custom_call_target="tpu_custom_call" | custom-call | flops 603979776 | bytes 6291456 | tf_op jit(solution)/shard_map/partial_chunk/pallas_call | solution.py:146
  36.0 1.5 %collective-permute-start.12 = (bf16[384,768]{1,0:T(8,128)(2,1)}, bf16[384,768]{1,0:T(8,128)(2,1)S(1)}, u32[]{:S(2)}, u32[]{:S(2)}) collective-permute-start(bf16[384,768]{1,0:T(8,128)(2,1)} %get-tuple-element.13), channel_id=1, source_target_pairs={{0,4},{1,5},{2,6},{3,7},{4,0},{5,1},{6,2},{7,3},{8,12},{9,13},{10,... | collective-permute-start | bytes 1769480 | tf_op jit(solution)/shard_map/ppermute | solution.py:24
  37.5 0.0 collective-permute-done.5.refs_6_.refs_1_
  37.5 0.7 copy-done.10
  38.1 0.7 copy-done.11
  38.8 6.6 %slot_gradients.1 = (bf16[4,96,1536]{2,1,0:T(8,128)(2,1)}, f32[4,1,128]{2,1,0:T(1,128)}) custom-call(s32[2]{0:T(128)} %pad_add_fusion.where_ref, bf16[4,96,1536]{2,1,0:T(8,128)(2,1)} %bitcast.21, bf16[1,768,2048]{2,1,0:T(8,128)(2,1)} %w_ref.1, bf16[128,2048]{1,0:T(8,128)(2,1)} %refs_0_.5, f32[8,128]{1,0:T(8,128)} %copy-done.12, f32[8,128]{1,0:T(8,128)} %copy-done.13, ...), custom_call_target="tpu_custom_call" | custom-call | flops 1207959552 | bytes 8388608 | tf_op jit(solution)/shard_map/slot_gradients/pallas_call | solution.py:170
  45.5 3.3 %all-to-all-start = ((f32[4,1,128]{2,1,0:T(1,128)}), f32[4,1,128]{2,1,0:T(1,128)S(1)}, u32[]{:S(2)}, u32[]{:S(2)}) async-start(f32[4,1,128]{2,1,0:T(1,128)} %get-tuple-element.18), calls=%async_computation | async-start | bytes 4096 | tf_op jit(solution)/shard_map/all_to_all | solution.py:253
  48.8 4.1 %partial_chunk.5 = (f32[384,768]{1,0:T(8,128)}, bf16[384,768]{1,0:T(8,128)(2,1)}) custom-call(bf16[768,512]{1,0:T(8,128)(2,1)} %scaled_by_token.1.at_ref, bf16[128,2048]{1,0:T(8,128)(2,1)} %refs_0_.5, bf16[128,768]{1,0:T(8,128)(2,1)} %copy-done.10, bf16[128,768]{1,0:T(8,128)(2,1)} %copy-done.6, bf16[128,768]{1,0:T(8,128)(2,1)} %copy-done.11), custom_call_target="tpu_custom_call" | custom-call | flops 603979776 | bytes 6291456 | tf_op jit(solution)/shard_map/partial_chunk/pallas_call | solution.py:146
  52.9 0.5 collective-permute-start.18
  53.4 0.0 copy-start.16
  53.4 0.1 convert_add_fusion.2
  53.6 2.6 %collective-permute-start.16 = (bf16[192,512]{1,0:T(8,128)(2,1)S(1)}, bf16[192,512]{1,0:T(8,128)(2,1)S(1)}, u32[]{:S(2)}, u32[]{:S(2)}) collective-permute-start(bf16[192,512]{1,0:T(8,128)(2,1)S(1)} %slice.122), channel_id=1, source_target_pairs={{0,16},{1,17},{2,18},{3,19},{4,20},{5,21},{6,22},{7,23},{8,24},{9,... | collective-permute-start | bytes 589832 | tf_op jit(solution)/shard_map/ppermute | solution.py:24
  56.2 0.6 fusion.5
  56.8 8.8 %collective-permute-done.16 = bf16[192,512]{1,0:T(8,128)(2,1)S(1)} collective-permute-done((bf16[192,512]{1,0:T(8,128)(2,1)S(1)}, bf16[192,512]{1,0:T(8,128)(2,1)S(1)}, u32[]{:S(2)}, u32[]{:S(2)}) %collective-permute-start.16) | collective-permute-done | bytes 196640 | tf_op jit(solution)/shard_map/ppermute | solution.py:24
  65.7 1.6 %collective-permute-start.17 = (bf16[96,512]{1,0:T(8,128)(2,1)S(1)}, bf16[96,512]{1,0:T(8,128)(2,1)S(1)}, u32[]{:S(2)}, u32[]{:S(2)}) collective-permute-start(bf16[96,512]{1,0:T(8,128)(2,1)S(1)} %slice.125), channel_id=1, source_target_pairs={{0,4},{1,5},{2,6},{3,7},{4,0},{5,1},{6,2},{7,3},{8,12},{9,13},{10,... | collective-permute-start | bytes 294920 | tf_op jit(solution)/shard_map/ppermute | solution.py:24
  67.3 0.1 convert_add_fusion.1
  67.4 0.1 collective-permute-start.13
  67.5 1.5 %collective-permute-done.18 = bf16[384,768]{1,0:T(8,128)(2,1)S(1)} collective-permute-done((bf16[384,768]{1,0:T(8,128)(2,1)}, bf16[384,768]{1,0:T(8,128)(2,1)S(1)}, u32[]{:S(2)}, u32[]{:S(2)}) %collective-permute-start.18) | collective-permute-done | bytes 589856 | tf_op jit(solution)/shard_map/ppermute | solution.py:24
  69.0 0.1 convert_add_fusion
  69.2 0.7 collective-permute-start.19
  69.9 1.0 %collective-permute-done.17 = bf16[96,512]{1,0:T(8,128)(2,1)S(1)} collective-permute-done((bf16[96,512]{1,0:T(8,128)(2,1)S(1)}, bf16[96,512]{1,0:T(8,128)(2,1)S(1)}, u32[]{:S(2)}, u32[]{:S(2)}) %collective-permute-start.17) | collective-permute-done | bytes 98336 | tf_op jit(solution)/shard_map/ppermute | solution.py:24
  70.9 6.5 %collective-permute-done.13 = bf16[192,768]{1,0:T(8,128)(2,1)S(1)} collective-permute-done((bf16[192,768]{1,0:T(8,128)(2,1)S(1)}, bf16[192,768]{1,0:T(8,128)(2,1)S(1)}, u32[]{:S(2)}, u32[]{:S(2)}) %collective-permute-start.13) | collective-permute-done | bytes 294944 | tf_op jit(solution)/shard_map/ppermute | solution.py:24
  77.4 0.1 slice_add_fusion.1
  77.5 1.2 %collective-permute-start.14 = (bf16[96,768]{1,0:T(8,128)(2,1)S(1)}, bf16[96,768]{1,0:T(8,128)(2,1)S(1)}, u32[]{:S(2)}, u32[]{:S(2)}) collective-permute-start(bf16[96,768]{1,0:T(8,128)(2,1)S(1)} %slice.124), channel_id=1, source_target_pairs={{0,16},{1,17},{2,18},{3,19},{4,20},{5,21},{6,22},{7,23},{8,24},{9,... | collective-permute-start | bytes 442376 | tf_op jit(solution)/shard_map/ppermute | solution.py:24
  78.7 6.6 %collective-permute-done.19 = bf16[192,768]{1,0:T(8,128)(2,1)S(1)} collective-permute-done((bf16[192,768]{1,0:T(8,128)(2,1)S(1)}, bf16[192,768]{1,0:T(8,128)(2,1)S(1)}, u32[]{:S(2)}, u32[]{:S(2)}) %collective-permute-start.19) | collective-permute-done | bytes 294944 | tf_op jit(solution)/shard_map/ppermute | solution.py:24
  85.3 0.1 slice_add_fusion
  85.4 0.1 collective-permute-start.20
  85.5 2.6 %collective-permute-done.14 = bf16[96,768]{1,0:T(8,128)(2,1)S(1)} collective-permute-done((bf16[96,768]{1,0:T(8,128)(2,1)S(1)}, bf16[96,768]{1,0:T(8,128)(2,1)S(1)}, u32[]{:S(2)}, u32[]{:S(2)}) %collective-permute-start.14) | collective-permute-done | bytes 147488 | tf_op jit(solution)/shard_map/ppermute | solution.py:24
  88.1 4.4 %collective-permute-done.20 = bf16[96,768]{1,0:T(8,128)(2,1)S(1)} collective-permute-done((bf16[96,768]{1,0:T(8,128)(2,1)S(1)}, bf16[96,768]{1,0:T(8,128)(2,1)S(1)}, u32[]{:S(2)}, u32[]{:S(2)}) %collective-permute-start.20) | collective-permute-done | bytes 147488 | tf_op jit(solution)/shard_map/ppermute | solution.py:24
  92.6 0.1 maximum_bitcast_fusion
  92.6 1.7 %copy.8 = f32[1,1,96,2048]{3,1,2,0:T(1,128)} copy(f32[1,1,96,2048]{3,2,1,0:T(8,128)S(1)} %maximum_bitcast_fusion) | data formatting | bytes 1572864
  (46 shorter events, 0.4 us)
Async XLA Ops:
  1.5 19.3 %collective-permute-start.7 = (bf16[128,512]{1,0:T(8,128)(2,1)S(1)}, bf16[128,512]{1,0:T(8,128)(2,1)S(1)}, u32[]{:S(2)}, u32[]{:S(2)}) collective-permute-start(bf16[128,512]{1,0:T(8,128)(2,1)S(1)} %slice.64), channel_id=1, source_target_pairs={{0,2},{1,3},{2,0},{3,1},{4,6},{5,7},{6,4},{7,5},{8,10},{9,11},{10,... | collective-permute-start | bytes 393224 | tf_op jit(solution)/shard_map/ppermute | solution.py:24
  4.6 16.4 %collective-permute-start.4 = (bf16[128,512]{1,0:T(8,128)(2,1)S(1)}, bf16[128,512]{1,0:T(8,128)(2,1)S(1)}, u32[]{:S(2)}, u32[]{:S(2)}) collective-permute-start(bf16[128,512]{1,0:T(8,128)(2,1)S(1)} %slice.64), channel_id=1, source_target_pairs={{0,1},{1,0},{2,3},{3,2},{4,5},{5,4},{6,7},{7,6},{8,9},{9,8},{10,11... | collective-permute-start | bytes 393224 | tf_op jit(solution)/shard_map/ppermute | solution.py:24
  5.6 14.7 %collective-permute-start.6 = (bf16[128,768]{1,0:T(8,128)(2,1)S(1)}, bf16[128,768]{1,0:T(8,128)(2,1)S(1)}, u32[]{:S(2)}, u32[]{:S(2)}) collective-permute-start(bf16[128,768]{1,0:T(8,128)(2,1)S(1)} %get-tuple-element.20), channel_id=1, source_target_pairs={{0,2},{1,3},{2,0},{3,1},{4,6},{5,7},{6,4},{7,5},{8,10},{9,11},{10,... | collective-permute-start | bytes 589832 | tf_op jit(solution)/shard_map/ppermute | solution.py:24
  5.8 15.6 %collective-permute-start.8 = (bf16[128,768]{1,0:T(8,128)(2,1)S(1)}, bf16[128,768]{1,0:T(8,128)(2,1)S(1)}, u32[]{:S(2)}, u32[]{:S(2)}) collective-permute-start(bf16[128,768]{1,0:T(8,128)(2,1)S(1)} %get-tuple-element.19), channel_id=1, source_target_pairs={{0,2},{1,3},{2,0},{3,1},{4,6},{5,7},{6,4},{7,5},{8,10},{9,11},{10,... | collective-permute-start | bytes 589832 | tf_op jit(solution)/shard_map/ppermute | solution.py:24
  9.2 12.9 %copy-start.12 = (f32[8,128]{1,0:T(8,128)}, f32[8,128]{1,0:T(8,128)S(1)}, u32[]{:S(2)}) copy-start(f32[8,128]{1,0:T(8,128)S(1)} %maximum_maximum_fusion.refs_0_) | copy-start | bytes 12292
  9.2 1.2 %collective-permute-start = (f32[8,128]{1,0:T(8,128)S(1)}, f32[8,128]{1,0:T(8,128)S(1)}, u32[]{:S(2)}, u32[]{:S(2)}) collective-permute-start(f32[8,128]{1,0:T(8,128)S(1)} %maximum_maximum_fusion.refs_0_), channel_id=1, source_target_pairs={{0,1},{1,0},{2,3},{3,2},{4,5},{5,4},{6,7},{7,6},{8,9},{9,8},{10,11... | collective-permute-start | bytes 12296 | tf_op jit(solution)/shard_map/ppermute | solution.py:24
  10.4 11.8 %copy-start.13 = (f32[8,128]{1,0:T(8,128)}, f32[8,128]{1,0:T(8,128)S(1)}, u32[]{:S(2)}) copy-start(f32[8,128]{1,0:T(8,128)S(1)} %collective-permute-done.refs_1_) | copy-start | bytes 12292
  10.4 6.9 %collective-permute-start.1 = (f32[8,128]{1,0:T(8,128)S(1)}, f32[8,128]{1,0:T(8,128)S(1)}, u32[]{:S(2)}, u32[]{:S(2)}) collective-permute-start(f32[8,128]{1,0:T(8,128)S(1)} %maximum_maximum_fusion.refs_0_), channel_id=1, source_target_pairs={{0,2},{1,3},{2,0},{3,1},{4,6},{5,7},{6,4},{7,5},{8,10},{9,11},{10,... | collective-permute-start | bytes 12296 | tf_op jit(solution)/shard_map/ppermute | solution.py:24
  17.3 4.8 %copy-start.14 = (f32[8,128]{1,0:T(8,128)}, f32[8,128]{1,0:T(8,128)S(1)}, u32[]{:S(2)}) copy-start(f32[8,128]{1,0:T(8,128)S(1)} %collective-permute-done.1.refs_2_) | copy-start | bytes 12292
  17.3 3.0 %collective-permute-start.2 = (f32[8,128]{1,0:T(8,128)S(1)}, f32[8,128]{1,0:T(8,128)S(1)}, u32[]{:S(2)}, u32[]{:S(2)}) collective-permute-start(f32[8,128]{1,0:T(8,128)S(1)} %maximum_maximum_fusion.refs_0_), channel_id=1, source_target_pairs={{0,3},{1,2},{2,1},{3,0},{4,7},{5,6},{6,5},{7,4},{8,11},{9,10},{10,... | collective-permute-start | bytes 12296 | tf_op jit(solution)/shard_map/ppermute | solution.py:24
  20.4 1.8 %copy-start.15 = (f32[8,128]{1,0:T(8,128)}, f32[8,128]{1,0:T(8,128)S(1)}, u32[]{:S(2)}) copy-start(f32[8,128]{1,0:T(8,128)S(1)} %collective-permute-done.2.refs_3_) | copy-start | bytes 12292
  20.4 10.2 %collective-permute-start.3 = (bf16[128,768]{1,0:T(8,128)(2,1)S(1)}, bf16[128,768]{1,0:T(8,128)(2,1)S(1)}, u32[]{:S(2)}, u32[]{:S(2)}) collective-permute-start(bf16[128,768]{1,0:T(8,128)(2,1)S(1)} %get-tuple-element.20), channel_id=1, source_target_pairs={{0,1},{1,0},{2,3},{3,2},{4,5},{5,4},{6,7},{7,6},{8,9},{9,8},{10,11... | collective-permute-start | bytes 589832 | tf_op jit(solution)/shard_map/ppermute | solution.py:24
  20.4 8.5 %copy-start.7 = (bf16[128,768]{1,0:T(8,128)(2,1)}, bf16[128,768]{1,0:T(8,128)(2,1)S(1)}, u32[]{:S(2)}) copy-start(bf16[128,768]{1,0:T(8,128)(2,1)S(1)} %collective-permute-done.6.refs_7_.refs_2_) | copy-start | bytes 589828
  20.4 10.1 %collective-permute-start.9 = (bf16[128,768]{1,0:T(8,128)(2,1)S(1)}, bf16[128,768]{1,0:T(8,128)(2,1)S(1)}, u32[]{:S(2)}, u32[]{:S(2)}) collective-permute-start(bf16[128,768]{1,0:T(8,128)(2,1)S(1)} %collective-permute-done.6.refs_7_.refs_2_), channel_id=1, source_target_pairs={{0,1},{1,0},{2,3},{3,2},{4,5},{5,4},{6,7},{7,6},{8,9},{9,8},{10,11... | collective-permute-start | bytes 589832 | tf_op jit(solution)/shard_map/ppermute | solution.py:24
  20.9 4.4 %copy-start.3 = (bf16[128,512]{1,0:T(8,128)(2,1)}, bf16[128,512]{1,0:T(8,128)(2,1)S(1)}, u32[]{:S(2)}) copy-start(bf16[128,512]{1,0:T(8,128)(2,1)S(1)} %collective-permute-done.7.refs_8_.refs_2_) | copy-start | bytes 393220
  20.9 4.4 %collective-permute-start.10 = (bf16[128,512]{1,0:T(8,128)(2,1)S(1)}, bf16[128,512]{1,0:T(8,128)(2,1)S(1)}, u32[]{:S(2)}, u32[]{:S(2)}) collective-permute-start(bf16[128,512]{1,0:T(8,128)(2,1)S(1)} %collective-permute-done.7.refs_8_.refs_2_), channel_id=1, source_target_pairs={{0,1},{1,0},{2,3},{3,2},{4,5},{5,4},{6,7},{7,6},{8,9},{9,8},{10,11... | collective-permute-start | bytes 393224 | tf_op jit(solution)/shard_map/ppermute | solution.py:24
  21.0 4.4 %copy-start.4 = (bf16[128,512]{1,0:T(8,128)(2,1)}, bf16[128,512]{1,0:T(8,128)(2,1)S(1)}, u32[]{:S(2)}) copy-start(bf16[128,512]{1,0:T(8,128)(2,1)S(1)} %collective-permute-done.4.refs_5_.refs_1_) | copy-start | bytes 393220
  21.0 16.5 %collective-permute-start.5 = (bf16[128,768]{1,0:T(8,128)(2,1)S(1)}, bf16[128,768]{1,0:T(8,128)(2,1)S(1)}, u32[]{:S(2)}, u32[]{:S(2)}) collective-permute-start(bf16[128,768]{1,0:T(8,128)(2,1)S(1)} %get-tuple-element.19), channel_id=1, source_target_pairs={{0,1},{1,0},{2,3},{3,2},{4,5},{5,4},{6,7},{7,6},{8,9},{9,8},{10,11... | collective-permute-start | bytes 589832 | tf_op jit(solution)/shard_map/ppermute | solution.py:24
  21.4 7.5 %copy-start.6 = (bf16[128,768]{1,0:T(8,128)(2,1)}, bf16[128,768]{1,0:T(8,128)(2,1)S(1)}, u32[]{:S(2)}) copy-start(bf16[128,768]{1,0:T(8,128)(2,1)S(1)} %collective-permute-done.8.refs_9_.refs_2_) | copy-start | bytes 589828
  21.4 16.1 %collective-permute-start.11 = (bf16[128,768]{1,0:T(8,128)(2,1)S(1)}, bf16[128,768]{1,0:T(8,128)(2,1)S(1)}, u32[]{:S(2)}, u32[]{:S(2)}) collective-permute-start(bf16[128,768]{1,0:T(8,128)(2,1)S(1)} %collective-permute-done.8.refs_9_.refs_2_), channel_id=1, source_target_pairs={{0,1},{1,0},{2,3},{3,2},{4,5},{5,4},{6,7},{7,6},{8,9},{9,8},{10,11... | collective-permute-start | bytes 589832 | tf_op jit(solution)/shard_map/ppermute | solution.py:24
  25.3 0.7 copy-start.5
  28.9 24.5 %collective-permute-start.15 = (bf16[384,512]{1,0:T(8,128)(2,1)}, bf16[384,512]{1,0:T(8,128)(2,1)S(1)}, u32[]{:S(2)}, u32[]{:S(2)}) collective-permute-start(bf16[384,512]{1,0:T(8,128)(2,1)} %get-tuple-element.15), channel_id=1, source_target_pairs={{0,8},{1,9},{2,10},{3,11},{4,12},{5,13},{6,14},{7,15},{8,0},{9,1},... | collective-permute-start | bytes 1179656 | tf_op jit(solution)/shard_map/ppermute | solution.py:24
  30.5 0.7 copy-start.8
  31.2 0.7 copy-start.9
  36.0 31.3 %collective-permute-start.12 = (bf16[384,768]{1,0:T(8,128)(2,1)}, bf16[384,768]{1,0:T(8,128)(2,1)S(1)}, u32[]{:S(2)}, u32[]{:S(2)}) collective-permute-start(bf16[384,768]{1,0:T(8,128)(2,1)} %get-tuple-element.13), channel_id=1, source_target_pairs={{0,4},{1,5},{2,6},{3,7},{4,0},{5,1},{6,2},{7,3},{8,12},{9,13},{10,... | collective-permute-start | bytes 1769480 | tf_op jit(solution)/shard_map/ppermute | solution.py:24
  37.5 0.7 copy-start.10
  38.1 0.7 copy-start.11
  45.5 7.9 %copy-start.2 = (f32[384,512]{1,0:T(8,128)S(1)}, f32[384,512]{1,0:T(8,128)}, u32[]{:S(2)}) copy-start(f32[384,512]{1,0:T(8,128)} %get-tuple-element.14) | copy-start | bytes 2359300
  45.5 7.9 %all-to-all-start = ((f32[4,1,128]{2,1,0:T(1,128)}), f32[4,1,128]{2,1,0:T(1,128)S(1)}, u32[]{:S(2)}, u32[]{:S(2)}) async-start(f32[4,1,128]{2,1,0:T(1,128)} %get-tuple-element.18), calls=%async_computation | async-start | bytes 4096 | tf_op jit(solution)/shard_map/all_to_all | solution.py:253
  52.9 16.2 %collective-permute-start.18 = (bf16[384,768]{1,0:T(8,128)(2,1)}, bf16[384,768]{1,0:T(8,128)(2,1)S(1)}, u32[]{:S(2)}, u32[]{:S(2)}) collective-permute-start(bf16[384,768]{1,0:T(8,128)(2,1)} %get-tuple-element.17), channel_id=1, source_target_pairs={{0,4},{1,5},{2,6},{3,7},{4,0},{5,1},{6,2},{7,3},{8,12},{9,13},{10,... | collective-permute-start | bytes 1769480 | tf_op jit(solution)/shard_map/ppermute | solution.py:24
  53.4 2.8 %copy-start.16 = (s32[128,2]{0,1:T(2,128)S(1)}, s32[128,2]{0,1:T(2,128)}, u32[]{:S(2)}) copy-start(s32[128,2]{0,1:T(2,128)} %param.6) | copy-start | bytes 3076
  53.6 13.7 %copy-start = (f32[384,768]{1,0:T(8,128)S(1)}, f32[384,768]{1,0:T(8,128)}, u32[]{:S(2)}) copy-start(f32[384,768]{1,0:T(8,128)} %get-tuple-element.12) | copy-start | bytes 3538948
  53.6 12.0 %collective-permute-start.16 = (bf16[192,512]{1,0:T(8,128)(2,1)S(1)}, bf16[192,512]{1,0:T(8,128)(2,1)S(1)}, u32[]{:S(2)}, u32[]{:S(2)}) collective-permute-start(bf16[192,512]{1,0:T(8,128)(2,1)S(1)} %slice.122), channel_id=1, source_target_pairs={{0,16},{1,17},{2,18},{3,19},{4,20},{5,21},{6,22},{7,23},{8,24},{9,... | collective-permute-start | bytes 589832 | tf_op jit(solution)/shard_map/ppermute | solution.py:24
  65.7 5.1 %collective-permute-start.17 = (bf16[96,512]{1,0:T(8,128)(2,1)S(1)}, bf16[96,512]{1,0:T(8,128)(2,1)S(1)}, u32[]{:S(2)}, u32[]{:S(2)}) collective-permute-start(bf16[96,512]{1,0:T(8,128)(2,1)S(1)} %slice.125), channel_id=1, source_target_pairs={{0,4},{1,5},{2,6},{3,7},{4,0},{5,1},{6,2},{7,3},{8,12},{9,13},{10,... | collective-permute-start | bytes 294920 | tf_op jit(solution)/shard_map/ppermute | solution.py:24
  67.3 1.8 %copy-start.1 = (f32[384,768]{1,0:T(8,128)S(1)}, f32[384,768]{1,0:T(8,128)}, u32[]{:S(2)}) copy-start(f32[384,768]{1,0:T(8,128)} %get-tuple-element.16) | copy-start | bytes 3538948
  67.4 10.0 %collective-permute-start.13 = (bf16[192,768]{1,0:T(8,128)(2,1)S(1)}, bf16[192,768]{1,0:T(8,128)(2,1)S(1)}, u32[]{:S(2)}, u32[]{:S(2)}) collective-permute-start(bf16[192,768]{1,0:T(8,128)(2,1)S(1)} %slice.121), channel_id=1, source_target_pairs={{0,8},{1,9},{2,10},{3,11},{4,12},{5,13},{6,14},{7,15},{8,0},{9,1},... | collective-permute-start | bytes 884744 | tf_op jit(solution)/shard_map/ppermute | solution.py:24
  69.2 16.1 %collective-permute-start.19 = (bf16[192,768]{1,0:T(8,128)(2,1)S(1)}, bf16[192,768]{1,0:T(8,128)(2,1)S(1)}, u32[]{:S(2)}, u32[]{:S(2)}) collective-permute-start(bf16[192,768]{1,0:T(8,128)(2,1)S(1)} %slice.120), channel_id=1, source_target_pairs={{0,8},{1,9},{2,10},{3,11},{4,12},{5,13},{6,14},{7,15},{8,0},{9,1},... | collective-permute-start | bytes 884744 | tf_op jit(solution)/shard_map/ppermute | solution.py:24
  77.5 10.6 %collective-permute-start.14 = (bf16[96,768]{1,0:T(8,128)(2,1)S(1)}, bf16[96,768]{1,0:T(8,128)(2,1)S(1)}, u32[]{:S(2)}, u32[]{:S(2)}) collective-permute-start(bf16[96,768]{1,0:T(8,128)(2,1)S(1)} %slice.124), channel_id=1, source_target_pairs={{0,16},{1,17},{2,18},{3,19},{4,20},{5,21},{6,22},{7,23},{8,24},{9,... | collective-permute-start | bytes 442376 | tf_op jit(solution)/shard_map/ppermute | solution.py:24
  85.4 7.1 %collective-permute-start.20 = (bf16[96,768]{1,0:T(8,128)(2,1)S(1)}, bf16[96,768]{1,0:T(8,128)(2,1)S(1)}, u32[]{:S(2)}, u32[]{:S(2)}) collective-permute-start(bf16[96,768]{1,0:T(8,128)(2,1)S(1)} %slice.123), channel_id=1, source_target_pairs={{0,16},{1,17},{2,18},{3,19},{4,20},{5,21},{6,22},{7,23},{8,24},{9,... | collective-permute-start | bytes 442376 | tf_op jit(solution)/shard_map/ppermute | solution.py:24

commit v2 on v1

v2 whole, which is shorter than its diff:
```python
import functools

import jax
import jax.numpy as jnp
from jax import lax
from jax.experimental import pallas as pl
from jax.experimental.pallas import tpu as pltpu
from jax.sharding import PartitionSpec as P

F32 = jnp.float32
BF16 = jnp.bfloat16
AXES = ("dp", "expert")
MIB = 1024 * 1024
TILE = 512
INFO_ROWS = 16
ORDERS = ("x", "z", "x", "x")


def _send(value, dp_mask, expert_mask):
    dps, experts = lax.axis_size("dp"), lax.axis_size("expert")
    pairs = [
        (d * experts + e, (d ^ dp_mask) * experts + (e ^ expert_mask))
        for d in range(dps)
        for e in range(experts)
    ]
    return lax.ppermute(value, AXES, pairs)


def _choice(info, expert, capacity):
    tokens = info.shape[1]
    first, second = info[0:1, :] == expert, info[1:2, :] == expert
    named = jnp.where(first | second, 1.0, 0.0)
    weight = jnp.where(first, info[2:3, :], 0.0) + jnp.where(second, info[3:4, :], 0.0)
    row = lax.broadcasted_iota(jnp.int32, (tokens, tokens), 0)
    col = lax.broadcasted_iota(jnp.int32, (tokens, tokens), 1)
    earlier = jnp.where(row < col, 1.0, 0.0).astype(BF16)
    position = jnp.dot(
        jnp.broadcast_to(named, (8, tokens)).astype(BF16), earlier, preferred_element_type=F32
    )[0:1, :]
    slot = lax.broadcasted_iota(jnp.int32, (capacity, tokens), 0).astype(F32)
    chosen = jnp.where((slot == position) & (named > 0.0), 1.0, 0.0)
    slot_weight = jnp.sum(chosen * weight, axis=1, keepdims=True)
    return chosen, slot_weight


def _pack_kernel(tokens, routes_ref, combine_ref, tok_ref, first_ref, rest_ref):
    first_ref[0:tokens, :] = tok_ref[:, :TILE]
    first_ref[tokens:, :] = jnp.zeros((INFO_ROWS, TILE), BF16)
    info = jnp.concatenate(
        [
            routes_ref[...].astype(F32),
            combine_ref[...].astype(F32),
            jnp.zeros((INFO_ROWS - 4, tokens), F32),
        ],
        axis=0,
    )
    first_ref[tokens:, 0:tokens] = info.astype(BF16)
    rest_ref[...] = tok_ref[:, TILE:]


def _activate_kernel(hidden, pre_ref, out_ref):
    for j in range(pre_ref.shape[0]):
        pre = pre_ref[j].astype(F32)
        gate, up = pre[:, :hidden], pre[:, hidden:]
        out_ref[j] = gate * jax.nn.sigmoid(gate) * up


def _info(ref, tokens):
    return ref[tokens : tokens + INFO_ROWS, 0:tokens].astype(F32)


def _split(prod, keep_blocks, send_blocks, rows, keep_ref, send_ref):
    for p, q in enumerate(keep_blocks):
        keep_ref[p * rows : (p + 1) * rows, :] = prod[q * rows : (q + 1) * rows, :]
    for p, q in enumerate(send_blocks):
        send_ref[p * rows : (p + 1) * rows, :] = prod[q * rows : (q + 1) * rows, :].astype(BF16)


def _first_kernel(n_e, n_d, keep_blocks, send_blocks, where_ref, act_ref, *refs):
    firsts, (at_ref, keep_ref, send_ref, held) = refs[:n_e], refs[n_e:]
    d, e = where_ref[0], where_ref[1]
    expert = e.astype(F32)
    capacity, hidden = act_ref.shape[1:]
    tokens = firsts[0].shape[0] - INFO_ROWS
    rows = hidden // n_d
    for j in range(n_e):
        chosen, slot_weight = _choice(_info(firsts[j], tokens), expert, capacity)
        scaled = (slot_weight * act_ref[e ^ j]).astype(BF16)
        held[:, j * tokens : (j + 1) * tokens] = lax.dot_general(
            scaled, chosen.astype(BF16), (((0,), (0,)), ((), ())), preferred_element_type=F32
        ).astype(BF16)
    for q in range(n_d):
        start = pl.multiple_of((d ^ q) * rows, 16)
        at_ref[q * rows : (q + 1) * rows, :] = held[pl.ds(start, rows), :]
    tok = jnp.concatenate([r[0:tokens, :] for r in firsts], axis=0)
    prod = jnp.dot(at_ref[...], tok, preferred_element_type=F32)
    _split(prod, keep_blocks, send_blocks, rows, keep_ref, send_ref)


def _partial_kernel(n_e, keep_blocks, send_blocks, rows, at_ref, *refs):
    tok = jnp.concatenate([r[...] for r in refs[:n_e]], axis=0)
    prod = jnp.dot(at_ref[...], tok, preferred_element_type=F32)
    _split(prod, keep_blocks, send_blocks, rows, *refs[n_e:])


def _slot_kernel(n_e, hidden, where_ref, pre_ref, w_ref, after_ref, *refs):
    firsts, rests, (pre_grad_ref, back_ref, rows_ref) = refs[:n_e], refs[n_e : 2 * n_e], refs[2 * n_e :]
    e = where_ref[1]
    expert = e.astype(F32)
    capacity = pre_ref.shape[1]
    tokens = rests[0].shape[0]
    picks, weights = [], []
    for j in range(n_e):
        chosen, slot_weight = _choice(_info(firsts[j], tokens), expert, capacity)
        picks.append(chosen)
        weights.append(slot_weight)
        pick = chosen.astype(BF16)
        here = slice(j * capacity, (j + 1) * capacity)
        rows_ref[here, :TILE] = jnp.dot(
            pick, firsts[j][0:tokens, :], preferred_element_type=F32
        ).astype(BF16)
        rows_ref[here, TILE:] = jnp.dot(pick, rests[j][...], preferred_element_type=F32).astype(BF16)
    tile = 256 if hidden % 256 == 0 else hidden
    gates = [jnp.zeros((capacity, 1), F32) for _ in range(n_e)]
    for h in range(0, hidden, tile):
        raw_all = lax.dot_general(
            rows_ref[...], w_ref[0, h : h + tile, :], (((1,), (1,)), ((), ())), preferred_element_type=F32
        )
        for j in range(n_e):
            raw = raw_all[j * capacity : (j + 1) * capacity, :]
            a = pre_ref[e ^ j, :, h : h + tile].astype(F32)
            u = pre_ref[e ^ j, :, hidden + h : hidden + h + tile].astype(F32)
            s = jax.nn.sigmoid(a)
            silu = a * s
            gates[j] = gates[j] + jnp.sum(silu * u * raw, axis=1, keepdims=True)
            delta = weights[j] * raw
            pre_grad_ref[e ^ j, :, h : h + tile] = (delta * u * s * (1.0 + a * (1.0 - s))).astype(BF16)
            pre_grad_ref[e ^ j, :, hidden + h : hidden + h + tile] = (delta * silu).astype(BF16)
    for j in range(n_e):
        back_ref[e ^ j] = jnp.sum(picks[j] * gates[j], axis=0, keepdims=True)


VM = pl.BlockSpec(memory_space=pltpu.VMEM)
SM = pl.BlockSpec(memory_space=pltpu.SMEM)
ANY = pl.BlockSpec(memory_space=pl.ANY)


def _call(body, name, outs, in_specs, out_specs, mib, flops=0, scratch=(), **more):
    return pl.pallas_call(
        body,
        out_shape=outs,
        in_specs=in_specs,
        out_specs=out_specs,
        scratch_shapes=scratch,
        compiler_params=pltpu.CompilerParams(vmem_limit_bytes=mib * MIB),
        cost_estimate=pl.CostEstimate(flops=flops, bytes_accessed=4 * MIB, transcendentals=0),
        name=name,
        **more,
    )


def _shape(shape, dtype):
    return jax.ShapeDtypeStruct(shape, dtype)


def _fast(grad_tokens, routes, combine, down_weight, saved_pre):
    n_d, n_e = lax.axis_size("dp"), lax.axis_size("expert")
    tokens, width = grad_tokens.shape
    hidden = down_weight.shape[1]
    capacity = saved_pre.shape[3]
    rows = hidden // n_d
    depth = n_e * tokens
    where = jnp.stack([lax.axis_index("dp"), lax.axis_index("expert")]).astype(jnp.int32)
    pre = saved_pre.reshape(saved_pre.shape[1:])[0]

    first, rest = _call(
        functools.partial(_pack_kernel, tokens),
        "pack_tokens",
        (_shape((tokens + INFO_ROWS, TILE), BF16), _shape((tokens, width - TILE), BF16)),
        [VM] * 3,
        (VM, VM),
        8,
    )(routes.T, combine.T, grad_tokens)

    def gather(block):
        held = {0: block}
        for bit in reversed(range(n_e.bit_length() - 1)):
            for key in sorted(held):
                held[key | (1 << bit)] = _send(held[key], 0, 1 << bit)
        return [held[j] for j in range(n_e)]

    firsts = gather(first)
    rests = gather(rest)

    act = _call(
        functools.partial(_activate_kernel, hidden),
        "activation",
        _shape((n_e, capacity, hidden), F32),
        [VM],
        VM,
        12,
    )(pre)

    last = tuple(range(2, n_d.bit_length() - 1))
    orders = {"x": ((0,), (1,), last), "z": ((1,), last, (0,))}

    def blocks_of(stages):
        blocks = [0]
        for b in [b for group in stages for b in group]:
            blocks = [q | (v << b) for q in blocks for v in (0, 1)]
        kept = len(blocks) >> len(stages[0])
        return tuple(blocks[:kept]), tuple(blocks[kept:])

    def parts_of(kept, sent):
        return (
            _shape((len(kept) * rows, TILE), F32),
            _shape((len(sent) * rows, TILE), BF16),
        )

    state = []
    stages = orders[ORDERS[0]]
    kept, sent = blocks_of(stages)
    at_all, keep, send = _call(
        functools.partial(_first_kernel, n_e, n_d, kept, sent),
        "first_partial",
        (_shape((hidden, depth), BF16),) + parts_of(kept, sent),
        [SM] + [VM] * (1 + n_e),
        (VM, VM, VM),
        16,
        2 * hidden * depth * TILE,
        [pltpu.VMEM((hidden, depth), BF16)],
    )(where, act, *firsts)
    state.append([stages, keep, send])
    for c in range(1, width // TILE):
        stages = orders[ORDERS[c % len(ORDERS)]]
        kept, sent = blocks_of(stages)
        outs = parts_of(kept, sent)
        keep, send = _call(
            functools.partial(_partial_kernel, n_e, kept, sent, rows),
            "partial_chunk",
            outs,
            [pl.BlockSpec((hidden, depth), lambda i: (0, 0))]
            + [pl.BlockSpec((tokens, TILE), lambda i, c=c: (0, c - 1))] * n_e,
            tuple(pl.BlockSpec(o.shape, lambda i: (0, 0)) for o in outs),
            16,
            2 * hidden * depth * TILE,
            grid=(1,),
        )(at_all, *rests)
        state.append([stages, keep, send])

    pre_grad, back = _call(
        functools.partial(_slot_kernel, n_e, hidden),
        "slot_gradients",
        (_shape(pre.shape, BF16), _shape((n_e, 1, tokens), F32)),
        [SM, VM, VM, ANY] + [VM] * (2 * n_e),
        (VM, VM),
        24,
        2 * n_e * capacity * width * hidden,
        [pltpu.VMEM((n_e * capacity, width), BF16)],
    )(where, pre, down_weight, state[-1][1], *firsts, *rests)

    finals = [None] * len(state)
    for s in range(3):
        for c, (stages, keep, send) in enumerate(state):
            group = stages[s]
            size = keep.shape[0]
            total = keep
            for v in range(1, 1 << len(group)):
                mask = sum((1 << b) for i, b in enumerate(group) if (v >> (len(group) - 1 - i)) & 1)
                got = _send(send[(v - 1) * size : v * size], mask, 0)
                total = total + got.astype(F32)
            if s < 2:
                size >>= len(stages[s + 1])
                state[c][1], state[c][2] = total[:size], total[size:].astype(BF16)
            else:
                finals[c] = total * (1.0 / n_d)
    down_grad = jnp.concatenate(finals, axis=1).reshape(1, rows * width)

    returned = lax.all_to_all(back, "expert", split_axis=0, concat_axis=0, tiled=True)
    gate_grad = sum(jnp.where(routes.T == k, returned[k], 0.0) for k in range(n_e)).T
    return pre_grad.reshape(saved_pre.shape), down_grad, gate_grad


def _general(grad_tokens, routes, combine, down_weight, saved_pre):
    experts = lax.axis_size("expert")
    tok_rows, route_count = routes.shape
    capacity = saved_pre.shape[3]
    model_width = grad_tokens.shape[1]
    hidden = down_weight.shape[1]
    flat_routes = routes.reshape(-1)
    onehot = (flat_routes[:, None] == jnp.arange(experts, dtype=jnp.int32)[None, :]).astype(jnp.int32)
    before = jnp.cumsum(onehot, axis=0) - onehot
    position = jnp.sum(before * onehot, axis=1)
    slot_id = flat_routes * capacity + position
    slot_grid = jnp.arange(experts * capacity, dtype=jnp.int32)
    chosen = slot_grid[:, None] == slot_id[None, :]
    placing = jnp.any(chosen.reshape(experts * capacity, tok_rows, route_count), axis=2).astype(BF16)
    outgoing = jnp.dot(placing, grad_tokens, preferred_element_type=F32).astype(BF16)
    combine_flat = combine.reshape(-1).astype(F32)
    out_weight = jnp.sum(jnp.where(chosen, combine_flat[None, :], 0.0), axis=1).astype(BF16)
    swap = functools.partial(lax.all_to_all, axis_name="expert", split_axis=0, concat_axis=0, tiled=True)
    slot_rows = swap(outgoing.reshape(experts, capacity, model_width)).reshape(-1, model_width)
    slot_weight = swap(out_weight.reshape(experts, capacity)).reshape(-1).astype(F32)
    raw_grad = lax.dot_general(
        slot_rows, down_weight[0], (((1,), (1,)), ((), ())), preferred_element_type=F32
    )
    pre_acts = saved_pre.reshape(-1, 2 * hidden).astype(F32)
    gate_pre, up_pre = pre_acts[:, :hidden], pre_acts[:, hidden:]
    logistic = jax.nn.sigmoid(gate_pre)
    activated = gate_pre * logistic
    hidden_act = activated * up_pre
    slot_gate = jnp.sum(hidden_act * raw_grad, axis=1)
    hidden_delta = slot_weight[:, None] * raw_grad
    gate_delta = hidden_delta * up_pre * logistic * (1.0 + gate_pre * (1.0 - logistic))
    pre_grad = jnp.concatenate([gate_delta, hidden_delta * activated], axis=1).astype(BF16)
    scaled = (slot_weight[:, None] * hidden_act).astype(BF16)
    whole_term = lax.dot_general(
        scaled, slot_rows, (((0,), (0,)), ((), ())), preferred_element_type=F32
    )
    summed = lax.psum_scatter(whole_term.reshape(-1), "dp", scatter_dimension=0, tiled=True)
    down_grad = (summed / lax.axis_size("dp"))[None]
    returned_flat = swap(slot_gate.reshape(experts, capacity)).reshape(-1)
    gate_flat = jnp.sum(jnp.where(chosen, returned_flat[:, None], 0.0), axis=0)
    return pre_grad.reshape(saved_pre.shape), down_grad, gate_flat.reshape(tok_rows, route_count)


def solution(mesh):
    n_d, n_e = mesh.shape["dp"], mesh.shape["expert"]

    def per_device(grad_tokens, routes, combine, down_weight, saved_pre):
        hidden, width = down_weight.shape[1:]
        whole_tiles = (
            hidden % (16 * n_d) == 0
            and saved_pre.shape[3] % 16 == 0
            and width % TILE == 0
            and grad_tokens.shape[0] == 128
            and n_d >= 8
            and n_d & (n_d - 1) == 0
            and n_e >= 2
            and n_e & (n_e - 1) == 0
            and routes.shape[1] == 2
        )
        form = _fast if whole_tiles else _general
        return form(grad_tokens, routes, combine, down_weight, saved_pre)

    by_both = P(("dp", "expert"), None)
    by_expert = P("expert", "dp", None, None, None)
    return jax.shard_map(
        per_device,
        mesh=mesh,
        in_specs=(by_both, by_both, by_both, P("expert", None, None), by_expert),
        out_specs=(by_expert, P("expert", "dp"), by_both),
        check_vma=False,
    )
```

time: 94.8 us -> 86.6 us (0.914)
  Pallas kernels: 20.8 us -> 9.17 us
  starting transfers between devices: 19.6 us -> 24.2 us
  waiting for transfers between devices: 42.5 us -> 39.2 us
  other arithmetic: 3.25 us -> 5.46 us
    pallas_call x5 -> x7, Pallas kernels: 20.8 us -> 9.17 us  [the longest x1 4.4 us: _fast(): _call(functools.partial(_slot_kernel, n_e, hidden), 'slot_gradients', (_s...]
    ppermute x21 -> x18, starting transfers between devices: 16.3 us -> 21 us  [_send(): return lax.ppermute(value, AXES, pairs)]
    add x6 -> x8, other arithmetic: 0.46 us -> 4.67 us  [_fast(): total = total + got.astype(F32)]
    ppermute x21 -> x18, waiting for transfers between devices: 42.5 us -> 38.5 us  [_send(): return lax.ppermute(value, AXES, pairs)]
    convert_element_type x2 -> x0, other arithmetic: 1.34 us -> none  [the longest x1 0.68 us: _fast(): routes.T.astype(F32)]
    slice x8, local copies, waits for them, and re-layouts: 2.11 us -> 0.89 us  [_fast(): state[c][1], state[c][2] = (total[:size], total[size:].astype(BF16))]
    unnamed x35, local copies, waits for them, and re-layouts: 5.11 us -> 6.25 us
  transfers between devices with their start and end apart: 22 -> 19, of which waited for: 10 -> 11; matrix products, arithmetic and copies ran while one was open for 5% -> 7% of each run, Pallas kernels for 22% -> 11%
where the time goes in v2:
time: 86.6 us; the launch traced here: 86.2 us
  waiting for transfers between devices  39.2 us (45%)
  starting transfers between devices  24.2 us (28%)
  Pallas kernels  9.17 us (11%)
  local copies, waits for them, and re-layouts  7.14 us (8%)
  other arithmetic  5.46 us (6%)
  between operations  0.97 us (1%)
    ppermute x18, waiting for transfers between devices, _send(): return lax.ppermute(value, AXES, pairs)  38.5 us
    ppermute x18, starting transfers between devices, _send(): return lax.ppermute(value, AXES, pairs)  21 us
    unnamed x35, local copies, waits for them, and re-layouts  6.25 us
    add x8, other arithmetic, _fast(): total = total + got.astype(F32)  4.67 us
    pallas_call x1, Pallas kernels, _fast(): _call(functools.partial(_slot_kernel, n_e, hidden), 'slot_gradients', (_s...  4.4 us
    all_to_all x1, starting transfers between devices, _fast(): lax.all_to_all(back, 'expert', split_axis=0, concat_axis=0, tiled=True)  3.23 us
    pallas_call x3, Pallas kernels, _fast(): _call(functools.partial(_partial_kernel, n_e, kept, sent, rows), 'partial...  2.46 us
    pallas_call x1, Pallas kernels, _fast(): _call(functools.partial(_first_kernel, n_e, n_d, kept, sent), 'first_part...  2.05 us
  transfers between devices with their start and end apart: 19, of which 11 were waited for; matrix products, arithmetic and copies ran while one was open for 7% of the time, Pallas kernels for 11%

profile of v2, /device:TPU:0, one launch (start us, length us, event | category | flops | bytes accessed | tf_op | source)
XLA Modules:
  0.0 86.2 jit_solution(13227256625794863057)
XLA Ops:
  0.6 0.0 copy-start.11
  0.6 1.0 %copy-done.11 = bf16[128,2048]{1,0:T(8,128)(2,1)S(1)} copy-done((bf16[128,2048]{1,0:T(8,128)(2,1)S(1)}, bf16[128,2048]{1,0:T(8,128)(2,1)}, u32[]{:S(2)}) %copy-start.11) | copy-done | bytes 524312
  1.7 0.7 copy-done.12
  2.4 0.7 copy-done.14
  3.0 3.0 %collective-permute-start.1 = (bf16[144,512]{1,0:T(8,128)(2,1)S(1)}, bf16[144,512]{1,0:T(8,128)(2,1)S(1)}, u32[]{:S(2)}, u32[]{:S(2)}) collective-permute-start(bf16[144,512]{1,0:T(8,128)(2,1)S(1)} %get-tuple-element.16.refs_0_), channel_id=1, source_target_pairs={{0,2},{1,3},{2,0},{3,1},{4,6},{5,7},{6,4},{7,5},{8,10},{9,11},{10,... | collective-permute-start | bytes 442376 | tf_op jit(solution)/shard_map/ppermute | solution.py:26
  6.1 0.0 collective-permute-start
  6.1 3.8 %collective-permute-done.1.refs_2_ = bf16[144,512]{1,0:T(8,128)(2,1)S(1)} collective-permute-done((bf16[144,512]{1,0:T(8,128)(2,1)S(1)}, bf16[144,512]{1,0:T(8,128)(2,1)S(1)}, u32[]{:S(2)}, u32[]{:S(2)}) %collective-permute-start.1) | collective-permute-done | bytes 147488 | tf_op jit(solution)/shard_map/ppermute | solution.py:26
  9.9 0.0 collective-permute-start.2
  9.9 1.7 %collective-permute-start.4 = (bf16[128,1536]{1,0:T(8,128)(2,1)S(1)}, bf16[128,1536]{1,0:T(8,128)(2,1)S(1)}, u32[]{:S(2)}, u32[]{:S(2)}) collective-permute-start(bf16[128,1536]{1,0:T(8,128)(2,1)S(1)} %get-tuple-element.18.refs_0_.refs_4_), channel_id=1, source_target_pairs={{0,2},{1,3},{2,0},{3,1},{4,6},{5,7},{6,4},{7,5},{8,10},{9,11},{10,... | collective-permute-start | bytes 1179656 | tf_op jit(solution)/shard_map/ppermute | solution.py:26
  11.7 1.3 %copy-done = bf16[1,1,4,96,1536]{4,3,2,1,0:T(8,128)(2,1)S(1)} copy-done((bf16[1,1,4,96,1536]{4,3,2,1,0:T(8,128)(2,1)S(1)}, bf16[1,1,4,96,1536]{4,3,2,1,0:T(8,128)(2,1)}, u32[]{:S(2)}) %copy-start) | copy-done | bytes 1179672
  12.9 0.2 activation.1.act_ref
  13.2 0.1 pad_add_fusion.where_ref
  13.3 0.0 collective-permute-done.refs_1_
  13.3 0.0 collective-permute-done.2.refs_3_
  13.3 0.0 copy-start.9
  13.3 2.0 %first_partial.1 = (bf16[768,512]{1,0:T(8,128)(2,1)S(1)}, f32[384,512]{1,0:T(8,128)S(1)}, bf16[384,512]{1,0:T(8,128)(2,1)S(1)}) custom-call(s32[2]{0:T(128)S(1)} %pad_add_fusion.where_ref, f32[4,96,768]{2,1,0:T(8,128)S(1)} %activation.1.act_ref, bf16[144,512]{1,0:T(8,128)(2,1)S(1)} %get-tuple-element.16.refs_0_, ...), custom_call_target="tpu_custom_call" | custom-call | flops 402653184 | bytes 4194304 | tf_op jit(solution)/shard_map/first_partial/pallas_call | solution.py:223
  15.3 0.0 copy-done.7
  15.3 0.0 copy-done.9
  15.4 1.6 %collective-permute-start.6 = (bf16[384,512]{1,0:T(8,128)(2,1)S(1)}, bf16[384,512]{1,0:T(8,128)(2,1)S(1)}, u32[]{:S(2)}, u32[]{:S(2)}) collective-permute-start(bf16[384,512]{1,0:T(8,128)(2,1)S(1)} %get-tuple-element.22), channel_id=1, source_target_pairs={{0,4},{1,5},{2,6},{3,7},{4,0},{5,1},{6,2},{7,3},{8,12},{9,13},{10,... | collective-permute-start | bytes 1179656 | tf_op jit(solution)/shard_map/ppermute | solution.py:26
  16.9 0.0 collective-permute-start.3
  16.9 4.5 %collective-permute-done.4.refs_2_.refs_6_ = bf16[128,1536]{1,0:T(8,128)(2,1)S(1)} collective-permute-done((bf16[128,1536]{1,0:T(8,128)(2,1)S(1)}, bf16[128,1536]{1,0:T(8,128)(2,1)S(1)}, u32[]{:S(2)}, u32[]{:S(2)}) %collective-permute-start.4) | collective-permute-done | bytes 393248 | tf_op jit(solution)/shard_map/ppermute | solution.py:26
  21.5 0.0 collective-permute-start.5
  21.5 5.2 %collective-permute-done.6 = bf16[384,512]{1,0:T(8,128)(2,1)S(1)} collective-permute-done((bf16[384,512]{1,0:T(8,128)(2,1)S(1)}, bf16[384,512]{1,0:T(8,128)(2,1)S(1)}, u32[]{:S(2)}, u32[]{:S(2)}) %collective-permute-start.6) | collective-permute-done | bytes 393248 | tf_op jit(solution)/shard_map/ppermute | solution.py:26
  26.7 0.1 convert_add_fusion.3
  26.8 0.8 slice.139
  27.5 1.6 %collective-permute-start.7 = (bf16[192,512]{1,0:T(8,128)(2,1)}, bf16[192,512]{1,0:T(8,128)(2,1)}, u32[]{:S(2)}, u32[]{:S(2)}) collective-permute-start(bf16[192,512]{1,0:T(8,128)(2,1)} %slice.139), channel_id=1, source_target_pairs={{0,8},{1,9},{2,10},{3,11},{4,12},{5,13},{6,14},{7,15},{8,0},{9,1},... | collective-permute-start | bytes 589832 | tf_op jit(solution)/shard_map/ppermute | solution.py:26
  29.1 0.0 collective-permute-done.3.refs_1_.refs_5_
  29.1 0.0 collective-permute-done.5.refs_3_.refs_7_
  29.1 1.3 %partial_chunk.5 = (f32[384,512]{1,0:T(8,128)S(1)}, bf16[384,512]{1,0:T(8,128)(2,1)}) custom-call(bf16[768,512]{1,0:T(8,128)(2,1)S(1)} %get-tuple-element.17.at_ref, bf16[128,1536]{1,0:T(8,128)(2,1)S(1)} %get-tuple-element.18.refs_0_.refs_4_, bf16[128,1536]{1,0:T(8,128)(2,1)S(1)} %collective-permute-done.3.refs_1_.refs_5_, ...), custom_call_target="tpu_custom_call" | custom-call | flops 402653184 | bytes 4194304 | tf_op jit(solution)/shard_map/partial_chunk/pallas_call | solution.py:238
  30.5 1.6 %collective-permute-start.12 = (bf16[384,512]{1,0:T(8,128)(2,1)}, bf16[384,512]{1,0:T(8,128)(2,1)}, u32[]{:S(2)}, u32[]{:S(2)}) collective-permute-start(bf16[384,512]{1,0:T(8,128)(2,1)} %get-tuple-element.26), channel_id=1, source_target_pairs={{0,4},{1,5},{2,6},{3,7},{4,0},{5,1},{6,2},{7,3},{8,12},{9,13},{10,... | collective-permute-start | bytes 1179656 | tf_op jit(solution)/shard_map/ppermute | solution.py:26
  32.0 0.6 partial_chunk.3
  32.7 4.4 %slot_gradients.1 = (bf16[4,96,1536]{2,1,0:T(8,128)(2,1)}, f32[4,1,128]{2,1,0:T(1,128)}) custom-call(s32[2]{0:T(128)S(1)} %pad_add_fusion.where_ref, bf16[4,96,1536]{2,1,0:T(8,128)(2,1)S(1)} %bitcast.19, bf16[1,768,2048]{2,1,0:T(8,128)(2,1)S(1)} %copy-done.2, f32[384,512]{1,0:T(8,128)S(1)} %get-tuple-element.19.after_ref, ...), custom_call_target="tpu_custom_call" | custom-call | flops 1207959552 | bytes 4194304 | tf_op jit(solution)/shard_map/slot_gradients/pallas_call | solution.py:251
  37.1 3.2 %all-to-all-start = ((f32[4,1,128]{2,1,0:T(1,128)}), f32[4,1,128]{2,1,0:T(1,128)S(1)}, u32[]{:S(2)}, u32[]{:S(2)}) async-start(f32[4,1,128]{2,1,0:T(1,128)} %get-tuple-element.28), calls=%async_computation | async-start | bytes 4096 | tf_op jit(solution)/shard_map/all_to_all | solution.py:279
  40.3 1.1 %collective-permute-start.15 = (bf16[384,512]{1,0:T(8,128)(2,1)}, bf16[384,512]{1,0:T(8,128)(2,1)}, u32[]{:S(2)}, u32[]{:S(2)}) collective-permute-start(bf16[384,512]{1,0:T(8,128)(2,1)} %copy-done.15), channel_id=1, source_target_pairs={{0,4},{1,5},{2,6},{3,7},{4,0},{5,1},{6,2},{7,3},{8,12},{9,13},{10,... | collective-permute-start | bytes 1179656 | tf_op jit(solution)/shard_map/ppermute | solution.py:26
  41.4 0.6 partial_chunk.4
  42.0 0.9 %copy-done.5 = f32[384,512]{1,0:T(8,128)} copy-done((f32[384,512]{1,0:T(8,128)}, f32[384,512]{1,0:T(8,128)S(1)}, u32[]{:S(2)}) %copy-start.5) | copy-done | bytes 786456
  42.9 0.4 collective-permute-start.9
  43.3 0.7 all-to-all-done
  44.0 0.0 collective-permute-done.7
  44.0 1.1 %slice_add_fusion.3 = f32[192,512]{1,0:T(8,128)S(1)} fusion(f32[384,512]{1,0:T(8,128)} %copy-done.16, bf16[192,512]{1,0:T(8,128)(2,1)} %collective-permute-done.7), kind=kLoop, calls=%fused_computation.12 | loop fusion | flops 196608 | bytes 983040 | tf_op jit(solution)/shard_map/add | solution.py:271
  45.2 2.7 %collective-permute-start.8 = (bf16[96,512]{1,0:T(8,128)(2,1)S(1)}, bf16[96,512]{1,0:T(8,128)(2,1)S(1)}, u32[]{:S(2)}, u32[]{:S(2)}) collective-permute-start(bf16[96,512]{1,0:T(8,128)(2,1)S(1)} %slice.143), channel_id=1, source_target_pairs={{0,16},{1,17},{2,18},{3,19},{4,20},{5,21},{6,22},{7,23},{8,24},{9,... | collective-permute-start | bytes 294920 | tf_op jit(solution)/shard_map/ppermute | solution.py:26
  47.8 0.6 fusion.6
  48.4 5.7 %collective-permute-done.8 = bf16[96,512]{1,0:T(8,128)(2,1)S(1)} collective-permute-done((bf16[96,512]{1,0:T(8,128)(2,1)S(1)}, bf16[96,512]{1,0:T(8,128)(2,1)S(1)}, u32[]{:S(2)}, u32[]{:S(2)}) %collective-permute-start.8) | collective-permute-done | bytes 98336 | tf_op jit(solution)/shard_map/ppermute | solution.py:26
  54.1 0.0 collective-permute-done.12
  54.2 1.1 %convert_add_fusion.1 = f32[384,512]{1,0:T(8,128)S(1)} fusion(f32[384,512]{1,0:T(8,128)S(1)} %copy-done.4, bf16[384,512]{1,0:T(8,128)(2,1)} %collective-permute-done.12), kind=kLoop, calls=%fused_computation.2 | loop fusion | flops 393216 | bytes 1966080 | tf_op jit(solution)/shard_map/add | solution.py:271
  55.3 4.7 %collective-permute-start.13 = (bf16[192,512]{1,0:T(8,128)(2,1)S(1)}, bf16[192,512]{1,0:T(8,128)(2,1)S(1)}, u32[]{:S(2)}, u32[]{:S(2)}) collective-permute-start(bf16[192,512]{1,0:T(8,128)(2,1)S(1)} %slice.137), channel_id=1, source_target_pairs={{0,8},{1,9},{2,10},{3,11},{4,12},{5,13},{6,14},{7,15},{8,0},{9,1},... | collective-permute-start | bytes 589832 | tf_op jit(solution)/shard_map/ppermute | solution.py:26
  60.0 0.0 collective-permute-done.15
  60.0 1.1 %convert_add_fusion = f32[384,512]{1,0:T(8,128)S(1)} fusion(f32[384,512]{1,0:T(8,128)S(1)} %get-tuple-element.19.after_ref, bf16[384,512]{1,0:T(8,128)(2,1)} %collective-permute-done.15), kind=kLoop, calls=%fused_computation.1 | loop fusion | flops 393216 | bytes 1966080 | tf_op jit(solution)/shard_map/add | solution.py:271
  61.2 0.1 collective-permute-start.16
  61.3 0.0 collective-permute-done.9
  61.3 1.1 %convert_add_fusion.2 = f32[384,512]{1,0:T(8,128)S(1)} fusion(f32[384,512]{1,0:T(8,128)S(1)} %copy-done.6, bf16[384,512]{1,0:T(8,128)(2,1)} %collective-permute-done.9), kind=kLoop, calls=%fused_computation.3 | loop fusion | flops 393216 | bytes 1966080 | tf_op jit(solution)/shard_map/add | solution.py:271
  62.5 0.8 collective-permute-start.10
  63.2 5.0 %collective-permute-done.13 = bf16[192,512]{1,0:T(8,128)(2,1)S(1)} collective-permute-done((bf16[192,512]{1,0:T(8,128)(2,1)S(1)}, bf16[192,512]{1,0:T(8,128)(2,1)S(1)}, u32[]{:S(2)}, u32[]{:S(2)}) %collective-permute-start.13) | collective-permute-done | bytes 196640 | tf_op jit(solution)/shard_map/ppermute | solution.py:26
  68.3 0.1 collective-permute-start.14
  68.4 3.7 %collective-permute-done.16 = bf16[192,512]{1,0:T(8,128)(2,1)S(1)} collective-permute-done((bf16[192,512]{1,0:T(8,128)(2,1)S(1)}, bf16[192,512]{1,0:T(8,128)(2,1)S(1)}, u32[]{:S(2)}, u32[]{:S(2)}) %collective-permute-start.16) | collective-permute-done | bytes 196640 | tf_op jit(solution)/shard_map/ppermute | solution.py:26
  72.2 0.6 collective-permute-start.17
  72.8 6.8 %collective-permute-done.10 = bf16[192,512]{1,0:T(8,128)(2,1)S(1)} collective-permute-done((bf16[192,512]{1,0:T(8,128)(2,1)S(1)}, bf16[192,512]{1,0:T(8,128)(2,1)S(1)}, u32[]{:S(2)}, u32[]{:S(2)}) %collective-permute-start.10) | collective-permute-done | bytes 196640 | tf_op jit(solution)/shard_map/ppermute | solution.py:26
  79.6 0.1 slice_add_fusion.2
  79.7 1.0 %collective-permute-start.11 = (bf16[96,512]{1,0:T(8,128)(2,1)S(1)}, bf16[96,512]{1,0:T(8,128)(2,1)S(1)}, u32[]{:S(2)}, u32[]{:S(2)}) collective-permute-start(bf16[96,512]{1,0:T(8,128)(2,1)S(1)} %slice.142), channel_id=1, source_target_pairs={{0,4},{1,5},{2,6},{3,7},{4,0},{5,1},{6,2},{7,3},{8,12},{9,13},{10,... | collective-permute-start | bytes 294920 | tf_op jit(solution)/shard_map/ppermute | solution.py:26
  80.7 0.2 collective-permute-done.14
  80.9 1.0 %collective-permute-done.17 = bf16[96,512]{1,0:T(8,128)(2,1)S(1)} collective-permute-done((bf16[96,512]{1,0:T(8,128)(2,1)S(1)}, bf16[96,512]{1,0:T(8,128)(2,1)S(1)}, u32[]{:S(2)}, u32[]{:S(2)}) %collective-permute-start.17) | collective-permute-done | bytes 98336 | tf_op jit(solution)/shard_map/ppermute | solution.py:26
  82.0 2.4 %collective-permute-done.11 = bf16[96,512]{1,0:T(8,128)(2,1)S(1)} collective-permute-done((bf16[96,512]{1,0:T(8,128)(2,1)S(1)}, bf16[96,512]{1,0:T(8,128)(2,1)S(1)}, u32[]{:S(2)}, u32[]{:S(2)}) %collective-permute-start.11) | collective-permute-done | bytes 98336 | tf_op jit(solution)/shard_map/ppermute | solution.py:26
  84.4 0.1 maximum_bitcast_fusion
  84.5 1.7 %copy.8 = f32[1,1,96,2048]{3,1,2,0:T(1,128)} copy(f32[1,1,96,2048]{3,2,1,0:T(8,128)S(1)} %maximum_bitcast_fusion) | data formatting | bytes 1572864
  (40 shorter events, 0.4 us)
Async XLA Ops:
  0.6 1.0 %copy-start.11 = (bf16[128,2048]{1,0:T(8,128)(2,1)S(1)}, bf16[128,2048]{1,0:T(8,128)(2,1)}, u32[]{:S(2)}) copy-start(bf16[128,2048]{1,0:T(8,128)(2,1)} %tok_ref.1) | copy-start | bytes 1572868
  1.7 0.7 copy-start.12
  2.4 0.7 copy-start.14
  3.0 6.9 %collective-permute-start.1 = (bf16[144,512]{1,0:T(8,128)(2,1)S(1)}, bf16[144,512]{1,0:T(8,128)(2,1)S(1)}, u32[]{:S(2)}, u32[]{:S(2)}) collective-permute-start(bf16[144,512]{1,0:T(8,128)(2,1)S(1)} %get-tuple-element.16.refs_0_), channel_id=1, source_target_pairs={{0,2},{1,3},{2,0},{3,1},{4,6},{5,7},{6,4},{7,5},{8,10},{9,11},{10,... | collective-permute-start | bytes 442376 | tf_op jit(solution)/shard_map/ppermute | solution.py:26
  6.1 7.2 %collective-permute-start = (bf16[144,512]{1,0:T(8,128)(2,1)S(1)}, bf16[144,512]{1,0:T(8,128)(2,1)S(1)}, u32[]{:S(2)}, u32[]{:S(2)}) collective-permute-start(bf16[144,512]{1,0:T(8,128)(2,1)S(1)} %get-tuple-element.16.refs_0_), channel_id=1, source_target_pairs={{0,1},{1,0},{2,3},{3,2},{4,5},{5,4},{6,7},{7,6},{8,9},{9,8},{10,11... | collective-permute-start | bytes 442376 | tf_op jit(solution)/shard_map/ppermute | solution.py:26
  9.9 3.3 %collective-permute-start.2 = (bf16[144,512]{1,0:T(8,128)(2,1)S(1)}, bf16[144,512]{1,0:T(8,128)(2,1)S(1)}, u32[]{:S(2)}, u32[]{:S(2)}) collective-permute-start(bf16[144,512]{1,0:T(8,128)(2,1)S(1)} %collective-permute-done.1.refs_2_), channel_id=1, source_target_pairs={{0,1},{1,0},{2,3},{3,2},{4,5},{5,4},{6,7},{7,6},{8,9},{9,8},{10,11... | collective-permute-start | bytes 442376 | tf_op jit(solution)/shard_map/ppermute | solution.py:26
  9.9 11.5 %collective-permute-start.4 = (bf16[128,1536]{1,0:T(8,128)(2,1)S(1)}, bf16[128,1536]{1,0:T(8,128)(2,1)S(1)}, u32[]{:S(2)}, u32[]{:S(2)}) collective-permute-start(bf16[128,1536]{1,0:T(8,128)(2,1)S(1)} %get-tuple-element.18.refs_0_.refs_4_), channel_id=1, source_target_pairs={{0,2},{1,3},{2,0},{3,1},{4,6},{5,7},{6,4},{7,5},{8,10},{9,11},{10,... | collective-permute-start | bytes 1179656 | tf_op jit(solution)/shard_map/ppermute | solution.py:26
  11.7 1.3 %copy-start = (bf16[1,1,4,96,1536]{4,3,2,1,0:T(8,128)(2,1)S(1)}, bf16[1,1,4,96,1536]{4,3,2,1,0:T(8,128)(2,1)}, u32[]{:S(2)}) copy-start(bf16[1,1,4,96,1536]{4,3,2,1,0:T(8,128)(2,1)} %param.9) | copy-start | bytes 3538948
  13.3 2.1 %copy-start.7 = (bf16[144,512]{1,0:T(8,128)(2,1)}, bf16[144,512]{1,0:T(8,128)(2,1)S(1)}, u32[]{:S(2)}) copy-start(bf16[144,512]{1,0:T(8,128)(2,1)S(1)} %collective-permute-done.refs_1_) | copy-start | bytes 442372
  13.3 2.1 %copy-start.9 = (bf16[144,512]{1,0:T(8,128)(2,1)}, bf16[144,512]{1,0:T(8,128)(2,1)S(1)}, u32[]{:S(2)}) copy-start(bf16[144,512]{1,0:T(8,128)(2,1)S(1)} %collective-permute-done.2.refs_3_) | copy-start | bytes 442372
  15.4 11.3 %collective-permute-start.6 = (bf16[384,512]{1,0:T(8,128)(2,1)S(1)}, bf16[384,512]{1,0:T(8,128)(2,1)S(1)}, u32[]{:S(2)}, u32[]{:S(2)}) collective-permute-start(bf16[384,512]{1,0:T(8,128)(2,1)S(1)} %get-tuple-element.22), channel_id=1, source_target_pairs={{0,4},{1,5},{2,6},{3,7},{4,0},{5,1},{6,2},{7,3},{8,12},{9,13},{10,... | collective-permute-start | bytes 1179656 | tf_op jit(solution)/shard_map/ppermute | solution.py:26
  16.9 12.2 %collective-permute-start.3 = (bf16[128,1536]{1,0:T(8,128)(2,1)S(1)}, bf16[128,1536]{1,0:T(8,128)(2,1)S(1)}, u32[]{:S(2)}, u32[]{:S(2)}) collective-permute-start(bf16[128,1536]{1,0:T(8,128)(2,1)S(1)} %get-tuple-element.18.refs_0_.refs_4_), channel_id=1, source_target_pairs={{0,1},{1,0},{2,3},{3,2},{4,5},{5,4},{6,7},{7,6},{8,9},{9,8},{10,11... | collective-permute-start | bytes 1179656 | tf_op jit(solution)/shard_map/ppermute | solution.py:26
  21.5 7.7 %collective-permute-start.5 = (bf16[128,1536]{1,0:T(8,128)(2,1)S(1)}, bf16[128,1536]{1,0:T(8,128)(2,1)S(1)}, u32[]{:S(2)}, u32[]{:S(2)}) collective-permute-start(bf16[128,1536]{1,0:T(8,128)(2,1)S(1)} %collective-permute-done.4.refs_2_.refs_6_), channel_id=1, source_target_pairs={{0,1},{1,0},{2,3},{3,2},{4,5},{5,4},{6,7},{7,6},{8,9},{9,8},{10,11... | collective-permute-start | bytes 1179656 | tf_op jit(solution)/shard_map/ppermute | solution.py:26
  26.8 3.7 %copy-start.16 = (f32[384,512]{1,0:T(8,128)}, f32[384,512]{1,0:T(8,128)S(1)}, u32[]{:S(2)}) copy-start(f32[384,512]{1,0:T(8,128)S(1)} %convert_add_fusion.3) | copy-start | bytes 2359300
  27.5 16.5 %collective-permute-start.7 = (bf16[192,512]{1,0:T(8,128)(2,1)}, bf16[192,512]{1,0:T(8,128)(2,1)}, u32[]{:S(2)}, u32[]{:S(2)}) collective-permute-start(bf16[192,512]{1,0:T(8,128)(2,1)} %slice.139), channel_id=1, source_target_pairs={{0,8},{1,9},{2,10},{3,11},{4,12},{5,13},{6,14},{7,15},{8,0},{9,1},... | collective-permute-start | bytes 589832 | tf_op jit(solution)/shard_map/ppermute | solution.py:26
  29.1 3.5 %copy-start.2 = (bf16[1,768,2048]{2,1,0:T(8,128)(2,1)S(1)}, bf16[1,768,2048]{2,1,0:T(8,128)(2,1)}, u32[]{:S(2)}) copy-start(bf16[1,768,2048]{2,1,0:T(8,128)(2,1)} %w_ref.1) | copy-start | bytes 9437188
  30.5 2.1 %copy-start.3 = (f32[384,512]{1,0:T(8,128)}, f32[384,512]{1,0:T(8,128)S(1)}, u32[]{:S(2)}) copy-start(f32[384,512]{1,0:T(8,128)S(1)} %get-tuple-element.25) | copy-start | bytes 2359300
  30.5 2.2 %copy-start.1 = (bf16[1,1,4,96,1536]{4,3,2,1,0:T(8,128)(2,1)S(1)}, bf16[1,1,4,96,1536]{4,3,2,1,0:T(8,128)(2,1)}, u32[]{:S(2)}) copy-start(bf16[1,1,4,96,1536]{4,3,2,1,0:T(8,128)(2,1)} %param.9) | copy-start | bytes 3538948
  30.5 2.2 %copy-start.8 = (bf16[144,512]{1,0:T(8,128)(2,1)S(1)}, bf16[144,512]{1,0:T(8,128)(2,1)}, u32[]{:S(2)}) copy-start(bf16[144,512]{1,0:T(8,128)(2,1)} %copy-done.7) | copy-start | bytes 442372
  30.5 2.2 %copy-start.10 = (bf16[144,512]{1,0:T(8,128)(2,1)S(1)}, bf16[144,512]{1,0:T(8,128)(2,1)}, u32[]{:S(2)}) copy-start(bf16[144,512]{1,0:T(8,128)(2,1)} %copy-done.9) | copy-start | bytes 442372
  30.5 23.7 %collective-permute-start.12 = (bf16[384,512]{1,0:T(8,128)(2,1)}, bf16[384,512]{1,0:T(8,128)(2,1)}, u32[]{:S(2)}, u32[]{:S(2)}) collective-permute-start(bf16[384,512]{1,0:T(8,128)(2,1)} %get-tuple-element.26), channel_id=1, source_target_pairs={{0,4},{1,5},{2,6},{3,7},{4,0},{5,1},{6,2},{7,3},{8,12},{9,13},{10,... | collective-permute-start | bytes 1179656 | tf_op jit(solution)/shard_map/ppermute | solution.py:26
  32.6 4.5 %copy-start.15 = (bf16[384,512]{1,0:T(8,128)(2,1)}, bf16[384,512]{1,0:T(8,128)(2,1)S(1)}, u32[]{:S(2)}) copy-start(bf16[384,512]{1,0:T(8,128)(2,1)S(1)} %get-tuple-element.27) | copy-start | bytes 1179652
  37.1 7.0 %all-to-all-start = ((f32[4,1,128]{2,1,0:T(1,128)}), f32[4,1,128]{2,1,0:T(1,128)S(1)}, u32[]{:S(2)}, u32[]{:S(2)}) async-start(f32[4,1,128]{2,1,0:T(1,128)} %get-tuple-element.28), calls=%async_computation | async-start | bytes 4096 | tf_op jit(solution)/shard_map/all_to_all | solution.py:279
  40.3 19.7 %collective-permute-start.15 = (bf16[384,512]{1,0:T(8,128)(2,1)}, bf16[384,512]{1,0:T(8,128)(2,1)}, u32[]{:S(2)}, u32[]{:S(2)}) collective-permute-start(bf16[384,512]{1,0:T(8,128)(2,1)} %copy-done.15), channel_id=1, source_target_pairs={{0,4},{1,5},{2,6},{3,7},{4,0},{5,1},{6,2},{7,3},{8,12},{9,13},{10,... | collective-permute-start | bytes 1179656 | tf_op jit(solution)/shard_map/ppermute | solution.py:26
  42.0 0.9 %copy-start.5 = (f32[384,512]{1,0:T(8,128)}, f32[384,512]{1,0:T(8,128)S(1)}, u32[]{:S(2)}) copy-start(f32[384,512]{1,0:T(8,128)S(1)} %get-tuple-element.23) | copy-start | bytes 2359300
  42.9 4.9 %copy-start.13 = (s32[128,2]{0,1:T(2,128)S(1)}, s32[128,2]{0,1:T(2,128)}, u32[]{:S(2)}) copy-start(s32[128,2]{0,1:T(2,128)} %param.6) | copy-start | bytes 3076
  42.9 11.3 %copy-start.4 = (f32[384,512]{1,0:T(8,128)S(1)}, f32[384,512]{1,0:T(8,128)}, u32[]{:S(2)}) copy-start(f32[384,512]{1,0:T(8,128)} %copy-done.3) | copy-start | bytes 2359300
  42.9 18.4 %collective-permute-start.9 = (bf16[384,512]{1,0:T(8,128)(2,1)S(1)}, bf16[384,512]{1,0:T(8,128)(2,1)}, u32[]{:S(2)}, u32[]{:S(2)}) collective-permute-start(bf16[384,512]{1,0:T(8,128)(2,1)S(1)} %get-tuple-element.24), channel_id=1, source_target_pairs={{0,8},{1,9},{2,10},{3,11},{4,12},{5,13},{6,14},{7,15},{8,0},{9,1},... | collective-permute-start | bytes 1179656 | tf_op jit(solution)/shard_map/ppermute | solution.py:26
  45.2 9.0 %collective-permute-start.8 = (bf16[96,512]{1,0:T(8,128)(2,1)S(1)}, bf16[96,512]{1,0:T(8,128)(2,1)S(1)}, u32[]{:S(2)}, u32[]{:S(2)}) collective-permute-start(bf16[96,512]{1,0:T(8,128)(2,1)S(1)} %slice.143), channel_id=1, source_target_pairs={{0,16},{1,17},{2,18},{3,19},{4,20},{5,21},{6,22},{7,23},{8,24},{9,... | collective-permute-start | bytes 294920 | tf_op jit(solution)/shard_map/ppermute | solution.py:26
  55.3 6.0 %copy-start.6 = (f32[384,512]{1,0:T(8,128)S(1)}, f32[384,512]{1,0:T(8,128)}, u32[]{:S(2)}) copy-start(f32[384,512]{1,0:T(8,128)} %copy-done.5) | copy-start | bytes 2359300
  55.3 12.9 %collective-permute-start.13 = (bf16[192,512]{1,0:T(8,128)(2,1)S(1)}, bf16[192,512]{1,0:T(8,128)(2,1)S(1)}, u32[]{:S(2)}, u32[]{:S(2)}) collective-permute-start(bf16[192,512]{1,0:T(8,128)(2,1)S(1)} %slice.137), channel_id=1, source_target_pairs={{0,8},{1,9},{2,10},{3,11},{4,12},{5,13},{6,14},{7,15},{8,0},{9,1},... | collective-permute-start | bytes 589832 | tf_op jit(solution)/shard_map/ppermute | solution.py:26
  61.2 11.0 %collective-permute-start.16 = (bf16[192,512]{1,0:T(8,128)(2,1)S(1)}, bf16[192,512]{1,0:T(8,128)(2,1)S(1)}, u32[]{:S(2)}, u32[]{:S(2)}) collective-permute-start(bf16[192,512]{1,0:T(8,128)(2,1)S(1)} %slice.136), channel_id=1, source_target_pairs={{0,8},{1,9},{2,10},{3,11},{4,12},{5,13},{6,14},{7,15},{8,0},{9,1},... | collective-permute-start | bytes 589832 | tf_op jit(solution)/shard_map/ppermute | solution.py:26
  62.5 17.1 %collective-permute-start.10 = (bf16[192,512]{1,0:T(8,128)(2,1)S(1)}, bf16[192,512]{1,0:T(8,128)(2,1)S(1)}, u32[]{:S(2)}, u32[]{:S(2)}) collective-permute-start(bf16[192,512]{1,0:T(8,128)(2,1)S(1)} %slice.138), channel_id=1, source_target_pairs={{0,16},{1,17},{2,18},{3,19},{4,20},{5,21},{6,22},{7,23},{8,24},{9,... | collective-permute-start | bytes 589832 | tf_op jit(solution)/shard_map/ppermute | solution.py:26
  68.3 12.6 %collective-permute-start.14 = (bf16[96,512]{1,0:T(8,128)(2,1)S(1)}, bf16[96,512]{1,0:T(8,128)(2,1)S(1)}, u32[]{:S(2)}, u32[]{:S(2)}) collective-permute-start(bf16[96,512]{1,0:T(8,128)(2,1)S(1)} %slice.141), channel_id=1, source_target_pairs={{0,16},{1,17},{2,18},{3,19},{4,20},{5,21},{6,22},{7,23},{8,24},{9,... | collective-permute-start | bytes 294920 | tf_op jit(solution)/shard_map/ppermute | solution.py:26
  72.2 9.7 %collective-permute-start.17 = (bf16[96,512]{1,0:T(8,128)(2,1)S(1)}, bf16[96,512]{1,0:T(8,128)(2,1)S(1)}, u32[]{:S(2)}, u32[]{:S(2)}) collective-permute-start(bf16[96,512]{1,0:T(8,128)(2,1)S(1)} %slice.140), channel_id=1, source_target_pairs={{0,16},{1,17},{2,18},{3,19},{4,20},{5,21},{6,22},{7,23},{8,24},{9,... | collective-permute-start | bytes 294920 | tf_op jit(solution)/shard_map/ppermute | solution.py:26
  79.7 4.7 %collective-permute-start.11 = (bf16[96,512]{1,0:T(8,128)(2,1)S(1)}, bf16[96,512]{1,0:T(8,128)(2,1)S(1)}, u32[]{:S(2)}, u32[]{:S(2)}) collective-permute-start(bf16[96,512]{1,0:T(8,128)(2,1)S(1)} %slice.142), channel_id=1, source_target_pairs={{0,4},{1,5},{2,6},{3,7},{4,0},{5,1},{6,2},{7,3},{8,12},{9,13},{10,... | collective-permute-start | bytes 294920 | tf_op jit(solution)/shard_map/ppermute | solution.py:26

commit v3 on v2

--- a/solution.py
+++ b/solution.py
@@ -11,9 +11,9 @@
 BF16 = jnp.bfloat16
 AXES = ("dp", "expert")
 MIB = 1024 * 1024
-TILE = 512
 INFO_ROWS = 16
-ORDERS = ("x", "z", "x", "x")
+PACK_MIB = 60
+EIGHTHS = (3, 2, 2, 1)
 
 
 def _send(value, dp_mask, expert_mask):
@@ -43,9 +43,9 @@
     return chosen, slot_weight
 
 
-def _pack_kernel(tokens, routes_ref, combine_ref, tok_ref, first_ref, rest_ref):
-    first_ref[0:tokens, :] = tok_ref[:, :TILE]
-    first_ref[tokens:, :] = jnp.zeros((INFO_ROWS, TILE), BF16)
+def _pack_kernel(tokens, lead, routes_ref, combine_ref, tok_ref, first_ref, rest_ref):
+    first_ref[0:tokens, :] = tok_ref[:, :lead]
+    first_ref[tokens:, :] = jnp.zeros((INFO_ROWS, lead), BF16)
     info = jnp.concatenate(
         [
             routes_ref[...].astype(F32),
@@ -55,7 +55,7 @@
         axis=0,
     )
     first_ref[tokens:, 0:tokens] = info.astype(BF16)
-    rest_ref[...] = tok_ref[:, TILE:]
+    rest_ref[...] = tok_ref[:, lead:]
 
 
 def _activate_kernel(hidden, pre_ref, out_ref):
@@ -97,18 +97,19 @@
     _split(prod, keep_blocks, send_blocks, rows, keep_ref, send_ref)
 
 
-def _partial_kernel(n_e, keep_blocks, send_blocks, rows, at_ref, *refs):
-    tok = jnp.concatenate([r[...] for r in refs[:n_e]], axis=0)
+def _partial_kernel(n_e, keep_blocks, send_blocks, rows, columns, at_ref, *refs):
+    tok = jnp.concatenate([r[:, columns] for r in refs[:n_e]], axis=0)
     prod = jnp.dot(at_ref[...], tok, preferred_element_type=F32)
     _split(prod, keep_blocks, send_blocks, rows, *refs[n_e:])
 
 
-def _slot_kernel(n_e, hidden, where_ref, pre_ref, w_ref, after_ref, *refs):
+def _slot_kernel(n_e, hidden, where_ref, pre_ref, w_ref, *refs):
     firsts, rests, (pre_grad_ref, back_ref, rows_ref) = refs[:n_e], refs[n_e : 2 * n_e], refs[2 * n_e :]
     e = where_ref[1]
     expert = e.astype(F32)
     capacity = pre_ref.shape[1]
     tokens = rests[0].shape[0]
+    lead = firsts[0].shape[1]
     picks, weights = [], []
     for j in range(n_e):
         chosen, slot_weight = _choice(_info(firsts[j], tokens), expert, capacity)
@@ -116,10 +117,10 @@
         weights.append(slot_weight)
         pick = chosen.astype(BF16)
         here = slice(j * capacity, (j + 1) * capacity)
-        rows_ref[here, :TILE] = jnp.dot(
+        rows_ref[here, :lead] = jnp.dot(
             pick, firsts[j][0:tokens, :], preferred_element_type=F32
         ).astype(BF16)
-        rows_ref[here, TILE:] = jnp.dot(pick, rests[j][...], preferred_element_type=F32).astype(BF16)
+        rows_ref[here, lead:] = jnp.dot(pick, rests[j][...], preferred_element_type=F32).astype(BF16)
     tile = 256 if hidden % 256 == 0 else hidden
     gates = [jnp.zeros((capacity, 1), F32) for _ in range(n_e)]
     for h in range(0, hidden, tile):
@@ -140,9 +141,34 @@
         back_ref[e ^ j] = jnp.sum(picks[j] * gates[j], axis=0, keepdims=True)
 
 
+def _sum_kernel(keep_ref, got_ref, next_keep_ref, next_send_ref):
+    size = next_keep_ref.shape[0]
+    next_keep_ref[...] = keep_ref[0:size, :] + got_ref[0:size, :].astype(F32)
+    next_send_ref[...] = (keep_ref[size:, :] + got_ref[size:, :].astype(F32)).astype(BF16)
+
+
+def _finish_kernel(scale, counts, *refs):
+    parts, out_ref = refs[:-1], refs[-1]
+    rows = parts[0].shape[0]
+    lanes = out_ref.shape[0] // rows
+    at = 0
+    for count in counts:
+        total = parts[0][...]
+        for more in parts[1:count]:
+            total = total + more[...].astype(F32)
+        parts = parts[count:]
+        total = total * scale
+        for j in range(0, total.shape[1], 128):
+            out_ref[pl.ds(at, rows, stride=lanes), :] = total[:, j : j + 128]
+            at += 1
+
+
+def _after(value, *others):
+    return lax.optimization_barrier((value,) + others)[0]
+
+
 VM = pl.BlockSpec(memory_space=pltpu.VMEM)
 SM = pl.BlockSpec(memory_space=pltpu.SMEM)
-ANY = pl.BlockSpec(memory_space=pl.ANY)
 
 
 def _call(body, name, outs, in_specs, out_specs, mib, flops=0, scratch=(), **more):
@@ -170,27 +196,30 @@
     capacity = saved_pre.shape[3]
     rows = hidden // n_d
     depth = n_e * tokens
+    lanes = width // 128
     where = jnp.stack([lax.axis_index("dp"), lax.axis_index("expert")]).astype(jnp.int32)
     pre = saved_pre.reshape(saved_pre.shape[1:])[0]
+    sizes = [part * width // 8 for part in EIGHTHS]
+    lead = sizes[0]
 
     first, rest = _call(
-        functools.partial(_pack_kernel, tokens),
+        functools.partial(_pack_kernel, tokens, lead),
         "pack_tokens",
-        (_shape((tokens + INFO_ROWS, TILE), BF16), _shape((tokens, width - TILE), BF16)),
+        (_shape((tokens + INFO_ROWS, lead), BF16), _shape((tokens, width - lead), BF16)),
         [VM] * 3,
         (VM, VM),
-        8,
+        PACK_MIB,
     )(routes.T, combine.T, grad_tokens)
 
-    def gather(block):
+    def gather(block, *later):
         held = {0: block}
         for bit in reversed(range(n_e.bit_length() - 1)):
             for key in sorted(held):
-                held[key | (1 << bit)] = _send(held[key], 0, 1 << bit)
+                value = _after(held[key], *later) if later and bit == 0 else held[key]
+                held[key | (1 << bit)] = _send(value, 0, 1 << bit)
         return [held[j] for j in range(n_e)]
 
     firsts = gather(first)
-    rests = gather(rest)
 
     act = _call(
         functools.partial(_activate_kernel, hidden),
@@ -202,7 +231,7 @@
     )(pre)
 
     last = tuple(range(2, n_d.bit_length() - 1))
-    orders = {"x": ((0,), (1,), last), "z": ((1,), last, (0,))}
+    by_x, by_z, at_once = ((0,), (1,), last), ((1,), last, (0,)), ((0,), (1,) + last)
 
     def blocks_of(stages):
         blocks = [0]
@@ -211,72 +240,110 @@
         kept = len(blocks) >> len(stages[0])
         return tuple(blocks[:kept]), tuple(blocks[kept:])
 
-    def parts_of(kept, sent):
-        return (
-            _shape((len(kept) * rows, TILE), F32),
-            _shape((len(sent) * rows, TILE), BF16),
-        )
-
-    state = []
-    stages = orders[ORDERS[0]]
-    kept, sent = blocks_of(stages)
-    at_all, keep, send = _call(
+    def halves(kept, sent, size):
+        return _shape((kept * rows, size), F32), _shape((sent * rows, size), BF16)
+
+    def exchange(send, size, group):
+        got = []
+        for v in range(1, 1 << len(group)):
+            mask = sum((1 << b) for i, b in enumerate(group) if (v >> (len(group) - 1 - i)) & 1)
+            got.append(_send(send[(v - 1) * size : v * size], mask, 0))
+        return got
+
+    def merge(keep, got):
+        for more in got[:-1]:
+            keep = keep + more.astype(F32)
+        return keep, got[-1]
+
+    def add(keep, got, group):
+        keep, got = merge(keep, got)
+        size = keep.shape[0] // rows
+        kept = size >> len(group)
+        return _call(
+            _sum_kernel,
+            "sum_halves",
+            halves(kept, size - kept, keep.shape[1]),
+            [VM, VM],
+            (VM, VM),
+            8,
+        )(keep, got)
+
+    kept, sent = blocks_of(by_x)
+    at_all, keep_a, send_a = _call(
         functools.partial(_first_kernel, n_e, n_d, kept, sent),
         "first_partial",
-        (_shape((hidden, depth), BF16),) + parts_of(kept, sent),
+        (_shape((hidden, depth), BF16),) + halves(len(kept), len(sent), lead),
         [SM] + [VM] * (1 + n_e),
         (VM, VM, VM),
         16,
-        2 * hidden * depth * TILE,
+        2 * hidden * depth * lead,
         [pltpu.VMEM((hidden, depth), BF16)],
     )(where, act, *firsts)
-    state.append([stages, keep, send])
-    for c in range(1, width // TILE):
-        stages = orders[ORDERS[c % len(ORDERS)]]
+    got_a = exchange(send_a, keep_a.shape[0], by_x[0])
+
+    rests = gather(_after(rest, firsts[n_e // 2]), send_a)
+    rests[0] = rest
+
+    def partial(chunk, stages):
         kept, sent = blocks_of(stages)
-        outs = parts_of(kept, sent)
-        keep, send = _call(
-            functools.partial(_partial_kernel, n_e, kept, sent, rows),
+        start = sum(sizes[1:chunk])
+        columns = slice(start, start + sizes[chunk])
+        return _call(
+            functools.partial(_partial_kernel, n_e, kept, sent, rows, columns),
             "partial_chunk",
-            outs,
-            [pl.BlockSpec((hidden, depth), lambda i: (0, 0))]
-            + [pl.BlockSpec((tokens, TILE), lambda i, c=c: (0, c - 1))] * n_e,
-            tuple(pl.BlockSpec(o.shape, lambda i: (0, 0)) for o in outs),
+            halves(len(kept), len(sent), sizes[chunk]),
+            [VM] * (1 + n_e),
+            (VM, VM),
             16,
-            2 * hidden * depth * TILE,
-            grid=(1,),
+            2 * hidden * depth * sizes[chunk],
         )(at_all, *rests)
-        state.append([stages, keep, send])
-
+
+    keep_b, send_b = partial(1, by_x)
+    keep_c, send_c = partial(2, at_once)
+    keep_z, send_z = partial(3, by_z)
+
+    got_z = exchange(send_z, keep_z.shape[0], by_z[0])
     pre_grad, back = _call(
         functools.partial(_slot_kernel, n_e, hidden),
         "slot_gradients",
         (_shape(pre.shape, BF16), _shape((n_e, 1, tokens), F32)),
-        [SM, VM, VM, ANY] + [VM] * (2 * n_e),
+        [SM] + [VM] * (2 + 2 * n_e),
         (VM, VM),
         24,
         2 * n_e * capacity * width * hidden,
         [pltpu.VMEM((n_e * capacity, width), BF16)],
-    )(where, pre, down_weight, state[-1][1], *firsts, *rests)
-
-    finals = [None] * len(state)
-    for s in range(3):
-        for c, (stages, keep, send) in enumerate(state):
-            group = stages[s]
-            size = keep.shape[0]
-            total = keep
-            for v in range(1, 1 << len(group)):
-                mask = sum((1 << b) for i, b in enumerate(group) if (v >> (len(group) - 1 - i)) & 1)
-                got = _send(send[(v - 1) * size : v * size], mask, 0)
-                total = total + got.astype(F32)
-            if s < 2:
-                size >>= len(stages[s + 1])
-                state[c][1], state[c][2] = total[:size], total[size:].astype(BF16)
-            else:
-                finals[c] = total * (1.0 / n_d)
-    down_grad = jnp.concatenate(finals, axis=1).reshape(1, rows * width)
-
+    )(_after(where, send_b, send_c, send_z), pre, down_weight, *firsts, *rests)
     returned = lax.all_to_all(back, "expert", split_axis=0, concat_axis=0, tiled=True)
+
+    got_b = exchange(_after(send_b, back, *got_a), keep_b.shape[0], by_x[0])
+    keep_a, send_a = add(_after(keep_a, back, send_z), got_a, by_x[1])
+    got_a = exchange(send_a, keep_a.shape[0], by_x[1])
+
+    got_c = exchange(_after(send_c, returned, *got_b, *got_z, *got_a), keep_c.shape[0], at_once[0])
+    keep_b, send_b = add(keep_b, got_b, by_x[1])
+    got_b = exchange(send_b, keep_b.shape[0], by_x[1])
+    keep_z, send_z = add(keep_z, got_z, by_z[1])
+    got_z = exchange(send_z, keep_z.shape[0], by_z[1])
+    keep_a, send_a = add(keep_a, got_a, by_x[2])
+    end_a = [keep_a] + exchange(send_a, keep_a.shape[0], by_x[2])
+
+    keep_c, send_c = add(_after(keep_c, *got_z, *got_b, end_a[1]), got_c, at_once[1])
+    end_c = [keep_c] + exchange(send_c, keep_c.shape[0], at_once[1])
+    keep_b, send_b = add(keep_b, got_b, by_x[2])
+    end_b = [keep_b] + exchange(send_b, keep_b.shape[0], by_x[2])
+    keep_z, send_z = add(keep_z, got_z, by_z[2])
+    end_z = [keep_z] + exchange(send_z, keep_z.shape[0], by_z[2])
+
+    ends = (end_a, end_b, end_c, end_z)
+    down_grad = _call(
+        functools.partial(_finish_kernel, 1.0 / n_d, tuple(len(end) for end in ends)),
+        "finish",
+        _shape((rows * lanes, 128), F32),
+        [VM] * sum(len(end) for end in ends),
+        VM,
+        8,
+    )(*[part for end in ends for part in end]).reshape(1, rows * width)
+
     gate_grad = sum(jnp.where(routes.T == k, returned[k], 0.0) for k in range(n_e)).T
     return pre_grad.reshape(saved_pre.shape), down_grad, gate_grad
 
@@ -332,7 +399,7 @@
         whole_tiles = (
             hidden % (16 * n_d) == 0
             and saved_pre.shape[3] % 16 == 0
-            and width % TILE == 0
+            and width % 1024 == 0
             and grad_tokens.shape[0] == 128
             and n_d >= 8
             and n_d & (n_d - 1) == 0

time: 86.6 us -> 74.8 us (0.86)
  waiting for transfers between devices: 39.2 us -> 28.6 us
  blocking collectives: 0 us -> 6.08 us
  other arithmetic: 5.46 us -> 0.65 us
  local copies, waits for them, and re-layouts: 7.14 us -> 2.82 us
  Pallas kernels: 9.17 us -> 12.1 us
    ppermute x18 -> x19, waiting for transfers between devices: 38.5 us -> 28.6 us  [_send(): return lax.ppermute(value, AXES, pairs)]
    all_to_all x0 -> x1, blocking collectives: none -> 6.08 us  [_fast(): lax.all_to_all(back, 'expert', split_axis=0, concat_axis=0, tiled=True)]
    add x8 -> x0, other arithmetic: 4.67 us -> none  [_fast(): total = total + got.astype(F32)]
    unnamed x35 -> x12, local copies, waits for them, and re-layouts: 6.25 us -> 2.79 us
    all_to_all x1 -> x0, starting transfers between devices: 3.23 us -> none  [_fast(): lax.all_to_all(back, 'expert', split_axis=0, concat_axis=0, tiled=True)]
    pallas_call x4 -> x12, Pallas kernels: 2.49 us -> 5.19 us  [the longest x1 1.89 us: _fast(): _call(functools.partial(_pack_kernel, tokens, lead), 'pack_tokens', (_sha...]
    ppermute x18 -> x19, starting transfers between devices: 21 us -> 23.5 us  [_send(): return lax.ppermute(value, AXES, pairs)]
    slice x8 -> x1, local copies, waits for them, and re-layouts: 0.89 us -> 0.02 us  [exchange(): got.append(_send(send[(v - 1) * size:v * size], mask, 0))]
  transfers between devices with their start and end apart: 19 -> 19, of which waited for: 11 -> 9; matrix products, arithmetic and copies ran while one was open for 7% -> 1% of each run, Pallas kernels for 11% -> 12%
where the time goes in v3:
time: 74.8 us; the launch traced here: 74.5 us
  waiting for transfers between devices  28.6 us (38%)
  starting transfers between devices  23.5 us (31%)
  Pallas kernels  12.1 us (16%)
  blocking collectives  6.08 us (8%)
  local copies, waits for them, and re-layouts  2.82 us (4%)
    ppermute x19, waiting for transfers between devices, _send(): return lax.ppermute(value, AXES, pairs)  28.6 us
    ppermute x19, starting transfers between devices, _send(): return lax.ppermute(value, AXES, pairs)  23.5 us
    all_to_all x1, blocking collectives, _fast(): lax.all_to_all(back, 'expert', split_axis=0, concat_axis=0, tiled=True)  6.08 us
    pallas_call x1, Pallas kernels, _fast(): _call(functools.partial(_slot_kernel, n_e, hidden), 'slot_gradients', (_s...  4.44 us
    unnamed x12, local copies, waits for them, and re-layouts  2.79 us
    pallas_call x1, Pallas kernels, _fast(): _call(functools.partial(_first_kernel, n_e, n_d, kept, sent), 'first_part...  2.25 us
    pallas_call x1, Pallas kernels, _fast(): _call(functools.partial(_pack_kernel, tokens, lead), 'pack_tokens', (_sha...  1.89 us
    pallas_call x3, Pallas kernels, partial(): _call(functools.partial(_partial_kernel, n_e, kept, sent, rows, columns),...  1.51 us
  transfers between devices with their start and end apart: 19, of which 9 were waited for; matrix products, arithmetic and copies ran while one was open for 1% of the time, Pallas kernels for 12%

profile of v3, /device:TPU:0, one launch (start us, length us, event | category | flops | bytes accessed | tf_op | source)
XLA Modules:
  0.0 74.5 jit_solution(6680316215921959459)
XLA Ops:
  0.6 1.9 %pack_tokens.1 = (bf16[144,768]{1,0:T(8,128)(2,1)}, bf16[128,1280]{1,0:T(8,128)(2,1)}) custom-call(s32[2,128]{1,0:T(2,128)} %bitcast.18, bf16[2,128]{1,0:T(2,128)(2,1)} %bitcast.19, bf16[128,2048]{1,0:T(8,128)(2,1)} %tok_ref.1), custom_call_target="tpu_custom_call" | custom-call | bytes 4194304 | tf_op jit(solution)/shard_map/pack_tokens/pallas_call | solution.py:205
  2.5 3.0 %collective-permute-start.1 = (bf16[144,768]{1,0:T(8,128)(2,1)}, bf16[144,768]{1,0:T(8,128)(2,1)S(1)}, u32[]{:S(2)}, u32[]{:S(2)}) collective-permute-start(bf16[144,768]{1,0:T(8,128)(2,1)} %get-tuple-element.38.refs_0_), channel_id=1, source_target_pairs={{0,2},{1,3},{2,0},{3,1},{4,6},{5,7},{6,4},{7,5},{8,10},{9,11},{10,... | collective-permute-start | bytes 663560 | tf_op jit(solution)/shard_map/ppermute | solution.py:26
  5.5 0.0 collective-permute-start
  5.5 5.6 %collective-permute-done.1.refs_2_ = bf16[144,768]{1,0:T(8,128)(2,1)S(1)} collective-permute-done((bf16[144,768]{1,0:T(8,128)(2,1)}, bf16[144,768]{1,0:T(8,128)(2,1)S(1)}, u32[]{:S(2)}, u32[]{:S(2)}) %collective-permute-start.1) | collective-permute-done | bytes 221216 | tf_op jit(solution)/shard_map/ppermute | solution.py:26
  11.1 0.0 collective-permute-start.2
  11.1 1.7 %collective-permute-start.4 = (bf16[128,1280]{1,0:T(8,128)(2,1)}, bf16[128,1280]{1,0:T(8,128)(2,1)S(1)}, u32[]{:S(2)}, u32[]{:S(2)}) collective-permute-start(bf16[128,1280]{1,0:T(8,128)(2,1)} %get-tuple-element.43.refs_0_.refs_4_), channel_id=1, source_target_pairs={{0,2},{1,3},{2,0},{3,1},{4,6},{5,7},{6,4},{7,5},{8,10},{9,11},{10,... | collective-permute-start | bytes 983048 | tf_op jit(solution)/shard_map/ppermute | solution.py:26
  12.9 0.0 copy-start.1
  12.9 1.3 %copy-done.1 = bf16[1,1,4,96,1536]{4,3,2,1,0:T(8,128)(2,1)S(1)} copy-done((bf16[1,1,4,96,1536]{4,3,2,1,0:T(8,128)(2,1)S(1)}, bf16[1,1,4,96,1536]{4,3,2,1,0:T(8,128)(2,1)}, u32[]{:S(2)}) %copy-start.1) | copy-done | bytes 1179672
  14.1 0.0 copy-start.4
  14.1 0.2 activation.1.act_ref
  14.4 0.0 copy-start
  14.4 0.1 pad_add_fusion.where_ref
  14.5 0.0 collective-permute-done.refs_1_
  14.5 0.0 collective-permute-done.2.refs_3_
  14.5 0.6 copy-done.4
  15.1 2.3 %first_partial.1 = (bf16[768,512]{1,0:T(8,128)(2,1)S(1)}, f32[384,768]{1,0:T(8,128)S(1)}, bf16[384,768]{1,0:T(8,128)(2,1)S(1)}) custom-call(s32[2]{0:T(128)S(1)} %pad_add_fusion.where_ref, f32[4,96,768]{2,1,0:T(8,128)S(1)} %activation.1.act_ref, bf16[144,768]{1,0:T(8,128)(2,1)S(1)} %copy-done.4, bf16[144,768]{1,0:T(8,128)(2,1)S(1)} %collective-permute-done.refs_1_, ...), custom_call_target="tpu_custom_call" | custom-call | flops 603979776 | bytes 4194304 | tf_op jit(solution)/shard_map/first_partial/pallas_call | solution.py:272
  17.3 1.6 %collective-permute-start.6 = (bf16[384,768]{1,0:T(8,128)(2,1)S(1)}, bf16[384,768]{1,0:T(8,128)(2,1)S(1)}, u32[]{:S(2)}, u32[]{:S(2)}) collective-permute-start(bf16[384,768]{1,0:T(8,128)(2,1)S(1)} %get-tuple-element.42), channel_id=1, source_target_pairs={{0,4},{1,5},{2,6},{3,7},{4,0},{5,1},{6,2},{7,3},{8,12},{9,13},{10,... | collective-permute-start | bytes 1769480 | tf_op jit(solution)/shard_map/ppermute | solution.py:26
  18.9 0.0 copy-done
  18.9 0.0 collective-permute-start.3
  18.9 2.6 %collective-permute-done.4.refs_2_.refs_6_ = bf16[128,1280]{1,0:T(8,128)(2,1)S(1)} collective-permute-done((bf16[128,1280]{1,0:T(8,128)(2,1)}, bf16[128,1280]{1,0:T(8,128)(2,1)S(1)}, u32[]{:S(2)}, u32[]{:S(2)}) %collective-permute-start.4) | collective-permute-done | bytes 327712 | tf_op jit(solution)/shard_map/ppermute | solution.py:26
  21.5 0.0 collective-permute-start.5
  21.5 0.0 collective-permute-done.3.refs_1_.refs_5_
  21.5 1.6 %collective-permute-done.5.refs_3_.refs_7_ = bf16[128,1280]{1,0:T(8,128)(2,1)S(1)} collective-permute-done((bf16[128,1280]{1,0:T(8,128)(2,1)S(1)}, bf16[128,1280]{1,0:T(8,128)(2,1)S(1)}, u32[]{:S(2)}, u32[]{:S(2)}) %collective-permute-start.5) | collective-permute-done | bytes 327712 | tf_op jit(solution)/shard_map/ppermute | solution.py:26
  23.1 0.4 partial_chunk.5
  23.5 0.6 partial_chunk.4
  24.0 0.0 copy-start.2
  24.1 0.6 partial_chunk.3
  24.6 0.3 copy-done.3
  25.0 0.6 copy-done.2
  25.6 4.4 %slot_gradients.1 = (bf16[4,96,1536]{2,1,0:T(8,128)(2,1)}, f32[4,1,128]{2,1,0:T(1,128)S(1)}) custom-call(s32[2]{0:T(128)S(1)} %pad_add_fusion.where_ref, bf16[4,96,1536]{2,1,0:T(8,128)(2,1)S(1)} %bitcast.16, bf16[1,768,2048]{2,1,0:T(8,128)(2,1)S(1)} %copy-done.3, bf16[144,768]{1,0:T(8,128)(2,1)S(1)} %copy-done.4, ...), custom_call_target="tpu_custom_call" | custom-call | flops 1207959552 | bytes 4194304 | tf_op jit(solution)/shard_map/slot_gradients/pallas_call | solution.py:306
  30.0 2.9 %collective-permute-done.6.got_ref = bf16[384,768]{1,0:T(8,128)(2,1)S(1)} collective-permute-done((bf16[384,768]{1,0:T(8,128)(2,1)S(1)}, bf16[384,768]{1,0:T(8,128)(2,1)S(1)}, u32[]{:S(2)}, u32[]{:S(2)}) %collective-permute-start.6) | collective-permute-done | bytes 589856 | tf_op jit(solution)/shard_map/ppermute | solution.py:26
  32.9 1.5 %collective-permute-start.9 = (bf16[384,512]{1,0:T(8,128)(2,1)S(1)}, bf16[384,512]{1,0:T(8,128)(2,1)S(1)}, u32[]{:S(2)}, u32[]{:S(2)}) collective-permute-start(bf16[384,512]{1,0:T(8,128)(2,1)S(1)} %get-tuple-element.58), channel_id=1, source_target_pairs={{0,4},{1,5},{2,6},{3,7},{4,0},{5,1},{6,2},{7,3},{8,12},{9,13},{10,... | collective-permute-start | bytes 1179656 | tf_op jit(solution)/shard_map/ppermute | solution.py:26
  34.4 0.1 sum_halves.7
  34.5 1.6 %collective-permute-start.7 = (bf16[192,768]{1,0:T(8,128)(2,1)S(1)}, bf16[192,768]{1,0:T(8,128)(2,1)S(1)}, u32[]{:S(2)}, u32[]{:S(2)}) collective-permute-start(bf16[192,768]{1,0:T(8,128)(2,1)S(1)} %get-tuple-element.54), channel_id=1, source_target_pairs={{0,8},{1,9},{2,10},{3,11},{4,12},{5,13},{6,14},{7,15},{8,0},{9,1},... | collective-permute-start | bytes 884744 | tf_op jit(solution)/shard_map/ppermute | solution.py:26
  36.1 0.4 collective-permute-start.12
  36.6 6.1 %all_to_all.5 = f32[4,1,128]{2,1,0:T(1,128)S(1)} all-to-all(f32[4,1,128]{2,1,0:T(1,128)S(1)} %get-tuple-element.51), channel_id=1, replica_groups=mesh['dp'=8,'expert'=4] {'expert'}, dimensions={0} | all-to-all | bytes 4096 | tf_op jit(solution)/shard_map/all_to_all | solution.py:316
  42.7 4.1 %collective-permute-done.12.got_ref = bf16[384,256]{1,0:T(8,128)(2,1)S(1)} collective-permute-done((bf16[384,256]{1,0:T(8,128)(2,1)S(1)}, bf16[384,256]{1,0:T(8,128)(2,1)S(1)}, u32[]{:S(2)}, u32[]{:S(2)}) %collective-permute-start.12) | collective-permute-done | bytes 196640 | tf_op jit(solution)/shard_map/ppermute | solution.py:26
  46.8 0.0 collective-permute-done.7.got_ref
  46.8 0.0 collective-permute-done.9.got_ref
  46.8 0.5 collective-permute-start.14
  47.4 0.1 sum_halves.11
  47.4 2.7 %collective-permute-start.13 = (bf16[192,256]{1,0:T(8,128)(2,1)S(1)}, bf16[192,256]{1,0:T(8,128)(2,1)S(1)}, u32[]{:S(2)}, u32[]{:S(2)}) collective-permute-start(bf16[192,256]{1,0:T(8,128)(2,1)S(1)} %get-tuple-element.65), channel_id=1, source_target_pairs={{0,16},{1,17},{2,18},{3,19},{4,20},{5,21},{6,22},{7,23},{8,24},{9,... | collective-permute-start | bytes 294920 | tf_op jit(solution)/shard_map/ppermute | solution.py:26
  50.1 0.1 sum_halves.8
  50.1 0.4 collective-permute-start.8
  50.5 0.1 sum_halves.9
  50.6 1.6 %collective-permute-start.10 = (bf16[192,512]{1,0:T(8,128)(2,1)S(1)}, bf16[192,512]{1,0:T(8,128)(2,1)S(1)}, u32[]{:S(2)}, u32[]{:S(2)}) collective-permute-start(bf16[192,512]{1,0:T(8,128)(2,1)S(1)} %get-tuple-element.60), channel_id=1, source_target_pairs={{0,8},{1,9},{2,10},{3,11},{4,12},{5,13},{6,14},{7,15},{8,0},{9,1},... | collective-permute-start | bytes 589832 | tf_op jit(solution)/shard_map/ppermute | solution.py:26
  52.3 5.3 %collective-permute-done.13.got_ref = bf16[192,256]{1,0:T(8,128)(2,1)S(1)} collective-permute-done((bf16[192,256]{1,0:T(8,128)(2,1)S(1)}, bf16[192,256]{1,0:T(8,128)(2,1)S(1)}, u32[]{:S(2)}, u32[]{:S(2)}) %collective-permute-start.13) | collective-permute-done | bytes 98336 | tf_op jit(solution)/shard_map/ppermute | solution.py:26
  57.6 1.6 %collective-permute-start.18 = (bf16[96,256]{1,0:T(8,128)(2,1)S(1)}, bf16[96,256]{1,0:T(8,128)(2,1)S(1)}, u32[]{:S(2)}, u32[]{:S(2)}) collective-permute-start(bf16[96,256]{1,0:T(8,128)(2,1)S(1)} %get-tuple-element.72), channel_id=1, source_target_pairs={{0,4},{1,5},{2,6},{3,7},{4,0},{5,1},{6,2},{7,3},{8,12},{9,13},{10,... | collective-permute-start | bytes 147464 | tf_op jit(solution)/shard_map/ppermute | solution.py:26
  59.1 0.7 collective-permute-done.8.refs_1_
  59.8 0.0 collective-permute-done.10.got_ref
  59.8 2.0 %collective-permute-start.11 = (bf16[96,512]{1,0:T(8,128)(2,1)S(1)}, bf16[96,512]{1,0:T(8,128)(2,1)S(1)}, u32[]{:S(2)}, u32[]{:S(2)}) collective-permute-start(bf16[96,512]{1,0:T(8,128)(2,1)S(1)} %get-tuple-element.62), channel_id=1, source_target_pairs={{0,16},{1,17},{2,18},{3,19},{4,20},{5,21},{6,22},{7,23},{8,24},{9,... | collective-permute-start | bytes 294920 | tf_op jit(solution)/shard_map/ppermute | solution.py:26
  61.9 0.0 collective-permute-done.14.got_ref
  61.9 0.1 sum_halves.12
  62.0 1.0 %collective-permute-start.15 = (bf16[96,512]{1,0:T(8,128)(2,1)S(1)}, bf16[96,512]{1,0:T(8,128)(2,1)S(1)}, u32[]{:S(2)}, u32[]{:S(2)}) collective-permute-start(bf16[96,512]{1,0:T(8,128)(2,1)S(1)} %get-tuple-element.75), channel_id=1, source_target_pairs={{0,16},{1,17},{2,18},{3,19},{4,20},{5,21},{6,22},{7,23},{8,24},{9,... | collective-permute-start | bytes 294920 | tf_op jit(solution)/shard_map/ppermute | solution.py:26
  63.0 1.5 %collective-permute-start.16 = (bf16[96,512]{1,0:T(8,128)(2,1)S(1)}, bf16[96,512]{1,0:T(8,128)(2,1)S(1)}, u32[]{:S(2)}, u32[]{:S(2)}) collective-permute-start(bf16[96,512]{1,0:T(8,128)(2,1)S(1)} %get-tuple-element.74), channel_id=1, source_target_pairs={{0,8},{1,9},{2,10},{3,11},{4,12},{5,13},{6,14},{7,15},{8,0},{9,1},... | collective-permute-start | bytes 294920 | tf_op jit(solution)/shard_map/ppermute | solution.py:26
  64.6 2.3 %collective-permute-start.17 = (bf16[96,512]{1,0:T(8,128)(2,1)S(1)}, bf16[96,512]{1,0:T(8,128)(2,1)S(1)}, u32[]{:S(2)}, u32[]{:S(2)}) collective-permute-start(bf16[96,512]{1,0:T(8,128)(2,1)S(1)} %get-tuple-element.73), channel_id=1, source_target_pairs={{0,24},{1,25},{2,26},{3,27},{4,28},{5,29},{6,30},{7,31},{8,16},{9,... | collective-permute-start | bytes 294920 | tf_op jit(solution)/shard_map/ppermute | solution.py:26
  66.9 0.0 copy-done.5
  66.9 0.6 fusion.2
  67.4 0.0 collective-permute-done.18.refs_9_
  67.4 0.9 %collective-permute-done.11.refs_3_ = bf16[96,512]{1,0:T(8,128)(2,1)S(1)} collective-permute-done((bf16[96,512]{1,0:T(8,128)(2,1)S(1)}, bf16[96,512]{1,0:T(8,128)(2,1)S(1)}, u32[]{:S(2)}, u32[]{:S(2)}) %collective-permute-start.11) | collective-permute-done | bytes 98336 | tf_op jit(solution)/shard_map/ppermute | solution.py:26
  68.4 4.9 %collective-permute-done.15.refs_5_ = bf16[96,512]{1,0:T(8,128)(2,1)S(1)} collective-permute-done((bf16[96,512]{1,0:T(8,128)(2,1)S(1)}, bf16[96,512]{1,0:T(8,128)(2,1)S(1)}, u32[]{:S(2)}, u32[]{:S(2)}) %collective-permute-start.15) | collective-permute-done | bytes 98336 | tf_op jit(solution)/shard_map/ppermute | solution.py:26
  73.2 0.0 collective-permute-done.16.refs_6_
  73.2 0.0 collective-permute-done.17.refs_7_
  73.2 1.3 %finish.1 = f32[1536,128]{1,0:T(8,128)} custom-call(f32[96,768]{1,0:T(8,128)S(1)} %get-tuple-element.55.refs_0_, bf16[96,768]{1,0:T(8,128)(2,1)S(1)} %collective-permute-done.8.refs_1_, f32[96,512]{1,0:T(8,128)S(1)} %get-tuple-element.61.refs_2_, bf16[96,512]{1,0:T(8,128)(2,1)S(1)} %collective-permute-done.11.refs_3_, ...), custom_call_target="tpu_custom_call" | custom-call | bytes 4194304 | tf_op jit(solution)/shard_map/finish/pallas_call | solution.py:338
  (6 shorter events, 0.1 us)
Async XLA Ops:
  2.5 8.6 %collective-permute-start.1 = (bf16[144,768]{1,0:T(8,128)(2,1)}, bf16[144,768]{1,0:T(8,128)(2,1)S(1)}, u32[]{:S(2)}, u32[]{:S(2)}) collective-permute-start(bf16[144,768]{1,0:T(8,128)(2,1)} %get-tuple-element.38.refs_0_), channel_id=1, source_target_pairs={{0,2},{1,3},{2,0},{3,1},{4,6},{5,7},{6,4},{7,5},{8,10},{9,11},{10,... | collective-permute-start | bytes 663560 | tf_op jit(solution)/shard_map/ppermute | solution.py:26
  5.5 9.0 %collective-permute-start = (bf16[144,768]{1,0:T(8,128)(2,1)}, bf16[144,768]{1,0:T(8,128)(2,1)S(1)}, u32[]{:S(2)}, u32[]{:S(2)}) collective-permute-start(bf16[144,768]{1,0:T(8,128)(2,1)} %get-tuple-element.38.refs_0_), channel_id=1, source_target_pairs={{0,1},{1,0},{2,3},{3,2},{4,5},{5,4},{6,7},{7,6},{8,9},{9,8},{10,11... | collective-permute-start | bytes 663560 | tf_op jit(solution)/shard_map/ppermute | solution.py:26
  11.1 3.4 %collective-permute-start.2 = (bf16[144,768]{1,0:T(8,128)(2,1)S(1)}, bf16[144,768]{1,0:T(8,128)(2,1)S(1)}, u32[]{:S(2)}, u32[]{:S(2)}) collective-permute-start(bf16[144,768]{1,0:T(8,128)(2,1)S(1)} %collective-permute-done.1.refs_2_), channel_id=1, source_target_pairs={{0,1},{1,0},{2,3},{3,2},{4,5},{5,4},{6,7},{7,6},{8,9},{9,8},{10,11... | collective-permute-start | bytes 663560 | tf_op jit(solution)/shard_map/ppermute | solution.py:26
  11.1 10.3 %collective-permute-start.4 = (bf16[128,1280]{1,0:T(8,128)(2,1)}, bf16[128,1280]{1,0:T(8,128)(2,1)S(1)}, u32[]{:S(2)}, u32[]{:S(2)}) collective-permute-start(bf16[128,1280]{1,0:T(8,128)(2,1)} %get-tuple-element.43.refs_0_.refs_4_), channel_id=1, source_target_pairs={{0,2},{1,3},{2,0},{3,1},{4,6},{5,7},{6,4},{7,5},{8,10},{9,11},{10,... | collective-permute-start | bytes 983048 | tf_op jit(solution)/shard_map/ppermute | solution.py:26
  12.9 1.3 %copy-start.1 = (bf16[1,1,4,96,1536]{4,3,2,1,0:T(8,128)(2,1)S(1)}, bf16[1,1,4,96,1536]{4,3,2,1,0:T(8,128)(2,1)}, u32[]{:S(2)}) copy-start(bf16[1,1,4,96,1536]{4,3,2,1,0:T(8,128)(2,1)} %param.9) | copy-start | bytes 3538948
  14.1 0.9 %copy-start.4 = (bf16[144,768]{1,0:T(8,128)(2,1)S(1)}, bf16[144,768]{1,0:T(8,128)(2,1)}, u32[]{:S(2)}) copy-start(bf16[144,768]{1,0:T(8,128)(2,1)} %get-tuple-element.38.refs_0_) | copy-start | bytes 663556
  14.4 4.5 %copy-start = (bf16[128,1280]{1,0:T(8,128)(2,1)S(1)}, bf16[128,1280]{1,0:T(8,128)(2,1)}, u32[]{:S(2)}) copy-start(bf16[128,1280]{1,0:T(8,128)(2,1)} %get-tuple-element.43.refs_0_.refs_4_) | copy-start | bytes 983044
  17.3 15.5 %collective-permute-start.6 = (bf16[384,768]{1,0:T(8,128)(2,1)S(1)}, bf16[384,768]{1,0:T(8,128)(2,1)S(1)}, u32[]{:S(2)}, u32[]{:S(2)}) collective-permute-start(bf16[384,768]{1,0:T(8,128)(2,1)S(1)} %get-tuple-element.42), channel_id=1, source_target_pairs={{0,4},{1,5},{2,6},{3,7},{4,0},{5,1},{6,2},{7,3},{8,12},{9,13},{10,... | collective-permute-start | bytes 1769480 | tf_op jit(solution)/shard_map/ppermute | solution.py:26
  18.9 2.6 %collective-permute-start.3 = (bf16[128,1280]{1,0:T(8,128)(2,1)S(1)}, bf16[128,1280]{1,0:T(8,128)(2,1)S(1)}, u32[]{:S(2)}, u32[]{:S(2)}) collective-permute-start(bf16[128,1280]{1,0:T(8,128)(2,1)S(1)} %copy-done), channel_id=1, source_target_pairs={{0,1},{1,0},{2,3},{3,2},{4,5},{5,4},{6,7},{7,6},{8,9},{9,8},{10,11... | collective-permute-start | bytes 983048 | tf_op jit(solution)/shard_map/ppermute | solution.py:26
  21.5 1.6 %collective-permute-start.5 = (bf16[128,1280]{1,0:T(8,128)(2,1)S(1)}, bf16[128,1280]{1,0:T(8,128)(2,1)S(1)}, u32[]{:S(2)}, u32[]{:S(2)}) collective-permute-start(bf16[128,1280]{1,0:T(8,128)(2,1)S(1)} %collective-permute-done.4.refs_2_.refs_6_), channel_id=1, source_target_pairs={{0,1},{1,0},{2,3},{3,2},{4,5},{5,4},{6,7},{7,6},{8,9},{9,8},{10,11... | collective-permute-start | bytes 983048 | tf_op jit(solution)/shard_map/ppermute | solution.py:26
  23.1 1.9 %copy-start.3 = (bf16[1,768,2048]{2,1,0:T(8,128)(2,1)S(1)}, bf16[1,768,2048]{2,1,0:T(8,128)(2,1)}, u32[]{:S(2)}) copy-start(bf16[1,768,2048]{2,1,0:T(8,128)(2,1)} %w_ref.1) | copy-start | bytes 9437188
  24.0 1.5 %copy-start.2 = (bf16[1,1,4,96,1536]{4,3,2,1,0:T(8,128)(2,1)S(1)}, bf16[1,1,4,96,1536]{4,3,2,1,0:T(8,128)(2,1)}, u32[]{:S(2)}) copy-start(bf16[1,1,4,96,1536]{4,3,2,1,0:T(8,128)(2,1)} %param.9) | copy-start | bytes 3538948
  32.9 14.0 %collective-permute-start.9 = (bf16[384,512]{1,0:T(8,128)(2,1)S(1)}, bf16[384,512]{1,0:T(8,128)(2,1)S(1)}, u32[]{:S(2)}, u32[]{:S(2)}) collective-permute-start(bf16[384,512]{1,0:T(8,128)(2,1)S(1)} %get-tuple-element.58), channel_id=1, source_target_pairs={{0,4},{1,5},{2,6},{3,7},{4,0},{5,1},{6,2},{7,3},{8,12},{9,13},{10,... | collective-permute-start | bytes 1179656 | tf_op jit(solution)/shard_map/ppermute | solution.py:26
  34.5 12.3 %collective-permute-start.7 = (bf16[192,768]{1,0:T(8,128)(2,1)S(1)}, bf16[192,768]{1,0:T(8,128)(2,1)S(1)}, u32[]{:S(2)}, u32[]{:S(2)}) collective-permute-start(bf16[192,768]{1,0:T(8,128)(2,1)S(1)} %get-tuple-element.54), channel_id=1, source_target_pairs={{0,8},{1,9},{2,10},{3,11},{4,12},{5,13},{6,14},{7,15},{8,0},{9,1},... | collective-permute-start | bytes 884744 | tf_op jit(solution)/shard_map/ppermute | solution.py:26
  36.1 10.7 %collective-permute-start.12 = (bf16[384,256]{1,0:T(8,128)(2,1)S(1)}, bf16[384,256]{1,0:T(8,128)(2,1)S(1)}, u32[]{:S(2)}, u32[]{:S(2)}) collective-permute-start(bf16[384,256]{1,0:T(8,128)(2,1)S(1)} %get-tuple-element.47), channel_id=1, source_target_pairs={{0,8},{1,9},{2,10},{3,11},{4,12},{5,13},{6,14},{7,15},{8,0},{9,1},... | collective-permute-start | bytes 589832 | tf_op jit(solution)/shard_map/ppermute | solution.py:26
  46.8 15.0 %collective-permute-start.14 = (bf16[384,512]{1,0:T(8,128)(2,1)S(1)}, bf16[384,512]{1,0:T(8,128)(2,1)S(1)}, u32[]{:S(2)}, u32[]{:S(2)}) collective-permute-start(bf16[384,512]{1,0:T(8,128)(2,1)S(1)} %get-tuple-element.67), channel_id=1, source_target_pairs={{0,4},{1,5},{2,6},{3,7},{4,0},{5,1},{6,2},{7,3},{8,12},{9,13},{10,... | collective-permute-start | bytes 1179656 | tf_op jit(solution)/shard_map/ppermute | solution.py:26
  47.4 10.1 %collective-permute-start.13 = (bf16[192,256]{1,0:T(8,128)(2,1)S(1)}, bf16[192,256]{1,0:T(8,128)(2,1)S(1)}, u32[]{:S(2)}, u32[]{:S(2)}) collective-permute-start(bf16[192,256]{1,0:T(8,128)(2,1)S(1)} %get-tuple-element.65), channel_id=1, source_target_pairs={{0,16},{1,17},{2,18},{3,19},{4,20},{5,21},{6,22},{7,23},{8,24},{9,... | collective-permute-start | bytes 294920 | tf_op jit(solution)/shard_map/ppermute | solution.py:26
  50.1 9.7 %collective-permute-start.8 = (bf16[96,768]{1,0:T(8,128)(2,1)S(1)}, bf16[96,768]{1,0:T(8,128)(2,1)S(1)}, u32[]{:S(2)}, u32[]{:S(2)}) collective-permute-start(bf16[96,768]{1,0:T(8,128)(2,1)S(1)} %get-tuple-element.56), channel_id=1, source_target_pairs={{0,16},{1,17},{2,18},{3,19},{4,20},{5,21},{6,22},{7,23},{8,24},{9,... | collective-permute-start | bytes 442376 | tf_op jit(solution)/shard_map/ppermute | solution.py:26
  50.6 9.2 %collective-permute-start.10 = (bf16[192,512]{1,0:T(8,128)(2,1)S(1)}, bf16[192,512]{1,0:T(8,128)(2,1)S(1)}, u32[]{:S(2)}, u32[]{:S(2)}) collective-permute-start(bf16[192,512]{1,0:T(8,128)(2,1)S(1)} %get-tuple-element.60), channel_id=1, source_target_pairs={{0,8},{1,9},{2,10},{3,11},{4,12},{5,13},{6,14},{7,15},{8,0},{9,1},... | collective-permute-start | bytes 589832 | tf_op jit(solution)/shard_map/ppermute | solution.py:26
  57.6 9.9 %collective-permute-start.18 = (bf16[96,256]{1,0:T(8,128)(2,1)S(1)}, bf16[96,256]{1,0:T(8,128)(2,1)S(1)}, u32[]{:S(2)}, u32[]{:S(2)}) collective-permute-start(bf16[96,256]{1,0:T(8,128)(2,1)S(1)} %get-tuple-element.72), channel_id=1, source_target_pairs={{0,4},{1,5},{2,6},{3,7},{4,0},{5,1},{6,2},{7,3},{8,12},{9,13},{10,... | collective-permute-start | bytes 147464 | tf_op jit(solution)/shard_map/ppermute | solution.py:26
  59.8 7.1 %copy-start.5 = (s32[128,2]{0,1:T(2,128)S(1)}, s32[128,2]{0,1:T(2,128)}, u32[]{:S(2)}) copy-start(s32[128,2]{0,1:T(2,128)} %param.6) | copy-start | bytes 3076
  59.8 8.5 %collective-permute-start.11 = (bf16[96,512]{1,0:T(8,128)(2,1)S(1)}, bf16[96,512]{1,0:T(8,128)(2,1)S(1)}, u32[]{:S(2)}, u32[]{:S(2)}) collective-permute-start(bf16[96,512]{1,0:T(8,128)(2,1)S(1)} %get-tuple-element.62), channel_id=1, source_target_pairs={{0,16},{1,17},{2,18},{3,19},{4,20},{5,21},{6,22},{7,23},{8,24},{9,... | collective-permute-start | bytes 294920 | tf_op jit(solution)/shard_map/ppermute | solution.py:26
  62.0 11.3 %collective-permute-start.15 = (bf16[96,512]{1,0:T(8,128)(2,1)S(1)}, bf16[96,512]{1,0:T(8,128)(2,1)S(1)}, u32[]{:S(2)}, u32[]{:S(2)}) collective-permute-start(bf16[96,512]{1,0:T(8,128)(2,1)S(1)} %get-tuple-element.75), channel_id=1, source_target_pairs={{0,16},{1,17},{2,18},{3,19},{4,20},{5,21},{6,22},{7,23},{8,24},{9,... | collective-permute-start | bytes 294920 | tf_op jit(solution)/shard_map/ppermute | solution.py:26
  63.0 10.2 %collective-permute-start.16 = (bf16[96,512]{1,0:T(8,128)(2,1)S(1)}, bf16[96,512]{1,0:T(8,128)(2,1)S(1)}, u32[]{:S(2)}, u32[]{:S(2)}) collective-permute-start(bf16[96,512]{1,0:T(8,128)(2,1)S(1)} %get-tuple-element.74), channel_id=1, source_target_pairs={{0,8},{1,9},{2,10},{3,11},{4,12},{5,13},{6,14},{7,15},{8,0},{9,1},... | collective-permute-start | bytes 294920 | tf_op jit(solution)/shard_map/ppermute | solution.py:26
  64.6 8.7 %collective-permute-start.17 = (bf16[96,512]{1,0:T(8,128)(2,1)S(1)}, bf16[96,512]{1,0:T(8,128)(2,1)S(1)}, u32[]{:S(2)}, u32[]{:S(2)}) collective-permute-start(bf16[96,512]{1,0:T(8,128)(2,1)S(1)} %get-tuple-element.73), channel_id=1, source_target_pairs={{0,24},{1,25},{2,26},{3,27},{4,28},{5,29},{6,30},{7,31},{8,16},{9,... | collective-permute-start | bytes 294920 | tf_op jit(solution)/shard_map/ppermute | solution.py:26

commit v4 on v3

--- a/solution.py
+++ b/solution.py
@@ -13,7 +13,8 @@
 MIB = 1024 * 1024
 INFO_ROWS = 16
 PACK_MIB = 60
-EIGHTHS = (3, 2, 2, 1)
+LEAD_FLOPS = 6 * 10**9
+SIXTEENTHS = (6, 5, 3, 2)
 
 
 def _send(value, dp_mask, expert_mask):
@@ -43,8 +44,8 @@
     return chosen, slot_weight
 
 
-def _pack_kernel(tokens, lead, routes_ref, combine_ref, tok_ref, first_ref, rest_ref):
-    first_ref[0:tokens, :] = tok_ref[:, :lead]
+def _pack_kernel(tokens, lead, routes_ref, combine_ref, tok_ref, first_ref):
+    first_ref[0:tokens, :] = tok_ref[...]
     first_ref[tokens:, :] = jnp.zeros((INFO_ROWS, lead), BF16)
     info = jnp.concatenate(
         [
@@ -55,7 +56,6 @@
         axis=0,
     )
     first_ref[tokens:, 0:tokens] = info.astype(BF16)
-    rest_ref[...] = tok_ref[:, lead:]
 
 
 def _activate_kernel(hidden, pre_ref, out_ref):
@@ -103,29 +103,44 @@
     _split(prod, keep_blocks, send_blocks, rows, *refs[n_e:])
 
 
-def _slot_kernel(n_e, hidden, where_ref, pre_ref, w_ref, *refs):
-    firsts, rests, (pre_grad_ref, back_ref, rows_ref) = refs[:n_e], refs[n_e : 2 * n_e], refs[2 * n_e :]
+def _lead_kernel(n_e, capacity, where_ref, w_ref, *refs):
+    firsts, raw_ref, rows_ref = refs[:n_e], refs[n_e], refs[n_e + 1]
+    expert = where_ref[1].astype(F32)
+    lead = firsts[0].shape[1]
+    tokens = firsts[0].shape[0] - INFO_ROWS
+    for j in range(n_e):
+        chosen, _ = _choice(_info(firsts[j], tokens), expert, capacity)
+        rows_ref[j * capacity : (j + 1) * capacity, :] = jnp.dot(
+            chosen.astype(BF16), firsts[j][0:tokens, :], preferred_element_type=F32
+        ).astype(BF16)
+    raw_ref[...] = lax.dot_general(
+        rows_ref[...], w_ref[0, :, 0:lead], (((1,), (1,)), ((), ())), preferred_element_type=F32
+    )
+
+
+def _slot_kernel(n_e, hidden, where_ref, pre_ref, w_ref, raw_ref, *refs):
+    infos, rests, (pre_grad_ref, back_ref, rows_ref) = refs[:n_e], refs[n_e : 2 * n_e], refs[2 * n_e :]
     e = where_ref[1]
     expert = e.astype(F32)
     capacity = pre_ref.shape[1]
     tokens = rests[0].shape[0]
-    lead = firsts[0].shape[1]
+    lead = infos[0].shape[1]
     picks, weights = [], []
     for j in range(n_e):
-        chosen, slot_weight = _choice(_info(firsts[j], tokens), expert, capacity)
+        chosen, slot_weight = _choice(_info(infos[j], tokens), expert, capacity)
         picks.append(chosen)
         weights.append(slot_weight)
-        pick = chosen.astype(BF16)
-        here = slice(j * capacity, (j + 1) * capacity)
-        rows_ref[here, :lead] = jnp.dot(
-            pick, firsts[j][0:tokens, :], preferred_element_type=F32
+        rows_ref[j * capacity : (j + 1) * capacity, :] = jnp.dot(
+            chosen.astype(BF16), rests[j][...], preferred_element_type=F32
         ).astype(BF16)
-        rows_ref[here, lead:] = jnp.dot(pick, rests[j][...], preferred_element_type=F32).astype(BF16)
     tile = 256 if hidden % 256 == 0 else hidden
     gates = [jnp.zeros((capacity, 1), F32) for _ in range(n_e)]
     for h in range(0, hidden, tile):
-        raw_all = lax.dot_general(
-            rows_ref[...], w_ref[0, h : h + tile, :], (((1,), (1,)), ((), ())), preferred_element_type=F32
+        raw_all = raw_ref[:, h : h + tile] + lax.dot_general(
+            rows_ref[...],
+            w_ref[0, h : h + tile, lead:],
+            (((1,), (1,)), ((), ())),
+            preferred_element_type=F32,
         )
         for j in range(n_e):
             raw = raw_all[j * capacity : (j + 1) * capacity, :]
@@ -199,27 +214,35 @@
     lanes = width // 128
     where = jnp.stack([lax.axis_index("dp"), lax.axis_index("expert")]).astype(jnp.int32)
     pre = saved_pre.reshape(saved_pre.shape[1:])[0]
-    sizes = [part * width // 8 for part in EIGHTHS]
+    sizes = [part * width // 16 for part in SIXTEENTHS]
     lead = sizes[0]
 
-    first, rest = _call(
+    whole = lambda i: (0, 0)
+    first = _call(
         functools.partial(_pack_kernel, tokens, lead),
         "pack_tokens",
-        (_shape((tokens + INFO_ROWS, lead), BF16), _shape((tokens, width - lead), BF16)),
-        [VM] * 3,
-        (VM, VM),
+        _shape((tokens + INFO_ROWS, lead), BF16),
+        [
+            pl.BlockSpec((routes.shape[1], tokens), whole),
+            pl.BlockSpec((routes.shape[1], tokens), whole),
+            pl.BlockSpec((tokens, lead), whole),
+        ],
+        pl.BlockSpec((tokens + INFO_ROWS, lead), whole),
         PACK_MIB,
+        grid=(1,),
     )(routes.T, combine.T, grad_tokens)
+    rest = grad_tokens[:, lead:]
 
     def gather(block, *later):
         held = {0: block}
         for bit in reversed(range(n_e.bit_length() - 1)):
             for key in sorted(held):
-                value = _after(held[key], *later) if later and bit == 0 else held[key]
-                held[key | (1 << bit)] = _send(value, 0, 1 << bit)
+                if later and bit == 0:
+                    held[key] = _after(held[key], *later)
+                held[key | (1 << bit)] = _send(held[key], 0, 1 << bit)
         return [held[j] for j in range(n_e)]
 
-    firsts = gather(first)
+    firsts = gather(first, rest)
 
     act = _call(
         functools.partial(_activate_kernel, hidden),
@@ -227,7 +250,7 @@
         _shape((n_e, capacity, hidden), F32),
         [VM],
         VM,
-        12,
+        6,
     )(pre)
 
     last = tuple(range(2, n_d.bit_length() - 1))
@@ -275,14 +298,24 @@
         (_shape((hidden, depth), BF16),) + halves(len(kept), len(sent), lead),
         [SM] + [VM] * (1 + n_e),
         (VM, VM, VM),
-        16,
+        10,
         2 * hidden * depth * lead,
         [pltpu.VMEM((hidden, depth), BF16)],
     )(where, act, *firsts)
     got_a = exchange(send_a, keep_a.shape[0], by_x[0])
 
-    rests = gather(_after(rest, firsts[n_e // 2]), send_a)
-    rests[0] = rest
+    raw_lead = _call(
+        functools.partial(_lead_kernel, n_e, capacity),
+        "raw_lead",
+        _shape((n_e * capacity, hidden), F32),
+        [SM] + [VM] * (1 + n_e),
+        VM,
+        10,
+        LEAD_FLOPS,
+        [pltpu.VMEM((n_e * capacity, lead), BF16)],
+    )(_after(where, send_a), down_weight, *firsts)
+
+    rests = gather(_after(rest, firsts[n_e // 2]), raw_lead)
 
     def partial(chunk, stages):
         kept, sent = blocks_of(stages)
@@ -294,7 +327,7 @@
             halves(len(kept), len(sent), sizes[chunk]),
             [VM] * (1 + n_e),
             (VM, VM),
-            16,
+            8,
             2 * hidden * depth * sizes[chunk],
         )(at_all, *rests)
 
@@ -307,33 +340,35 @@
         functools.partial(_slot_kernel, n_e, hidden),
         "slot_gradients",
         (_shape(pre.shape, BF16), _shape((n_e, 1, tokens), F32)),
-        [SM] + [VM] * (2 + 2 * n_e),
+        [SM] + [VM] * (3 + 2 * n_e),
         (VM, VM),
-        24,
-        2 * n_e * capacity * width * hidden,
-        [pltpu.VMEM((n_e * capacity, width), BF16)],
-    )(_after(where, send_b, send_c, send_z), pre, down_weight, *firsts, *rests)
-    returned = lax.all_to_all(back, "expert", split_axis=0, concat_axis=0, tiled=True)
-
-    got_b = exchange(_after(send_b, back, *got_a), keep_b.shape[0], by_x[0])
+        14,
+        2 * n_e * capacity * (width - lead) * hidden,
+        [pltpu.VMEM((n_e * capacity, width - lead), BF16)],
+    )(_after(where, send_b, send_c, send_z), pre, down_weight, raw_lead, *firsts, *rests)
+    keep_z, send_z = add(keep_z, got_z, by_z[1])
+    got_z = exchange(send_z, keep_z.shape[0], by_z[1])
+
+    got_b = exchange(_after(send_b, back, send_z, *got_a), keep_b.shape[0], by_x[0])
     keep_a, send_a = add(_after(keep_a, back, send_z), got_a, by_x[1])
     got_a = exchange(send_a, keep_a.shape[0], by_x[1])
+
+    returned = lax.all_to_all(
+        _after(back, send_a, send_z), "expert", split_axis=0, concat_axis=0, tiled=True
+    )
 
     got_c = exchange(_after(send_c, returned, *got_b, *got_z, *got_a), keep_c.shape[0], at_once[0])
     keep_b, send_b = add(keep_b, got_b, by_x[1])
     got_b = exchange(send_b, keep_b.shape[0], by_x[1])
-    keep_z, send_z = add(keep_z, got_z, by_z[1])
-    got_z = exchange(send_z, keep_z.shape[0], by_z[1])
     keep_a, send_a = add(keep_a, got_a, by_x[2])
     end_a = [keep_a] + exchange(send_a, keep_a.shape[0], by_x[2])
-
-    keep_c, send_c = add(_after(keep_c, *got_z, *got_b, end_a[1]), got_c, at_once[1])
-    end_c = [keep_c] + exchange(send_c, keep_c.shape[0], at_once[1])
     keep_b, send_b = add(keep_b, got_b, by_x[2])
     end_b = [keep_b] + exchange(send_b, keep_b.shape[0], by_x[2])
-    keep_z, send_z = add(keep_z, got_z, by_z[2])
+
+    keep_c, send_c = add(_after(keep_c, send_b, end_a[1]), got_c, at_once[1])
+    end_c = [keep_c] + exchange(send_c, keep_c.shape[0], at_once[1])
+    keep_z, send_z = add(_after(keep_z, send_c), got_z, by_z[2])
     end_z = [keep_z] + exchange(send_z, keep_z.shape[0], by_z[2])
-
     ends = (end_a, end_b, end_c, end_z)
     down_grad = _call(
         functools.partial(_finish_kernel, 1.0 / n_d, tuple(len(end) for end in ends)),
@@ -399,7 +434,7 @@
         whole_tiles = (
             hidden % (16 * n_d) == 0
             and saved_pre.shape[3] % 16 == 0
-            and width % 1024 == 0
+            and width % 2048 == 0
             and grad_tokens.shape[0] == 128
             and n_d >= 8
             and n_d & (n_d - 1) == 0

time: 74.8 us -> 68.6 us (0.917)
  waiting for transfers between devices: 28.6 us -> 19.8 us
  starting transfers between devices: 23.5 us -> 26.5 us
  local copies, waits for them, and re-layouts: 2.82 us -> 1.08 us
  Pallas kernels: 12.1 us -> 13.3 us
    ppermute x19, waiting for transfers between devices: 28.6 us -> 19.8 us  [_send(): return lax.ppermute(value, AXES, pairs)]
    ppermute x19, starting transfers between devices: 23.5 us -> 26.5 us  [_send(): return lax.ppermute(value, AXES, pairs)]
    unnamed x12 -> x8, local copies, waits for them, and re-layouts: 2.79 us -> 0.02 us
    pallas_call x1 -> x2, Pallas kernels: 1.89 us -> 3.59 us  [the longest x1 1.83 us: _fast(): _call(functools.partial(_lead_kernel, n_e, capacity), 'raw_lead', _shape(...]
    slice x0 -> x1, local copies, waits for them, and re-layouts: none -> 1.03 us  [_fast(): rest = grad_tokens[:, lead:]]
  transfers between devices with their start and end apart: 19 -> 19, of which waited for: 9 -> 8; matrix products, arithmetic and copies ran while one was open for 1% -> 2% of each run, Pallas kernels for 12% -> 15%
where the time goes in v4:
time: 68.6 us; the launch traced here: 68.4 us
  starting transfers between devices  26.5 us (39%)
  waiting for transfers between devices  19.8 us (29%)
  Pallas kernels  13.3 us (19%)
  blocking collectives  6.27 us (9%)
  local copies, waits for them, and re-layouts  1.08 us (2%)
  between operations  0.77 us (1%)
    ppermute x19, starting transfers between devices, _send(): return lax.ppermute(value, AXES, pairs)  26.5 us
    ppermute x19, waiting for transfers between devices, _send(): return lax.ppermute(value, AXES, pairs)  19.8 us
    all_to_all x1, blocking collectives, _fast(): lax.all_to_all(_after(back, send_a, send_z), 'expert', split_axis=0, conc...  6.27 us
    pallas_call x1, Pallas kernels, _fast(): _call(functools.partial(_slot_kernel, n_e, hidden), 'slot_gradients', (_s...  3.71 us
    pallas_call x1, Pallas kernels, _fast(): _call(functools.partial(_first_kernel, n_e, n_d, kept, sent), 'first_part...  2.26 us
    pallas_call x1, Pallas kernels, _fast(): _call(functools.partial(_lead_kernel, n_e, capacity), 'raw_lead', _shape(...  1.83 us
    pallas_call x1, Pallas kernels, _fast(): _call(functools.partial(_pack_kernel, tokens, lead), 'pack_tokens', _shap...  1.76 us
    pallas_call x3, Pallas kernels, partial(): _call(functools.partial(_partial_kernel, n_e, kept, sent, rows, columns),...  1.71 us
  transfers between devices with their start and end apart: 19, of which 8 were waited for; matrix products, arithmetic and copies ran while one was open for 2% of the time, Pallas kernels for 15%

profile of v4, /device:TPU:0, one launch (start us, length us, event | category | flops | bytes accessed | tf_op | source)
XLA Modules:
  0.0 68.4 jit_solution(12989328567897893114)
XLA Ops:
  0.6 0.0 copy-start
  0.6 1.8 %pack_tokens.1.refs_0_ = bf16[144,768]{1,0:T(8,128)(2,1)} custom-call(s32[2,128]{1,0:T(2,128)} %bitcast.18, bf16[2,128]{1,0:T(2,128)(2,1)} %bitcast.19, bf16[128,2048]{1,0:T(8,128)(2,1)} %tok_ref.1), custom_call_target="tpu_custom_call" | custom-call | bytes 4194304 | tf_op jit(solution)/shard_map/pack_tokens/pallas_call | solution.py:221
  2.4 3.0 %collective-permute-start.1 = (bf16[144,768]{1,0:T(8,128)(2,1)}, bf16[144,768]{1,0:T(8,128)(2,1)S(1)}, u32[]{:S(2)}, u32[]{:S(2)}) collective-permute-start(bf16[144,768]{1,0:T(8,128)(2,1)} %pack_tokens.1.refs_0_), channel_id=1, source_target_pairs={{0,2},{1,3},{2,0},{3,1},{4,6},{5,7},{6,4},{7,5},{8,10},{9,11},{10,... | collective-permute-start | bytes 663560 | tf_op jit(solution)/shard_map/ppermute | solution.py:27
  5.4 0.0 copy-start.2
  5.4 1.0 %slice.24.refs_0_.refs_4_ = bf16[128,1280]{1,0:T(8,128)(2,1)S(1)} slice(bf16[128,2048]{1,0:T(8,128)(2,1)} %tok_ref.1), slice={[0:128], [768:2048]} | slice | bytes 655360 | tf_op jit(solution)/shard_map/slice | solution.py:234
  6.4 0.1 collective-permute-start
  6.5 4.5 %collective-permute-done.1.refs_2_ = bf16[144,768]{1,0:T(8,128)(2,1)S(1)} collective-permute-done((bf16[144,768]{1,0:T(8,128)(2,1)}, bf16[144,768]{1,0:T(8,128)(2,1)S(1)}, u32[]{:S(2)}, u32[]{:S(2)}) %collective-permute-start.1) | collective-permute-done | bytes 221216 | tf_op jit(solution)/shard_map/ppermute | solution.py:27
  11.0 0.0 collective-permute-start.2
  11.0 0.0 copy-done
  11.0 0.2 activation.1.act_ref
  11.3 0.1 pad_add_fusion.where_ref
  11.3 1.7 %collective-permute-start.4 = (bf16[128,1280]{1,0:T(8,128)(2,1)S(1)}, bf16[128,1280]{1,0:T(8,128)(2,1)S(1)}, u32[]{:S(2)}, u32[]{:S(2)}) collective-permute-start(bf16[128,1280]{1,0:T(8,128)(2,1)S(1)} %slice.24.refs_0_.refs_4_), channel_id=1, source_target_pairs={{0,2},{1,3},{2,0},{3,1},{4,6},{5,7},{6,4},{7,5},{8,10},{9,11},{10,... | collective-permute-start | bytes 983048 | tf_op jit(solution)/shard_map/ppermute | solution.py:27
  13.1 0.0 collective-permute-done.refs_1_
  13.1 0.0 collective-permute-done.2.refs_3_
  13.1 0.0 copy-done.2
  13.1 2.3 %first_partial.1 = (bf16[768,512]{1,0:T(8,128)(2,1)S(1)}, f32[384,768]{1,0:T(8,128)S(1)}, bf16[384,768]{1,0:T(8,128)(2,1)S(1)}) custom-call(s32[2]{0:T(128)S(1)} %pad_add_fusion.where_ref, f32[4,96,768]{2,1,0:T(8,128)S(1)} %activation.1.act_ref, bf16[144,768]{1,0:T(8,128)(2,1)S(1)} %copy-done.2, bf16[144,768]{1,0:T(8,128)(2,1)S(1)} %collective-permute-done.refs_1_, ...), custom_call_target="tpu_custom_call" | custom-call | flops 603979776 | bytes 4194304 | tf_op jit(solution)/shard_map/first_partial/pallas_call | solution.py:295
  15.4 1.6 %collective-permute-start.7 = (bf16[384,768]{1,0:T(8,128)(2,1)S(1)}, bf16[384,768]{1,0:T(8,128)(2,1)S(1)}, u32[]{:S(2)}, u32[]{:S(2)}) collective-permute-start(bf16[384,768]{1,0:T(8,128)(2,1)S(1)} %get-tuple-element.45), channel_id=1, source_target_pairs={{0,4},{1,5},{2,6},{3,7},{4,0},{5,1},{6,2},{7,3},{8,12},{9,13},{10,... | collective-permute-start | bytes 1769480 | tf_op jit(solution)/shard_map/ppermute | solution.py:27
  16.9 0.0 copy-done.1
  16.9 1.8 %raw_lead.1.raw_ref = f32[384,768]{1,0:T(8,128)S(1)} custom-call(s32[2]{0:T(128)S(1)} %pad_add_fusion.where_ref, bf16[1,768,2048]{2,1,0:T(8,128)(2,1)S(1)} %copy-done.1, bf16[144,768]{1,0:T(8,128)(2,1)S(1)} %copy-done.2, bf16[144,768]{1,0:T(8,128)(2,1)S(1)} %collective-permute-done.refs_1_, bf16[144,768]{1,0:T(8,128)(2,1)S(1)} %collective-permute-done.1.refs_2_, ...), custom_call_target="tpu_custom_call" | custom-call | flops 6000000000 | bytes 4194304 | tf_op jit(solution)/shard_map/raw_lead/pallas_call | solution.py:307
  18.8 0.1 collective-permute-start.3
  18.8 2.6 %collective-permute-done.4.refs_2_.refs_6_ = bf16[128,1280]{1,0:T(8,128)(2,1)S(1)} collective-permute-done((bf16[128,1280]{1,0:T(8,128)(2,1)S(1)}, bf16[128,1280]{1,0:T(8,128)(2,1)S(1)}, u32[]{:S(2)}, u32[]{:S(2)}) %collective-permute-start.4) | collective-permute-done | bytes 327712 | tf_op jit(solution)/shard_map/ppermute | solution.py:27
  21.5 0.0 collective-permute-start.5
  21.5 0.0 collective-permute-done.3.refs_1_.refs_5_
  21.5 1.6 %collective-permute-done.5.refs_3_.refs_7_ = bf16[128,1280]{1,0:T(8,128)(2,1)S(1)} collective-permute-done((bf16[128,1280]{1,0:T(8,128)(2,1)S(1)}, bf16[128,1280]{1,0:T(8,128)(2,1)S(1)}, u32[]{:S(2)}, u32[]{:S(2)}) %collective-permute-start.5) | collective-permute-done | bytes 327712 | tf_op jit(solution)/shard_map/ppermute | solution.py:27
  23.1 0.4 partial_chunk.5
  23.5 1.9 %collective-permute-start.6 = (bf16[384,256]{1,0:T(8,128)(2,1)S(1)}, bf16[384,256]{1,0:T(8,128)(2,1)S(1)}, u32[]{:S(2)}, u32[]{:S(2)}) collective-permute-start(bf16[384,256]{1,0:T(8,128)(2,1)S(1)} %get-tuple-element.51), channel_id=1, source_target_pairs={{0,8},{1,9},{2,10},{3,11},{4,12},{5,13},{6,14},{7,15},{8,0},{9,1},... | collective-permute-start | bytes 589832 | tf_op jit(solution)/shard_map/ppermute | solution.py:27
  25.3 0.6 partial_chunk.4
  25.9 0.8 %partial_chunk.3 = (f32[384,640]{1,0:T(8,128)S(1)}, bf16[384,640]{1,0:T(8,128)(2,1)S(1)}) custom-call(bf16[768,512]{1,0:T(8,128)(2,1)S(1)} %get-tuple-element.43.at_ref, bf16[128,1280]{1,0:T(8,128)(2,1)S(1)} %slice.24.refs_0_.refs_4_, bf16[128,1280]{1,0:T(8,128)(2,1)S(1)} %collective-permute-done.3.refs_1_.refs_5_, ...), custom_call_target="tpu_custom_call" | custom-call | flops 503316480 | bytes 4194304 | tf_op jit(solution)/shard_map/partial_chunk/pallas_call | solution.py:324
  26.7 3.7 %slot_gradients.1 = (bf16[4,96,1536]{2,1,0:T(8,128)(2,1)}, f32[4,1,128]{2,1,0:T(1,128)S(1)}) custom-call(s32[2]{0:T(128)S(1)} %pad_add_fusion.where_ref, bf16[4,96,1536]{2,1,0:T(8,128)(2,1)S(1)} %bitcast.16, bf16[1,768,2048]{2,1,0:T(8,128)(2,1)S(1)} %copy-done.1, f32[384,768]{1,0:T(8,128)S(1)} %raw_lead.1.raw_ref, bf16[144,768]{1,0:T(8,128)(2,1)S(1)} %copy-done.2, ...), custom_call_target="tpu_custom_call" | custom-call | flops 754974720 | bytes 4194304 | tf_op jit(solution)/shard_map/slot_gradients/pallas_call | solution.py:339
  30.4 0.1 collective-permute-done.6.got_ref
  30.5 0.1 sum_halves.7
  30.6 0.3 collective-permute-done.7.got_ref
  30.9 1.5 %collective-permute-start.10 = (bf16[384,640]{1,0:T(8,128)(2,1)S(1)}, bf16[384,640]{1,0:T(8,128)(2,1)S(1)}, u32[]{:S(2)}, u32[]{:S(2)}) collective-permute-start(bf16[384,640]{1,0:T(8,128)(2,1)S(1)} %get-tuple-element.64), channel_id=1, source_target_pairs={{0,4},{1,5},{2,6},{3,7},{4,0},{5,1},{6,2},{7,3},{8,12},{9,13},{10,... | collective-permute-start | bytes 1474568 | tf_op jit(solution)/shard_map/ppermute | solution.py:27
  32.4 0.1 sum_halves.8
  32.5 1.6 %collective-permute-start.8 = (bf16[192,768]{1,0:T(8,128)(2,1)S(1)}, bf16[192,768]{1,0:T(8,128)(2,1)S(1)}, u32[]{:S(2)}, u32[]{:S(2)}) collective-permute-start(bf16[192,768]{1,0:T(8,128)(2,1)S(1)} %get-tuple-element.60), channel_id=1, source_target_pairs={{0,8},{1,9},{2,10},{3,11},{4,12},{5,13},{6,14},{7,15},{8,0},{9,1},... | collective-permute-start | bytes 884744 | tf_op jit(solution)/shard_map/ppermute | solution.py:27
  34.2 2.6 %collective-permute-start.13 = (bf16[192,256]{1,0:T(8,128)(2,1)S(1)}, bf16[192,256]{1,0:T(8,128)(2,1)S(1)}, u32[]{:S(2)}, u32[]{:S(2)}) collective-permute-start(bf16[192,256]{1,0:T(8,128)(2,1)S(1)} %get-tuple-element.57), channel_id=1, source_target_pairs={{0,16},{1,17},{2,18},{3,19},{4,20},{5,21},{6,22},{7,23},{8,24},{9,... | collective-permute-start | bytes 294920 | tf_op jit(solution)/shard_map/ppermute | solution.py:27
  36.8 6.3 %all_to_all.5 = f32[4,1,128]{2,1,0:T(1,128)S(1)} all-to-all(f32[4,1,128]{2,1,0:T(1,128)S(1)} %get-tuple-element.71), channel_id=1, replica_groups=mesh['dp'=8,'expert'=4] {'expert'}, dimensions={0} | all-to-all | bytes 4096 | tf_op jit(solution)/shard_map/all_to_all | solution.py:356
  43.0 0.0 collective-permute-done.13.got_ref
  43.0 0.0 collective-permute-done.8.got_ref
  43.0 0.5 collective-permute-done.10.got_ref
  43.5 1.5 %collective-permute-start.14 = (bf16[384,384]{1,0:T(8,128)(2,1)S(1)}, bf16[384,384]{1,0:T(8,128)(2,1)S(1)}, u32[]{:S(2)}, u32[]{:S(2)}) collective-permute-start(bf16[384,384]{1,0:T(8,128)(2,1)S(1)} %get-tuple-element.72), channel_id=1, source_target_pairs={{0,4},{1,5},{2,6},{3,7},{4,0},{5,1},{6,2},{7,3},{8,12},{9,13},{10,... | collective-permute-start | bytes 884744 | tf_op jit(solution)/shard_map/ppermute | solution.py:27
  45.0 0.1 sum_halves.10
  45.1 1.5 %collective-permute-start.11 = (bf16[192,640]{1,0:T(8,128)(2,1)S(1)}, bf16[192,640]{1,0:T(8,128)(2,1)S(1)}, u32[]{:S(2)}, u32[]{:S(2)}) collective-permute-start(bf16[192,640]{1,0:T(8,128)(2,1)S(1)} %get-tuple-element.66), channel_id=1, source_target_pairs={{0,8},{1,9},{2,10},{3,11},{4,12},{5,13},{6,14},{7,15},{8,0},{9,1},... | collective-permute-start | bytes 737288 | tf_op jit(solution)/shard_map/ppermute | solution.py:27
  46.6 0.1 sum_halves.9
  46.7 2.7 %collective-permute-start.9 = (bf16[96,768]{1,0:T(8,128)(2,1)S(1)}, bf16[96,768]{1,0:T(8,128)(2,1)S(1)}, u32[]{:S(2)}, u32[]{:S(2)}) collective-permute-start(bf16[96,768]{1,0:T(8,128)(2,1)S(1)} %get-tuple-element.62), channel_id=1, source_target_pairs={{0,16},{1,17},{2,18},{3,19},{4,20},{5,21},{6,22},{7,23},{8,24},{9,... | collective-permute-start | bytes 442376 | tf_op jit(solution)/shard_map/ppermute | solution.py:27
  49.3 5.3 %collective-permute-done.11.got_ref = bf16[192,640]{1,0:T(8,128)(2,1)S(1)} collective-permute-done((bf16[192,640]{1,0:T(8,128)(2,1)S(1)}, bf16[192,640]{1,0:T(8,128)(2,1)S(1)}, u32[]{:S(2)}, u32[]{:S(2)}) %collective-permute-start.11) | collective-permute-done | bytes 245792 | tf_op jit(solution)/shard_map/ppermute | solution.py:27
  54.6 0.0 copy-start.3
  54.6 0.1 sum_halves.11
  54.7 1.4 %collective-permute-start.12 = (bf16[96,640]{1,0:T(8,128)(2,1)S(1)}, bf16[96,640]{1,0:T(8,128)(2,1)S(1)}, u32[]{:S(2)}, u32[]{:S(2)}) collective-permute-start(bf16[96,640]{1,0:T(8,128)(2,1)S(1)} %get-tuple-element.68), channel_id=1, source_target_pairs={{0,16},{1,17},{2,18},{3,19},{4,20},{5,21},{6,22},{7,23},{8,24},{9,... | collective-permute-start | bytes 368648 | tf_op jit(solution)/shard_map/ppermute | solution.py:27
  56.1 0.0 collective-permute-done.9.refs_1_
  56.1 0.0 collective-permute-done.14.got_ref
  56.1 0.1 sum_halves.12
  56.2 0.6 collective-permute-start.18
  56.8 2.6 %collective-permute-start.15 = (bf16[96,384]{1,0:T(8,128)(2,1)S(1)}, bf16[96,384]{1,0:T(8,128)(2,1)S(1)}, u32[]{:S(2)}, u32[]{:S(2)}) collective-permute-start(bf16[96,384]{1,0:T(8,128)(2,1)S(1)} %get-tuple-element.81), channel_id=1, source_target_pairs={{0,16},{1,17},{2,18},{3,19},{4,20},{5,21},{6,22},{7,23},{8,24},{9,... | collective-permute-start | bytes 221192 | tf_op jit(solution)/shard_map/ppermute | solution.py:27
  59.4 0.0 collective-permute-start.16
  59.4 2.3 %collective-permute-start.17 = (bf16[96,384]{1,0:T(8,128)(2,1)S(1)}, bf16[96,384]{1,0:T(8,128)(2,1)S(1)}, u32[]{:S(2)}, u32[]{:S(2)}) collective-permute-start(bf16[96,384]{1,0:T(8,128)(2,1)S(1)} %get-tuple-element.79), channel_id=1, source_target_pairs={{0,24},{1,25},{2,26},{3,27},{4,28},{5,29},{6,30},{7,31},{8,16},{9,... | collective-permute-start | bytes 221192 | tf_op jit(solution)/shard_map/ppermute | solution.py:27
  61.7 0.0 copy-done.3
  61.7 0.6 fusion.2
  62.3 0.0 collective-permute-done.18.refs_9_
  62.3 4.8 %collective-permute-done.15.refs_5_ = bf16[96,384]{1,0:T(8,128)(2,1)S(1)} collective-permute-done((bf16[96,384]{1,0:T(8,128)(2,1)S(1)}, bf16[96,384]{1,0:T(8,128)(2,1)S(1)}, u32[]{:S(2)}, u32[]{:S(2)}) %collective-permute-start.15) | collective-permute-done | bytes 73760 | tf_op jit(solution)/shard_map/ppermute | solution.py:27
  67.0 0.0 collective-permute-done.16.refs_6_
  67.0 0.0 collective-permute-done.17.refs_7_
  67.1 0.0 collective-permute-done.12.refs_3_
  67.1 1.3 %finish.1 = f32[1536,128]{1,0:T(8,128)} custom-call(f32[96,768]{1,0:T(8,128)S(1)} %get-tuple-element.61.refs_0_, bf16[96,768]{1,0:T(8,128)(2,1)S(1)} %collective-permute-done.9.refs_1_, f32[96,640]{1,0:T(8,128)S(1)} %get-tuple-element.67.refs_2_, bf16[96,640]{1,0:T(8,128)(2,1)S(1)} %collective-permute-done.12.refs_3_, ...), custom_call_target="tpu_custom_call" | custom-call | bytes 4194304 | tf_op jit(solution)/shard_map/finish/pallas_call | solution.py:373
  (4 shorter events, 0.0 us)
Async XLA Ops:
  0.6 10.4 %copy-start = (bf16[1,1,4,96,1536]{4,3,2,1,0:T(8,128)(2,1)S(1)}, bf16[1,1,4,96,1536]{4,3,2,1,0:T(8,128)(2,1)}, u32[]{:S(2)}) copy-start(bf16[1,1,4,96,1536]{4,3,2,1,0:T(8,128)(2,1)} %param.9) | copy-start | bytes 3538948
  2.4 8.6 %collective-permute-start.1 = (bf16[144,768]{1,0:T(8,128)(2,1)}, bf16[144,768]{1,0:T(8,128)(2,1)S(1)}, u32[]{:S(2)}, u32[]{:S(2)}) collective-permute-start(bf16[144,768]{1,0:T(8,128)(2,1)} %pack_tokens.1.refs_0_), channel_id=1, source_target_pairs={{0,2},{1,3},{2,0},{3,1},{4,6},{5,7},{6,4},{7,5},{8,10},{9,11},{10,... | collective-permute-start | bytes 663560 | tf_op jit(solution)/shard_map/ppermute | solution.py:27
  5.4 7.7 %copy-start.2 = (bf16[144,768]{1,0:T(8,128)(2,1)S(1)}, bf16[144,768]{1,0:T(8,128)(2,1)}, u32[]{:S(2)}) copy-start(bf16[144,768]{1,0:T(8,128)(2,1)} %pack_tokens.1.refs_0_) | copy-start | bytes 663556
  6.4 6.7 %collective-permute-start = (bf16[144,768]{1,0:T(8,128)(2,1)}, bf16[144,768]{1,0:T(8,128)(2,1)S(1)}, u32[]{:S(2)}, u32[]{:S(2)}) collective-permute-start(bf16[144,768]{1,0:T(8,128)(2,1)} %pack_tokens.1.refs_0_), channel_id=1, source_target_pairs={{0,1},{1,0},{2,3},{3,2},{4,5},{5,4},{6,7},{7,6},{8,9},{9,8},{10,11... | collective-permute-start | bytes 663560 | tf_op jit(solution)/shard_map/ppermute | solution.py:27
  11.0 2.1 %collective-permute-start.2 = (bf16[144,768]{1,0:T(8,128)(2,1)S(1)}, bf16[144,768]{1,0:T(8,128)(2,1)S(1)}, u32[]{:S(2)}, u32[]{:S(2)}) collective-permute-start(bf16[144,768]{1,0:T(8,128)(2,1)S(1)} %collective-permute-done.1.refs_2_), channel_id=1, source_target_pairs={{0,1},{1,0},{2,3},{3,2},{4,5},{5,4},{6,7},{7,6},{8,9},{9,8},{10,11... | collective-permute-start | bytes 663560 | tf_op jit(solution)/shard_map/ppermute | solution.py:27
  11.0 5.9 %copy-start.1 = (bf16[1,768,2048]{2,1,0:T(8,128)(2,1)S(1)}, bf16[1,768,2048]{2,1,0:T(8,128)(2,1)}, u32[]{:S(2)}) copy-start(bf16[1,768,2048]{2,1,0:T(8,128)(2,1)} %w_ref.3) | copy-start | bytes 9437188
  11.3 10.1 %collective-permute-start.4 = (bf16[128,1280]{1,0:T(8,128)(2,1)S(1)}, bf16[128,1280]{1,0:T(8,128)(2,1)S(1)}, u32[]{:S(2)}, u32[]{:S(2)}) collective-permute-start(bf16[128,1280]{1,0:T(8,128)(2,1)S(1)} %slice.24.refs_0_.refs_4_), channel_id=1, source_target_pairs={{0,2},{1,3},{2,0},{3,1},{4,6},{5,7},{6,4},{7,5},{8,10},{9,11},{10,... | collective-permute-start | bytes 983048 | tf_op jit(solution)/shard_map/ppermute | solution.py:27
  15.4 15.5 %collective-permute-start.7 = (bf16[384,768]{1,0:T(8,128)(2,1)S(1)}, bf16[384,768]{1,0:T(8,128)(2,1)S(1)}, u32[]{:S(2)}, u32[]{:S(2)}) collective-permute-start(bf16[384,768]{1,0:T(8,128)(2,1)S(1)} %get-tuple-element.45), channel_id=1, source_target_pairs={{0,4},{1,5},{2,6},{3,7},{4,0},{5,1},{6,2},{7,3},{8,12},{9,13},{10,... | collective-permute-start | bytes 1769480 | tf_op jit(solution)/shard_map/ppermute | solution.py:27
  18.8 2.7 %collective-permute-start.3 = (bf16[128,1280]{1,0:T(8,128)(2,1)S(1)}, bf16[128,1280]{1,0:T(8,128)(2,1)S(1)}, u32[]{:S(2)}, u32[]{:S(2)}) collective-permute-start(bf16[128,1280]{1,0:T(8,128)(2,1)S(1)} %slice.24.refs_0_.refs_4_), channel_id=1, source_target_pairs={{0,1},{1,0},{2,3},{3,2},{4,5},{5,4},{6,7},{7,6},{8,9},{9,8},{10,11... | collective-permute-start | bytes 983048 | tf_op jit(solution)/shard_map/ppermute | solution.py:27
  21.5 1.6 %collective-permute-start.5 = (bf16[128,1280]{1,0:T(8,128)(2,1)S(1)}, bf16[128,1280]{1,0:T(8,128)(2,1)S(1)}, u32[]{:S(2)}, u32[]{:S(2)}) collective-permute-start(bf16[128,1280]{1,0:T(8,128)(2,1)S(1)} %collective-permute-done.4.refs_2_.refs_6_), channel_id=1, source_target_pairs={{0,1},{1,0},{2,3},{3,2},{4,5},{5,4},{6,7},{7,6},{8,9},{9,8},{10,11... | collective-permute-start | bytes 983048 | tf_op jit(solution)/shard_map/ppermute | solution.py:27
  23.5 7.1 %collective-permute-start.6 = (bf16[384,256]{1,0:T(8,128)(2,1)S(1)}, bf16[384,256]{1,0:T(8,128)(2,1)S(1)}, u32[]{:S(2)}, u32[]{:S(2)}) collective-permute-start(bf16[384,256]{1,0:T(8,128)(2,1)S(1)} %get-tuple-element.51), channel_id=1, source_target_pairs={{0,8},{1,9},{2,10},{3,11},{4,12},{5,13},{6,14},{7,15},{8,0},{9,1},... | collective-permute-start | bytes 589832 | tf_op jit(solution)/shard_map/ppermute | solution.py:27
  30.9 12.6 %collective-permute-start.10 = (bf16[384,640]{1,0:T(8,128)(2,1)S(1)}, bf16[384,640]{1,0:T(8,128)(2,1)S(1)}, u32[]{:S(2)}, u32[]{:S(2)}) collective-permute-start(bf16[384,640]{1,0:T(8,128)(2,1)S(1)} %get-tuple-element.64), channel_id=1, source_target_pairs={{0,4},{1,5},{2,6},{3,7},{4,0},{5,1},{6,2},{7,3},{8,12},{9,13},{10,... | collective-permute-start | bytes 1474568 | tf_op jit(solution)/shard_map/ppermute | solution.py:27
  32.5 10.5 %collective-permute-start.8 = (bf16[192,768]{1,0:T(8,128)(2,1)S(1)}, bf16[192,768]{1,0:T(8,128)(2,1)S(1)}, u32[]{:S(2)}, u32[]{:S(2)}) collective-permute-start(bf16[192,768]{1,0:T(8,128)(2,1)S(1)} %get-tuple-element.60), channel_id=1, source_target_pairs={{0,8},{1,9},{2,10},{3,11},{4,12},{5,13},{6,14},{7,15},{8,0},{9,1},... | collective-permute-start | bytes 884744 | tf_op jit(solution)/shard_map/ppermute | solution.py:27
  34.2 8.9 %collective-permute-start.13 = (bf16[192,256]{1,0:T(8,128)(2,1)S(1)}, bf16[192,256]{1,0:T(8,128)(2,1)S(1)}, u32[]{:S(2)}, u32[]{:S(2)}) collective-permute-start(bf16[192,256]{1,0:T(8,128)(2,1)S(1)} %get-tuple-element.57), channel_id=1, source_target_pairs={{0,16},{1,17},{2,18},{3,19},{4,20},{5,21},{6,22},{7,23},{8,24},{9,... | collective-permute-start | bytes 294920 | tf_op jit(solution)/shard_map/ppermute | solution.py:27
  43.5 12.6 %collective-permute-start.14 = (bf16[384,384]{1,0:T(8,128)(2,1)S(1)}, bf16[384,384]{1,0:T(8,128)(2,1)S(1)}, u32[]{:S(2)}, u32[]{:S(2)}) collective-permute-start(bf16[384,384]{1,0:T(8,128)(2,1)S(1)} %get-tuple-element.72), channel_id=1, source_target_pairs={{0,4},{1,5},{2,6},{3,7},{4,0},{5,1},{6,2},{7,3},{8,12},{9,13},{10,... | collective-permute-start | bytes 884744 | tf_op jit(solution)/shard_map/ppermute | solution.py:27
  45.1 9.5 %collective-permute-start.11 = (bf16[192,640]{1,0:T(8,128)(2,1)S(1)}, bf16[192,640]{1,0:T(8,128)(2,1)S(1)}, u32[]{:S(2)}, u32[]{:S(2)}) collective-permute-start(bf16[192,640]{1,0:T(8,128)(2,1)S(1)} %get-tuple-element.66), channel_id=1, source_target_pairs={{0,8},{1,9},{2,10},{3,11},{4,12},{5,13},{6,14},{7,15},{8,0},{9,1},... | collective-permute-start | bytes 737288 | tf_op jit(solution)/shard_map/ppermute | solution.py:27
  46.7 9.4 %collective-permute-start.9 = (bf16[96,768]{1,0:T(8,128)(2,1)S(1)}, bf16[96,768]{1,0:T(8,128)(2,1)S(1)}, u32[]{:S(2)}, u32[]{:S(2)}) collective-permute-start(bf16[96,768]{1,0:T(8,128)(2,1)S(1)} %get-tuple-element.62), channel_id=1, source_target_pairs={{0,16},{1,17},{2,18},{3,19},{4,20},{5,21},{6,22},{7,23},{8,24},{9,... | collective-permute-start | bytes 442376 | tf_op jit(solution)/shard_map/ppermute | solution.py:27
  54.6 7.0 %copy-start.3 = (s32[128,2]{0,1:T(2,128)S(1)}, s32[128,2]{0,1:T(2,128)}, u32[]{:S(2)}) copy-start(s32[128,2]{0,1:T(2,128)} %param.6) | copy-start | bytes 3076
  54.7 12.4 %collective-permute-start.12 = (bf16[96,640]{1,0:T(8,128)(2,1)S(1)}, bf16[96,640]{1,0:T(8,128)(2,1)S(1)}, u32[]{:S(2)}, u32[]{:S(2)}) collective-permute-start(bf16[96,640]{1,0:T(8,128)(2,1)S(1)} %get-tuple-element.68), channel_id=1, source_target_pairs={{0,16},{1,17},{2,18},{3,19},{4,20},{5,21},{6,22},{7,23},{8,24},{9,... | collective-permute-start | bytes 368648 | tf_op jit(solution)/shard_map/ppermute | solution.py:27
  56.2 6.0 %collective-permute-start.18 = (bf16[96,256]{1,0:T(8,128)(2,1)S(1)}, bf16[96,256]{1,0:T(8,128)(2,1)S(1)}, u32[]{:S(2)}, u32[]{:S(2)}) collective-permute-start(bf16[96,256]{1,0:T(8,128)(2,1)S(1)} %get-tuple-element.78), channel_id=1, source_target_pairs={{0,4},{1,5},{2,6},{3,7},{4,0},{5,1},{6,2},{7,3},{8,12},{9,13},{10,... | collective-permute-start | bytes 147464 | tf_op jit(solution)/shard_map/ppermute | solution.py:27
  56.8 10.2 %collective-permute-start.15 = (bf16[96,384]{1,0:T(8,128)(2,1)S(1)}, bf16[96,384]{1,0:T(8,128)(2,1)S(1)}, u32[]{:S(2)}, u32[]{:S(2)}) collective-permute-start(bf16[96,384]{1,0:T(8,128)(2,1)S(1)} %get-tuple-element.81), channel_id=1, source_target_pairs={{0,16},{1,17},{2,18},{3,19},{4,20},{5,21},{6,22},{7,23},{8,24},{9,... | collective-permute-start | bytes 221192 | tf_op jit(solution)/shard_map/ppermute | solution.py:27
  59.4 7.7 %collective-permute-start.16 = (bf16[96,384]{1,0:T(8,128)(2,1)S(1)}, bf16[96,384]{1,0:T(8,128)(2,1)S(1)}, u32[]{:S(2)}, u32[]{:S(2)}) collective-permute-start(bf16[96,384]{1,0:T(8,128)(2,1)S(1)} %get-tuple-element.80), channel_id=1, source_target_pairs={{0,8},{1,9},{2,10},{3,11},{4,12},{5,13},{6,14},{7,15},{8,0},{9,1},... | collective-permute-start | bytes 221192 | tf_op jit(solution)/shard_map/ppermute | solution.py:27
  59.4 7.7 %collective-permute-start.17 = (bf16[96,384]{1,0:T(8,128)(2,1)S(1)}, bf16[96,384]{1,0:T(8,128)(2,1)S(1)}, u32[]{:S(2)}, u32[]{:S(2)}) collective-permute-start(bf16[96,384]{1,0:T(8,128)(2,1)S(1)} %get-tuple-element.79), channel_id=1, source_target_pairs={{0,24},{1,25},{2,26},{3,27},{4,28},{5,29},{6,30},{7,31},{8,16},{9,... | collective-permute-start | bytes 221192 | tf_op jit(solution)/shard_map/ppermute | solution.py:27

commit v5 on v4

--- a/solution.py
+++ b/solution.py
@@ -14,7 +14,7 @@
 INFO_ROWS = 16
 PACK_MIB = 60
 LEAD_FLOPS = 6 * 10**9
-SIXTEENTHS = (6, 5, 3, 2)
+SIXTEENTHS = {"a": 5, "z": 4, "b": 4, "c": 3}
 
 
 def _send(value, dp_mask, expert_mask):
@@ -76,8 +76,8 @@
         send_ref[p * rows : (p + 1) * rows, :] = prod[q * rows : (q + 1) * rows, :].astype(BF16)
 
 
-def _first_kernel(n_e, n_d, keep_blocks, send_blocks, where_ref, act_ref, *refs):
-    firsts, (at_ref, keep_ref, send_ref, held) = refs[:n_e], refs[n_e:]
+def _first_kernel(n_e, n_d, blocks_a, blocks_z, where_ref, act_ref, *refs):
+    firsts, (at_ref, keep_a_ref, send_a_ref, keep_z_ref, send_z_ref, held) = refs[:n_e], refs[n_e:]
     d, e = where_ref[0], where_ref[1]
     expert = e.astype(F32)
     capacity, hidden = act_ref.shape[1:]
@@ -94,7 +94,9 @@
         at_ref[q * rows : (q + 1) * rows, :] = held[pl.ds(start, rows), :]
     tok = jnp.concatenate([r[0:tokens, :] for r in firsts], axis=0)
     prod = jnp.dot(at_ref[...], tok, preferred_element_type=F32)
-    _split(prod, keep_blocks, send_blocks, rows, keep_ref, send_ref)
+    size = keep_a_ref.shape[1]
+    _split(prod[:, :size], *blocks_a, rows, keep_a_ref, send_a_ref)
+    _split(prod[:, size:], *blocks_z, rows, keep_z_ref, send_z_ref)
 
 
 def _partial_kernel(n_e, keep_blocks, send_blocks, rows, columns, at_ref, *refs):
@@ -194,7 +196,7 @@
         out_specs=out_specs,
         scratch_shapes=scratch,
         compiler_params=pltpu.CompilerParams(vmem_limit_bytes=mib * MIB),
-        cost_estimate=pl.CostEstimate(flops=flops, bytes_accessed=4 * MIB, transcendentals=0),
+        cost_estimate=pl.CostEstimate(flops=flops, bytes_accessed=0, transcendentals=0),
         name=name,
         **more,
     )
@@ -214,8 +216,8 @@
     lanes = width // 128
     where = jnp.stack([lax.axis_index("dp"), lax.axis_index("expert")]).astype(jnp.int32)
     pre = saved_pre.reshape(saved_pre.shape[1:])[0]
-    sizes = [part * width // 16 for part in SIXTEENTHS]
-    lead = sizes[0]
+    sizes = {name: part * width // 16 for name, part in SIXTEENTHS.items()}
+    lead = sizes["a"] + sizes["z"]
 
     whole = lambda i: (0, 0)
     first = _call(
@@ -291,18 +293,21 @@
             8,
         )(keep, got)
 
-    kept, sent = blocks_of(by_x)
-    at_all, keep_a, send_a = _call(
-        functools.partial(_first_kernel, n_e, n_d, kept, sent),
+    blocks_a, blocks_z = blocks_of(by_x), blocks_of(by_z)
+    at_all, keep_a, send_a, keep_z, send_z = _call(
+        functools.partial(_first_kernel, n_e, n_d, blocks_a, blocks_z),
         "first_partial",
-        (_shape((hidden, depth), BF16),) + halves(len(kept), len(sent), lead),
+        (_shape((hidden, depth), BF16),)
+        + halves(*map(len, blocks_a), sizes["a"])
+        + halves(*map(len, blocks_z), sizes["z"]),
         [SM] + [VM] * (1 + n_e),
-        (VM, VM, VM),
-        10,
+        (VM,) * 5,
+        14,
         2 * hidden * depth * lead,
         [pltpu.VMEM((hidden, depth), BF16)],
     )(where, act, *firsts)
     got_a = exchange(send_a, keep_a.shape[0], by_x[0])
+    got_z = exchange(send_z, keep_z.shape[0], by_z[0])
 
     raw_lead = _call(
         functools.partial(_lead_kernel, n_e, capacity),
@@ -317,25 +322,21 @@
 
     rests = gather(_after(rest, firsts[n_e // 2]), raw_lead)
 
-    def partial(chunk, stages):
+    def partial(start, size, stages):
         kept, sent = blocks_of(stages)
-        start = sum(sizes[1:chunk])
-        columns = slice(start, start + sizes[chunk])
         return _call(
-            functools.partial(_partial_kernel, n_e, kept, sent, rows, columns),
+            functools.partial(_partial_kernel, n_e, kept, sent, rows, slice(start, start + size)),
             "partial_chunk",
-            halves(len(kept), len(sent), sizes[chunk]),
+            halves(len(kept), len(sent), size),
             [VM] * (1 + n_e),
             (VM, VM),
             8,
-            2 * hidden * depth * sizes[chunk],
+            0,
         )(at_all, *rests)
 
-    keep_b, send_b = partial(1, by_x)
-    keep_c, send_c = partial(2, at_once)
-    keep_z, send_z = partial(3, by_z)
-
-    got_z = exchange(send_z, keep_z.shape[0], by_z[0])
+    keep_b, send_b = partial(0, sizes["b"], by_x)
+    keep_c, send_c = partial(sizes["b"], sizes["c"], at_once)
+
     pre_grad, back = _call(
         functools.partial(_slot_kernel, n_e, hidden),
         "slot_gradients",
@@ -343,16 +344,14 @@
         [SM] + [VM] * (3 + 2 * n_e),
         (VM, VM),
         14,
-        2 * n_e * capacity * (width - lead) * hidden,
+        0,
         [pltpu.VMEM((n_e * capacity, width - lead), BF16)],
-    )(_after(where, send_b, send_c, send_z), pre, down_weight, raw_lead, *firsts, *rests)
-    keep_z, send_z = add(keep_z, got_z, by_z[1])
+    )(_after(where, send_b, send_c), pre, down_weight, raw_lead, *firsts, *rests)
+    got_b = exchange(_after(send_b, back, *got_a), keep_b.shape[0], by_x[0])
+    keep_a, send_a = add(_after(keep_a, back), got_a, by_x[1])
+    got_a = exchange(send_a, keep_a.shape[0], by_x[1])
+    keep_z, send_z = add(_after(keep_z, back), got_z, by_z[1])
     got_z = exchange(send_z, keep_z.shape[0], by_z[1])
-
-    got_b = exchange(_after(send_b, back, send_z, *got_a), keep_b.shape[0], by_x[0])
-    keep_a, send_a = add(_after(keep_a, back, send_z), got_a, by_x[1])
-    got_a = exchange(send_a, keep_a.shape[0], by_x[1])
-
     returned = lax.all_to_all(
         _after(back, send_a, send_z), "expert", split_axis=0, concat_axis=0, tiled=True
     )
@@ -360,16 +359,17 @@
     got_c = exchange(_after(send_c, returned, *got_b, *got_z, *got_a), keep_c.shape[0], at_once[0])
     keep_b, send_b = add(keep_b, got_b, by_x[1])
     got_b = exchange(send_b, keep_b.shape[0], by_x[1])
-    keep_a, send_a = add(keep_a, got_a, by_x[2])
+    keep_a, send_a = add(_after(keep_a, send_b), got_a, by_x[2])
     end_a = [keep_a] + exchange(send_a, keep_a.shape[0], by_x[2])
+    keep_z, send_z = add(_after(keep_z, send_a, send_b), got_z, by_z[2])
+    end_z = [keep_z] + exchange(send_z, keep_z.shape[0], by_z[2])
     keep_b, send_b = add(keep_b, got_b, by_x[2])
     end_b = [keep_b] + exchange(send_b, keep_b.shape[0], by_x[2])
 
-    keep_c, send_c = add(_after(keep_c, send_b, end_a[1]), got_c, at_once[1])
+    keep_c, send_c = add(_after(keep_c, send_b, end_a[1], end_z[1]), got_c, at_once[1])
     end_c = [keep_c] + exchange(send_c, keep_c.shape[0], at_once[1])
-    keep_z, send_z = add(_after(keep_z, send_c), got_z, by_z[2])
-    end_z = [keep_z] + exchange(send_z, keep_z.shape[0], by_z[2])
-    ends = (end_a, end_b, end_c, end_z)
+
+    ends = (end_a, end_z, end_b, end_c)
     down_grad = _call(
         functools.partial(_finish_kernel, 1.0 / n_d, tuple(len(end) for end in ends)),
         "finish",

time: 68.6 us -> 67 us (0.977)
  waiting for transfers between devices: 19.8 us -> 17.5 us
  starting transfers between devices: 26.5 us -> 27.2 us
    ppermute x19, waiting for transfers between devices: 19.8 us -> 17.5 us  [_send(): return lax.ppermute(value, AXES, pairs)]
    pallas_call x4 -> x3, Pallas kernels: 3.96 us -> 3.8 us  [the longest x1 2.67 us: _fast(): _call(functools.partial(_first_kernel, n_e, n_d, blocks_a, blocks_z), 'fi...]
  transfers between devices with their start and end apart: 19 -> 19, of which waited for: 8 -> 10; matrix products, arithmetic and copies ran while one was open for 2% -> 2% of each run, Pallas kernels for 15% -> 15%
where the time goes in v5:
time: 67 us; the launch traced here: 66.5 us
  starting transfers between devices  27.2 us (41%)
  waiting for transfers between devices  17.5 us (26%)
  Pallas kernels  13.4 us (20%)
  blocking collectives  6.08 us (9%)
  local copies, waits for them, and re-layouts  1 us (1%)
  between operations  0.76 us (1%)
    ppermute x19, starting transfers between devices, _send(): return lax.ppermute(value, AXES, pairs)  27.2 us
    ppermute x19, waiting for transfers between devices, _send(): return lax.ppermute(value, AXES, pairs)  17.5 us
    all_to_all x1, blocking collectives, _fast(): lax.all_to_all(_after(back, send_a, send_z), 'expert', split_axis=0, conc...  6.08 us
    pallas_call x1, Pallas kernels, _fast(): _call(functools.partial(_slot_kernel, n_e, hidden), 'slot_gradients', (_s...  3.5 us
    pallas_call x1, Pallas kernels, _fast(): _call(functools.partial(_first_kernel, n_e, n_d, blocks_a, blocks_z), 'fi...  2.67 us
    pallas_call x1, Pallas kernels, _fast(): _call(functools.partial(_lead_kernel, n_e, capacity), 'raw_lead', _shape(...  2.27 us
    pallas_call x1, Pallas kernels, _fast(): _call(functools.partial(_pack_kernel, tokens, lead), 'pack_tokens', _shap...  1.84 us
  transfers between devices with their start and end apart: 19, of which 10 were waited for; matrix products, arithmetic and copies ran while one was open for 2% of the time, Pallas kernels for 15%

profile of v5, /device:TPU:0, one launch (start us, length us, event | category | flops | bytes accessed | tf_op | source)
XLA Modules:
  0.0 66.5 jit_solution(7700075491330255680)
XLA Ops:
  0.6 0.0 copy-start
  0.6 1.8 %pack_tokens.1.refs_0_ = bf16[144,1152]{1,0:T(8,128)(2,1)} custom-call(s32[2,128]{1,0:T(2,128)} %bitcast.18, bf16[2,128]{1,0:T(2,128)(2,1)} %bitcast.19, bf16[128,2048]{1,0:T(8,128)(2,1)} %tok_ref.1), custom_call_target="tpu_custom_call" | custom-call | tf_op jit(solution)/shard_map/pack_tokens/pallas_call | solution.py:223
  2.5 3.0 %collective-permute-start.1 = (bf16[144,1152]{1,0:T(8,128)(2,1)}, bf16[144,1152]{1,0:T(8,128)(2,1)S(1)}, u32[]{:S(2)}, u32[]{:S(2)}) collective-permute-start(bf16[144,1152]{1,0:T(8,128)(2,1)} %pack_tokens.1.refs_0_), channel_id=1, source_target_pairs={{0,2},{1,3},{2,0},{3,1},{4,6},{5,7},{6,4},{7,5},{8,10},{9,11},{10,... | collective-permute-start | bytes 995336 | tf_op jit(solution)/shard_map/ppermute | solution.py:27
  5.5 1.0 %slice.24.refs_0_.refs_4_ = bf16[128,896]{1,0:T(8,128)(2,1)S(1)} slice(bf16[128,2048]{1,0:T(8,128)(2,1)} %tok_ref.1), slice={[0:128], [1152:2048]} | slice | bytes 458752 | tf_op jit(solution)/shard_map/slice | solution.py:236
  6.4 0.1 collective-permute-start
  6.5 7.0 %collective-permute-done.1.refs_2_ = bf16[144,1152]{1,0:T(8,128)(2,1)S(1)} collective-permute-done((bf16[144,1152]{1,0:T(8,128)(2,1)}, bf16[144,1152]{1,0:T(8,128)(2,1)S(1)}, u32[]{:S(2)}, u32[]{:S(2)}) %collective-permute-start.1) | collective-permute-done | bytes 331808 | tf_op jit(solution)/shard_map/ppermute | solution.py:27
  13.5 0.0 collective-permute-start.2
  13.5 0.0 copy-done
  13.5 0.0 copy-start.2
  13.5 0.2 activation.1.act_ref
  13.7 0.1 pad_add_fusion.where_ref
  13.8 0.0 copy-start.1
  13.8 1.8 %collective-permute-start.4 = (bf16[128,896]{1,0:T(8,128)(2,1)S(1)}, bf16[128,896]{1,0:T(8,128)(2,1)S(1)}, u32[]{:S(2)}, u32[]{:S(2)}) collective-permute-start(bf16[128,896]{1,0:T(8,128)(2,1)S(1)} %slice.24.refs_0_.refs_4_), channel_id=1, source_target_pairs={{0,2},{1,3},{2,0},{3,1},{4,6},{5,7},{6,4},{7,5},{8,10},{9,11},{10,... | collective-permute-start | bytes 688136 | tf_op jit(solution)/shard_map/ppermute | solution.py:27
  15.6 0.0 collective-permute-done.refs_1_
  15.6 0.0 collective-permute-done.2.refs_3_
  15.6 0.0 copy-done.2
  15.6 2.7 %first_partial.1 = (bf16[768,512]{1,0:T(8,128)(2,1)S(1)}, f32[384,640]{1,0:T(8,128)S(1)}, bf16[384,640]{1,0:T(8,128)(2,1)S(1)}, f32[384,512]{1,0:T(8,128)S(1)}, bf16[384,512]{1,0:T(8,128)(2,1)S(1)}) custom-call(s32[2]{0:T(128)S(1)} %pad_add_fusion.where_ref, f32[4,96,768]{2,1,0:T(8,128)S(1)} %activation.1.act_ref, bf16[144,1152]{1,0:T(8,128)(2,1)S(1)} %copy-done.2, ...), custom_call_target="tpu_custom_call" | custom-call | flops 905969664 | tf_op jit(solution)/shard_map/first_partial/pallas_call | solution.py:297
  18.2 1.6 %collective-permute-start.6 = (bf16[384,640]{1,0:T(8,128)(2,1)S(1)}, bf16[384,640]{1,0:T(8,128)(2,1)S(1)}, u32[]{:S(2)}, u32[]{:S(2)}) collective-permute-start(bf16[384,640]{1,0:T(8,128)(2,1)S(1)} %get-tuple-element.47), channel_id=1, source_target_pairs={{0,4},{1,5},{2,6},{3,7},{4,0},{5,1},{6,2},{7,3},{8,12},{9,13},{10,... | collective-permute-start | bytes 1474568 | tf_op jit(solution)/shard_map/ppermute | solution.py:27
  19.8 0.0 copy-done.1
  19.8 2.3 %raw_lead.1.raw_ref = f32[384,768]{1,0:T(8,128)S(1)} custom-call(s32[2]{0:T(128)S(1)} %pad_add_fusion.where_ref, bf16[1,768,2048]{2,1,0:T(8,128)(2,1)S(1)} %copy-done.1, bf16[144,1152]{1,0:T(8,128)(2,1)S(1)} %copy-done.2, bf16[144,1152]{1,0:T(8,128)(2,1)S(1)} %collective-permute-done.refs_1_, bf16[144,1152]{1,0:T(8,128)(2,1)S(1)} %collective-permute-done.1.refs_2_, ...), custom_call_target="tpu_custom_call" | custom-call | flops 6000000000 | tf_op jit(solution)/shard_map/raw_lead/pallas_call | solution.py:312
  22.1 0.0 collective-permute-done.4.refs_2_.refs_6_
  22.1 0.1 collective-permute-start.3
  22.2 0.5 collective-permute-start.5
  22.7 1.6 %collective-permute-start.10 = (bf16[384,512]{1,0:T(8,128)(2,1)S(1)}, bf16[384,512]{1,0:T(8,128)(2,1)S(1)}, u32[]{:S(2)}, u32[]{:S(2)}) collective-permute-start(bf16[384,512]{1,0:T(8,128)(2,1)S(1)} %get-tuple-element.68), channel_id=1, source_target_pairs={{0,8},{1,9},{2,10},{3,11},{4,12},{5,13},{6,14},{7,15},{8,0},{9,1},... | collective-permute-start | bytes 1179656 | tf_op jit(solution)/shard_map/ppermute | solution.py:27
  24.2 0.0 collective-permute-done.3.refs_1_.refs_5_
  24.2 0.0 collective-permute-done.5.refs_3_.refs_7_
  24.2 0.6 partial_chunk.3
  24.8 0.6 partial_chunk.2
  25.4 3.5 %slot_gradients.1 = (bf16[4,96,1536]{2,1,0:T(8,128)(2,1)}, f32[4,1,128]{2,1,0:T(1,128)S(1)}) custom-call(s32[2]{0:T(128)S(1)} %pad_add_fusion.where_ref, bf16[4,96,1536]{2,1,0:T(8,128)(2,1)S(1)} %bitcast.16, bf16[1,768,2048]{2,1,0:T(8,128)(2,1)S(1)} %copy-done.1, f32[384,768]{1,0:T(8,128)S(1)} %raw_lead.1.raw_ref, bf16[144,1152]{1,0:T(8,128)(2,1)S(1)} %copy-done.2, ...), custom_call_target="tpu_custom_call" | custom-call | tf_op jit(solution)/shard_map/slot_gradients/pallas_call | solution.py:340
  28.9 2.8 %collective-permute-done.6.got_ref = bf16[384,640]{1,0:T(8,128)(2,1)S(1)} collective-permute-done((bf16[384,640]{1,0:T(8,128)(2,1)S(1)}, bf16[384,640]{1,0:T(8,128)(2,1)S(1)}, u32[]{:S(2)}, u32[]{:S(2)}) %collective-permute-start.6) | collective-permute-done | bytes 491552 | tf_op jit(solution)/shard_map/ppermute | solution.py:27
  31.6 1.5 %collective-permute-start.7 = (bf16[384,512]{1,0:T(8,128)(2,1)S(1)}, bf16[384,512]{1,0:T(8,128)(2,1)S(1)}, u32[]{:S(2)}, u32[]{:S(2)}) collective-permute-start(bf16[384,512]{1,0:T(8,128)(2,1)S(1)} %get-tuple-element.60), channel_id=1, source_target_pairs={{0,4},{1,5},{2,6},{3,7},{4,0},{5,1},{6,2},{7,3},{8,12},{9,13},{10,... | collective-permute-start | bytes 1179656 | tf_op jit(solution)/shard_map/ppermute | solution.py:27
  33.1 0.1 sum_halves.7
  33.2 1.6 %collective-permute-start.8 = (bf16[192,640]{1,0:T(8,128)(2,1)S(1)}, bf16[192,640]{1,0:T(8,128)(2,1)S(1)}, u32[]{:S(2)}, u32[]{:S(2)}) collective-permute-start(bf16[192,640]{1,0:T(8,128)(2,1)S(1)} %get-tuple-element.63), channel_id=1, source_target_pairs={{0,8},{1,9},{2,10},{3,11},{4,12},{5,13},{6,14},{7,15},{8,0},{9,1},... | collective-permute-start | bytes 737288 | tf_op jit(solution)/shard_map/ppermute | solution.py:27
  34.9 0.0 collective-permute-done.10.got_ref
  34.9 0.1 sum_halves.10
  34.9 2.7 %collective-permute-start.11 = (bf16[192,512]{1,0:T(8,128)(2,1)S(1)}, bf16[192,512]{1,0:T(8,128)(2,1)S(1)}, u32[]{:S(2)}, u32[]{:S(2)}) collective-permute-start(bf16[192,512]{1,0:T(8,128)(2,1)S(1)} %get-tuple-element.71), channel_id=1, source_target_pairs={{0,16},{1,17},{2,18},{3,19},{4,20},{5,21},{6,22},{7,23},{8,24},{9,... | collective-permute-start | bytes 589832 | tf_op jit(solution)/shard_map/ppermute | solution.py:27
  37.6 6.1 %all_to_all.5 = f32[4,1,128]{2,1,0:T(1,128)S(1)} all-to-all(f32[4,1,128]{2,1,0:T(1,128)S(1)} %get-tuple-element.79), channel_id=1, replica_groups=mesh['dp'=8,'expert'=4] {'expert'}, dimensions={0} | all-to-all | bytes 4096 | tf_op jit(solution)/shard_map/all_to_all | solution.py:355
  43.7 0.0 collective-permute-done.11.got_ref
  43.7 0.8 %collective-permute-done.8.got_ref = bf16[192,640]{1,0:T(8,128)(2,1)S(1)} collective-permute-done((bf16[192,640]{1,0:T(8,128)(2,1)S(1)}, bf16[192,640]{1,0:T(8,128)(2,1)S(1)}, u32[]{:S(2)}, u32[]{:S(2)}) %collective-permute-start.8) | collective-permute-done | bytes 245792 | tf_op jit(solution)/shard_map/ppermute | solution.py:27
  44.5 0.0 collective-permute-done.7.got_ref
  44.5 0.5 collective-permute-start.15
  45.0 0.1 sum_halves.8
  45.1 2.7 %collective-permute-start.13 = (bf16[192,512]{1,0:T(8,128)(2,1)S(1)}, bf16[192,512]{1,0:T(8,128)(2,1)S(1)}, u32[]{:S(2)}, u32[]{:S(2)}) collective-permute-start(bf16[192,512]{1,0:T(8,128)(2,1)S(1)} %get-tuple-element.61), channel_id=1, source_target_pairs={{0,8},{1,9},{2,10},{3,11},{4,12},{5,13},{6,14},{7,15},{8,0},{9,1},... | collective-permute-start | bytes 589832 | tf_op jit(solution)/shard_map/ppermute | solution.py:27
  47.8 2.9 %collective-permute-start.9 = (bf16[96,640]{1,0:T(8,128)(2,1)S(1)}, bf16[96,640]{1,0:T(8,128)(2,1)S(1)}, u32[]{:S(2)}, u32[]{:S(2)}) collective-permute-start(bf16[96,640]{1,0:T(8,128)(2,1)S(1)} %get-tuple-element.65), channel_id=1, source_target_pairs={{0,16},{1,17},{2,18},{3,19},{4,20},{5,21},{6,22},{7,23},{8,24},{9,... | collective-permute-start | bytes 368648 | tf_op jit(solution)/shard_map/ppermute | solution.py:27
  50.7 0.0 copy-start.3
  50.8 0.9 %collective-permute-start.12 = (bf16[96,512]{1,0:T(8,128)(2,1)S(1)}, bf16[96,512]{1,0:T(8,128)(2,1)S(1)}, u32[]{:S(2)}, u32[]{:S(2)}) collective-permute-start(bf16[96,512]{1,0:T(8,128)(2,1)S(1)} %get-tuple-element.73), channel_id=1, source_target_pairs={{0,4},{1,5},{2,6},{3,7},{4,0},{5,1},{6,2},{7,3},{8,12},{9,13},{10,... | collective-permute-start | bytes 294920 | tf_op jit(solution)/shard_map/ppermute | solution.py:27
  51.7 1.9 %collective-permute-done.13.got_ref = bf16[192,512]{1,0:T(8,128)(2,1)S(1)} collective-permute-done((bf16[192,512]{1,0:T(8,128)(2,1)S(1)}, bf16[192,512]{1,0:T(8,128)(2,1)S(1)}, u32[]{:S(2)}, u32[]{:S(2)}) %collective-permute-start.13) | collective-permute-done | bytes 196640 | tf_op jit(solution)/shard_map/ppermute | solution.py:27
  53.7 1.4 %collective-permute-start.14 = (bf16[96,512]{1,0:T(8,128)(2,1)S(1)}, bf16[96,512]{1,0:T(8,128)(2,1)S(1)}, u32[]{:S(2)}, u32[]{:S(2)}) collective-permute-start(bf16[96,512]{1,0:T(8,128)(2,1)S(1)} %get-tuple-element.76), channel_id=1, source_target_pairs={{0,16},{1,17},{2,18},{3,19},{4,20},{5,21},{6,22},{7,23},{8,24},{9,... | collective-permute-start | bytes 294920 | tf_op jit(solution)/shard_map/ppermute | solution.py:27
  55.1 0.4 collective-permute-done.12.refs_3_
  55.4 1.7 %collective-permute-done.9.refs_1_ = bf16[96,640]{1,0:T(8,128)(2,1)S(1)} collective-permute-done((bf16[96,640]{1,0:T(8,128)(2,1)S(1)}, bf16[96,640]{1,0:T(8,128)(2,1)S(1)}, u32[]{:S(2)}, u32[]{:S(2)}) %collective-permute-start.9) | collective-permute-done | bytes 122912 | tf_op jit(solution)/shard_map/ppermute | solution.py:27
  57.2 0.0 collective-permute-done.15.got_ref
  57.2 0.1 sum_halves.13
  57.2 2.7 %collective-permute-start.18 = (bf16[96,384]{1,0:T(8,128)(2,1)S(1)}, bf16[96,384]{1,0:T(8,128)(2,1)S(1)}, u32[]{:S(2)}, u32[]{:S(2)}) collective-permute-start(bf16[96,384]{1,0:T(8,128)(2,1)S(1)} %get-tuple-element.83), channel_id=1, source_target_pairs={{0,24},{1,25},{2,26},{3,27},{4,28},{5,29},{6,30},{7,31},{8,16},{9,... | collective-permute-start | bytes 221192 | tf_op jit(solution)/shard_map/ppermute | solution.py:27
  59.9 0.0 collective-permute-start.17
  59.9 1.8 %collective-permute-start.16 = (bf16[96,384]{1,0:T(8,128)(2,1)S(1)}, bf16[96,384]{1,0:T(8,128)(2,1)S(1)}, u32[]{:S(2)}, u32[]{:S(2)}) collective-permute-start(bf16[96,384]{1,0:T(8,128)(2,1)S(1)} %get-tuple-element.85), channel_id=1, source_target_pairs={{0,16},{1,17},{2,18},{3,19},{4,20},{5,21},{6,22},{7,23},{8,24},{9,... | collective-permute-start | bytes 221192 | tf_op jit(solution)/shard_map/ppermute | solution.py:27
  61.7 0.0 copy-done.3
  61.7 0.6 fusion.2
  62.3 0.1 collective-permute-done.14.refs_5_
  62.4 1.2 %collective-permute-done.18.refs_9_ = bf16[96,384]{1,0:T(8,128)(2,1)S(1)} collective-permute-done((bf16[96,384]{1,0:T(8,128)(2,1)S(1)}, bf16[96,384]{1,0:T(8,128)(2,1)S(1)}, u32[]{:S(2)}, u32[]{:S(2)}) %collective-permute-start.18) | collective-permute-done | bytes 73760 | tf_op jit(solution)/shard_map/ppermute | solution.py:27
  63.6 0.8 %collective-permute-done.17.refs_8_ = bf16[96,384]{1,0:T(8,128)(2,1)S(1)} collective-permute-done((bf16[96,384]{1,0:T(8,128)(2,1)S(1)}, bf16[96,384]{1,0:T(8,128)(2,1)S(1)}, u32[]{:S(2)}, u32[]{:S(2)}) %collective-permute-start.17) | collective-permute-done | bytes 73760 | tf_op jit(solution)/shard_map/ppermute | solution.py:27
  64.4 0.8 %collective-permute-done.16.refs_7_ = bf16[96,384]{1,0:T(8,128)(2,1)S(1)} collective-permute-done((bf16[96,384]{1,0:T(8,128)(2,1)S(1)}, bf16[96,384]{1,0:T(8,128)(2,1)S(1)}, u32[]{:S(2)}, u32[]{:S(2)}) %collective-permute-start.16) | collective-permute-done | bytes 73760 | tf_op jit(solution)/shard_map/ppermute | solution.py:27
  65.2 1.3 %finish.1 = f32[1536,128]{1,0:T(8,128)} custom-call(f32[96,640]{1,0:T(8,128)S(1)} %get-tuple-element.64.refs_0_, bf16[96,640]{1,0:T(8,128)(2,1)S(1)} %collective-permute-done.9.refs_1_, f32[96,512]{1,0:T(8,128)S(1)} %get-tuple-element.72.refs_2_, bf16[96,512]{1,0:T(8,128)(2,1)S(1)} %collective-permute-done.12.refs_3_, ...), custom_call_target="tpu_custom_call" | custom-call | tf_op jit(solution)/shard_map/finish/pallas_call | solution.py:373
  (5 shorter events, 0.1 us)
Async XLA Ops:
  0.6 12.8 %copy-start = (bf16[1,1,4,96,1536]{4,3,2,1,0:T(8,128)(2,1)S(1)}, bf16[1,1,4,96,1536]{4,3,2,1,0:T(8,128)(2,1)}, u32[]{:S(2)}) copy-start(bf16[1,1,4,96,1536]{4,3,2,1,0:T(8,128)(2,1)} %param.9) | copy-start | bytes 3538948
  2.5 11.0 %collective-permute-start.1 = (bf16[144,1152]{1,0:T(8,128)(2,1)}, bf16[144,1152]{1,0:T(8,128)(2,1)S(1)}, u32[]{:S(2)}, u32[]{:S(2)}) collective-permute-start(bf16[144,1152]{1,0:T(8,128)(2,1)} %pack_tokens.1.refs_0_), channel_id=1, source_target_pairs={{0,2},{1,3},{2,0},{3,1},{4,6},{5,7},{6,4},{7,5},{8,10},{9,11},{10,... | collective-permute-start | bytes 995336 | tf_op jit(solution)/shard_map/ppermute | solution.py:27
  6.4 9.1 %collective-permute-start = (bf16[144,1152]{1,0:T(8,128)(2,1)}, bf16[144,1152]{1,0:T(8,128)(2,1)S(1)}, u32[]{:S(2)}, u32[]{:S(2)}) collective-permute-start(bf16[144,1152]{1,0:T(8,128)(2,1)} %pack_tokens.1.refs_0_), channel_id=1, source_target_pairs={{0,1},{1,0},{2,3},{3,2},{4,5},{5,4},{6,7},{7,6},{8,9},{9,8},{10,11... | collective-permute-start | bytes 995336 | tf_op jit(solution)/shard_map/ppermute | solution.py:27
  13.5 2.1 %collective-permute-start.2 = (bf16[144,1152]{1,0:T(8,128)(2,1)S(1)}, bf16[144,1152]{1,0:T(8,128)(2,1)S(1)}, u32[]{:S(2)}, u32[]{:S(2)}) collective-permute-start(bf16[144,1152]{1,0:T(8,128)(2,1)S(1)} %collective-permute-done.1.refs_2_), channel_id=1, source_target_pairs={{0,1},{1,0},{2,3},{3,2},{4,5},{5,4},{6,7},{7,6},{8,9},{9,8},{10,11... | collective-permute-start | bytes 995336 | tf_op jit(solution)/shard_map/ppermute | solution.py:27
  13.5 2.1 %copy-start.2 = (bf16[144,1152]{1,0:T(8,128)(2,1)S(1)}, bf16[144,1152]{1,0:T(8,128)(2,1)}, u32[]{:S(2)}) copy-start(bf16[144,1152]{1,0:T(8,128)(2,1)} %pack_tokens.1.refs_0_) | copy-start | bytes 995332
  13.8 6.0 %copy-start.1 = (bf16[1,768,2048]{2,1,0:T(8,128)(2,1)S(1)}, bf16[1,768,2048]{2,1,0:T(8,128)(2,1)}, u32[]{:S(2)}) copy-start(bf16[1,768,2048]{2,1,0:T(8,128)(2,1)} %w_ref.3) | copy-start | bytes 9437188
  13.8 8.3 %collective-permute-start.4 = (bf16[128,896]{1,0:T(8,128)(2,1)S(1)}, bf16[128,896]{1,0:T(8,128)(2,1)S(1)}, u32[]{:S(2)}, u32[]{:S(2)}) collective-permute-start(bf16[128,896]{1,0:T(8,128)(2,1)S(1)} %slice.24.refs_0_.refs_4_), channel_id=1, source_target_pairs={{0,2},{1,3},{2,0},{3,1},{4,6},{5,7},{6,4},{7,5},{8,10},{9,11},{10,... | collective-permute-start | bytes 688136 | tf_op jit(solution)/shard_map/ppermute | solution.py:27
  18.2 13.4 %collective-permute-start.6 = (bf16[384,640]{1,0:T(8,128)(2,1)S(1)}, bf16[384,640]{1,0:T(8,128)(2,1)S(1)}, u32[]{:S(2)}, u32[]{:S(2)}) collective-permute-start(bf16[384,640]{1,0:T(8,128)(2,1)S(1)} %get-tuple-element.47), channel_id=1, source_target_pairs={{0,4},{1,5},{2,6},{3,7},{4,0},{5,1},{6,2},{7,3},{8,12},{9,13},{10,... | collective-permute-start | bytes 1474568 | tf_op jit(solution)/shard_map/ppermute | solution.py:27
  22.1 2.2 %collective-permute-start.3 = (bf16[128,896]{1,0:T(8,128)(2,1)S(1)}, bf16[128,896]{1,0:T(8,128)(2,1)S(1)}, u32[]{:S(2)}, u32[]{:S(2)}) collective-permute-start(bf16[128,896]{1,0:T(8,128)(2,1)S(1)} %slice.24.refs_0_.refs_4_), channel_id=1, source_target_pairs={{0,1},{1,0},{2,3},{3,2},{4,5},{5,4},{6,7},{7,6},{8,9},{9,8},{10,11... | collective-permute-start | bytes 688136 | tf_op jit(solution)/shard_map/ppermute | solution.py:27
  22.2 2.1 %collective-permute-start.5 = (bf16[128,896]{1,0:T(8,128)(2,1)S(1)}, bf16[128,896]{1,0:T(8,128)(2,1)S(1)}, u32[]{:S(2)}, u32[]{:S(2)}) collective-permute-start(bf16[128,896]{1,0:T(8,128)(2,1)S(1)} %collective-permute-done.4.refs_2_.refs_6_), channel_id=1, source_target_pairs={{0,1},{1,0},{2,3},{3,2},{4,5},{5,4},{6,7},{7,6},{8,9},{9,8},{10,11... | collective-permute-start | bytes 688136 | tf_op jit(solution)/shard_map/ppermute | solution.py:27
  22.7 12.2 %collective-permute-start.10 = (bf16[384,512]{1,0:T(8,128)(2,1)S(1)}, bf16[384,512]{1,0:T(8,128)(2,1)S(1)}, u32[]{:S(2)}, u32[]{:S(2)}) collective-permute-start(bf16[384,512]{1,0:T(8,128)(2,1)S(1)} %get-tuple-element.68), channel_id=1, source_target_pairs={{0,8},{1,9},{2,10},{3,11},{4,12},{5,13},{6,14},{7,15},{8,0},{9,1},... | collective-permute-start | bytes 1179656 | tf_op jit(solution)/shard_map/ppermute | solution.py:27
  31.6 12.8 %collective-permute-start.7 = (bf16[384,512]{1,0:T(8,128)(2,1)S(1)}, bf16[384,512]{1,0:T(8,128)(2,1)S(1)}, u32[]{:S(2)}, u32[]{:S(2)}) collective-permute-start(bf16[384,512]{1,0:T(8,128)(2,1)S(1)} %get-tuple-element.60), channel_id=1, source_target_pairs={{0,4},{1,5},{2,6},{3,7},{4,0},{5,1},{6,2},{7,3},{8,12},{9,13},{10,... | collective-permute-start | bytes 1179656 | tf_op jit(solution)/shard_map/ppermute | solution.py:27
  33.2 11.3 %collective-permute-start.8 = (bf16[192,640]{1,0:T(8,128)(2,1)S(1)}, bf16[192,640]{1,0:T(8,128)(2,1)S(1)}, u32[]{:S(2)}, u32[]{:S(2)}) collective-permute-start(bf16[192,640]{1,0:T(8,128)(2,1)S(1)} %get-tuple-element.63), channel_id=1, source_target_pairs={{0,8},{1,9},{2,10},{3,11},{4,12},{5,13},{6,14},{7,15},{8,0},{9,1},... | collective-permute-start | bytes 737288 | tf_op jit(solution)/shard_map/ppermute | solution.py:27
  34.9 8.7 %collective-permute-start.11 = (bf16[192,512]{1,0:T(8,128)(2,1)S(1)}, bf16[192,512]{1,0:T(8,128)(2,1)S(1)}, u32[]{:S(2)}, u32[]{:S(2)}) collective-permute-start(bf16[192,512]{1,0:T(8,128)(2,1)S(1)} %get-tuple-element.71), channel_id=1, source_target_pairs={{0,16},{1,17},{2,18},{3,19},{4,20},{5,21},{6,22},{7,23},{8,24},{9,... | collective-permute-start | bytes 589832 | tf_op jit(solution)/shard_map/ppermute | solution.py:27
  44.5 12.7 %collective-permute-start.15 = (bf16[384,384]{1,0:T(8,128)(2,1)S(1)}, bf16[384,384]{1,0:T(8,128)(2,1)S(1)}, u32[]{:S(2)}, u32[]{:S(2)}) collective-permute-start(bf16[384,384]{1,0:T(8,128)(2,1)S(1)} %get-tuple-element.80), channel_id=1, source_target_pairs={{0,4},{1,5},{2,6},{3,7},{4,0},{5,1},{6,2},{7,3},{8,12},{9,13},{10,... | collective-permute-start | bytes 884744 | tf_op jit(solution)/shard_map/ppermute | solution.py:27
  45.1 8.5 %collective-permute-start.13 = (bf16[192,512]{1,0:T(8,128)(2,1)S(1)}, bf16[192,512]{1,0:T(8,128)(2,1)S(1)}, u32[]{:S(2)}, u32[]{:S(2)}) collective-permute-start(bf16[192,512]{1,0:T(8,128)(2,1)S(1)} %get-tuple-element.61), channel_id=1, source_target_pairs={{0,8},{1,9},{2,10},{3,11},{4,12},{5,13},{6,14},{7,15},{8,0},{9,1},... | collective-permute-start | bytes 589832 | tf_op jit(solution)/shard_map/ppermute | solution.py:27
  47.8 9.3 %collective-permute-start.9 = (bf16[96,640]{1,0:T(8,128)(2,1)S(1)}, bf16[96,640]{1,0:T(8,128)(2,1)S(1)}, u32[]{:S(2)}, u32[]{:S(2)}) collective-permute-start(bf16[96,640]{1,0:T(8,128)(2,1)S(1)} %get-tuple-element.65), channel_id=1, source_target_pairs={{0,16},{1,17},{2,18},{3,19},{4,20},{5,21},{6,22},{7,23},{8,24},{9,... | collective-permute-start | bytes 368648 | tf_op jit(solution)/shard_map/ppermute | solution.py:27
  50.7 11.0 %copy-start.3 = (s32[128,2]{0,1:T(2,128)S(1)}, s32[128,2]{0,1:T(2,128)}, u32[]{:S(2)}) copy-start(s32[128,2]{0,1:T(2,128)} %param.6) | copy-start | bytes 3076
  50.8 4.7 %collective-permute-start.12 = (bf16[96,512]{1,0:T(8,128)(2,1)S(1)}, bf16[96,512]{1,0:T(8,128)(2,1)S(1)}, u32[]{:S(2)}, u32[]{:S(2)}) collective-permute-start(bf16[96,512]{1,0:T(8,128)(2,1)S(1)} %get-tuple-element.73), channel_id=1, source_target_pairs={{0,4},{1,5},{2,6},{3,7},{4,0},{5,1},{6,2},{7,3},{8,12},{9,13},{10,... | collective-permute-start | bytes 294920 | tf_op jit(solution)/shard_map/ppermute | solution.py:27
  53.7 8.7 %collective-permute-start.14 = (bf16[96,512]{1,0:T(8,128)(2,1)S(1)}, bf16[96,512]{1,0:T(8,128)(2,1)S(1)}, u32[]{:S(2)}, u32[]{:S(2)}) collective-permute-start(bf16[96,512]{1,0:T(8,128)(2,1)S(1)} %get-tuple-element.76), channel_id=1, source_target_pairs={{0,16},{1,17},{2,18},{3,19},{4,20},{5,21},{6,22},{7,23},{8,24},{9,... | collective-permute-start | bytes 294920 | tf_op jit(solution)/shard_map/ppermute | solution.py:27
  57.2 6.3 %collective-permute-start.18 = (bf16[96,384]{1,0:T(8,128)(2,1)S(1)}, bf16[96,384]{1,0:T(8,128)(2,1)S(1)}, u32[]{:S(2)}, u32[]{:S(2)}) collective-permute-start(bf16[96,384]{1,0:T(8,128)(2,1)S(1)} %get-tuple-element.83), channel_id=1, source_target_pairs={{0,24},{1,25},{2,26},{3,27},{4,28},{5,29},{6,30},{7,31},{8,16},{9,... | collective-permute-start | bytes 221192 | tf_op jit(solution)/shard_map/ppermute | solution.py:27
  59.9 4.4 %collective-permute-start.17 = (bf16[96,384]{1,0:T(8,128)(2,1)S(1)}, bf16[96,384]{1,0:T(8,128)(2,1)S(1)}, u32[]{:S(2)}, u32[]{:S(2)}) collective-permute-start(bf16[96,384]{1,0:T(8,128)(2,1)S(1)} %get-tuple-element.84), channel_id=1, source_target_pairs={{0,8},{1,9},{2,10},{3,11},{4,12},{5,13},{6,14},{7,15},{8,0},{9,1},... | collective-permute-start | bytes 221192 | tf_op jit(solution)/shard_map/ppermute | solution.py:27
  59.9 5.3 %collective-permute-start.16 = (bf16[96,384]{1,0:T(8,128)(2,1)S(1)}, bf16[96,384]{1,0:T(8,128)(2,1)S(1)}, u32[]{:S(2)}, u32[]{:S(2)}) collective-permute-start(bf16[96,384]{1,0:T(8,128)(2,1)S(1)} %get-tuple-element.85), channel_id=1, source_target_pairs={{0,16},{1,17},{2,18},{3,19},{4,20},{5,21},{6,22},{7,23},{8,24},{9,... | collective-permute-start | bytes 221192 | tf_op jit(solution)/shard_map/ppermute | solution.py:27

commit v6 on v5

--- a/solution.py
+++ b/solution.py
@@ -12,7 +12,7 @@
 AXES = ("dp", "expert")
 MIB = 1024 * 1024
 INFO_ROWS = 16
-PACK_MIB = 60
+PACK_MIB = 8
 LEAD_FLOPS = 6 * 10**9
 SIXTEENTHS = {"a": 5, "z": 4, "b": 4, "c": 3}
 
@@ -223,16 +223,16 @@
     first = _call(
         functools.partial(_pack_kernel, tokens, lead),
         "pack_tokens",
-        _shape((tokens + INFO_ROWS, lead), BF16),
+        pltpu.VMEM((tokens + INFO_ROWS, lead), BF16),
         [
             pl.BlockSpec((routes.shape[1], tokens), whole),
             pl.BlockSpec((routes.shape[1], tokens), whole),
             pl.BlockSpec((tokens, lead), whole),
         ],
-        pl.BlockSpec((tokens + INFO_ROWS, lead), whole),
+        VM,
         PACK_MIB,
         grid=(1,),
-    )(routes.T, combine.T, grad_tokens)
+    )(*(pltpu.with_memory_space_constraint(v, pltpu.HBM) for v in (routes.T, combine.T, grad_tokens)))
     rest = grad_tokens[:, lead:]
 
     def gather(block, *later):
@@ -347,16 +347,16 @@
         0,
         [pltpu.VMEM((n_e * capacity, width - lead), BF16)],
     )(_after(where, send_b, send_c), pre, down_weight, raw_lead, *firsts, *rests)
-    got_b = exchange(_after(send_b, back, *got_a), keep_b.shape[0], by_x[0])
+    keep_z, send_z = add(_after(keep_z, back), got_z, by_z[1])
+    got_z = exchange(send_z, keep_z.shape[0], by_z[1])
+    got_b = exchange(_after(send_b, back, send_z, *got_a), keep_b.shape[0], by_x[0])
     keep_a, send_a = add(_after(keep_a, back), got_a, by_x[1])
     got_a = exchange(send_a, keep_a.shape[0], by_x[1])
-    keep_z, send_z = add(_after(keep_z, back), got_z, by_z[1])
-    got_z = exchange(send_z, keep_z.shape[0], by_z[1])
     returned = lax.all_to_all(
         _after(back, send_a, send_z), "expert", split_axis=0, concat_axis=0, tiled=True
     )
 
-    got_c = exchange(_after(send_c, returned, *got_b, *got_z, *got_a), keep_c.shape[0], at_once[0])
+    got_c = exchange(_after(send_c, returned, *got_b), keep_c.shape[0], at_once[0])
     keep_b, send_b = add(keep_b, got_b, by_x[1])
     got_b = exchange(send_b, keep_b.shape[0], by_x[1])
     keep_a, send_a = add(_after(keep_a, send_b), got_a, by_x[2])

time: 67 us -> 66.2 us (0.988)
  waiting for transfers between devices: 17.5 us -> 21.1 us
  starting transfers between devices: 27.2 us -> 23.7 us
  Pallas kernels: 13.4 us -> 12.7 us
    ppermute x19, waiting for transfers between devices: 17.5 us -> 21.1 us  [_send(): return lax.ppermute(value, AXES, pairs)]
    ppermute x19, starting transfers between devices: 27.2 us -> 23.7 us  [_send(): return lax.ppermute(value, AXES, pairs)]
    pallas_call x1, Pallas kernels: 1.84 us -> 1.12 us  [_fast(): _call(functools.partial(_pack_kernel, tokens, lead), 'pack_tokens', pltpu...]
  transfers between devices with their start and end apart: 19 -> 19, of which waited for: 10 -> 9; matrix products, arithmetic and copies ran while one was open for 2% -> 2% of each run, Pallas kernels for 15% -> 16%
where the time goes in v6:
time: 66.2 us; the launch traced here: 66 us
  starting transfers between devices  23.7 us (36%)
  waiting for transfers between devices  21.1 us (32%)
  Pallas kernels  12.7 us (19%)
  blocking collectives  6.08 us (9%)
  local copies, waits for them, and re-layouts  1 us (2%)
  between operations  0.76 us (1%)
    ppermute x19, starting transfers between devices, _send(): return lax.ppermute(value, AXES, pairs)  23.7 us
    ppermute x19, waiting for transfers between devices, _send(): return lax.ppermute(value, AXES, pairs)  21.1 us
    all_to_all x1, blocking collectives, _fast(): lax.all_to_all(_after(back, send_a, send_z), 'expert', split_axis=0, conc...  6.08 us
    pallas_call x1, Pallas kernels, _fast(): _call(functools.partial(_slot_kernel, n_e, hidden), 'slot_gradients', (_s...  3.54 us
    pallas_call x1, Pallas kernels, _fast(): _call(functools.partial(_first_kernel, n_e, n_d, blocks_a, blocks_z), 'fi...  2.66 us
    pallas_call x1, Pallas kernels, _fast(): _call(functools.partial(_lead_kernel, n_e, capacity), 'raw_lead', _shape(...  2.27 us
  transfers between devices with their start and end apart: 19, of which 9 were waited for; matrix products, arithmetic and copies ran while one was open for 2% of the time, Pallas kernels for 16%

profile of v6, /device:TPU:0, one launch (start us, length us, event | category | flops | bytes accessed | tf_op | source)
XLA Modules:
  0.0 66.0 jit_solution(7394394164009500281)
XLA Ops:
  0.6 0.0 copy-start
  0.6 1.1 %pack_tokens.1.refs_0_ = bf16[144,1152]{1,0:T(8,128)(2,1)S(1)} custom-call(s32[2,128]{1,0:T(2,128)} %bitcast.18, bf16[2,128]{1,0:T(2,128)(2,1)} %bitcast.19, bf16[128,2048]{1,0:T(8,128)(2,1)} %tok_ref.1), custom_call_target="tpu_custom_call" | custom-call | tf_op jit(solution)/shard_map/pack_tokens/pallas_call | solution.py:223
  1.8 3.0 %collective-permute-start.1 = (bf16[144,1152]{1,0:T(8,128)(2,1)S(1)}, bf16[144,1152]{1,0:T(8,128)(2,1)S(1)}, u32[]{:S(2)}, u32[]{:S(2)}) collective-permute-start(bf16[144,1152]{1,0:T(8,128)(2,1)S(1)} %pack_tokens.1.refs_0_), channel_id=1, source_target_pairs={{0,2},{1,3},{2,0},{3,1},{4,6},{5,7},{6,4},{7,5},{8,10},{9,11},{10,... | collective-permute-start | bytes 995336 | tf_op jit(solution)/shard_map/ppermute | solution.py:27
  4.8 1.0 %slice.24.refs_0_.refs_4_ = bf16[128,896]{1,0:T(8,128)(2,1)S(1)} slice(bf16[128,2048]{1,0:T(8,128)(2,1)} %tok_ref.1), slice={[0:128], [1152:2048]} | slice | bytes 458752 | tf_op jit(solution)/shard_map/slice | solution.py:236
  5.8 0.1 collective-permute-start
  5.8 6.8 %collective-permute-done.1.refs_2_ = bf16[144,1152]{1,0:T(8,128)(2,1)S(1)} collective-permute-done((bf16[144,1152]{1,0:T(8,128)(2,1)S(1)}, bf16[144,1152]{1,0:T(8,128)(2,1)S(1)}, u32[]{:S(2)}, u32[]{:S(2)}) %collective-permute-start.1) | collective-permute-done | bytes 331808 | tf_op jit(solution)/shard_map/ppermute | solution.py:27
  12.6 0.0 collective-permute-start.2
  12.6 0.0 copy-done
  12.6 0.2 activation.1.act_ref
  12.8 0.1 pad_add_fusion.where_ref
  12.9 0.0 copy-start.1
  12.9 1.8 %collective-permute-start.4 = (bf16[128,896]{1,0:T(8,128)(2,1)S(1)}, bf16[128,896]{1,0:T(8,128)(2,1)S(1)}, u32[]{:S(2)}, u32[]{:S(2)}) collective-permute-start(bf16[128,896]{1,0:T(8,128)(2,1)S(1)} %slice.24.refs_0_.refs_4_), channel_id=1, source_target_pairs={{0,2},{1,3},{2,0},{3,1},{4,6},{5,7},{6,4},{7,5},{8,10},{9,11},{10,... | collective-permute-start | bytes 688136 | tf_op jit(solution)/shard_map/ppermute | solution.py:27
  14.7 0.0 collective-permute-done.refs_1_
  14.7 0.0 collective-permute-done.2.refs_3_
  14.7 2.7 %first_partial.1 = (bf16[768,512]{1,0:T(8,128)(2,1)S(1)}, f32[384,640]{1,0:T(8,128)S(1)}, bf16[384,640]{1,0:T(8,128)(2,1)S(1)}, f32[384,512]{1,0:T(8,128)S(1)}, bf16[384,512]{1,0:T(8,128)(2,1)S(1)}) custom-call(s32[2]{0:T(128)S(1)} %pad_add_fusion.where_ref, f32[4,96,768]{2,1,0:T(8,128)S(1)} %activation.1.act_ref, bf16[144,1152]{1,0:T(8,128)(2,1)S(1)} %pack_tokens.1.refs_0_, ...), custom_call_target="tpu_custom_call" | custom-call | flops 905969664 | tf_op jit(solution)/shard_map/first_partial/pallas_call | solution.py:297
  17.3 1.6 %collective-permute-start.6 = (bf16[384,640]{1,0:T(8,128)(2,1)S(1)}, bf16[384,640]{1,0:T(8,128)(2,1)S(1)}, u32[]{:S(2)}, u32[]{:S(2)}) collective-permute-start(bf16[384,640]{1,0:T(8,128)(2,1)S(1)} %get-tuple-element.47), channel_id=1, source_target_pairs={{0,4},{1,5},{2,6},{3,7},{4,0},{5,1},{6,2},{7,3},{8,12},{9,13},{10,... | collective-permute-start | bytes 1474568 | tf_op jit(solution)/shard_map/ppermute | solution.py:27
  18.9 1.6 %collective-permute-start.7 = (bf16[384,512]{1,0:T(8,128)(2,1)S(1)}, bf16[384,512]{1,0:T(8,128)(2,1)S(1)}, u32[]{:S(2)}, u32[]{:S(2)}) collective-permute-start(bf16[384,512]{1,0:T(8,128)(2,1)S(1)} %get-tuple-element.62), channel_id=1, source_target_pairs={{0,8},{1,9},{2,10},{3,11},{4,12},{5,13},{6,14},{7,15},{8,0},{9,1},... | collective-permute-start | bytes 1179656 | tf_op jit(solution)/shard_map/ppermute | solution.py:27
  20.5 0.0 copy-done.1
  20.5 2.3 %raw_lead.1.raw_ref = f32[384,768]{1,0:T(8,128)S(1)} custom-call(s32[2]{0:T(128)S(1)} %pad_add_fusion.where_ref, bf16[1,768,2048]{2,1,0:T(8,128)(2,1)S(1)} %copy-done.1, bf16[144,1152]{1,0:T(8,128)(2,1)S(1)} %pack_tokens.1.refs_0_, bf16[144,1152]{1,0:T(8,128)(2,1)S(1)} %collective-permute-done.refs_1_, bf16[144,1152]{1,0:T(8,128)(2,1)S(1)} %collective-permute-done.1.refs_2_, ...), custom_call_target="tpu_custom_call" | custom-call | flops 6000000000 | tf_op jit(solution)/shard_map/raw_lead/pallas_call | solution.py:312
  22.8 0.0 collective-permute-done.4.refs_2_.refs_6_
  22.8 0.1 collective-permute-start.3
  22.9 0.5 collective-permute-start.5
  23.3 1.0 %collective-permute-done.3.refs_1_.refs_5_ = bf16[128,896]{1,0:T(8,128)(2,1)S(1)} collective-permute-done((bf16[128,896]{1,0:T(8,128)(2,1)S(1)}, bf16[128,896]{1,0:T(8,128)(2,1)S(1)}, u32[]{:S(2)}, u32[]{:S(2)}) %collective-permute-start.3) | collective-permute-done | bytes 229408 | tf_op jit(solution)/shard_map/ppermute | solution.py:27
  24.3 0.3 collective-permute-done.5.refs_3_.refs_7_
  24.7 0.6 partial_chunk.3
  25.2 0.6 partial_chunk.2
  25.8 3.5 %slot_gradients.1 = (bf16[4,96,1536]{2,1,0:T(8,128)(2,1)}, f32[4,1,128]{2,1,0:T(1,128)S(1)}) custom-call(s32[2]{0:T(128)S(1)} %pad_add_fusion.where_ref, bf16[4,96,1536]{2,1,0:T(8,128)(2,1)S(1)} %bitcast.16, bf16[1,768,2048]{2,1,0:T(8,128)(2,1)S(1)} %copy-done.1, f32[384,768]{1,0:T(8,128)S(1)} %raw_lead.1.raw_ref, bf16[144,1152]{1,0:T(8,128)(2,1)S(1)} %pack_tokens.1.refs_0_, ...), custom_call_target="tpu_custom_call" | custom-call | tf_op jit(solution)/shard_map/slot_gradients/pallas_call | solution.py:340
  29.3 0.5 collective-permute-done.7.got_ref
  29.9 0.1 sum_halves.8
  29.9 0.8 %collective-permute-done.6.got_ref = bf16[384,640]{1,0:T(8,128)(2,1)S(1)} collective-permute-done((bf16[384,640]{1,0:T(8,128)(2,1)S(1)}, bf16[384,640]{1,0:T(8,128)(2,1)S(1)}, u32[]{:S(2)}, u32[]{:S(2)}) %collective-permute-start.6) | collective-permute-done | bytes 491552 | tf_op jit(solution)/shard_map/ppermute | solution.py:27
  30.8 1.5 %collective-permute-start.8 = (bf16[384,512]{1,0:T(8,128)(2,1)S(1)}, bf16[384,512]{1,0:T(8,128)(2,1)S(1)}, u32[]{:S(2)}, u32[]{:S(2)}) collective-permute-start(bf16[384,512]{1,0:T(8,128)(2,1)S(1)} %get-tuple-element.64), channel_id=1, source_target_pairs={{0,4},{1,5},{2,6},{3,7},{4,0},{5,1},{6,2},{7,3},{8,12},{9,13},{10,... | collective-permute-start | bytes 1179656 | tf_op jit(solution)/shard_map/ppermute | solution.py:27
  32.3 0.1 sum_halves.7
  32.4 1.6 %collective-permute-start.9 = (bf16[192,640]{1,0:T(8,128)(2,1)S(1)}, bf16[192,640]{1,0:T(8,128)(2,1)S(1)}, u32[]{:S(2)}, u32[]{:S(2)}) collective-permute-start(bf16[192,640]{1,0:T(8,128)(2,1)S(1)} %get-tuple-element.67), channel_id=1, source_target_pairs={{0,8},{1,9},{2,10},{3,11},{4,12},{5,13},{6,14},{7,15},{8,0},{9,1},... | collective-permute-start | bytes 737288 | tf_op jit(solution)/shard_map/ppermute | solution.py:27
  34.0 2.6 %collective-permute-start.11 = (bf16[192,512]{1,0:T(8,128)(2,1)S(1)}, bf16[192,512]{1,0:T(8,128)(2,1)S(1)}, u32[]{:S(2)}, u32[]{:S(2)}) collective-permute-start(bf16[192,512]{1,0:T(8,128)(2,1)S(1)} %get-tuple-element.63), channel_id=1, source_target_pairs={{0,16},{1,17},{2,18},{3,19},{4,20},{5,21},{6,22},{7,23},{8,24},{9,... | collective-permute-start | bytes 589832 | tf_op jit(solution)/shard_map/ppermute | solution.py:27
  36.6 6.1 %all_to_all.5 = f32[4,1,128]{2,1,0:T(1,128)S(1)} all-to-all(f32[4,1,128]{2,1,0:T(1,128)S(1)} %get-tuple-element.79), channel_id=1, replica_groups=mesh['dp'=8,'expert'=4] {'expert'}, dimensions={0} | all-to-all | bytes 4096 | tf_op jit(solution)/shard_map/all_to_all | solution.py:355
  42.7 0.0 collective-permute-done.8.got_ref
  42.7 0.5 collective-permute-start.15
  43.2 0.1 sum_halves.9
  43.3 1.1 %collective-permute-start.13 = (bf16[192,512]{1,0:T(8,128)(2,1)S(1)}, bf16[192,512]{1,0:T(8,128)(2,1)S(1)}, u32[]{:S(2)}, u32[]{:S(2)}) collective-permute-start(bf16[192,512]{1,0:T(8,128)(2,1)S(1)} %get-tuple-element.65), channel_id=1, source_target_pairs={{0,8},{1,9},{2,10},{3,11},{4,12},{5,13},{6,14},{7,15},{8,0},{9,1},... | collective-permute-start | bytes 589832 | tf_op jit(solution)/shard_map/ppermute | solution.py:27
  44.4 0.0 collective-permute-done.9.got_ref
  44.5 2.7 %collective-permute-start.10 = (bf16[96,640]{1,0:T(8,128)(2,1)S(1)}, bf16[96,640]{1,0:T(8,128)(2,1)S(1)}, u32[]{:S(2)}, u32[]{:S(2)}) collective-permute-start(bf16[96,640]{1,0:T(8,128)(2,1)S(1)} %get-tuple-element.69), channel_id=1, source_target_pairs={{0,16},{1,17},{2,18},{3,19},{4,20},{5,21},{6,22},{7,23},{8,24},{9,... | collective-permute-start | bytes 368648 | tf_op jit(solution)/shard_map/ppermute | solution.py:27
  47.1 0.0 copy-start.2
  47.1 0.0 collective-permute-done.11.got_ref
  47.2 0.6 collective-permute-start.12
  47.8 4.9 %collective-permute-done.13.got_ref = bf16[192,512]{1,0:T(8,128)(2,1)S(1)} collective-permute-done((bf16[192,512]{1,0:T(8,128)(2,1)S(1)}, bf16[192,512]{1,0:T(8,128)(2,1)S(1)}, u32[]{:S(2)}, u32[]{:S(2)}) %collective-permute-start.13) | collective-permute-done | bytes 196640 | tf_op jit(solution)/shard_map/ppermute | solution.py:27
  52.7 0.1 collective-permute-start.14
  52.8 1.0 %collective-permute-done.12.refs_3_ = bf16[96,512]{1,0:T(8,128)(2,1)S(1)} collective-permute-done((bf16[96,512]{1,0:T(8,128)(2,1)S(1)}, bf16[96,512]{1,0:T(8,128)(2,1)S(1)}, u32[]{:S(2)}, u32[]{:S(2)}) %collective-permute-start.12) | collective-permute-done | bytes 98336 | tf_op jit(solution)/shard_map/ppermute | solution.py:27
  53.8 0.0 collective-permute-done.10.refs_1_
  53.8 0.0 collective-permute-done.15.got_ref
  53.8 0.1 sum_halves.13
  53.9 0.9 %collective-permute-start.18 = (bf16[96,384]{1,0:T(8,128)(2,1)S(1)}, bf16[96,384]{1,0:T(8,128)(2,1)S(1)}, u32[]{:S(2)}, u32[]{:S(2)}) collective-permute-start(bf16[96,384]{1,0:T(8,128)(2,1)S(1)} %get-tuple-element.83), channel_id=1, source_target_pairs={{0,24},{1,25},{2,26},{3,27},{4,28},{5,29},{6,30},{7,31},{8,16},{9,... | collective-permute-start | bytes 221192 | tf_op jit(solution)/shard_map/ppermute | solution.py:27
  54.8 1.6 %collective-permute-start.17 = (bf16[96,384]{1,0:T(8,128)(2,1)S(1)}, bf16[96,384]{1,0:T(8,128)(2,1)S(1)}, u32[]{:S(2)}, u32[]{:S(2)}) collective-permute-start(bf16[96,384]{1,0:T(8,128)(2,1)S(1)} %get-tuple-element.84), channel_id=1, source_target_pairs={{0,8},{1,9},{2,10},{3,11},{4,12},{5,13},{6,14},{7,15},{8,0},{9,1},... | collective-permute-start | bytes 221192 | tf_op jit(solution)/shard_map/ppermute | solution.py:27
  56.4 1.9 %collective-permute-start.16 = (bf16[96,384]{1,0:T(8,128)(2,1)S(1)}, bf16[96,384]{1,0:T(8,128)(2,1)S(1)}, u32[]{:S(2)}, u32[]{:S(2)}) collective-permute-start(bf16[96,384]{1,0:T(8,128)(2,1)S(1)} %get-tuple-element.85), channel_id=1, source_target_pairs={{0,16},{1,17},{2,18},{3,19},{4,20},{5,21},{6,22},{7,23},{8,24},{9,... | collective-permute-start | bytes 221192 | tf_op jit(solution)/shard_map/ppermute | solution.py:27
  58.4 0.0 copy-done.2
  58.4 0.6 fusion.2
  59.0 3.7 %collective-permute-done.14.refs_5_ = bf16[96,512]{1,0:T(8,128)(2,1)S(1)} collective-permute-done((bf16[96,512]{1,0:T(8,128)(2,1)S(1)}, bf16[96,512]{1,0:T(8,128)(2,1)S(1)}, u32[]{:S(2)}, u32[]{:S(2)}) %collective-permute-start.14) | collective-permute-done | bytes 98336 | tf_op jit(solution)/shard_map/ppermute | solution.py:27
  62.7 0.0 collective-permute-done.18.refs_9_
  62.7 0.0 collective-permute-done.17.refs_8_
  62.7 2.0 %collective-permute-done.16.refs_7_ = bf16[96,384]{1,0:T(8,128)(2,1)S(1)} collective-permute-done((bf16[96,384]{1,0:T(8,128)(2,1)S(1)}, bf16[96,384]{1,0:T(8,128)(2,1)S(1)}, u32[]{:S(2)}, u32[]{:S(2)}) %collective-permute-start.16) | collective-permute-done | bytes 73760 | tf_op jit(solution)/shard_map/ppermute | solution.py:27
  64.7 1.3 %finish.1 = f32[1536,128]{1,0:T(8,128)} custom-call(f32[96,640]{1,0:T(8,128)S(1)} %get-tuple-element.68.refs_0_, bf16[96,640]{1,0:T(8,128)(2,1)S(1)} %collective-permute-done.10.refs_1_, f32[96,512]{1,0:T(8,128)S(1)} %get-tuple-element.72.refs_2_, bf16[96,512]{1,0:T(8,128)(2,1)S(1)} %collective-permute-done.12.refs_3_, ...), custom_call_target="tpu_custom_call" | custom-call | tf_op jit(solution)/shard_map/finish/pallas_call | solution.py:373
  (5 shorter events, 0.2 us)
Async XLA Ops:
  0.6 12.0 %copy-start = (bf16[1,1,4,96,1536]{4,3,2,1,0:T(8,128)(2,1)S(1)}, bf16[1,1,4,96,1536]{4,3,2,1,0:T(8,128)(2,1)}, u32[]{:S(2)}) copy-start(bf16[1,1,4,96,1536]{4,3,2,1,0:T(8,128)(2,1)} %param.9) | copy-start | bytes 3538948
  1.8 10.8 %collective-permute-start.1 = (bf16[144,1152]{1,0:T(8,128)(2,1)S(1)}, bf16[144,1152]{1,0:T(8,128)(2,1)S(1)}, u32[]{:S(2)}, u32[]{:S(2)}) collective-permute-start(bf16[144,1152]{1,0:T(8,128)(2,1)S(1)} %pack_tokens.1.refs_0_), channel_id=1, source_target_pairs={{0,2},{1,3},{2,0},{3,1},{4,6},{5,7},{6,4},{7,5},{8,10},{9,11},{10,... | collective-permute-start | bytes 995336 | tf_op jit(solution)/shard_map/ppermute | solution.py:27
  5.8 8.9 %collective-permute-start = (bf16[144,1152]{1,0:T(8,128)(2,1)S(1)}, bf16[144,1152]{1,0:T(8,128)(2,1)S(1)}, u32[]{:S(2)}, u32[]{:S(2)}) collective-permute-start(bf16[144,1152]{1,0:T(8,128)(2,1)S(1)} %pack_tokens.1.refs_0_), channel_id=1, source_target_pairs={{0,1},{1,0},{2,3},{3,2},{4,5},{5,4},{6,7},{7,6},{8,9},{9,8},{10,11... | collective-permute-start | bytes 995336 | tf_op jit(solution)/shard_map/ppermute | solution.py:27
  12.6 2.1 %collective-permute-start.2 = (bf16[144,1152]{1,0:T(8,128)(2,1)S(1)}, bf16[144,1152]{1,0:T(8,128)(2,1)S(1)}, u32[]{:S(2)}, u32[]{:S(2)}) collective-permute-start(bf16[144,1152]{1,0:T(8,128)(2,1)S(1)} %collective-permute-done.1.refs_2_), channel_id=1, source_target_pairs={{0,1},{1,0},{2,3},{3,2},{4,5},{5,4},{6,7},{7,6},{8,9},{9,8},{10,11... | collective-permute-start | bytes 995336 | tf_op jit(solution)/shard_map/ppermute | solution.py:27
  12.9 7.6 %copy-start.1 = (bf16[1,768,2048]{2,1,0:T(8,128)(2,1)S(1)}, bf16[1,768,2048]{2,1,0:T(8,128)(2,1)}, u32[]{:S(2)}) copy-start(bf16[1,768,2048]{2,1,0:T(8,128)(2,1)} %w_ref.3) | copy-start | bytes 9437188
  12.9 9.8 %collective-permute-start.4 = (bf16[128,896]{1,0:T(8,128)(2,1)S(1)}, bf16[128,896]{1,0:T(8,128)(2,1)S(1)}, u32[]{:S(2)}, u32[]{:S(2)}) collective-permute-start(bf16[128,896]{1,0:T(8,128)(2,1)S(1)} %slice.24.refs_0_.refs_4_), channel_id=1, source_target_pairs={{0,2},{1,3},{2,0},{3,1},{4,6},{5,7},{6,4},{7,5},{8,10},{9,11},{10,... | collective-permute-start | bytes 688136 | tf_op jit(solution)/shard_map/ppermute | solution.py:27
  17.3 13.4 %collective-permute-start.6 = (bf16[384,640]{1,0:T(8,128)(2,1)S(1)}, bf16[384,640]{1,0:T(8,128)(2,1)S(1)}, u32[]{:S(2)}, u32[]{:S(2)}) collective-permute-start(bf16[384,640]{1,0:T(8,128)(2,1)S(1)} %get-tuple-element.47), channel_id=1, source_target_pairs={{0,4},{1,5},{2,6},{3,7},{4,0},{5,1},{6,2},{7,3},{8,12},{9,13},{10,... | collective-permute-start | bytes 1474568 | tf_op jit(solution)/shard_map/ppermute | solution.py:27
  18.9 11.0 %collective-permute-start.7 = (bf16[384,512]{1,0:T(8,128)(2,1)S(1)}, bf16[384,512]{1,0:T(8,128)(2,1)S(1)}, u32[]{:S(2)}, u32[]{:S(2)}) collective-permute-start(bf16[384,512]{1,0:T(8,128)(2,1)S(1)} %get-tuple-element.62), channel_id=1, source_target_pairs={{0,8},{1,9},{2,10},{3,11},{4,12},{5,13},{6,14},{7,15},{8,0},{9,1},... | collective-permute-start | bytes 1179656 | tf_op jit(solution)/shard_map/ppermute | solution.py:27
  22.8 1.6 %collective-permute-start.3 = (bf16[128,896]{1,0:T(8,128)(2,1)S(1)}, bf16[128,896]{1,0:T(8,128)(2,1)S(1)}, u32[]{:S(2)}, u32[]{:S(2)}) collective-permute-start(bf16[128,896]{1,0:T(8,128)(2,1)S(1)} %slice.24.refs_0_.refs_4_), channel_id=1, source_target_pairs={{0,1},{1,0},{2,3},{3,2},{4,5},{5,4},{6,7},{7,6},{8,9},{9,8},{10,11... | collective-permute-start | bytes 688136 | tf_op jit(solution)/shard_map/ppermute | solution.py:27
  22.9 1.8 %collective-permute-start.5 = (bf16[128,896]{1,0:T(8,128)(2,1)S(1)}, bf16[128,896]{1,0:T(8,128)(2,1)S(1)}, u32[]{:S(2)}, u32[]{:S(2)}) collective-permute-start(bf16[128,896]{1,0:T(8,128)(2,1)S(1)} %collective-permute-done.4.refs_2_.refs_6_), channel_id=1, source_target_pairs={{0,1},{1,0},{2,3},{3,2},{4,5},{5,4},{6,7},{7,6},{8,9},{9,8},{10,11... | collective-permute-start | bytes 688136 | tf_op jit(solution)/shard_map/ppermute | solution.py:27
  30.8 11.9 %collective-permute-start.8 = (bf16[384,512]{1,0:T(8,128)(2,1)S(1)}, bf16[384,512]{1,0:T(8,128)(2,1)S(1)}, u32[]{:S(2)}, u32[]{:S(2)}) collective-permute-start(bf16[384,512]{1,0:T(8,128)(2,1)S(1)} %get-tuple-element.64), channel_id=1, source_target_pairs={{0,4},{1,5},{2,6},{3,7},{4,0},{5,1},{6,2},{7,3},{8,12},{9,13},{10,... | collective-permute-start | bytes 1179656 | tf_op jit(solution)/shard_map/ppermute | solution.py:27
  32.4 12.1 %collective-permute-start.9 = (bf16[192,640]{1,0:T(8,128)(2,1)S(1)}, bf16[192,640]{1,0:T(8,128)(2,1)S(1)}, u32[]{:S(2)}, u32[]{:S(2)}) collective-permute-start(bf16[192,640]{1,0:T(8,128)(2,1)S(1)} %get-tuple-element.67), channel_id=1, source_target_pairs={{0,8},{1,9},{2,10},{3,11},{4,12},{5,13},{6,14},{7,15},{8,0},{9,1},... | collective-permute-start | bytes 737288 | tf_op jit(solution)/shard_map/ppermute | solution.py:27
  34.0 13.1 %collective-permute-start.11 = (bf16[192,512]{1,0:T(8,128)(2,1)S(1)}, bf16[192,512]{1,0:T(8,128)(2,1)S(1)}, u32[]{:S(2)}, u32[]{:S(2)}) collective-permute-start(bf16[192,512]{1,0:T(8,128)(2,1)S(1)} %get-tuple-element.63), channel_id=1, source_target_pairs={{0,16},{1,17},{2,18},{3,19},{4,20},{5,21},{6,22},{7,23},{8,24},{9,... | collective-permute-start | bytes 589832 | tf_op jit(solution)/shard_map/ppermute | solution.py:27
  42.7 11.1 %collective-permute-start.15 = (bf16[384,384]{1,0:T(8,128)(2,1)S(1)}, bf16[384,384]{1,0:T(8,128)(2,1)S(1)}, u32[]{:S(2)}, u32[]{:S(2)}) collective-permute-start(bf16[384,384]{1,0:T(8,128)(2,1)S(1)} %get-tuple-element.80), channel_id=1, source_target_pairs={{0,4},{1,5},{2,6},{3,7},{4,0},{5,1},{6,2},{7,3},{8,12},{9,13},{10,... | collective-permute-start | bytes 884744 | tf_op jit(solution)/shard_map/ppermute | solution.py:27
  43.3 9.3 %collective-permute-start.13 = (bf16[192,512]{1,0:T(8,128)(2,1)S(1)}, bf16[192,512]{1,0:T(8,128)(2,1)S(1)}, u32[]{:S(2)}, u32[]{:S(2)}) collective-permute-start(bf16[192,512]{1,0:T(8,128)(2,1)S(1)} %get-tuple-element.65), channel_id=1, source_target_pairs={{0,8},{1,9},{2,10},{3,11},{4,12},{5,13},{6,14},{7,15},{8,0},{9,1},... | collective-permute-start | bytes 589832 | tf_op jit(solution)/shard_map/ppermute | solution.py:27
  44.5 9.3 %collective-permute-start.10 = (bf16[96,640]{1,0:T(8,128)(2,1)S(1)}, bf16[96,640]{1,0:T(8,128)(2,1)S(1)}, u32[]{:S(2)}, u32[]{:S(2)}) collective-permute-start(bf16[96,640]{1,0:T(8,128)(2,1)S(1)} %get-tuple-element.69), channel_id=1, source_target_pairs={{0,16},{1,17},{2,18},{3,19},{4,20},{5,21},{6,22},{7,23},{8,24},{9,... | collective-permute-start | bytes 368648 | tf_op jit(solution)/shard_map/ppermute | solution.py:27
  47.1 11.2 %copy-start.2 = (s32[128,2]{0,1:T(2,128)S(1)}, s32[128,2]{0,1:T(2,128)}, u32[]{:S(2)}) copy-start(s32[128,2]{0,1:T(2,128)} %param.6) | copy-start | bytes 3076
  47.2 6.6 %collective-permute-start.12 = (bf16[96,512]{1,0:T(8,128)(2,1)S(1)}, bf16[96,512]{1,0:T(8,128)(2,1)S(1)}, u32[]{:S(2)}, u32[]{:S(2)}) collective-permute-start(bf16[96,512]{1,0:T(8,128)(2,1)S(1)} %get-tuple-element.73), channel_id=1, source_target_pairs={{0,4},{1,5},{2,6},{3,7},{4,0},{5,1},{6,2},{7,3},{8,12},{9,13},{10,... | collective-permute-start | bytes 294920 | tf_op jit(solution)/shard_map/ppermute | solution.py:27
  52.7 10.0 %collective-permute-start.14 = (bf16[96,512]{1,0:T(8,128)(2,1)S(1)}, bf16[96,512]{1,0:T(8,128)(2,1)S(1)}, u32[]{:S(2)}, u32[]{:S(2)}) collective-permute-start(bf16[96,512]{1,0:T(8,128)(2,1)S(1)} %get-tuple-element.76), channel_id=1, source_target_pairs={{0,16},{1,17},{2,18},{3,19},{4,20},{5,21},{6,22},{7,23},{8,24},{9,... | collective-permute-start | bytes 294920 | tf_op jit(solution)/shard_map/ppermute | solution.py:27
  53.9 8.8 %collective-permute-start.18 = (bf16[96,384]{1,0:T(8,128)(2,1)S(1)}, bf16[96,384]{1,0:T(8,128)(2,1)S(1)}, u32[]{:S(2)}, u32[]{:S(2)}) collective-permute-start(bf16[96,384]{1,0:T(8,128)(2,1)S(1)} %get-tuple-element.83), channel_id=1, source_target_pairs={{0,24},{1,25},{2,26},{3,27},{4,28},{5,29},{6,30},{7,31},{8,16},{9,... | collective-permute-start | bytes 221192 | tf_op jit(solution)/shard_map/ppermute | solution.py:27
  54.8 7.8 %collective-permute-start.17 = (bf16[96,384]{1,0:T(8,128)(2,1)S(1)}, bf16[96,384]{1,0:T(8,128)(2,1)S(1)}, u32[]{:S(2)}, u32[]{:S(2)}) collective-permute-start(bf16[96,384]{1,0:T(8,128)(2,1)S(1)} %get-tuple-element.84), channel_id=1, source_target_pairs={{0,8},{1,9},{2,10},{3,11},{4,12},{5,13},{6,14},{7,15},{8,0},{9,1},... | collective-permute-start | bytes 221192 | tf_op jit(solution)/shard_map/ppermute | solution.py:27
  56.4 8.3 %collective-permute-start.16 = (bf16[96,384]{1,0:T(8,128)(2,1)S(1)}, bf16[96,384]{1,0:T(8,128)(2,1)S(1)}, u32[]{:S(2)}, u32[]{:S(2)}) collective-permute-start(bf16[96,384]{1,0:T(8,128)(2,1)S(1)} %get-tuple-element.85), channel_id=1, source_target_pairs={{0,16},{1,17},{2,18},{3,19},{4,20},{5,21},{6,22},{7,23},{8,24},{9,... | collective-permute-start | bytes 221192 | tf_op jit(solution)/shard_map/ppermute | solution.py:27

commit v7 on v6

--- a/solution.py
+++ b/solution.py
@@ -76,27 +76,52 @@
         send_ref[p * rows : (p + 1) * rows, :] = prod[q * rows : (q + 1) * rows, :].astype(BF16)
 
 
-def _first_kernel(n_e, n_d, blocks_a, blocks_z, where_ref, act_ref, *refs):
-    firsts, (at_ref, keep_a_ref, send_a_ref, keep_z_ref, send_z_ref, held) = refs[:n_e], refs[n_e:]
+def _some_rows(at_ref, blocks, rows):
+    return jnp.concatenate([at_ref[q * rows : (q + 1) * rows, :] for q in blocks], axis=0)
+
+
+def _first_kernel(n_e, n_d, sent, where_ref, act_ref, *refs):
+    firsts, (at_ref, send_ref, held) = refs[:n_e], refs[n_e:]
     d, e = where_ref[0], where_ref[1]
     expert = e.astype(F32)
     capacity, hidden = act_ref.shape[1:]
     tokens = firsts[0].shape[0] - INFO_ROWS
     rows = hidden // n_d
-    for j in range(n_e):
-        chosen, slot_weight = _choice(_info(firsts[j], tokens), expert, capacity)
-        scaled = (slot_weight * act_ref[e ^ j]).astype(BF16)
-        held[:, j * tokens : (j + 1) * tokens] = lax.dot_general(
-            scaled, chosen.astype(BF16), (((0,), (0,)), ((), ())), preferred_element_type=F32
+    none = jnp.zeros((capacity, tokens), F32)
+    for j in range(0, n_e, 2):
+        left, left_weight = _choice(_info(firsts[j], tokens), expert, capacity)
+        right, right_weight = _choice(_info(firsts[j + 1], tokens), expert, capacity)
+        scaled = jnp.concatenate(
+            [left_weight * act_ref[e ^ j], right_weight * act_ref[e ^ (j + 1)]], axis=0
+        ).astype(BF16)
+        chosen = jnp.concatenate(
+            [
+                jnp.concatenate([left, none], axis=1),
+                jnp.concatenate([none, right], axis=1),
+            ],
+            axis=0,
+        ).astype(BF16)
+        held[:, j * tokens : (j + 2) * tokens] = lax.dot_general(
+            scaled, chosen, (((0,), (0,)), ((), ())), preferred_element_type=F32
         ).astype(BF16)
     for q in range(n_d):
         start = pl.multiple_of((d ^ q) * rows, 16)
         at_ref[q * rows : (q + 1) * rows, :] = held[pl.ds(start, rows), :]
-    tok = jnp.concatenate([r[0:tokens, :] for r in firsts], axis=0)
+    tok = jnp.concatenate([r[0:tokens, : send_ref.shape[1]] for r in firsts], axis=0)
+    send_ref[...] = jnp.dot(
+        _some_rows(at_ref, sent, rows), tok, preferred_element_type=F32
+    ).astype(BF16)
+
+
+def _second_kernel(n_e, kept, blocks_z, rows, at_ref, *refs):
+    firsts, (keep_a_ref, keep_z_ref, send_z_ref) = refs[:n_e], refs[n_e:]
+    tokens = firsts[0].shape[0] - INFO_ROWS
+    size = keep_a_ref.shape[1]
+    tok = jnp.concatenate([r[0:tokens, size:] for r in firsts], axis=0)
     prod = jnp.dot(at_ref[...], tok, preferred_element_type=F32)
-    size = keep_a_ref.shape[1]
-    _split(prod[:, :size], *blocks_a, rows, keep_a_ref, send_a_ref)
-    _split(prod[:, size:], *blocks_z, rows, keep_z_ref, send_z_ref)
+    _split(prod, *blocks_z, rows, keep_z_ref, send_z_ref)
+    tok = jnp.concatenate([r[0:tokens, :size] for r in firsts], axis=0)
+    keep_a_ref[...] = jnp.dot(_some_rows(at_ref, kept, rows), tok, preferred_element_type=F32)
 
 
 def _partial_kernel(n_e, keep_blocks, send_blocks, rows, columns, at_ref, *refs):
@@ -294,18 +319,25 @@
         )(keep, got)
 
     blocks_a, blocks_z = blocks_of(by_x), blocks_of(by_z)
-    at_all, keep_a, send_a, keep_z, send_z = _call(
-        functools.partial(_first_kernel, n_e, n_d, blocks_a, blocks_z),
-        "first_partial",
-        (_shape((hidden, depth), BF16),)
-        + halves(*map(len, blocks_a), sizes["a"])
-        + halves(*map(len, blocks_z), sizes["z"]),
+    keep_shape, send_shape = halves(*map(len, blocks_a), sizes["a"])
+    at_all, send_a = _call(
+        functools.partial(_first_kernel, n_e, n_d, blocks_a[1]),
+        "first_send",
+        (_shape((hidden, depth), BF16), send_shape),
         [SM] + [VM] * (1 + n_e),
-        (VM,) * 5,
-        14,
-        2 * hidden * depth * lead,
+        (VM, VM),
+        12,
+        0,
         [pltpu.VMEM((hidden, depth), BF16)],
     )(where, act, *firsts)
+    keep_a, keep_z, send_z = _call(
+        functools.partial(_second_kernel, n_e, blocks_a[0], blocks_z, rows),
+        "first_keep",
+        (keep_shape,) + halves(*map(len, blocks_z), sizes["z"]),
+        [VM] * (1 + n_e),
+        (VM,) * 3,
+        12,
+    )(_after(at_all, send_a), *firsts)
     got_a = exchange(send_a, keep_a.shape[0], by_x[0])
     got_z = exchange(send_z, keep_z.shape[0], by_z[0])
 

time: 66.2 us -> 65.5 us (0.989)
    pallas_call x1 -> x2, Pallas kernels: 2.66 us -> 2.6 us  [the longest x1 1.7 us: _fast(): _call(functools.partial(_first_kernel, n_e, n_d, blocks_a[1]), 'first_sen...]
  transfers between devices with their start and end apart: 19 -> 19, of which waited for: 9 -> 8; matrix products, arithmetic and copies ran while one was open for 2% -> 2% of each run, Pallas kernels for 16% -> 16%
where the time goes in v7:
time: 65.5 us; the launch traced here: 65.3 us
  starting transfers between devices  23.6 us (36%)
  waiting for transfers between devices  20.5 us (31%)
  Pallas kernels  12.7 us (19%)
  blocking collectives  6.08 us (9%)
  local copies, waits for them, and re-layouts  1 us (2%)
  between operations  0.78 us (1%)
    ppermute x19, starting transfers between devices, _send(): return lax.ppermute(value, AXES, pairs)  23.6 us
    ppermute x19, waiting for transfers between devices, _send(): return lax.ppermute(value, AXES, pairs)  20.5 us
    all_to_all x1, blocking collectives, _fast(): lax.all_to_all(_after(back, send_a, send_z), 'expert', split_axis=0, conc...  6.08 us
    pallas_call x1, Pallas kernels, _fast(): _call(functools.partial(_slot_kernel, n_e, hidden), 'slot_gradients', (_s...  3.55 us
    pallas_call x1, Pallas kernels, _fast(): _call(functools.partial(_lead_kernel, n_e, capacity), 'raw_lead', _shape(...  2.28 us
    pallas_call x1, Pallas kernels, _fast(): _call(functools.partial(_first_kernel, n_e, n_d, blocks_a[1]), 'first_sen...  1.7 us
  transfers between devices with their start and end apart: 19, of which 8 were waited for; matrix products, arithmetic and copies ran while one was open for 2% of the time, Pallas kernels for 16%

profile of v7, /device:TPU:0, one launch (start us, length us, event | category | flops | bytes accessed | tf_op | source)
XLA Modules:
  0.0 65.3 jit_solution(9766340060714460519)
XLA Ops:
  0.6 0.0 copy-start
  0.6 1.1 %pack_tokens.1.refs_0_ = bf16[144,1152]{1,0:T(8,128)(2,1)S(1)} custom-call(s32[2,128]{1,0:T(2,128)} %bitcast.18, bf16[2,128]{1,0:T(2,128)(2,1)} %bitcast.19, bf16[128,2048]{1,0:T(8,128)(2,1)} %tok_ref.1), custom_call_target="tpu_custom_call" | custom-call | tf_op jit(solution)/shard_map/pack_tokens/pallas_call | solution.py:248
  1.8 3.0 %collective-permute-start.1 = (bf16[144,1152]{1,0:T(8,128)(2,1)S(1)}, bf16[144,1152]{1,0:T(8,128)(2,1)S(1)}, u32[]{:S(2)}, u32[]{:S(2)}) collective-permute-start(bf16[144,1152]{1,0:T(8,128)(2,1)S(1)} %pack_tokens.1.refs_0_), channel_id=1, source_target_pairs={{0,2},{1,3},{2,0},{3,1},{4,6},{5,7},{6,4},{7,5},{8,10},{9,11},{10,... | collective-permute-start | bytes 995336 | tf_op jit(solution)/shard_map/ppermute | solution.py:27
  4.8 1.0 %slice.24.refs_0_.refs_4_ = bf16[128,896]{1,0:T(8,128)(2,1)S(1)} slice(bf16[128,2048]{1,0:T(8,128)(2,1)} %tok_ref.1), slice={[0:128], [1152:2048]} | slice | bytes 458752 | tf_op jit(solution)/shard_map/slice | solution.py:261
  5.8 0.1 collective-permute-start
  5.8 6.8 %collective-permute-done.1.refs_2_ = bf16[144,1152]{1,0:T(8,128)(2,1)S(1)} collective-permute-done((bf16[144,1152]{1,0:T(8,128)(2,1)S(1)}, bf16[144,1152]{1,0:T(8,128)(2,1)S(1)}, u32[]{:S(2)}, u32[]{:S(2)}) %collective-permute-start.1) | collective-permute-done | bytes 331808 | tf_op jit(solution)/shard_map/ppermute | solution.py:27
  12.6 0.0 collective-permute-start.2
  12.6 0.0 copy-done
  12.6 0.2 activation.1.act_ref
  12.8 0.1 pad_add_fusion.where_ref
  12.9 1.7 %collective-permute-start.4 = (bf16[128,896]{1,0:T(8,128)(2,1)S(1)}, bf16[128,896]{1,0:T(8,128)(2,1)S(1)}, u32[]{:S(2)}, u32[]{:S(2)}) collective-permute-start(bf16[128,896]{1,0:T(8,128)(2,1)S(1)} %slice.24.refs_0_.refs_4_), channel_id=1, source_target_pairs={{0,2},{1,3},{2,0},{3,1},{4,6},{5,7},{6,4},{7,5},{8,10},{9,11},{10,... | collective-permute-start | bytes 688136 | tf_op jit(solution)/shard_map/ppermute | solution.py:27
  14.7 0.0 collective-permute-done.refs_1_
  14.7 0.0 collective-permute-done.2.refs_3_
  14.7 0.0 copy-start.1
  14.7 1.7 %first_send.1 = (bf16[768,512]{1,0:T(8,128)(2,1)S(1)}, bf16[384,640]{1,0:T(8,128)(2,1)S(1)}) custom-call(s32[2]{0:T(128)S(1)} %pad_add_fusion.where_ref, f32[4,96,768]{2,1,0:T(8,128)S(1)} %activation.1.act_ref, bf16[144,1152]{1,0:T(8,128)(2,1)S(1)} %pack_tokens.1.refs_0_, bf16[144,1152]{1,0:T(8,128)(2,1)S(1)} %collective-permute-done.refs_1_, ...), custom_call_target="tpu_custom_call" | custom-call | tf_op jit(solution)/shard_map/first_send/pallas_call | solution.py:323
  16.4 1.6 %collective-permute-start.6 = (bf16[384,640]{1,0:T(8,128)(2,1)S(1)}, bf16[384,640]{1,0:T(8,128)(2,1)S(1)}, u32[]{:S(2)}, u32[]{:S(2)}) collective-permute-start(bf16[384,640]{1,0:T(8,128)(2,1)S(1)} %get-tuple-element.48), channel_id=1, source_target_pairs={{0,4},{1,5},{2,6},{3,7},{4,0},{5,1},{6,2},{7,3},{8,12},{9,13},{10,... | collective-permute-start | bytes 1474568 | tf_op jit(solution)/shard_map/ppermute | solution.py:27
  17.9 0.9 %first_keep.1 = (f32[384,640]{1,0:T(8,128)S(1)}, f32[384,512]{1,0:T(8,128)S(1)}, bf16[384,512]{1,0:T(8,128)(2,1)S(1)}) custom-call(bf16[768,512]{1,0:T(8,128)(2,1)S(1)} %get-tuple-element.46.at_ref, bf16[144,1152]{1,0:T(8,128)(2,1)S(1)} %pack_tokens.1.refs_0_, bf16[144,1152]{1,0:T(8,128)(2,1)S(1)} %collective-permute-done.refs_1_, ...), custom_call_target="tpu_custom_call" | custom-call | tf_op jit(solution)/shard_map/first_keep/pallas_call | solution.py:333
  18.8 1.6 %collective-permute-start.7 = (bf16[384,512]{1,0:T(8,128)(2,1)S(1)}, bf16[384,512]{1,0:T(8,128)(2,1)S(1)}, u32[]{:S(2)}, u32[]{:S(2)}) collective-permute-start(bf16[384,512]{1,0:T(8,128)(2,1)S(1)} %get-tuple-element.63), channel_id=1, source_target_pairs={{0,8},{1,9},{2,10},{3,11},{4,12},{5,13},{6,14},{7,15},{8,0},{9,1},... | collective-permute-start | bytes 1179656 | tf_op jit(solution)/shard_map/ppermute | solution.py:27
  20.5 0.0 copy-done.1
  20.5 2.3 %raw_lead.1.raw_ref = f32[384,768]{1,0:T(8,128)S(1)} custom-call(s32[2]{0:T(128)S(1)} %pad_add_fusion.where_ref, bf16[1,768,2048]{2,1,0:T(8,128)(2,1)S(1)} %copy-done.1, bf16[144,1152]{1,0:T(8,128)(2,1)S(1)} %pack_tokens.1.refs_0_, bf16[144,1152]{1,0:T(8,128)(2,1)S(1)} %collective-permute-done.refs_1_, bf16[144,1152]{1,0:T(8,128)(2,1)S(1)} %collective-permute-done.1.refs_2_, ...), custom_call_target="tpu_custom_call" | custom-call | flops 6000000000 | tf_op jit(solution)/shard_map/raw_lead/pallas_call | solution.py:344
  22.8 0.0 collective-permute-done.4.refs_2_.refs_6_
  22.8 0.1 collective-permute-start.3
  22.9 0.5 collective-permute-start.5
  23.4 1.0 %collective-permute-done.3.refs_1_.refs_5_ = bf16[128,896]{1,0:T(8,128)(2,1)S(1)} collective-permute-done((bf16[128,896]{1,0:T(8,128)(2,1)S(1)}, bf16[128,896]{1,0:T(8,128)(2,1)S(1)}, u32[]{:S(2)}, u32[]{:S(2)}) %collective-permute-start.3) | collective-permute-done | bytes 229408 | tf_op jit(solution)/shard_map/ppermute | solution.py:27
  24.3 0.3 collective-permute-done.5.refs_3_.refs_7_
  24.7 0.6 partial_chunk.3
  25.2 0.6 partial_chunk.2
  25.8 3.5 %slot_gradients.1 = (bf16[4,96,1536]{2,1,0:T(8,128)(2,1)}, f32[4,1,128]{2,1,0:T(1,128)S(1)}) custom-call(s32[2]{0:T(128)S(1)} %pad_add_fusion.where_ref, bf16[4,96,1536]{2,1,0:T(8,128)(2,1)S(1)} %bitcast.16, bf16[1,768,2048]{2,1,0:T(8,128)(2,1)S(1)} %copy-done.1, f32[384,768]{1,0:T(8,128)S(1)} %raw_lead.1.raw_ref, bf16[144,1152]{1,0:T(8,128)(2,1)S(1)} %pack_tokens.1.refs_0_, ...), custom_call_target="tpu_custom_call" | custom-call | tf_op jit(solution)/shard_map/slot_gradients/pallas_call | solution.py:372
  29.4 0.5 collective-permute-done.7.got_ref
  29.9 0.1 sum_halves.8
  30.0 0.0 collective-permute-done.6.got_ref
  30.0 1.3 %collective-permute-start.8 = (bf16[384,512]{1,0:T(8,128)(2,1)S(1)}, bf16[384,512]{1,0:T(8,128)(2,1)S(1)}, u32[]{:S(2)}, u32[]{:S(2)}) collective-permute-start(bf16[384,512]{1,0:T(8,128)(2,1)S(1)} %get-tuple-element.65), channel_id=1, source_target_pairs={{0,4},{1,5},{2,6},{3,7},{4,0},{5,1},{6,2},{7,3},{8,12},{9,13},{10,... | collective-permute-start | bytes 1179656 | tf_op jit(solution)/shard_map/ppermute | solution.py:27
  31.3 0.1 sum_halves.7
  31.4 1.6 %collective-permute-start.9 = (bf16[192,640]{1,0:T(8,128)(2,1)S(1)}, bf16[192,640]{1,0:T(8,128)(2,1)S(1)}, u32[]{:S(2)}, u32[]{:S(2)}) collective-permute-start(bf16[192,640]{1,0:T(8,128)(2,1)S(1)} %get-tuple-element.68), channel_id=1, source_target_pairs={{0,8},{1,9},{2,10},{3,11},{4,12},{5,13},{6,14},{7,15},{8,0},{9,1},... | collective-permute-start | bytes 737288 | tf_op jit(solution)/shard_map/ppermute | solution.py:27
  33.1 2.6 %collective-permute-start.11 = (bf16[192,512]{1,0:T(8,128)(2,1)S(1)}, bf16[192,512]{1,0:T(8,128)(2,1)S(1)}, u32[]{:S(2)}, u32[]{:S(2)}) collective-permute-start(bf16[192,512]{1,0:T(8,128)(2,1)S(1)} %get-tuple-element.64), channel_id=1, source_target_pairs={{0,16},{1,17},{2,18},{3,19},{4,20},{5,21},{6,22},{7,23},{8,24},{9,... | collective-permute-start | bytes 589832 | tf_op jit(solution)/shard_map/ppermute | solution.py:27
  35.6 6.1 %all_to_all.5 = f32[4,1,128]{2,1,0:T(1,128)S(1)} all-to-all(f32[4,1,128]{2,1,0:T(1,128)S(1)} %get-tuple-element.80), channel_id=1, replica_groups=mesh['dp'=8,'expert'=4] {'expert'}, dimensions={0} | all-to-all | bytes 4096 | tf_op jit(solution)/shard_map/all_to_all | solution.py:387
  41.7 0.0 collective-permute-done.8.got_ref
  41.7 0.8 %collective-permute-start.15 = (bf16[384,384]{1,0:T(8,128)(2,1)S(1)}, bf16[384,384]{1,0:T(8,128)(2,1)S(1)}, u32[]{:S(2)}, u32[]{:S(2)}) collective-permute-start(bf16[384,384]{1,0:T(8,128)(2,1)S(1)} %get-tuple-element.81), channel_id=1, source_target_pairs={{0,4},{1,5},{2,6},{3,7},{4,0},{5,1},{6,2},{7,3},{8,12},{9,13},{10,... | collective-permute-start | bytes 884744 | tf_op jit(solution)/shard_map/ppermute | solution.py:27
  42.5 0.1 sum_halves.9
  42.6 0.9 %collective-permute-start.13 = (bf16[192,512]{1,0:T(8,128)(2,1)S(1)}, bf16[192,512]{1,0:T(8,128)(2,1)S(1)}, u32[]{:S(2)}, u32[]{:S(2)}) collective-permute-start(bf16[192,512]{1,0:T(8,128)(2,1)S(1)} %get-tuple-element.66), channel_id=1, source_target_pairs={{0,8},{1,9},{2,10},{3,11},{4,12},{5,13},{6,14},{7,15},{8,0},{9,1},... | collective-permute-start | bytes 589832 | tf_op jit(solution)/shard_map/ppermute | solution.py:27
  43.4 0.0 collective-permute-done.9.got_ref
  43.4 0.1 sum_halves.10
  43.5 2.6 %collective-permute-start.10 = (bf16[96,640]{1,0:T(8,128)(2,1)S(1)}, bf16[96,640]{1,0:T(8,128)(2,1)S(1)}, u32[]{:S(2)}, u32[]{:S(2)}) collective-permute-start(bf16[96,640]{1,0:T(8,128)(2,1)S(1)} %get-tuple-element.70), channel_id=1, source_target_pairs={{0,16},{1,17},{2,18},{3,19},{4,20},{5,21},{6,22},{7,23},{8,24},{9,... | collective-permute-start | bytes 368648 | tf_op jit(solution)/shard_map/ppermute | solution.py:27
  46.2 0.0 copy-start.2
  46.2 0.0 collective-permute-done.11.got_ref
  46.2 0.1 sum_halves.11
  46.2 0.6 collective-permute-start.12
  46.8 5.1 %collective-permute-done.13.got_ref = bf16[192,512]{1,0:T(8,128)(2,1)S(1)} collective-permute-done((bf16[192,512]{1,0:T(8,128)(2,1)S(1)}, bf16[192,512]{1,0:T(8,128)(2,1)S(1)}, u32[]{:S(2)}, u32[]{:S(2)}) %collective-permute-start.13) | collective-permute-done | bytes 196640 | tf_op jit(solution)/shard_map/ppermute | solution.py:27
  52.0 0.1 collective-permute-start.14
  52.0 0.8 %collective-permute-done.12.refs_3_ = bf16[96,512]{1,0:T(8,128)(2,1)S(1)} collective-permute-done((bf16[96,512]{1,0:T(8,128)(2,1)S(1)}, bf16[96,512]{1,0:T(8,128)(2,1)S(1)}, u32[]{:S(2)}, u32[]{:S(2)}) %collective-permute-start.12) | collective-permute-done | bytes 98336 | tf_op jit(solution)/shard_map/ppermute | solution.py:27
  52.9 0.0 collective-permute-done.10.refs_1_
  52.9 0.0 collective-permute-done.15.got_ref
  52.9 0.1 sum_halves.13
  53.0 1.5 %collective-permute-start.18 = (bf16[96,384]{1,0:T(8,128)(2,1)S(1)}, bf16[96,384]{1,0:T(8,128)(2,1)S(1)}, u32[]{:S(2)}, u32[]{:S(2)}) collective-permute-start(bf16[96,384]{1,0:T(8,128)(2,1)S(1)} %get-tuple-element.84), channel_id=1, source_target_pairs={{0,24},{1,25},{2,26},{3,27},{4,28},{5,29},{6,30},{7,31},{8,16},{9,... | collective-permute-start | bytes 221192 | tf_op jit(solution)/shard_map/ppermute | solution.py:27
  54.4 1.2 %collective-permute-start.17 = (bf16[96,384]{1,0:T(8,128)(2,1)S(1)}, bf16[96,384]{1,0:T(8,128)(2,1)S(1)}, u32[]{:S(2)}, u32[]{:S(2)}) collective-permute-start(bf16[96,384]{1,0:T(8,128)(2,1)S(1)} %get-tuple-element.85), channel_id=1, source_target_pairs={{0,8},{1,9},{2,10},{3,11},{4,12},{5,13},{6,14},{7,15},{8,0},{9,1},... | collective-permute-start | bytes 221192 | tf_op jit(solution)/shard_map/ppermute | solution.py:27
  55.7 1.7 %collective-permute-start.16 = (bf16[96,384]{1,0:T(8,128)(2,1)S(1)}, bf16[96,384]{1,0:T(8,128)(2,1)S(1)}, u32[]{:S(2)}, u32[]{:S(2)}) collective-permute-start(bf16[96,384]{1,0:T(8,128)(2,1)S(1)} %get-tuple-element.86), channel_id=1, source_target_pairs={{0,16},{1,17},{2,18},{3,19},{4,20},{5,21},{6,22},{7,23},{8,24},{9,... | collective-permute-start | bytes 221192 | tf_op jit(solution)/shard_map/ppermute | solution.py:27
  57.4 0.0 copy-done.2
  57.4 0.6 fusion.2
  58.0 4.0 %collective-permute-done.14.refs_5_ = bf16[96,512]{1,0:T(8,128)(2,1)S(1)} collective-permute-done((bf16[96,512]{1,0:T(8,128)(2,1)S(1)}, bf16[96,512]{1,0:T(8,128)(2,1)S(1)}, u32[]{:S(2)}, u32[]{:S(2)}) %collective-permute-start.14) | collective-permute-done | bytes 98336 | tf_op jit(solution)/shard_map/ppermute | solution.py:27
  62.0 0.0 collective-permute-done.18.refs_9_
  62.0 0.0 collective-permute-done.17.refs_8_
  62.0 2.0 %collective-permute-done.16.refs_7_ = bf16[96,384]{1,0:T(8,128)(2,1)S(1)} collective-permute-done((bf16[96,384]{1,0:T(8,128)(2,1)S(1)}, bf16[96,384]{1,0:T(8,128)(2,1)S(1)}, u32[]{:S(2)}, u32[]{:S(2)}) %collective-permute-start.16) | collective-permute-done | bytes 73760 | tf_op jit(solution)/shard_map/ppermute | solution.py:27
  64.0 1.3 %finish.1 = f32[1536,128]{1,0:T(8,128)} custom-call(f32[96,640]{1,0:T(8,128)S(1)} %get-tuple-element.69.refs_0_, bf16[96,640]{1,0:T(8,128)(2,1)S(1)} %collective-permute-done.10.refs_1_, f32[96,512]{1,0:T(8,128)S(1)} %get-tuple-element.73.refs_2_, bf16[96,512]{1,0:T(8,128)(2,1)S(1)} %collective-permute-done.12.refs_3_, ...), custom_call_target="tpu_custom_call" | custom-call | tf_op jit(solution)/shard_map/finish/pallas_call | solution.py:405
  (3 shorter events, 0.1 us)
Async XLA Ops:
  0.6 12.0 %copy-start = (bf16[1,1,4,96,1536]{4,3,2,1,0:T(8,128)(2,1)S(1)}, bf16[1,1,4,96,1536]{4,3,2,1,0:T(8,128)(2,1)}, u32[]{:S(2)}) copy-start(bf16[1,1,4,96,1536]{4,3,2,1,0:T(8,128)(2,1)} %param.9) | copy-start | bytes 3538948
  1.8 10.8 %collective-permute-start.1 = (bf16[144,1152]{1,0:T(8,128)(2,1)S(1)}, bf16[144,1152]{1,0:T(8,128)(2,1)S(1)}, u32[]{:S(2)}, u32[]{:S(2)}) collective-permute-start(bf16[144,1152]{1,0:T(8,128)(2,1)S(1)} %pack_tokens.1.refs_0_), channel_id=1, source_target_pairs={{0,2},{1,3},{2,0},{3,1},{4,6},{5,7},{6,4},{7,5},{8,10},{9,11},{10,... | collective-permute-start | bytes 995336 | tf_op jit(solution)/shard_map/ppermute | solution.py:27
  5.8 8.9 %collective-permute-start = (bf16[144,1152]{1,0:T(8,128)(2,1)S(1)}, bf16[144,1152]{1,0:T(8,128)(2,1)S(1)}, u32[]{:S(2)}, u32[]{:S(2)}) collective-permute-start(bf16[144,1152]{1,0:T(8,128)(2,1)S(1)} %pack_tokens.1.refs_0_), channel_id=1, source_target_pairs={{0,1},{1,0},{2,3},{3,2},{4,5},{5,4},{6,7},{7,6},{8,9},{9,8},{10,11... | collective-permute-start | bytes 995336 | tf_op jit(solution)/shard_map/ppermute | solution.py:27
  12.6 2.1 %collective-permute-start.2 = (bf16[144,1152]{1,0:T(8,128)(2,1)S(1)}, bf16[144,1152]{1,0:T(8,128)(2,1)S(1)}, u32[]{:S(2)}, u32[]{:S(2)}) collective-permute-start(bf16[144,1152]{1,0:T(8,128)(2,1)S(1)} %collective-permute-done.1.refs_2_), channel_id=1, source_target_pairs={{0,1},{1,0},{2,3},{3,2},{4,5},{5,4},{6,7},{7,6},{8,9},{9,8},{10,11... | collective-permute-start | bytes 995336 | tf_op jit(solution)/shard_map/ppermute | solution.py:27
  12.9 9.9 %collective-permute-start.4 = (bf16[128,896]{1,0:T(8,128)(2,1)S(1)}, bf16[128,896]{1,0:T(8,128)(2,1)S(1)}, u32[]{:S(2)}, u32[]{:S(2)}) collective-permute-start(bf16[128,896]{1,0:T(8,128)(2,1)S(1)} %slice.24.refs_0_.refs_4_), channel_id=1, source_target_pairs={{0,2},{1,3},{2,0},{3,1},{4,6},{5,7},{6,4},{7,5},{8,10},{9,11},{10,... | collective-permute-start | bytes 688136 | tf_op jit(solution)/shard_map/ppermute | solution.py:27
  14.7 5.8 %copy-start.1 = (bf16[1,768,2048]{2,1,0:T(8,128)(2,1)S(1)}, bf16[1,768,2048]{2,1,0:T(8,128)(2,1)}, u32[]{:S(2)}) copy-start(bf16[1,768,2048]{2,1,0:T(8,128)(2,1)} %w_ref.3) | copy-start | bytes 9437188
  16.4 13.6 %collective-permute-start.6 = (bf16[384,640]{1,0:T(8,128)(2,1)S(1)}, bf16[384,640]{1,0:T(8,128)(2,1)S(1)}, u32[]{:S(2)}, u32[]{:S(2)}) collective-permute-start(bf16[384,640]{1,0:T(8,128)(2,1)S(1)} %get-tuple-element.48), channel_id=1, source_target_pairs={{0,4},{1,5},{2,6},{3,7},{4,0},{5,1},{6,2},{7,3},{8,12},{9,13},{10,... | collective-permute-start | bytes 1474568 | tf_op jit(solution)/shard_map/ppermute | solution.py:27
  18.8 11.0 %collective-permute-start.7 = (bf16[384,512]{1,0:T(8,128)(2,1)S(1)}, bf16[384,512]{1,0:T(8,128)(2,1)S(1)}, u32[]{:S(2)}, u32[]{:S(2)}) collective-permute-start(bf16[384,512]{1,0:T(8,128)(2,1)S(1)} %get-tuple-element.63), channel_id=1, source_target_pairs={{0,8},{1,9},{2,10},{3,11},{4,12},{5,13},{6,14},{7,15},{8,0},{9,1},... | collective-permute-start | bytes 1179656 | tf_op jit(solution)/shard_map/ppermute | solution.py:27
  22.8 1.6 %collective-permute-start.3 = (bf16[128,896]{1,0:T(8,128)(2,1)S(1)}, bf16[128,896]{1,0:T(8,128)(2,1)S(1)}, u32[]{:S(2)}, u32[]{:S(2)}) collective-permute-start(bf16[128,896]{1,0:T(8,128)(2,1)S(1)} %slice.24.refs_0_.refs_4_), channel_id=1, source_target_pairs={{0,1},{1,0},{2,3},{3,2},{4,5},{5,4},{6,7},{7,6},{8,9},{9,8},{10,11... | collective-permute-start | bytes 688136 | tf_op jit(solution)/shard_map/ppermute | solution.py:27
  22.9 1.8 %collective-permute-start.5 = (bf16[128,896]{1,0:T(8,128)(2,1)S(1)}, bf16[128,896]{1,0:T(8,128)(2,1)S(1)}, u32[]{:S(2)}, u32[]{:S(2)}) collective-permute-start(bf16[128,896]{1,0:T(8,128)(2,1)S(1)} %collective-permute-done.4.refs_2_.refs_6_), channel_id=1, source_target_pairs={{0,1},{1,0},{2,3},{3,2},{4,5},{5,4},{6,7},{7,6},{8,9},{9,8},{10,11... | collective-permute-start | bytes 688136 | tf_op jit(solution)/shard_map/ppermute | solution.py:27
  30.0 11.7 %collective-permute-start.8 = (bf16[384,512]{1,0:T(8,128)(2,1)S(1)}, bf16[384,512]{1,0:T(8,128)(2,1)S(1)}, u32[]{:S(2)}, u32[]{:S(2)}) collective-permute-start(bf16[384,512]{1,0:T(8,128)(2,1)S(1)} %get-tuple-element.65), channel_id=1, source_target_pairs={{0,4},{1,5},{2,6},{3,7},{4,0},{5,1},{6,2},{7,3},{8,12},{9,13},{10,... | collective-permute-start | bytes 1179656 | tf_op jit(solution)/shard_map/ppermute | solution.py:27
  31.4 12.0 %collective-permute-start.9 = (bf16[192,640]{1,0:T(8,128)(2,1)S(1)}, bf16[192,640]{1,0:T(8,128)(2,1)S(1)}, u32[]{:S(2)}, u32[]{:S(2)}) collective-permute-start(bf16[192,640]{1,0:T(8,128)(2,1)S(1)} %get-tuple-element.68), channel_id=1, source_target_pairs={{0,8},{1,9},{2,10},{3,11},{4,12},{5,13},{6,14},{7,15},{8,0},{9,1},... | collective-permute-start | bytes 737288 | tf_op jit(solution)/shard_map/ppermute | solution.py:27
  33.1 13.1 %collective-permute-start.11 = (bf16[192,512]{1,0:T(8,128)(2,1)S(1)}, bf16[192,512]{1,0:T(8,128)(2,1)S(1)}, u32[]{:S(2)}, u32[]{:S(2)}) collective-permute-start(bf16[192,512]{1,0:T(8,128)(2,1)S(1)} %get-tuple-element.64), channel_id=1, source_target_pairs={{0,16},{1,17},{2,18},{3,19},{4,20},{5,21},{6,22},{7,23},{8,24},{9,... | collective-permute-start | bytes 589832 | tf_op jit(solution)/shard_map/ppermute | solution.py:27
  41.7 11.1 %collective-permute-start.15 = (bf16[384,384]{1,0:T(8,128)(2,1)S(1)}, bf16[384,384]{1,0:T(8,128)(2,1)S(1)}, u32[]{:S(2)}, u32[]{:S(2)}) collective-permute-start(bf16[384,384]{1,0:T(8,128)(2,1)S(1)} %get-tuple-element.81), channel_id=1, source_target_pairs={{0,4},{1,5},{2,6},{3,7},{4,0},{5,1},{6,2},{7,3},{8,12},{9,13},{10,... | collective-permute-start | bytes 884744 | tf_op jit(solution)/shard_map/ppermute | solution.py:27
  42.6 9.3 %collective-permute-start.13 = (bf16[192,512]{1,0:T(8,128)(2,1)S(1)}, bf16[192,512]{1,0:T(8,128)(2,1)S(1)}, u32[]{:S(2)}, u32[]{:S(2)}) collective-permute-start(bf16[192,512]{1,0:T(8,128)(2,1)S(1)} %get-tuple-element.66), channel_id=1, source_target_pairs={{0,8},{1,9},{2,10},{3,11},{4,12},{5,13},{6,14},{7,15},{8,0},{9,1},... | collective-permute-start | bytes 589832 | tf_op jit(solution)/shard_map/ppermute | solution.py:27
  43.5 9.4 %collective-permute-start.10 = (bf16[96,640]{1,0:T(8,128)(2,1)S(1)}, bf16[96,640]{1,0:T(8,128)(2,1)S(1)}, u32[]{:S(2)}, u32[]{:S(2)}) collective-permute-start(bf16[96,640]{1,0:T(8,128)(2,1)S(1)} %get-tuple-element.70), channel_id=1, source_target_pairs={{0,16},{1,17},{2,18},{3,19},{4,20},{5,21},{6,22},{7,23},{8,24},{9,... | collective-permute-start | bytes 368648 | tf_op jit(solution)/shard_map/ppermute | solution.py:27
  46.2 11.3 %copy-start.2 = (s32[128,2]{0,1:T(2,128)S(1)}, s32[128,2]{0,1:T(2,128)}, u32[]{:S(2)}) copy-start(s32[128,2]{0,1:T(2,128)} %param.6) | copy-start | bytes 3076
  46.2 6.6 %collective-permute-start.12 = (bf16[96,512]{1,0:T(8,128)(2,1)S(1)}, bf16[96,512]{1,0:T(8,128)(2,1)S(1)}, u32[]{:S(2)}, u32[]{:S(2)}) collective-permute-start(bf16[96,512]{1,0:T(8,128)(2,1)S(1)} %get-tuple-element.74), channel_id=1, source_target_pairs={{0,4},{1,5},{2,6},{3,7},{4,0},{5,1},{6,2},{7,3},{8,12},{9,13},{10,... | collective-permute-start | bytes 294920 | tf_op jit(solution)/shard_map/ppermute | solution.py:27
  52.0 10.0 %collective-permute-start.14 = (bf16[96,512]{1,0:T(8,128)(2,1)S(1)}, bf16[96,512]{1,0:T(8,128)(2,1)S(1)}, u32[]{:S(2)}, u32[]{:S(2)}) collective-permute-start(bf16[96,512]{1,0:T(8,128)(2,1)S(1)} %get-tuple-element.77), channel_id=1, source_target_pairs={{0,16},{1,17},{2,18},{3,19},{4,20},{5,21},{6,22},{7,23},{8,24},{9,... | collective-permute-start | bytes 294920 | tf_op jit(solution)/shard_map/ppermute | solution.py:27
  53.0 9.0 %collective-permute-start.18 = (bf16[96,384]{1,0:T(8,128)(2,1)S(1)}, bf16[96,384]{1,0:T(8,128)(2,1)S(1)}, u32[]{:S(2)}, u32[]{:S(2)}) collective-permute-start(bf16[96,384]{1,0:T(8,128)(2,1)S(1)} %get-tuple-element.84), channel_id=1, source_target_pairs={{0,24},{1,25},{2,26},{3,27},{4,28},{5,29},{6,30},{7,31},{8,16},{9,... | collective-permute-start | bytes 221192 | tf_op jit(solution)/shard_map/ppermute | solution.py:27
  54.4 7.5 %collective-permute-start.17 = (bf16[96,384]{1,0:T(8,128)(2,1)S(1)}, bf16[96,384]{1,0:T(8,128)(2,1)S(1)}, u32[]{:S(2)}, u32[]{:S(2)}) collective-permute-start(bf16[96,384]{1,0:T(8,128)(2,1)S(1)} %get-tuple-element.85), channel_id=1, source_target_pairs={{0,8},{1,9},{2,10},{3,11},{4,12},{5,13},{6,14},{7,15},{8,0},{9,1},... | collective-permute-start | bytes 221192 | tf_op jit(solution)/shard_map/ppermute | solution.py:27
  55.7 8.3 %collective-permute-start.16 = (bf16[96,384]{1,0:T(8,128)(2,1)S(1)}, bf16[96,384]{1,0:T(8,128)(2,1)S(1)}, u32[]{:S(2)}, u32[]{:S(2)}) collective-permute-start(bf16[96,384]{1,0:T(8,128)(2,1)S(1)} %get-tuple-element.86), channel_id=1, source_target_pairs={{0,16},{1,17},{2,18},{3,19},{4,20},{5,21},{6,22},{7,23},{8,24},{9,... | collective-permute-start | bytes 221192 | tf_op jit(solution)/shard_map/ppermute | solution.py:27

commit v8 on v7

--- a/solution.py
+++ b/solution.py
@@ -189,11 +189,14 @@
     next_send_ref[...] = (keep_ref[size:, :] + got_ref[size:, :].astype(F32)).astype(BF16)
 
 
-def _finish_kernel(scale, counts, *refs):
+def _finish_kernel(scale, first_lane, counts, *refs):
     parts, out_ref = refs[:-1], refs[-1]
-    rows = parts[0].shape[0]
+    rows = parts[-1].shape[0]
     lanes = out_ref.shape[0] // rows
-    at = 0
+    if first_lane:
+        out_ref[...] = parts[0][...]
+        parts = parts[1:]
+    at = first_lane
     for count in counts:
         total = parts[0][...]
         for more in parts[1:count]:
@@ -203,6 +206,9 @@
         for j in range(0, total.shape[1], 128):
             out_ref[pl.ds(at, rows, stride=lanes), :] = total[:, j : j + 128]
             at += 1
+    if not first_lane:
+        for at in range(at, lanes):
+            out_ref[pl.ds(at, rows, stride=lanes), :] = jnp.zeros((rows, 128), F32)
 
 
 def _after(value, *others):
@@ -401,15 +407,20 @@
     keep_c, send_c = add(_after(keep_c, send_b, end_a[1], end_z[1]), got_c, at_once[1])
     end_c = [keep_c] + exchange(send_c, keep_c.shape[0], at_once[1])
 
-    ends = (end_a, end_z, end_b, end_c)
-    down_grad = _call(
-        functools.partial(_finish_kernel, 1.0 / n_d, tuple(len(end) for end in ends)),
-        "finish",
-        _shape((rows * lanes, 128), F32),
-        [VM] * sum(len(end) for end in ends),
-        VM,
-        8,
-    )(*[part for end in ends for part in end]).reshape(1, rows * width)
+    def finish(first_lane, laid_out, ends):
+        return _call(
+            functools.partial(
+                _finish_kernel, 1.0 / n_d, first_lane, tuple(len(end) for end in ends)
+            ),
+            "finish",
+            _shape((rows * lanes, 128), F32),
+            [VM] * (len(laid_out) + sum(len(end) for end in ends)),
+            VM,
+            8,
+        )(*laid_out, *[part for end in ends for part in end])
+
+    laid_out = finish(0, [], (end_a, end_z))
+    down_grad = finish(lead // 128, [laid_out], (end_b, end_c)).reshape(1, rows * width)
 
     gate_grad = sum(jnp.where(routes.T == k, returned[k], 0.0) for k in range(n_e)).T
     return pre_grad.reshape(saved_pre.shape), down_grad, gate_grad

time: 65.5 us -> 65.3 us (level)
    pallas_call x1 -> x2, Pallas kernels: 1.31 us -> 1.51 us  [finish(): _call(functools.partial(_finish_kernel, 1.0 / n_d, first_lane, tuple((len...]
  transfers between devices with their start and end apart: 19 -> 19, of which waited for: 8 -> 8; matrix products, arithmetic and copies ran while one was open for 2% -> 3% of each run, Pallas kernels for 16% -> 16%
where the time goes in v8:
time: 65.3 us; the launch traced here: 65.1 us
  starting transfers between devices  23.6 us (36%)
  waiting for transfers between devices  20.1 us (31%)
  Pallas kernels  12.9 us (20%)
  blocking collectives  6.08 us (9%)
  local copies, waits for them, and re-layouts  1 us (2%)
  between operations  0.79 us (1%)
    ppermute x19, starting transfers between devices, _send(): return lax.ppermute(value, AXES, pairs)  23.6 us
    ppermute x19, waiting for transfers between devices, _send(): return lax.ppermute(value, AXES, pairs)  20.1 us
    all_to_all x1, blocking collectives, _fast(): lax.all_to_all(_after(back, send_a, send_z), 'expert', split_axis=0, conc...  6.08 us
    pallas_call x1, Pallas kernels, _fast(): _call(functools.partial(_slot_kernel, n_e, hidden), 'slot_gradients', (_s...  3.55 us
    pallas_call x1, Pallas kernels, _fast(): _call(functools.partial(_lead_kernel, n_e, capacity), 'raw_lead', _shape(...  2.28 us
    pallas_call x1, Pallas kernels, _fast(): _call(functools.partial(_first_kernel, n_e, n_d, blocks_a[1]), 'first_sen...  1.7 us
    pallas_call x2, Pallas kernels, finish(): _call(functools.partial(_finish_kernel, 1.0 / n_d, first_lane, tuple((len...  1.51 us
  transfers between devices with their start and end apart: 19, of which 8 were waited for; matrix products, arithmetic and copies ran while one was open for 3% of the time, Pallas kernels for 16%

profile of v8, /device:TPU:0, one launch (start us, length us, event | category | flops | bytes accessed | tf_op | source)
XLA Modules:
  0.0 65.1 jit_solution(6563536077642564004)
XLA Ops:
  0.6 0.0 copy-start
  0.6 1.1 %pack_tokens.1.refs_0_ = bf16[144,1152]{1,0:T(8,128)(2,1)S(1)} custom-call(s32[2,128]{1,0:T(2,128)} %bitcast.18, bf16[2,128]{1,0:T(2,128)(2,1)} %bitcast.19, bf16[128,2048]{1,0:T(8,128)(2,1)} %tok_ref.1), custom_call_target="tpu_custom_call" | custom-call | tf_op jit(solution)/shard_map/pack_tokens/pallas_call | solution.py:254
  1.8 3.0 %collective-permute-start.1 = (bf16[144,1152]{1,0:T(8,128)(2,1)S(1)}, bf16[144,1152]{1,0:T(8,128)(2,1)S(1)}, u32[]{:S(2)}, u32[]{:S(2)}) collective-permute-start(bf16[144,1152]{1,0:T(8,128)(2,1)S(1)} %pack_tokens.1.refs_0_), channel_id=1, source_target_pairs={{0,2},{1,3},{2,0},{3,1},{4,6},{5,7},{6,4},{7,5},{8,10},{9,11},{10,... | collective-permute-start | bytes 995336 | tf_op jit(solution)/shard_map/ppermute | solution.py:27
  4.8 1.0 %slice.24.refs_0_.refs_4_ = bf16[128,896]{1,0:T(8,128)(2,1)S(1)} slice(bf16[128,2048]{1,0:T(8,128)(2,1)} %tok_ref.1), slice={[0:128], [1152:2048]} | slice | bytes 458752 | tf_op jit(solution)/shard_map/slice | solution.py:267
  5.8 0.1 collective-permute-start
  5.8 6.8 %collective-permute-done.1.refs_2_ = bf16[144,1152]{1,0:T(8,128)(2,1)S(1)} collective-permute-done((bf16[144,1152]{1,0:T(8,128)(2,1)S(1)}, bf16[144,1152]{1,0:T(8,128)(2,1)S(1)}, u32[]{:S(2)}, u32[]{:S(2)}) %collective-permute-start.1) | collective-permute-done | bytes 331808 | tf_op jit(solution)/shard_map/ppermute | solution.py:27
  12.6 0.0 collective-permute-start.2
  12.6 0.0 copy-done
  12.6 0.2 activation.1.act_ref
  12.8 0.1 pad_add_fusion.where_ref
  12.9 1.7 %collective-permute-start.4 = (bf16[128,896]{1,0:T(8,128)(2,1)S(1)}, bf16[128,896]{1,0:T(8,128)(2,1)S(1)}, u32[]{:S(2)}, u32[]{:S(2)}) collective-permute-start(bf16[128,896]{1,0:T(8,128)(2,1)S(1)} %slice.24.refs_0_.refs_4_), channel_id=1, source_target_pairs={{0,2},{1,3},{2,0},{3,1},{4,6},{5,7},{6,4},{7,5},{8,10},{9,11},{10,... | collective-permute-start | bytes 688136 | tf_op jit(solution)/shard_map/ppermute | solution.py:27
  14.7 0.0 collective-permute-done.refs_1_
  14.7 0.0 collective-permute-done.2.refs_3_
  14.7 0.0 copy-start.1
  14.7 1.7 %first_send.1 = (bf16[768,512]{1,0:T(8,128)(2,1)S(1)}, bf16[384,640]{1,0:T(8,128)(2,1)S(1)}) custom-call(s32[2]{0:T(128)S(1)} %pad_add_fusion.where_ref, f32[4,96,768]{2,1,0:T(8,128)S(1)} %activation.1.act_ref, bf16[144,1152]{1,0:T(8,128)(2,1)S(1)} %pack_tokens.1.refs_0_, bf16[144,1152]{1,0:T(8,128)(2,1)S(1)} %collective-permute-done.refs_1_, ...), custom_call_target="tpu_custom_call" | custom-call | tf_op jit(solution)/shard_map/first_send/pallas_call | solution.py:329
  16.4 1.6 %collective-permute-start.6 = (bf16[384,640]{1,0:T(8,128)(2,1)S(1)}, bf16[384,640]{1,0:T(8,128)(2,1)S(1)}, u32[]{:S(2)}, u32[]{:S(2)}) collective-permute-start(bf16[384,640]{1,0:T(8,128)(2,1)S(1)} %get-tuple-element.48), channel_id=1, source_target_pairs={{0,4},{1,5},{2,6},{3,7},{4,0},{5,1},{6,2},{7,3},{8,12},{9,13},{10,... | collective-permute-start | bytes 1474568 | tf_op jit(solution)/shard_map/ppermute | solution.py:27
  17.9 0.9 %first_keep.1 = (f32[384,640]{1,0:T(8,128)S(1)}, f32[384,512]{1,0:T(8,128)S(1)}, bf16[384,512]{1,0:T(8,128)(2,1)S(1)}) custom-call(bf16[768,512]{1,0:T(8,128)(2,1)S(1)} %get-tuple-element.46.at_ref, bf16[144,1152]{1,0:T(8,128)(2,1)S(1)} %pack_tokens.1.refs_0_, bf16[144,1152]{1,0:T(8,128)(2,1)S(1)} %collective-permute-done.refs_1_, ...), custom_call_target="tpu_custom_call" | custom-call | tf_op jit(solution)/shard_map/first_keep/pallas_call | solution.py:339
  18.8 1.6 %collective-permute-start.7 = (bf16[384,512]{1,0:T(8,128)(2,1)S(1)}, bf16[384,512]{1,0:T(8,128)(2,1)S(1)}, u32[]{:S(2)}, u32[]{:S(2)}) collective-permute-start(bf16[384,512]{1,0:T(8,128)(2,1)S(1)} %get-tuple-element.63), channel_id=1, source_target_pairs={{0,8},{1,9},{2,10},{3,11},{4,12},{5,13},{6,14},{7,15},{8,0},{9,1},... | collective-permute-start | bytes 1179656 | tf_op jit(solution)/shard_map/ppermute | solution.py:27
  20.5 0.0 copy-done.1
  20.5 2.3 %raw_lead.1.raw_ref = f32[384,768]{1,0:T(8,128)S(1)} custom-call(s32[2]{0:T(128)S(1)} %pad_add_fusion.where_ref, bf16[1,768,2048]{2,1,0:T(8,128)(2,1)S(1)} %copy-done.1, bf16[144,1152]{1,0:T(8,128)(2,1)S(1)} %pack_tokens.1.refs_0_, bf16[144,1152]{1,0:T(8,128)(2,1)S(1)} %collective-permute-done.refs_1_, bf16[144,1152]{1,0:T(8,128)(2,1)S(1)} %collective-permute-done.1.refs_2_, ...), custom_call_target="tpu_custom_call" | custom-call | flops 6000000000 | tf_op jit(solution)/shard_map/raw_lead/pallas_call | solution.py:350
  22.8 0.0 collective-permute-done.4.refs_2_.refs_6_
  22.8 0.1 collective-permute-start.3
  22.9 0.5 collective-permute-start.5
  23.4 1.0 %collective-permute-done.3.refs_1_.refs_5_ = bf16[128,896]{1,0:T(8,128)(2,1)S(1)} collective-permute-done((bf16[128,896]{1,0:T(8,128)(2,1)S(1)}, bf16[128,896]{1,0:T(8,128)(2,1)S(1)}, u32[]{:S(2)}, u32[]{:S(2)}) %collective-permute-start.3) | collective-permute-done | bytes 229408 | tf_op jit(solution)/shard_map/ppermute | solution.py:27
  24.3 0.3 collective-permute-done.5.refs_3_.refs_7_
  24.7 0.6 partial_chunk.3
  25.2 0.6 partial_chunk.2
  25.8 3.5 %slot_gradients.1 = (bf16[4,96,1536]{2,1,0:T(8,128)(2,1)}, f32[4,1,128]{2,1,0:T(1,128)S(1)}) custom-call(s32[2]{0:T(128)S(1)} %pad_add_fusion.where_ref, bf16[4,96,1536]{2,1,0:T(8,128)(2,1)S(1)} %bitcast.16, bf16[1,768,2048]{2,1,0:T(8,128)(2,1)S(1)} %copy-done.1, f32[384,768]{1,0:T(8,128)S(1)} %raw_lead.1.raw_ref, bf16[144,1152]{1,0:T(8,128)(2,1)S(1)} %pack_tokens.1.refs_0_, ...), custom_call_target="tpu_custom_call" | custom-call | tf_op jit(solution)/shard_map/slot_gradients/pallas_call | solution.py:378
  29.4 0.5 collective-permute-done.7.got_ref
  29.9 0.1 sum_halves.8
  30.0 0.0 collective-permute-done.6.got_ref
  30.0 1.3 %collective-permute-start.8 = (bf16[384,512]{1,0:T(8,128)(2,1)S(1)}, bf16[384,512]{1,0:T(8,128)(2,1)S(1)}, u32[]{:S(2)}, u32[]{:S(2)}) collective-permute-start(bf16[384,512]{1,0:T(8,128)(2,1)S(1)} %get-tuple-element.65), channel_id=1, source_target_pairs={{0,4},{1,5},{2,6},{3,7},{4,0},{5,1},{6,2},{7,3},{8,12},{9,13},{10,... | collective-permute-start | bytes 1179656 | tf_op jit(solution)/shard_map/ppermute | solution.py:27
  31.3 0.1 sum_halves.7
  31.4 1.6 %collective-permute-start.9 = (bf16[192,640]{1,0:T(8,128)(2,1)S(1)}, bf16[192,640]{1,0:T(8,128)(2,1)S(1)}, u32[]{:S(2)}, u32[]{:S(2)}) collective-permute-start(bf16[192,640]{1,0:T(8,128)(2,1)S(1)} %get-tuple-element.68), channel_id=1, source_target_pairs={{0,8},{1,9},{2,10},{3,11},{4,12},{5,13},{6,14},{7,15},{8,0},{9,1},... | collective-permute-start | bytes 737288 | tf_op jit(solution)/shard_map/ppermute | solution.py:27
  33.1 2.6 %collective-permute-start.11 = (bf16[192,512]{1,0:T(8,128)(2,1)S(1)}, bf16[192,512]{1,0:T(8,128)(2,1)S(1)}, u32[]{:S(2)}, u32[]{:S(2)}) collective-permute-start(bf16[192,512]{1,0:T(8,128)(2,1)S(1)} %get-tuple-element.64), channel_id=1, source_target_pairs={{0,16},{1,17},{2,18},{3,19},{4,20},{5,21},{6,22},{7,23},{8,24},{9,... | collective-permute-start | bytes 589832 | tf_op jit(solution)/shard_map/ppermute | solution.py:27
  35.6 6.1 %all_to_all.5 = f32[4,1,128]{2,1,0:T(1,128)S(1)} all-to-all(f32[4,1,128]{2,1,0:T(1,128)S(1)} %get-tuple-element.80), channel_id=1, replica_groups=mesh['dp'=8,'expert'=4] {'expert'}, dimensions={0} | all-to-all | bytes 4096 | tf_op jit(solution)/shard_map/all_to_all | solution.py:393
  41.7 0.0 collective-permute-done.8.got_ref
  41.7 0.8 %collective-permute-start.15 = (bf16[384,384]{1,0:T(8,128)(2,1)S(1)}, bf16[384,384]{1,0:T(8,128)(2,1)S(1)}, u32[]{:S(2)}, u32[]{:S(2)}) collective-permute-start(bf16[384,384]{1,0:T(8,128)(2,1)S(1)} %get-tuple-element.81), channel_id=1, source_target_pairs={{0,4},{1,5},{2,6},{3,7},{4,0},{5,1},{6,2},{7,3},{8,12},{9,13},{10,... | collective-permute-start | bytes 884744 | tf_op jit(solution)/shard_map/ppermute | solution.py:27
  42.5 0.1 sum_halves.9
  42.6 0.9 %collective-permute-start.13 = (bf16[192,512]{1,0:T(8,128)(2,1)S(1)}, bf16[192,512]{1,0:T(8,128)(2,1)S(1)}, u32[]{:S(2)}, u32[]{:S(2)}) collective-permute-start(bf16[192,512]{1,0:T(8,128)(2,1)S(1)} %get-tuple-element.66), channel_id=1, source_target_pairs={{0,8},{1,9},{2,10},{3,11},{4,12},{5,13},{6,14},{7,15},{8,0},{9,1},... | collective-permute-start | bytes 589832 | tf_op jit(solution)/shard_map/ppermute | solution.py:27
  43.4 0.0 collective-permute-done.9.got_ref
  43.5 2.6 %collective-permute-start.10 = (bf16[96,640]{1,0:T(8,128)(2,1)S(1)}, bf16[96,640]{1,0:T(8,128)(2,1)S(1)}, u32[]{:S(2)}, u32[]{:S(2)}) collective-permute-start(bf16[96,640]{1,0:T(8,128)(2,1)S(1)} %get-tuple-element.70), channel_id=1, source_target_pairs={{0,16},{1,17},{2,18},{3,19},{4,20},{5,21},{6,22},{7,23},{8,24},{9,... | collective-permute-start | bytes 368648 | tf_op jit(solution)/shard_map/ppermute | solution.py:27
  46.1 0.0 copy-start.2
  46.1 0.0 collective-permute-done.11.got_ref
  46.1 0.1 sum_halves.11
  46.2 0.6 collective-permute-start.12
  46.8 5.1 %collective-permute-done.13.got_ref = bf16[192,512]{1,0:T(8,128)(2,1)S(1)} collective-permute-done((bf16[192,512]{1,0:T(8,128)(2,1)S(1)}, bf16[192,512]{1,0:T(8,128)(2,1)S(1)}, u32[]{:S(2)}, u32[]{:S(2)}) %collective-permute-start.13) | collective-permute-done | bytes 196640 | tf_op jit(solution)/shard_map/ppermute | solution.py:27
  52.0 0.1 collective-permute-start.14
  52.0 0.8 %collective-permute-done.12.refs_3_ = bf16[96,512]{1,0:T(8,128)(2,1)S(1)} collective-permute-done((bf16[96,512]{1,0:T(8,128)(2,1)S(1)}, bf16[96,512]{1,0:T(8,128)(2,1)S(1)}, u32[]{:S(2)}, u32[]{:S(2)}) %collective-permute-start.12) | collective-permute-done | bytes 98336 | tf_op jit(solution)/shard_map/ppermute | solution.py:27
  52.9 0.0 collective-permute-done.10.refs_1_
  52.9 0.0 collective-permute-done.15.got_ref
  52.9 0.1 sum_halves.13
  53.0 1.5 %collective-permute-start.18 = (bf16[96,384]{1,0:T(8,128)(2,1)S(1)}, bf16[96,384]{1,0:T(8,128)(2,1)S(1)}, u32[]{:S(2)}, u32[]{:S(2)}) collective-permute-start(bf16[96,384]{1,0:T(8,128)(2,1)S(1)} %get-tuple-element.84), channel_id=1, source_target_pairs={{0,24},{1,25},{2,26},{3,27},{4,28},{5,29},{6,30},{7,31},{8,16},{9,... | collective-permute-start | bytes 221192 | tf_op jit(solution)/shard_map/ppermute | solution.py:27
  54.4 1.3 %collective-permute-start.17 = (bf16[96,384]{1,0:T(8,128)(2,1)S(1)}, bf16[96,384]{1,0:T(8,128)(2,1)S(1)}, u32[]{:S(2)}, u32[]{:S(2)}) collective-permute-start(bf16[96,384]{1,0:T(8,128)(2,1)S(1)} %get-tuple-element.85), channel_id=1, source_target_pairs={{0,8},{1,9},{2,10},{3,11},{4,12},{5,13},{6,14},{7,15},{8,0},{9,1},... | collective-permute-start | bytes 221192 | tf_op jit(solution)/shard_map/ppermute | solution.py:27
  55.7 1.7 %collective-permute-start.16 = (bf16[96,384]{1,0:T(8,128)(2,1)S(1)}, bf16[96,384]{1,0:T(8,128)(2,1)S(1)}, u32[]{:S(2)}, u32[]{:S(2)}) collective-permute-start(bf16[96,384]{1,0:T(8,128)(2,1)S(1)} %get-tuple-element.86), channel_id=1, source_target_pairs={{0,16},{1,17},{2,18},{3,19},{4,20},{5,21},{6,22},{7,23},{8,24},{9,... | collective-permute-start | bytes 221192 | tf_op jit(solution)/shard_map/ppermute | solution.py:27
  57.4 0.0 copy-done.2
  57.4 0.6 fusion.2
  58.0 0.4 finish.2.refs_0_
  58.4 3.6 %collective-permute-done.14.refs_2_ = bf16[96,512]{1,0:T(8,128)(2,1)S(1)} collective-permute-done((bf16[96,512]{1,0:T(8,128)(2,1)S(1)}, bf16[96,512]{1,0:T(8,128)(2,1)S(1)}, u32[]{:S(2)}, u32[]{:S(2)}) %collective-permute-start.14) | collective-permute-done | bytes 98336 | tf_op jit(solution)/shard_map/ppermute | solution.py:27
  62.0 0.0 collective-permute-done.18.refs_6_
  62.0 0.0 collective-permute-done.17.refs_5_
  62.0 2.0 %collective-permute-done.16.refs_4_ = bf16[96,384]{1,0:T(8,128)(2,1)S(1)} collective-permute-done((bf16[96,384]{1,0:T(8,128)(2,1)S(1)}, bf16[96,384]{1,0:T(8,128)(2,1)S(1)}, u32[]{:S(2)}, u32[]{:S(2)}) %collective-permute-start.16) | collective-permute-done | bytes 73760 | tf_op jit(solution)/shard_map/ppermute | solution.py:27
  64.0 1.1 %finish.3 = f32[1536,128]{1,0:T(8,128)} custom-call(f32[1536,128]{1,0:T(8,128)S(1)} %finish.2.refs_0_, f32[96,512]{1,0:T(8,128)S(1)} %get-tuple-element.76.refs_1_, bf16[96,512]{1,0:T(8,128)(2,1)S(1)} %collective-permute-done.14.refs_2_, f32[96,384]{1,0:T(8,128)S(1)} %get-tuple-element.82.refs_3_, bf16[96,384]{1,0:T(8,128)(2,1)S(1)} %collective-permute-done.16.refs_4_, ...), custom_call_target="tpu_custom_call" | custom-call | tf_op jit(solution)/shard_map/finish/pallas_call | solution.py:411
  (4 shorter events, 0.1 us)
Async XLA Ops:
  0.6 12.0 %copy-start = (bf16[1,1,4,96,1536]{4,3,2,1,0:T(8,128)(2,1)S(1)}, bf16[1,1,4,96,1536]{4,3,2,1,0:T(8,128)(2,1)}, u32[]{:S(2)}) copy-start(bf16[1,1,4,96,1536]{4,3,2,1,0:T(8,128)(2,1)} %param.9) | copy-start | bytes 3538948
  1.8 10.8 %collective-permute-start.1 = (bf16[144,1152]{1,0:T(8,128)(2,1)S(1)}, bf16[144,1152]{1,0:T(8,128)(2,1)S(1)}, u32[]{:S(2)}, u32[]{:S(2)}) collective-permute-start(bf16[144,1152]{1,0:T(8,128)(2,1)S(1)} %pack_tokens.1.refs_0_), channel_id=1, source_target_pairs={{0,2},{1,3},{2,0},{3,1},{4,6},{5,7},{6,4},{7,5},{8,10},{9,11},{10,... | collective-permute-start | bytes 995336 | tf_op jit(solution)/shard_map/ppermute | solution.py:27
  5.8 8.9 %collective-permute-start = (bf16[144,1152]{1,0:T(8,128)(2,1)S(1)}, bf16[144,1152]{1,0:T(8,128)(2,1)S(1)}, u32[]{:S(2)}, u32[]{:S(2)}) collective-permute-start(bf16[144,1152]{1,0:T(8,128)(2,1)S(1)} %pack_tokens.1.refs_0_), channel_id=1, source_target_pairs={{0,1},{1,0},{2,3},{3,2},{4,5},{5,4},{6,7},{7,6},{8,9},{9,8},{10,11... | collective-permute-start | bytes 995336 | tf_op jit(solution)/shard_map/ppermute | solution.py:27
  12.6 2.1 %collective-permute-start.2 = (bf16[144,1152]{1,0:T(8,128)(2,1)S(1)}, bf16[144,1152]{1,0:T(8,128)(2,1)S(1)}, u32[]{:S(2)}, u32[]{:S(2)}) collective-permute-start(bf16[144,1152]{1,0:T(8,128)(2,1)S(1)} %collective-permute-done.1.refs_2_), channel_id=1, source_target_pairs={{0,1},{1,0},{2,3},{3,2},{4,5},{5,4},{6,7},{7,6},{8,9},{9,8},{10,11... | collective-permute-start | bytes 995336 | tf_op jit(solution)/shard_map/ppermute | solution.py:27
  12.9 9.9 %collective-permute-start.4 = (bf16[128,896]{1,0:T(8,128)(2,1)S(1)}, bf16[128,896]{1,0:T(8,128)(2,1)S(1)}, u32[]{:S(2)}, u32[]{:S(2)}) collective-permute-start(bf16[128,896]{1,0:T(8,128)(2,1)S(1)} %slice.24.refs_0_.refs_4_), channel_id=1, source_target_pairs={{0,2},{1,3},{2,0},{3,1},{4,6},{5,7},{6,4},{7,5},{8,10},{9,11},{10,... | collective-permute-start | bytes 688136 | tf_op jit(solution)/shard_map/ppermute | solution.py:27
  14.7 5.8 %copy-start.1 = (bf16[1,768,2048]{2,1,0:T(8,128)(2,1)S(1)}, bf16[1,768,2048]{2,1,0:T(8,128)(2,1)}, u32[]{:S(2)}) copy-start(bf16[1,768,2048]{2,1,0:T(8,128)(2,1)} %w_ref.3) | copy-start | bytes 9437188
  16.4 13.6 %collective-permute-start.6 = (bf16[384,640]{1,0:T(8,128)(2,1)S(1)}, bf16[384,640]{1,0:T(8,128)(2,1)S(1)}, u32[]{:S(2)}, u32[]{:S(2)}) collective-permute-start(bf16[384,640]{1,0:T(8,128)(2,1)S(1)} %get-tuple-element.48), channel_id=1, source_target_pairs={{0,4},{1,5},{2,6},{3,7},{4,0},{5,1},{6,2},{7,3},{8,12},{9,13},{10,... | collective-permute-start | bytes 1474568 | tf_op jit(solution)/shard_map/ppermute | solution.py:27
  18.8 11.0 %collective-permute-start.7 = (bf16[384,512]{1,0:T(8,128)(2,1)S(1)}, bf16[384,512]{1,0:T(8,128)(2,1)S(1)}, u32[]{:S(2)}, u32[]{:S(2)}) collective-permute-start(bf16[384,512]{1,0:T(8,128)(2,1)S(1)} %get-tuple-element.63), channel_id=1, source_target_pairs={{0,8},{1,9},{2,10},{3,11},{4,12},{5,13},{6,14},{7,15},{8,0},{9,1},... | collective-permute-start | bytes 1179656 | tf_op jit(solution)/shard_map/ppermute | solution.py:27
  22.8 1.6 %collective-permute-start.3 = (bf16[128,896]{1,0:T(8,128)(2,1)S(1)}, bf16[128,896]{1,0:T(8,128)(2,1)S(1)}, u32[]{:S(2)}, u32[]{:S(2)}) collective-permute-start(bf16[128,896]{1,0:T(8,128)(2,1)S(1)} %slice.24.refs_0_.refs_4_), channel_id=1, source_target_pairs={{0,1},{1,0},{2,3},{3,2},{4,5},{5,4},{6,7},{7,6},{8,9},{9,8},{10,11... | collective-permute-start | bytes 688136 | tf_op jit(solution)/shard_map/ppermute | solution.py:27
  22.9 1.8 %collective-permute-start.5 = (bf16[128,896]{1,0:T(8,128)(2,1)S(1)}, bf16[128,896]{1,0:T(8,128)(2,1)S(1)}, u32[]{:S(2)}, u32[]{:S(2)}) collective-permute-start(bf16[128,896]{1,0:T(8,128)(2,1)S(1)} %collective-permute-done.4.refs_2_.refs_6_), channel_id=1, source_target_pairs={{0,1},{1,0},{2,3},{3,2},{4,5},{5,4},{6,7},{7,6},{8,9},{9,8},{10,11... | collective-permute-start | bytes 688136 | tf_op jit(solution)/shard_map/ppermute | solution.py:27
  30.0 11.7 %collective-permute-start.8 = (bf16[384,512]{1,0:T(8,128)(2,1)S(1)}, bf16[384,512]{1,0:T(8,128)(2,1)S(1)}, u32[]{:S(2)}, u32[]{:S(2)}) collective-permute-start(bf16[384,512]{1,0:T(8,128)(2,1)S(1)} %get-tuple-element.65), channel_id=1, source_target_pairs={{0,4},{1,5},{2,6},{3,7},{4,0},{5,1},{6,2},{7,3},{8,12},{9,13},{10,... | collective-permute-start | bytes 1179656 | tf_op jit(solution)/shard_map/ppermute | solution.py:27
  31.4 12.0 %collective-permute-start.9 = (bf16[192,640]{1,0:T(8,128)(2,1)S(1)}, bf16[192,640]{1,0:T(8,128)(2,1)S(1)}, u32[]{:S(2)}, u32[]{:S(2)}) collective-permute-start(bf16[192,640]{1,0:T(8,128)(2,1)S(1)} %get-tuple-element.68), channel_id=1, source_target_pairs={{0,8},{1,9},{2,10},{3,11},{4,12},{5,13},{6,14},{7,15},{8,0},{9,1},... | collective-permute-start | bytes 737288 | tf_op jit(solution)/shard_map/ppermute | solution.py:27
  33.1 13.1 %collective-permute-start.11 = (bf16[192,512]{1,0:T(8,128)(2,1)S(1)}, bf16[192,512]{1,0:T(8,128)(2,1)S(1)}, u32[]{:S(2)}, u32[]{:S(2)}) collective-permute-start(bf16[192,512]{1,0:T(8,128)(2,1)S(1)} %get-tuple-element.64), channel_id=1, source_target_pairs={{0,16},{1,17},{2,18},{3,19},{4,20},{5,21},{6,22},{7,23},{8,24},{9,... | collective-permute-start | bytes 589832 | tf_op jit(solution)/shard_map/ppermute | solution.py:27
  41.7 11.1 %collective-permute-start.15 = (bf16[384,384]{1,0:T(8,128)(2,1)S(1)}, bf16[384,384]{1,0:T(8,128)(2,1)S(1)}, u32[]{:S(2)}, u32[]{:S(2)}) collective-permute-start(bf16[384,384]{1,0:T(8,128)(2,1)S(1)} %get-tuple-element.81), channel_id=1, source_target_pairs={{0,4},{1,5},{2,6},{3,7},{4,0},{5,1},{6,2},{7,3},{8,12},{9,13},{10,... | collective-permute-start | bytes 884744 | tf_op jit(solution)/shard_map/ppermute | solution.py:27
  42.6 9.3 %collective-permute-start.13 = (bf16[192,512]{1,0:T(8,128)(2,1)S(1)}, bf16[192,512]{1,0:T(8,128)(2,1)S(1)}, u32[]{:S(2)}, u32[]{:S(2)}) collective-permute-start(bf16[192,512]{1,0:T(8,128)(2,1)S(1)} %get-tuple-element.66), channel_id=1, source_target_pairs={{0,8},{1,9},{2,10},{3,11},{4,12},{5,13},{6,14},{7,15},{8,0},{9,1},... | collective-permute-start | bytes 589832 | tf_op jit(solution)/shard_map/ppermute | solution.py:27
  43.5 9.4 %collective-permute-start.10 = (bf16[96,640]{1,0:T(8,128)(2,1)S(1)}, bf16[96,640]{1,0:T(8,128)(2,1)S(1)}, u32[]{:S(2)}, u32[]{:S(2)}) collective-permute-start(bf16[96,640]{1,0:T(8,128)(2,1)S(1)} %get-tuple-element.70), channel_id=1, source_target_pairs={{0,16},{1,17},{2,18},{3,19},{4,20},{5,21},{6,22},{7,23},{8,24},{9,... | collective-permute-start | bytes 368648 | tf_op jit(solution)/shard_map/ppermute | solution.py:27
  46.1 11.3 %copy-start.2 = (s32[128,2]{0,1:T(2,128)S(1)}, s32[128,2]{0,1:T(2,128)}, u32[]{:S(2)}) copy-start(s32[128,2]{0,1:T(2,128)} %param.6) | copy-start | bytes 3076
  46.2 6.7 %collective-permute-start.12 = (bf16[96,512]{1,0:T(8,128)(2,1)S(1)}, bf16[96,512]{1,0:T(8,128)(2,1)S(1)}, u32[]{:S(2)}, u32[]{:S(2)}) collective-permute-start(bf16[96,512]{1,0:T(8,128)(2,1)S(1)} %get-tuple-element.74), channel_id=1, source_target_pairs={{0,4},{1,5},{2,6},{3,7},{4,0},{5,1},{6,2},{7,3},{8,12},{9,13},{10,... | collective-permute-start | bytes 294920 | tf_op jit(solution)/shard_map/ppermute | solution.py:27
  52.0 10.0 %collective-permute-start.14 = (bf16[96,512]{1,0:T(8,128)(2,1)S(1)}, bf16[96,512]{1,0:T(8,128)(2,1)S(1)}, u32[]{:S(2)}, u32[]{:S(2)}) collective-permute-start(bf16[96,512]{1,0:T(8,128)(2,1)S(1)} %get-tuple-element.77), channel_id=1, source_target_pairs={{0,16},{1,17},{2,18},{3,19},{4,20},{5,21},{6,22},{7,23},{8,24},{9,... | collective-permute-start | bytes 294920 | tf_op jit(solution)/shard_map/ppermute | solution.py:27
  53.0 9.0 %collective-permute-start.18 = (bf16[96,384]{1,0:T(8,128)(2,1)S(1)}, bf16[96,384]{1,0:T(8,128)(2,1)S(1)}, u32[]{:S(2)}, u32[]{:S(2)}) collective-permute-start(bf16[96,384]{1,0:T(8,128)(2,1)S(1)} %get-tuple-element.84), channel_id=1, source_target_pairs={{0,24},{1,25},{2,26},{3,27},{4,28},{5,29},{6,30},{7,31},{8,16},{9,... | collective-permute-start | bytes 221192 | tf_op jit(solution)/shard_map/ppermute | solution.py:27
  54.4 7.5 %collective-permute-start.17 = (bf16[96,384]{1,0:T(8,128)(2,1)S(1)}, bf16[96,384]{1,0:T(8,128)(2,1)S(1)}, u32[]{:S(2)}, u32[]{:S(2)}) collective-permute-start(bf16[96,384]{1,0:T(8,128)(2,1)S(1)} %get-tuple-element.85), channel_id=1, source_target_pairs={{0,8},{1,9},{2,10},{3,11},{4,12},{5,13},{6,14},{7,15},{8,0},{9,1},... | collective-permute-start | bytes 221192 | tf_op jit(solution)/shard_map/ppermute | solution.py:27
  55.7 8.3 %collective-permute-start.16 = (bf16[96,384]{1,0:T(8,128)(2,1)S(1)}, bf16[96,384]{1,0:T(8,128)(2,1)S(1)}, u32[]{:S(2)}, u32[]{:S(2)}) collective-permute-start(bf16[96,384]{1,0:T(8,128)(2,1)S(1)} %get-tuple-element.86), channel_id=1, source_target_pairs={{0,16},{1,17},{2,18},{3,19},{4,20},{5,21},{6,22},{7,23},{8,24},{9,... | collective-permute-start | bytes 221192 | tf_op jit(solution)/shard_map/ppermute | solution.py:27

commit v9 on v8

--- a/solution.py
+++ b/solution.py
@@ -391,7 +391,7 @@
     keep_a, send_a = add(_after(keep_a, back), got_a, by_x[1])
     got_a = exchange(send_a, keep_a.shape[0], by_x[1])
     returned = lax.all_to_all(
-        _after(back, send_a, send_z), "expert", split_axis=0, concat_axis=0, tiled=True
+        back, "expert", split_axis=0, concat_axis=0, tiled=True
     )
 
     got_c = exchange(_after(send_c, returned, *got_b), keep_c.shape[0], at_once[0])

time: 65.3 us -> 64.6 us (0.989)
  waiting for transfers between devices: 20.1 us -> 19.4 us
    ppermute x19, waiting for transfers between devices: 20.1 us -> 19.4 us  [_send(): return lax.ppermute(value, AXES, pairs)]
  transfers between devices with their start and end apart: 19 -> 19, of which waited for: 8 -> 8; matrix products, arithmetic and copies ran while one was open for 3% -> 3% of each run, Pallas kernels for 16% -> 17%
where the time goes in v9:
time: 64.6 us; the launch traced here: 64.4 us
  starting transfers between devices  23.6 us (37%)
  waiting for transfers between devices  19.4 us (30%)
  Pallas kernels  12.9 us (20%)
  blocking collectives  6.08 us (9%)
  local copies, waits for them, and re-layouts  1 us (2%)
  between operations  0.79 us (1%)
  other arithmetic  0.65 us (1%)
    ppermute x19, starting transfers between devices, _send(): return lax.ppermute(value, AXES, pairs)  23.6 us
    ppermute x19, waiting for transfers between devices, _send(): return lax.ppermute(value, AXES, pairs)  19.4 us
    all_to_all x1, blocking collectives, _fast(): lax.all_to_all(back, 'expert', split_axis=0, concat_axis=0, tiled=True)  6.08 us
    pallas_call x1, Pallas kernels, _fast(): _call(functools.partial(_slot_kernel, n_e, hidden), 'slot_gradients', (_s...  3.54 us
    pallas_call x1, Pallas kernels, _fast(): _call(functools.partial(_lead_kernel, n_e, capacity), 'raw_lead', _shape(...  2.28 us
    pallas_call x1, Pallas kernels, _fast(): _call(functools.partial(_first_kernel, n_e, n_d, blocks_a[1]), 'first_sen...  1.7 us
    pallas_call x2, Pallas kernels, finish(): _call(functools.partial(_finish_kernel, 1.0 / n_d, first_lane, tuple((len...  1.52 us
  transfers between devices with their start and end apart: 19, of which 8 were waited for; matrix products, arithmetic and copies ran while one was open for 3% of the time, Pallas kernels for 17%

profile of v9, /device:TPU:0, one launch (start us, length us, event | category | flops | bytes accessed | tf_op | source)
XLA Modules:
  0.0 64.4 jit_solution(8423853315375531225)
XLA Ops:
  0.6 0.0 copy-start
  0.6 1.1 %pack_tokens.1.refs_0_ = bf16[144,1152]{1,0:T(8,128)(2,1)S(1)} custom-call(s32[2,128]{1,0:T(2,128)} %bitcast.18, bf16[2,128]{1,0:T(2,128)(2,1)} %bitcast.19, bf16[128,2048]{1,0:T(8,128)(2,1)} %tok_ref.1), custom_call_target="tpu_custom_call" | custom-call | tf_op jit(solution)/shard_map/pack_tokens/pallas_call | solution.py:254
  1.8 3.0 %collective-permute-start.1 = (bf16[144,1152]{1,0:T(8,128)(2,1)S(1)}, bf16[144,1152]{1,0:T(8,128)(2,1)S(1)}, u32[]{:S(2)}, u32[]{:S(2)}) collective-permute-start(bf16[144,1152]{1,0:T(8,128)(2,1)S(1)} %pack_tokens.1.refs_0_), channel_id=1, source_target_pairs={{0,2},{1,3},{2,0},{3,1},{4,6},{5,7},{6,4},{7,5},{8,10},{9,11},{10,... | collective-permute-start | bytes 995336 | tf_op jit(solution)/shard_map/ppermute | solution.py:27
  4.8 1.0 %slice.24.refs_0_.refs_4_ = bf16[128,896]{1,0:T(8,128)(2,1)S(1)} slice(bf16[128,2048]{1,0:T(8,128)(2,1)} %tok_ref.1), slice={[0:128], [1152:2048]} | slice | bytes 458752 | tf_op jit(solution)/shard_map/slice | solution.py:267
  5.8 0.1 collective-permute-start
  5.8 6.8 %collective-permute-done.1.refs_2_ = bf16[144,1152]{1,0:T(8,128)(2,1)S(1)} collective-permute-done((bf16[144,1152]{1,0:T(8,128)(2,1)S(1)}, bf16[144,1152]{1,0:T(8,128)(2,1)S(1)}, u32[]{:S(2)}, u32[]{:S(2)}) %collective-permute-start.1) | collective-permute-done | bytes 331808 | tf_op jit(solution)/shard_map/ppermute | solution.py:27
  12.6 0.0 collective-permute-start.2
  12.6 0.0 copy-done
  12.6 0.2 activation.1.act_ref
  12.8 0.1 pad_add_fusion.where_ref
  12.9 1.7 %collective-permute-start.4 = (bf16[128,896]{1,0:T(8,128)(2,1)S(1)}, bf16[128,896]{1,0:T(8,128)(2,1)S(1)}, u32[]{:S(2)}, u32[]{:S(2)}) collective-permute-start(bf16[128,896]{1,0:T(8,128)(2,1)S(1)} %slice.24.refs_0_.refs_4_), channel_id=1, source_target_pairs={{0,2},{1,3},{2,0},{3,1},{4,6},{5,7},{6,4},{7,5},{8,10},{9,11},{10,... | collective-permute-start | bytes 688136 | tf_op jit(solution)/shard_map/ppermute | solution.py:27
  14.7 0.0 collective-permute-done.refs_1_
  14.7 0.0 collective-permute-done.2.refs_3_
  14.7 0.0 copy-start.1
  14.7 1.7 %first_send.1 = (bf16[768,512]{1,0:T(8,128)(2,1)S(1)}, bf16[384,640]{1,0:T(8,128)(2,1)S(1)}) custom-call(s32[2]{0:T(128)S(1)} %pad_add_fusion.where_ref, f32[4,96,768]{2,1,0:T(8,128)S(1)} %activation.1.act_ref, bf16[144,1152]{1,0:T(8,128)(2,1)S(1)} %pack_tokens.1.refs_0_, bf16[144,1152]{1,0:T(8,128)(2,1)S(1)} %collective-permute-done.refs_1_, ...), custom_call_target="tpu_custom_call" | custom-call | tf_op jit(solution)/shard_map/first_send/pallas_call | solution.py:329
  16.4 1.6 %collective-permute-start.6 = (bf16[384,640]{1,0:T(8,128)(2,1)S(1)}, bf16[384,640]{1,0:T(8,128)(2,1)S(1)}, u32[]{:S(2)}, u32[]{:S(2)}) collective-permute-start(bf16[384,640]{1,0:T(8,128)(2,1)S(1)} %get-tuple-element.47), channel_id=1, source_target_pairs={{0,4},{1,5},{2,6},{3,7},{4,0},{5,1},{6,2},{7,3},{8,12},{9,13},{10,... | collective-permute-start | bytes 1474568 | tf_op jit(solution)/shard_map/ppermute | solution.py:27
  17.9 0.9 %first_keep.1 = (f32[384,640]{1,0:T(8,128)S(1)}, f32[384,512]{1,0:T(8,128)S(1)}, bf16[384,512]{1,0:T(8,128)(2,1)S(1)}) custom-call(bf16[768,512]{1,0:T(8,128)(2,1)S(1)} %get-tuple-element.45.at_ref, bf16[144,1152]{1,0:T(8,128)(2,1)S(1)} %pack_tokens.1.refs_0_, bf16[144,1152]{1,0:T(8,128)(2,1)S(1)} %collective-permute-done.refs_1_, ...), custom_call_target="tpu_custom_call" | custom-call | tf_op jit(solution)/shard_map/first_keep/pallas_call | solution.py:339
  18.8 1.6 %collective-permute-start.7 = (bf16[384,512]{1,0:T(8,128)(2,1)S(1)}, bf16[384,512]{1,0:T(8,128)(2,1)S(1)}, u32[]{:S(2)}, u32[]{:S(2)}) collective-permute-start(bf16[384,512]{1,0:T(8,128)(2,1)S(1)} %get-tuple-element.62), channel_id=1, source_target_pairs={{0,8},{1,9},{2,10},{3,11},{4,12},{5,13},{6,14},{7,15},{8,0},{9,1},... | collective-permute-start | bytes 1179656 | tf_op jit(solution)/shard_map/ppermute | solution.py:27
  20.5 0.0 copy-done.1
  20.5 2.3 %raw_lead.1.raw_ref = f32[384,768]{1,0:T(8,128)S(1)} custom-call(s32[2]{0:T(128)S(1)} %pad_add_fusion.where_ref, bf16[1,768,2048]{2,1,0:T(8,128)(2,1)S(1)} %copy-done.1, bf16[144,1152]{1,0:T(8,128)(2,1)S(1)} %pack_tokens.1.refs_0_, bf16[144,1152]{1,0:T(8,128)(2,1)S(1)} %collective-permute-done.refs_1_, bf16[144,1152]{1,0:T(8,128)(2,1)S(1)} %collective-permute-done.1.refs_2_, ...), custom_call_target="tpu_custom_call" | custom-call | flops 6000000000 | tf_op jit(solution)/shard_map/raw_lead/pallas_call | solution.py:350
  22.8 0.1 collective-permute-start.3
  22.8 0.0 collective-permute-done.4.refs_2_.refs_6_
  22.9 0.5 collective-permute-start.5
  23.4 1.0 %collective-permute-done.3.refs_1_.refs_5_ = bf16[128,896]{1,0:T(8,128)(2,1)S(1)} collective-permute-done((bf16[128,896]{1,0:T(8,128)(2,1)S(1)}, bf16[128,896]{1,0:T(8,128)(2,1)S(1)}, u32[]{:S(2)}, u32[]{:S(2)}) %collective-permute-start.3) | collective-permute-done | bytes 229408 | tf_op jit(solution)/shard_map/ppermute | solution.py:27
  24.3 0.3 collective-permute-done.5.refs_3_.refs_7_
  24.7 0.6 partial_chunk.2
  25.2 0.6 partial_chunk.3
  25.8 3.5 %slot_gradients.1 = (bf16[4,96,1536]{2,1,0:T(8,128)(2,1)}, f32[4,1,128]{2,1,0:T(1,128)S(1)}) custom-call(s32[2]{0:T(128)S(1)} %pad_add_fusion.where_ref, bf16[4,96,1536]{2,1,0:T(8,128)(2,1)S(1)} %bitcast.16, bf16[1,768,2048]{2,1,0:T(8,128)(2,1)S(1)} %copy-done.1, f32[384,768]{1,0:T(8,128)S(1)} %raw_lead.1.raw_ref, bf16[144,1152]{1,0:T(8,128)(2,1)S(1)} %pack_tokens.1.refs_0_, ...), custom_call_target="tpu_custom_call" | custom-call | tf_op jit(solution)/shard_map/slot_gradients/pallas_call | solution.py:378
  29.4 0.5 collective-permute-done.7.got_ref
  29.9 0.1 sum_halves.8
  30.0 0.0 collective-permute-done.6.got_ref
  30.0 1.3 %collective-permute-start.8 = (bf16[384,512]{1,0:T(8,128)(2,1)S(1)}, bf16[384,512]{1,0:T(8,128)(2,1)S(1)}, u32[]{:S(2)}, u32[]{:S(2)}) collective-permute-start(bf16[384,512]{1,0:T(8,128)(2,1)S(1)} %get-tuple-element.64), channel_id=1, source_target_pairs={{0,4},{1,5},{2,6},{3,7},{4,0},{5,1},{6,2},{7,3},{8,12},{9,13},{10,... | collective-permute-start | bytes 1179656 | tf_op jit(solution)/shard_map/ppermute | solution.py:27
  31.3 0.1 sum_halves.7
  31.4 1.6 %collective-permute-start.9 = (bf16[192,640]{1,0:T(8,128)(2,1)S(1)}, bf16[192,640]{1,0:T(8,128)(2,1)S(1)}, u32[]{:S(2)}, u32[]{:S(2)}) collective-permute-start(bf16[192,640]{1,0:T(8,128)(2,1)S(1)} %get-tuple-element.67), channel_id=1, source_target_pairs={{0,8},{1,9},{2,10},{3,11},{4,12},{5,13},{6,14},{7,15},{8,0},{9,1},... | collective-permute-start | bytes 737288 | tf_op jit(solution)/shard_map/ppermute | solution.py:27
  33.1 2.6 %collective-permute-start.11 = (bf16[192,512]{1,0:T(8,128)(2,1)S(1)}, bf16[192,512]{1,0:T(8,128)(2,1)S(1)}, u32[]{:S(2)}, u32[]{:S(2)}) collective-permute-start(bf16[192,512]{1,0:T(8,128)(2,1)S(1)} %get-tuple-element.63), channel_id=1, source_target_pairs={{0,16},{1,17},{2,18},{3,19},{4,20},{5,21},{6,22},{7,23},{8,24},{9,... | collective-permute-start | bytes 589832 | tf_op jit(solution)/shard_map/ppermute | solution.py:27
  35.6 6.1 %all_to_all.5 = f32[4,1,128]{2,1,0:T(1,128)S(1)} all-to-all(f32[4,1,128]{2,1,0:T(1,128)S(1)} %get-tuple-element.56), channel_id=1, replica_groups=mesh['dp'=8,'expert'=4] {'expert'}, dimensions={0} | all-to-all | bytes 4096 | tf_op jit(solution)/shard_map/all_to_all | solution.py:393
  41.7 0.0 collective-permute-done.8.got_ref
  41.7 0.8 %collective-permute-start.15 = (bf16[384,384]{1,0:T(8,128)(2,1)S(1)}, bf16[384,384]{1,0:T(8,128)(2,1)S(1)}, u32[]{:S(2)}, u32[]{:S(2)}) collective-permute-start(bf16[384,384]{1,0:T(8,128)(2,1)S(1)} %get-tuple-element.79), channel_id=1, source_target_pairs={{0,4},{1,5},{2,6},{3,7},{4,0},{5,1},{6,2},{7,3},{8,12},{9,13},{10,... | collective-permute-start | bytes 884744 | tf_op jit(solution)/shard_map/ppermute | solution.py:27
  42.5 0.1 sum_halves.9
  42.6 0.9 %collective-permute-start.13 = (bf16[192,512]{1,0:T(8,128)(2,1)S(1)}, bf16[192,512]{1,0:T(8,128)(2,1)S(1)}, u32[]{:S(2)}, u32[]{:S(2)}) collective-permute-start(bf16[192,512]{1,0:T(8,128)(2,1)S(1)} %get-tuple-element.65), channel_id=1, source_target_pairs={{0,8},{1,9},{2,10},{3,11},{4,12},{5,13},{6,14},{7,15},{8,0},{9,1},... | collective-permute-start | bytes 589832 | tf_op jit(solution)/shard_map/ppermute | solution.py:27
  43.4 0.0 collective-permute-done.9.got_ref
  43.5 2.6 %collective-permute-start.10 = (bf16[96,640]{1,0:T(8,128)(2,1)S(1)}, bf16[96,640]{1,0:T(8,128)(2,1)S(1)}, u32[]{:S(2)}, u32[]{:S(2)}) collective-permute-start(bf16[96,640]{1,0:T(8,128)(2,1)S(1)} %get-tuple-element.69), channel_id=1, source_target_pairs={{0,16},{1,17},{2,18},{3,19},{4,20},{5,21},{6,22},{7,23},{8,24},{9,... | collective-permute-start | bytes 368648 | tf_op jit(solution)/shard_map/ppermute | solution.py:27
  46.1 0.0 copy-start.2
  46.1 0.0 collective-permute-done.11.got_ref
  46.1 0.1 sum_halves.11
  46.2 0.6 collective-permute-start.12
  46.8 5.1 %collective-permute-done.13.got_ref = bf16[192,512]{1,0:T(8,128)(2,1)S(1)} collective-permute-done((bf16[192,512]{1,0:T(8,128)(2,1)S(1)}, bf16[192,512]{1,0:T(8,128)(2,1)S(1)}, u32[]{:S(2)}, u32[]{:S(2)}) %collective-permute-start.13) | collective-permute-done | bytes 196640 | tf_op jit(solution)/shard_map/ppermute | solution.py:27
  52.0 0.1 collective-permute-start.14
  52.0 0.8 %collective-permute-done.12.refs_3_ = bf16[96,512]{1,0:T(8,128)(2,1)S(1)} collective-permute-done((bf16[96,512]{1,0:T(8,128)(2,1)S(1)}, bf16[96,512]{1,0:T(8,128)(2,1)S(1)}, u32[]{:S(2)}, u32[]{:S(2)}) %collective-permute-start.12) | collective-permute-done | bytes 98336 | tf_op jit(solution)/shard_map/ppermute | solution.py:27
  52.9 0.0 collective-permute-done.10.refs_1_
  52.9 0.0 collective-permute-done.15.got_ref
  52.9 0.1 sum_halves.13
  53.0 2.2 %collective-permute-start.16 = (bf16[96,384]{1,0:T(8,128)(2,1)S(1)}, bf16[96,384]{1,0:T(8,128)(2,1)S(1)}, u32[]{:S(2)}, u32[]{:S(2)}) collective-permute-start(bf16[96,384]{1,0:T(8,128)(2,1)S(1)} %get-tuple-element.84), channel_id=1, source_target_pairs={{0,16},{1,17},{2,18},{3,19},{4,20},{5,21},{6,22},{7,23},{8,24},{9,... | collective-permute-start | bytes 221192 | tf_op jit(solution)/shard_map/ppermute | solution.py:27
  55.1 0.0 collective-permute-start.17
  55.1 2.3 %collective-permute-start.18 = (bf16[96,384]{1,0:T(8,128)(2,1)S(1)}, bf16[96,384]{1,0:T(8,128)(2,1)S(1)}, u32[]{:S(2)}, u32[]{:S(2)}) collective-permute-start(bf16[96,384]{1,0:T(8,128)(2,1)S(1)} %get-tuple-element.82), channel_id=1, source_target_pairs={{0,24},{1,25},{2,26},{3,27},{4,28},{5,29},{6,30},{7,31},{8,16},{9,... | collective-permute-start | bytes 221192 | tf_op jit(solution)/shard_map/ppermute | solution.py:27
  57.4 0.0 copy-done.2
  57.4 0.6 fusion.2
  58.0 0.4 finish.2.refs_0_
  58.4 3.4 %collective-permute-done.14.refs_2_ = bf16[96,512]{1,0:T(8,128)(2,1)S(1)} collective-permute-done((bf16[96,512]{1,0:T(8,128)(2,1)S(1)}, bf16[96,512]{1,0:T(8,128)(2,1)S(1)}, u32[]{:S(2)}, u32[]{:S(2)}) %collective-permute-start.14) | collective-permute-done | bytes 98336 | tf_op jit(solution)/shard_map/ppermute | solution.py:27
  61.7 1.5 %collective-permute-done.16.refs_4_ = bf16[96,384]{1,0:T(8,128)(2,1)S(1)} collective-permute-done((bf16[96,384]{1,0:T(8,128)(2,1)S(1)}, bf16[96,384]{1,0:T(8,128)(2,1)S(1)}, u32[]{:S(2)}, u32[]{:S(2)}) %collective-permute-start.16) | collective-permute-done | bytes 73760 | tf_op jit(solution)/shard_map/ppermute | solution.py:27
  63.2 0.0 collective-permute-done.17.refs_5_
  63.2 0.0 collective-permute-done.18.refs_6_
  63.2 1.1 %finish.3 = f32[1536,128]{1,0:T(8,128)} custom-call(f32[1536,128]{1,0:T(8,128)S(1)} %finish.2.refs_0_, f32[96,512]{1,0:T(8,128)S(1)} %get-tuple-element.75.refs_1_, bf16[96,512]{1,0:T(8,128)(2,1)S(1)} %collective-permute-done.14.refs_2_, f32[96,384]{1,0:T(8,128)S(1)} %get-tuple-element.80.refs_3_, bf16[96,384]{1,0:T(8,128)(2,1)S(1)} %collective-permute-done.16.refs_4_, ...), custom_call_target="tpu_custom_call" | custom-call | tf_op jit(solution)/shard_map/finish/pallas_call | solution.py:411
  (4 shorter events, 0.1 us)
Async XLA Ops:
  0.6 12.0 %copy-start = (bf16[1,1,4,96,1536]{4,3,2,1,0:T(8,128)(2,1)S(1)}, bf16[1,1,4,96,1536]{4,3,2,1,0:T(8,128)(2,1)}, u32[]{:S(2)}) copy-start(bf16[1,1,4,96,1536]{4,3,2,1,0:T(8,128)(2,1)} %param.9) | copy-start | bytes 3538948
  1.8 10.8 %collective-permute-start.1 = (bf16[144,1152]{1,0:T(8,128)(2,1)S(1)}, bf16[144,1152]{1,0:T(8,128)(2,1)S(1)}, u32[]{:S(2)}, u32[]{:S(2)}) collective-permute-start(bf16[144,1152]{1,0:T(8,128)(2,1)S(1)} %pack_tokens.1.refs_0_), channel_id=1, source_target_pairs={{0,2},{1,3},{2,0},{3,1},{4,6},{5,7},{6,4},{7,5},{8,10},{9,11},{10,... | collective-permute-start | bytes 995336 | tf_op jit(solution)/shard_map/ppermute | solution.py:27
  5.8 8.9 %collective-permute-start = (bf16[144,1152]{1,0:T(8,128)(2,1)S(1)}, bf16[144,1152]{1,0:T(8,128)(2,1)S(1)}, u32[]{:S(2)}, u32[]{:S(2)}) collective-permute-start(bf16[144,1152]{1,0:T(8,128)(2,1)S(1)} %pack_tokens.1.refs_0_), channel_id=1, source_target_pairs={{0,1},{1,0},{2,3},{3,2},{4,5},{5,4},{6,7},{7,6},{8,9},{9,8},{10,11... | collective-permute-start | bytes 995336 | tf_op jit(solution)/shard_map/ppermute | solution.py:27
  12.6 2.1 %collective-permute-start.2 = (bf16[144,1152]{1,0:T(8,128)(2,1)S(1)}, bf16[144,1152]{1,0:T(8,128)(2,1)S(1)}, u32[]{:S(2)}, u32[]{:S(2)}) collective-permute-start(bf16[144,1152]{1,0:T(8,128)(2,1)S(1)} %collective-permute-done.1.refs_2_), channel_id=1, source_target_pairs={{0,1},{1,0},{2,3},{3,2},{4,5},{5,4},{6,7},{7,6},{8,9},{9,8},{10,11... | collective-permute-start | bytes 995336 | tf_op jit(solution)/shard_map/ppermute | solution.py:27
  12.9 9.9 %collective-permute-start.4 = (bf16[128,896]{1,0:T(8,128)(2,1)S(1)}, bf16[128,896]{1,0:T(8,128)(2,1)S(1)}, u32[]{:S(2)}, u32[]{:S(2)}) collective-permute-start(bf16[128,896]{1,0:T(8,128)(2,1)S(1)} %slice.24.refs_0_.refs_4_), channel_id=1, source_target_pairs={{0,2},{1,3},{2,0},{3,1},{4,6},{5,7},{6,4},{7,5},{8,10},{9,11},{10,... | collective-permute-start | bytes 688136 | tf_op jit(solution)/shard_map/ppermute | solution.py:27
  14.7 5.8 %copy-start.1 = (bf16[1,768,2048]{2,1,0:T(8,128)(2,1)S(1)}, bf16[1,768,2048]{2,1,0:T(8,128)(2,1)}, u32[]{:S(2)}) copy-start(bf16[1,768,2048]{2,1,0:T(8,128)(2,1)} %w_ref.3) | copy-start | bytes 9437188
  16.4 13.6 %collective-permute-start.6 = (bf16[384,640]{1,0:T(8,128)(2,1)S(1)}, bf16[384,640]{1,0:T(8,128)(2,1)S(1)}, u32[]{:S(2)}, u32[]{:S(2)}) collective-permute-start(bf16[384,640]{1,0:T(8,128)(2,1)S(1)} %get-tuple-element.47), channel_id=1, source_target_pairs={{0,4},{1,5},{2,6},{3,7},{4,0},{5,1},{6,2},{7,3},{8,12},{9,13},{10,... | collective-permute-start | bytes 1474568 | tf_op jit(solution)/shard_map/ppermute | solution.py:27
  18.8 11.0 %collective-permute-start.7 = (bf16[384,512]{1,0:T(8,128)(2,1)S(1)}, bf16[384,512]{1,0:T(8,128)(2,1)S(1)}, u32[]{:S(2)}, u32[]{:S(2)}) collective-permute-start(bf16[384,512]{1,0:T(8,128)(2,1)S(1)} %get-tuple-element.62), channel_id=1, source_target_pairs={{0,8},{1,9},{2,10},{3,11},{4,12},{5,13},{6,14},{7,15},{8,0},{9,1},... | collective-permute-start | bytes 1179656 | tf_op jit(solution)/shard_map/ppermute | solution.py:27
  22.8 1.6 %collective-permute-start.3 = (bf16[128,896]{1,0:T(8,128)(2,1)S(1)}, bf16[128,896]{1,0:T(8,128)(2,1)S(1)}, u32[]{:S(2)}, u32[]{:S(2)}) collective-permute-start(bf16[128,896]{1,0:T(8,128)(2,1)S(1)} %slice.24.refs_0_.refs_4_), channel_id=1, source_target_pairs={{0,1},{1,0},{2,3},{3,2},{4,5},{5,4},{6,7},{7,6},{8,9},{9,8},{10,11... | collective-permute-start | bytes 688136 | tf_op jit(solution)/shard_map/ppermute | solution.py:27
  22.9 1.8 %collective-permute-start.5 = (bf16[128,896]{1,0:T(8,128)(2,1)S(1)}, bf16[128,896]{1,0:T(8,128)(2,1)S(1)}, u32[]{:S(2)}, u32[]{:S(2)}) collective-permute-start(bf16[128,896]{1,0:T(8,128)(2,1)S(1)} %collective-permute-done.4.refs_2_.refs_6_), channel_id=1, source_target_pairs={{0,1},{1,0},{2,3},{3,2},{4,5},{5,4},{6,7},{7,6},{8,9},{9,8},{10,11... | collective-permute-start | bytes 688136 | tf_op jit(solution)/shard_map/ppermute | solution.py:27
  30.0 11.7 %collective-permute-start.8 = (bf16[384,512]{1,0:T(8,128)(2,1)S(1)}, bf16[384,512]{1,0:T(8,128)(2,1)S(1)}, u32[]{:S(2)}, u32[]{:S(2)}) collective-permute-start(bf16[384,512]{1,0:T(8,128)(2,1)S(1)} %get-tuple-element.64), channel_id=1, source_target_pairs={{0,4},{1,5},{2,6},{3,7},{4,0},{5,1},{6,2},{7,3},{8,12},{9,13},{10,... | collective-permute-start | bytes 1179656 | tf_op jit(solution)/shard_map/ppermute | solution.py:27
  31.4 12.0 %collective-permute-start.9 = (bf16[192,640]{1,0:T(8,128)(2,1)S(1)}, bf16[192,640]{1,0:T(8,128)(2,1)S(1)}, u32[]{:S(2)}, u32[]{:S(2)}) collective-permute-start(bf16[192,640]{1,0:T(8,128)(2,1)S(1)} %get-tuple-element.67), channel_id=1, source_target_pairs={{0,8},{1,9},{2,10},{3,11},{4,12},{5,13},{6,14},{7,15},{8,0},{9,1},... | collective-permute-start | bytes 737288 | tf_op jit(solution)/shard_map/ppermute | solution.py:27
  33.1 13.1 %collective-permute-start.11 = (bf16[192,512]{1,0:T(8,128)(2,1)S(1)}, bf16[192,512]{1,0:T(8,128)(2,1)S(1)}, u32[]{:S(2)}, u32[]{:S(2)}) collective-permute-start(bf16[192,512]{1,0:T(8,128)(2,1)S(1)} %get-tuple-element.63), channel_id=1, source_target_pairs={{0,16},{1,17},{2,18},{3,19},{4,20},{5,21},{6,22},{7,23},{8,24},{9,... | collective-permute-start | bytes 589832 | tf_op jit(solution)/shard_map/ppermute | solution.py:27
  41.7 11.1 %collective-permute-start.15 = (bf16[384,384]{1,0:T(8,128)(2,1)S(1)}, bf16[384,384]{1,0:T(8,128)(2,1)S(1)}, u32[]{:S(2)}, u32[]{:S(2)}) collective-permute-start(bf16[384,384]{1,0:T(8,128)(2,1)S(1)} %get-tuple-element.79), channel_id=1, source_target_pairs={{0,4},{1,5},{2,6},{3,7},{4,0},{5,1},{6,2},{7,3},{8,12},{9,13},{10,... | collective-permute-start | bytes 884744 | tf_op jit(solution)/shard_map/ppermute | solution.py:27
  42.6 9.3 %collective-permute-start.13 = (bf16[192,512]{1,0:T(8,128)(2,1)S(1)}, bf16[192,512]{1,0:T(8,128)(2,1)S(1)}, u32[]{:S(2)}, u32[]{:S(2)}) collective-permute-start(bf16[192,512]{1,0:T(8,128)(2,1)S(1)} %get-tuple-element.65), channel_id=1, source_target_pairs={{0,8},{1,9},{2,10},{3,11},{4,12},{5,13},{6,14},{7,15},{8,0},{9,1},... | collective-permute-start | bytes 589832 | tf_op jit(solution)/shard_map/ppermute | solution.py:27
  43.5 9.4 %collective-permute-start.10 = (bf16[96,640]{1,0:T(8,128)(2,1)S(1)}, bf16[96,640]{1,0:T(8,128)(2,1)S(1)}, u32[]{:S(2)}, u32[]{:S(2)}) collective-permute-start(bf16[96,640]{1,0:T(8,128)(2,1)S(1)} %get-tuple-element.69), channel_id=1, source_target_pairs={{0,16},{1,17},{2,18},{3,19},{4,20},{5,21},{6,22},{7,23},{8,24},{9,... | collective-permute-start | bytes 368648 | tf_op jit(solution)/shard_map/ppermute | solution.py:27
  46.1 11.3 %copy-start.2 = (s32[128,2]{0,1:T(2,128)S(1)}, s32[128,2]{0,1:T(2,128)}, u32[]{:S(2)}) copy-start(s32[128,2]{0,1:T(2,128)} %param.6) | copy-start | bytes 3076
  46.2 6.7 %collective-permute-start.12 = (bf16[96,512]{1,0:T(8,128)(2,1)S(1)}, bf16[96,512]{1,0:T(8,128)(2,1)S(1)}, u32[]{:S(2)}, u32[]{:S(2)}) collective-permute-start(bf16[96,512]{1,0:T(8,128)(2,1)S(1)} %get-tuple-element.73), channel_id=1, source_target_pairs={{0,4},{1,5},{2,6},{3,7},{4,0},{5,1},{6,2},{7,3},{8,12},{9,13},{10,... | collective-permute-start | bytes 294920 | tf_op jit(solution)/shard_map/ppermute | solution.py:27
  52.0 9.8 %collective-permute-start.14 = (bf16[96,512]{1,0:T(8,128)(2,1)S(1)}, bf16[96,512]{1,0:T(8,128)(2,1)S(1)}, u32[]{:S(2)}, u32[]{:S(2)}) collective-permute-start(bf16[96,512]{1,0:T(8,128)(2,1)S(1)} %get-tuple-element.76), channel_id=1, source_target_pairs={{0,16},{1,17},{2,18},{3,19},{4,20},{5,21},{6,22},{7,23},{8,24},{9,... | collective-permute-start | bytes 294920 | tf_op jit(solution)/shard_map/ppermute | solution.py:27
  53.0 10.3 %collective-permute-start.16 = (bf16[96,384]{1,0:T(8,128)(2,1)S(1)}, bf16[96,384]{1,0:T(8,128)(2,1)S(1)}, u32[]{:S(2)}, u32[]{:S(2)}) collective-permute-start(bf16[96,384]{1,0:T(8,128)(2,1)S(1)} %get-tuple-element.84), channel_id=1, source_target_pairs={{0,16},{1,17},{2,18},{3,19},{4,20},{5,21},{6,22},{7,23},{8,24},{9,... | collective-permute-start | bytes 221192 | tf_op jit(solution)/shard_map/ppermute | solution.py:27
  55.1 8.1 %collective-permute-start.17 = (bf16[96,384]{1,0:T(8,128)(2,1)S(1)}, bf16[96,384]{1,0:T(8,128)(2,1)S(1)}, u32[]{:S(2)}, u32[]{:S(2)}) collective-permute-start(bf16[96,384]{1,0:T(8,128)(2,1)S(1)} %get-tuple-element.83), channel_id=1, source_target_pairs={{0,8},{1,9},{2,10},{3,11},{4,12},{5,13},{6,14},{7,15},{8,0},{9,1},... | collective-permute-start | bytes 221192 | tf_op jit(solution)/shard_map/ppermute | solution.py:27
  55.1 8.1 %collective-permute-start.18 = (bf16[96,384]{1,0:T(8,128)(2,1)S(1)}, bf16[96,384]{1,0:T(8,128)(2,1)S(1)}, u32[]{:S(2)}, u32[]{:S(2)}) collective-permute-start(bf16[96,384]{1,0:T(8,128)(2,1)S(1)} %get-tuple-element.82), channel_id=1, source_target_pairs={{0,24},{1,25},{2,26},{3,27},{4,28},{5,29},{6,30},{7,31},{8,16},{9,... | collective-permute-start | bytes 221192 | tf_op jit(solution)/shard_map/ppermute | solution.py:27
